TPU v7x, 512 devices: a whole 4x4x16 slice. The times are simulated.
512 devices in a mesh: rep: 32 (over z_hi, x, core), grp: 16 (over y, z_lo).
Axes of the slice: x: 4, y: 4, z: 16 (z_hi: 4, z_lo: 4; z = z_hi * 4 + z_lo), core: 2. Of those that a mesh axis runs over, the one named last changes fastest.
Arguments:
- tokens: bfloat16 [98304, 2048], P(('rep', 'grp')), may hold values from -24 to 24
- norm_gain: float32 [2048], replicated, may hold values from 0.5 to 1.5
- weight_codes: int32 [2048, 512], P('grp'), may hold values from -127 to 127
- block_scales: float32 [16, 512], P('grp'), may hold values from 0.00013258251 to 0.00053033006
- key_grad: bfloat16 [98304, 512], P(('rep', 'grp')), may hold values from -6 to 6
Outputs:
- keys: bfloat16 [98304, 512], P(('rep', 'grp'))
- tokens_grad: bfloat16 [98304, 2048], P(('rep', 'grp'))
- weight_grad: float32 [2048, 512], P('grp')
- gain_grad: float32 [2048], replicated
Inputs may be any that keep to these rules, and one draw needn't show every extreme that they name: `weight_codes`: signed 8-bit codes.
All inputs are finite; a program needn't handle non-finite values.
Results may differ from a plain program's by a relative error of at most 0.0057.
Values may be sent and summed in bfloat16 or wider, within the bound.
No kernel may reach another device: no remote copies, remote signals or barrier semaphores. Data moves between devices by JAX's collectives and lax.ppermute only.
A program may use at most 64 MiB of HBM per device.

v0:
```python
import jax
import jax.numpy as jnp
from jax import lax
from jax.sharding import PartitionSpec as P

eps = 1e-05


def local(tokens, norm_gain, weight_codes, block_scales, key_grad):
    groups = lax.axis_size("grp")
    replicas = lax.axis_size("rep")
    devices = groups * replicas
    wide = tokens.astype(jnp.float32)
    inv_rms = lax.rsqrt(jnp.mean(wide * wide, axis=1, keepdims=True) + eps)
    unit = wide * inv_rms
    normed = (unit * norm_gain).astype(jnp.bfloat16)
    local_rows = weight_codes.shape[0]
    blocks = block_scales.shape[0]
    width = weight_codes.shape[1]
    weight = (
        (
            weight_codes.astype(jnp.float32).reshape(blocks, local_rows // blocks, width)
            * block_scales[:, None, :]
        )
        .reshape(local_rows, width)
        .astype(jnp.bfloat16)
    )
    columns = normed
    keys_wide = jnp.dot(
        columns,
        lax.all_gather(weight, "grp", axis=0, tiled=True),
        preferred_element_type=jnp.float32,
    )
    normed_grad = lax.dot_general(
        key_grad,
        lax.all_gather(weight, "grp", axis=0, tiled=True),
        (((1,), (1,)), ((), ())),
        preferred_element_type=jnp.float32,
    )
    keys = keys_wide.astype(jnp.bfloat16)
    gain_part = jnp.sum(normed_grad * unit, axis=0)
    columns = normed
    group_grad = lax.psum_scatter(
        lax.dot_general(
            columns, key_grad, (((0,), (0,)), ((), ())), preferred_element_type=jnp.float32
        ),
        "grp",
        scatter_dimension=0,
        tiled=True,
    )
    gain_total = lax.psum(gain_part, ("rep", "grp"))
    weight_total = lax.psum(group_grad, "rep")
    weight_grad = weight_total / devices
    gain_grad = gain_total / devices
    scaled_grad = normed_grad * norm_gain
    tokens_grad = (
        inv_rms * (scaled_grad - unit * jnp.mean(scaled_grad * unit, axis=1, keepdims=True))
    ).astype(jnp.bfloat16)
    return (keys, tokens_grad, weight_grad, gain_grad)


def solution(mesh):
    in_specs = (
        P(("rep", "grp"), None),
        P(),
        P("grp", None),
        P("grp", None),
        P(("rep", "grp"), None),
    )
    out_specs = (P(("rep", "grp"), None), P(("rep", "grp"), None), P("grp", None), P())
    return jax.shard_map(local, mesh=mesh, in_specs=in_specs, out_specs=out_specs, check_vma=False)
```

profile of v0, /device:TPU:1, one launch (start us, length us, event | category | flops | bytes accessed | tf_op | source)
XLA Modules:
  0.0 573.4 jit_solution(13232327707817529366)
XLA Ops:
  7.2 0.0 copy-start
  7.2 0.0 copy-start.1
  7.2 0.0 all-gather.2.cloned.1.call-start
  7.2 1.7 multiply_convert_fusion
  8.9 0.0 all-gather.2.cloned.1.call-update
  9.0 0.0 reduce-scatter.2.cloned.1.call-start
  9.0 1.4 fusion.10
  10.4 0.0 copy-done
  10.4 0.0 copy-done.1
  10.4 3.5 fusion.11
  13.9 0.0 reduce-scatter.2.cloned.1.call-update
  13.9 0.0 all-reduce.2.cloned.1.call-start
  14.0 85.1 %all-gather.2.cloned.1.call-done = bf16[2048,512]{1,0:T(8,128)(2,1)} async-done(((bf16[128,512]{1,0:T(8,128)(2,1)}), bf16[2048,512]{1,0:T(8,128)(2,1)}) %all-gather.2.cloned.1.call-update) | async-done | bytes 2097168 | tf_op jit(solution)/shard_map/all_gather | solution.py:31
  99.1 0.0 copy-done.2
  99.1 2.6 fusion.9
  101.7 1.3 fusion.8
  103.0 112.4 %reduce-scatter.2.cloned.1.call-done = f32[128,512]{1,0:T(8,128)} async-done(((f32[2048,512]{1,0:T(8,128)}), f32[128,512]{1,0:T(8,128)}) %reduce-scatter.2.cloned.1.call-update) | async-done | bytes 262160 | tf_op jit(solution)/shard_map/reduce_scatter | solution.py:43
  215.3 0.0 all-reduce.2.cloned.1.call-update
  215.4 0.0 copy-done.3
  215.4 1.3 convolution_convert_fusion
  216.7 106.3 %psum.15 = f32[2048]{0:T(1024)S(1)} all-reduce(f32[2048]{0:T(1024)S(1)} %get-tuple-element.4), channel_id=1, replica_groups=mesh['rep'=32,'grp'=16] {'rep','grp'}, use_global_device_ids=true, to_apply=%region_5.0 | all-reduce | flops 2048 | bytes 16384 | tf_op jit(solution)/shard_map/psum | solution.py:51
  323.1 0.6 broadcast_multiply_fusion.1
  323.7 241.5 %all-reduce.2.cloned.1.call-done = f32[128,512]{1,0:T(8,128)} async-done(((f32[128,512]{1,0:T(8,128)}), f32[128,512]{1,0:T(8,128)}) %all-reduce.2.cloned.1.call-update) | async-done | bytes 262160 | tf_op jit(solution)/shard_map/psum | solution.py:52
  565.2 1.7 broadcast_multiply_fusion
  (4 shorter events, 0.0 us)
Async XLA Ops:
  7.2 3.2 copy-start
  7.2 3.2 copy-start.1
  7.2 91.9 %all-gather.2.cloned.1.call-start = ((), (), s32[]{:S(2)}) async-start(), calls=%async_computation.1 | async-start | bytes 2228224 | tf_op jit(solution)/shard_map/all_gather | solution.py:31
  9.0 206.4 %reduce-scatter.2.cloned.1.call-start = ((), (), s32[]{:S(2)}) async-start(), calls=%async_computation.2 | async-start | bytes 4456448 | tf_op jit(solution)/shard_map/reduce_scatter | solution.py:43
  13.9 85.2 %copy-start.2 = (f32[2048]{0:T(1024)S(1)}, f32[2048]{0:T(1024)}, u32[]{:S(2)}) copy-start(f32[2048]{0:T(1024)} %param.6) | copy-start | bytes 24580
  13.9 551.2 %all-reduce.2.cloned.1.call-start = ((), (), s32[]{:S(2)}) async-start(), calls=%async_computation.3 | async-start | bytes 524288 | tf_op jit(solution)/shard_map/psum | solution.py:52
  101.7 113.7 %copy-start.3 = (bf16[2048,512]{1,0:T(8,128)(2,1)S(1)}, bf16[2048,512]{1,0:T(8,128)(2,1)}, u32[]{:S(2)}) copy-start(bf16[2048,512]{1,0:T(8,128)(2,1)} %all-gather.2.cloned.1.call-done) | copy-start | bytes 6291460
Sparse Core Ops, SparseCore 0:
  10.7 88.3 all-gather.1
  101.9 113.3 reduce-scatter.1
  218.2 346.8 all-reduce.1
where the time goes:
time: 574 us; the launch traced here: 573 us
  waiting for transfers between devices  439 us (76%)
  blocking collectives  106 us (18%)
  between operations  13.8 us (2%)
  matrix products  7.38 us (1%)
  other arithmetic  6.65 us (1%)
    psum x1, waiting for transfers between devices, local(): weight_total = lax.psum(group_grad, 'rep')  242 us
    reduce_scatter x1, waiting for transfers between devices, local(): lax.psum_scatter(lax.dot_general(columns, key_grad, (((0,), (0,)), ((), (...  112 us
    psum x1, blocking collectives, local(): gain_total = lax.psum(gain_part, ('rep', 'grp'))  106 us
    all_gather x1, waiting for transfers between devices, local(): lax.all_gather(weight, 'grp', axis=0, tiled=True)  85.1 us
  transfers between devices with their start and end apart: 3, of which 3 were waited for; matrix products, arithmetic and copies ran while one was open for 2% of the time, Pallas kernels for 0%

commit v1 on v0

v1 whole, which is shorter than its diff:
```python
import jax
import jax.numpy as jnp
from jax import lax
from jax.sharding import Mesh, PartitionSpec as P

eps = 1e-05
AXES = ("zh", "x", "core", "y", "zl")
SIZES = (4, 4, 2, 4, 4)
Z = ("zh", "zl")
f32, bf16 = jnp.float32, jnp.bfloat16


def exchange(blocks, axes):
    return lax.all_to_all(blocks, axes, 0, 0, tiled=False)


def everywhere(block, axes):
    peers = lax.axis_size(axes)
    return exchange(jnp.broadcast_to(block[None], (peers,) + block.shape), axes)


def swap(block):
    return lax.ppermute(block, "core", [(0, 1), (1, 0)])


def along_z(block, by_core):
    pairs = []
    for core in range(2):
        for z in range(16):
            target = (z + by_core[core]) % 16
            pairs.append(((z // 4 * 2 + core) * 4 + z % 4, (target // 4 * 2 + core) * 4 + target % 4))
    return lax.ppermute(block, ("zh", "core", "zl"), pairs)


def local(tokens, norm_gain, weight_codes, block_scales, key_grad):
    core = lax.axis_index("core")
    x = lax.axis_index("x")
    zl = lax.axis_index("zl")
    devices = 512
    half = 256
    wide = tokens.astype(f32)
    inv_rms = lax.rsqrt(jnp.mean(wide * wide, axis=1, keepdims=True) + eps)
    unit = wide * inv_rms
    normed = (unit * norm_gain).astype(bf16)

    def columns(array, which):
        return lax.dynamic_slice_in_dim(array, which * half, half, 1)

    def product(which):
        part = lax.dot_general(
            normed, columns(key_grad, which), (((0,), (0,)), ((), ())), preferred_element_type=f32
        )
        return part.reshape(4, 4, 4, 32, half).transpose(0, 2, 1, 3, 4).reshape(16, 4, 32, half)

    theirs = product(1 - core).astype(bf16)
    got = swap(theirs)
    codes = columns(weight_codes, core).astype(f32)
    weight = (codes * columns(block_scales, core)).astype(bf16)
    weight, _ = lax.optimization_barrier((weight, theirs))
    shard_y = everywhere(weight, "y")

    pair = (product(core) + got.astype(f32)).astype(bf16)
    square = exchange(pair, ("y", "x"))

    below = along_z(shard_y, (1, 1))
    above = along_z(shard_y, (-1, -1))
    across = along_z(shard_y, (2, -2))
    stack = jnp.stack([shard_y, above, across, below])

    partial = jnp.sum(square.astype(f32), axis=0)
    y = lax.axis_index("y")
    rows = lax.dynamic_slice(stack, (0, y, x * 32, 0), (4, 1, 32, half))[:, 0]
    mine = jnp.roll(rows, zl, axis=0)
    gain_part = jnp.sum(mine.astype(f32) * partial, axis=2)
    high = gain_part.astype(bf16)
    low = (gain_part - high.astype(f32)).astype(bf16)
    extra = jnp.zeros((32, 128), bf16).at[:, 0:4].set(high.T).at[:, 4:8].set(low.T)
    payload = jnp.concatenate(
        [partial.astype(bf16), jnp.broadcast_to(extra[None], (4, 32, 128))], axis=2
    )
    line = exchange(jnp.broadcast_to(payload[None], (4, 4, 32, 384)).reshape(16, 32, 384), Z)
    total = jnp.sum(line.astype(f32), axis=0)
    gain_rows = (total[:, 256:260] + total[:, 260:264]).T
    gain_all = everywhere(jnp.pad(gain_rows, ((0, 4), (0, 96))), ("y", "x", "core"))
    rows_all = everywhere(total[:, :256].astype(bf16), ("x", "core"))
    weight_grad = (
        rows_all.reshape(4, 2, 32, half).transpose(0, 2, 1, 3).reshape(128, 512).astype(f32) / devices
    )
    gain_sum = gain_all[:, :4, :32].reshape(4, 4, 2, 4, 32).sum(2)
    gain_grad = gain_sum.transpose(0, 2, 1, 3).reshape(2048) / (norm_gain * devices)

    other = swap(stack)
    left = jnp.where(core == 0, stack, other)
    right = jnp.where(core == 0, other, stack)
    whole = jnp.concatenate([left, right], axis=3)
    full = jnp.roll(whole, zl, axis=0).transpose(1, 0, 2, 3).reshape(2048, 512)
    keys = jnp.dot(normed, full, preferred_element_type=f32).astype(bf16)
    normed_grad = lax.dot_general(
        key_grad, full, (((1,), (1,)), ((), ())), preferred_element_type=f32
    )
    scaled_grad = normed_grad * norm_gain
    tokens_grad = (
        inv_rms * (scaled_grad - unit * jnp.mean(scaled_grad * unit, axis=1, keepdims=True))
    ).astype(bf16)
    return (keys, tokens_grad, weight_grad, gain_grad)


def solution(mesh):
    fine = Mesh(mesh.devices.reshape(SIZES), AXES)
    everyone = P(AXES, None)
    group = P(("y", "zl"), None)
    in_specs = (everyone, P(), group, group, everyone)
    out_specs = (everyone, everyone, group, P())
    return jax.shard_map(local, mesh=fine, in_specs=in_specs, out_specs=out_specs, check_vma=False)
```

time: 574 us -> 133 us (0.23)
  waiting for transfers between devices: 439 us -> 47 us
  blocking collectives: 106 us -> 9.05 us
  starting transfers between devices: 0.12 us -> 53.5 us
  between operations: 13.8 us -> 1 us
  other arithmetic: 6.65 us -> 13.2 us
    psum x1 -> x0, waiting for transfers between devices: 242 us -> none  [local(): weight_total = lax.psum(group_grad, 'rep')]
    reduce_scatter x1 -> x0, waiting for transfers between devices: 112 us -> none  [local(): lax.psum_scatter(lax.dot_general(columns, key_grad, (((0,), (0,)), ((), (...]
    psum x1 -> x0, blocking collectives: 106 us -> none  [local(): gain_total = lax.psum(gain_part, ('rep', 'grp'))]
    all_gather x1 -> x0, waiting for transfers between devices: 85.1 us -> none  [local(): lax.all_gather(weight, 'grp', axis=0, tiled=True)]
    all_to_all x0 -> x4, waiting for transfers between devices: none -> 38.2 us  [exchange(): return lax.all_to_all(blocks, axes, 0, 0, tiled=False)]
    all_to_all x0 -> x4, starting transfers between devices: none -> 29.7 us  [exchange(): return lax.all_to_all(blocks, axes, 0, 0, tiled=False)]
    ppermute x0 -> x5, starting transfers between devices: none -> 23.7 us  [the longest x3 13 us: along_z(): return lax.ppermute(block, ('zh', 'core', 'zl'), pairs)]
    all_to_all x0 -> x1, blocking collectives: none -> 9.05 us  [exchange(): return lax.all_to_all(blocks, axes, 0, 0, tiled=False)]
  transfers between devices with their start and end apart: 3 -> 9, of which waited for: 3 -> 6; matrix products, arithmetic and copies ran while one was open for 2% -> 9% of each run, Pallas kernels for 0% -> 0%
where the time goes in v1:
time: 133 us; the launch traced here: 132 us
  starting transfers between devices  53.5 us (40%)
  waiting for transfers between devices  47 us (35%)
  other arithmetic  13.2 us (10%)
  blocking collectives  9.05 us (7%)
  matrix products  4.6 us (3%)
  local copies, waits for them, and re-layouts  3.71 us (3%)
    all_to_all x4, waiting for transfers between devices, exchange(): return lax.all_to_all(blocks, axes, 0, 0, tiled=False)  38.2 us
    all_to_all x4, starting transfers between devices, exchange(): return lax.all_to_all(blocks, axes, 0, 0, tiled=False)  29.7 us
    ppermute x3, starting transfers between devices, along_z(): return lax.ppermute(block, ('zh', 'core', 'zl'), pairs)  13 us
    ppermute x2, starting transfers between devices, swap(): return lax.ppermute(block, 'core', [(0, 1), (1, 0)])  10.7 us
    all_to_all x1, blocking collectives, exchange(): return lax.all_to_all(blocks, axes, 0, 0, tiled=False)  9.05 us
    ppermute x3, waiting for transfers between devices, along_z(): return lax.ppermute(block, ('zh', 'core', 'zl'), pairs)  8.78 us
    convert_element_type x1, other arithmetic, local(): pair = (product(core) + got.astype(f32)).astype(bf16)  2.74 us
  transfers between devices with their start and end apart: 9, of which 6 were waited for; matrix products, arithmetic and copies ran while one was open for 9% of the time, Pallas kernels for 0%

profile of v1, /device:TPU:1, one launch (start us, length us, event | category | flops | bytes accessed | tf_op | source)
XLA Modules:
  0.0 132.0 jit_solution(8154599617141548080)
XLA Ops:
  0.7 1.4 %fusion.13 = f32[192]{0:T(256)S(1)} fusion(bf16[192,2048]{1,0:T(8,128)(2,1)} %param.9), kind=kLoop, calls=%fused_computation.23 | loop fusion | flops 1179456 | bytes 787200 | tf_op jit(solution)/shard_map/reduce_sum | solution.py:42
  2.1 1.7 %convolution_convert_fusion = bf16[2048,256]{1,0:T(8,128)(2,1)S(1)} fusion(bf16[192,512]{1,0:T(8,128)(2,1)S(1)} %copy-done, s32[]{:T(128)S(6)} %select_n.47, bf16[192,2048]{1,0:T(8,128)(2,1)} %param.9, f32[2048]{0:T(1024)} %param.10, f32[192]{0:T(256)S(1)} %add_rsqrt_fusion), kind=kOutput, calls=%fused_computation.4 | convolution fusion | flops 203423744 | bytes 1942532 | tf_op jit(solution)/shard_map/dot_general | solution.py:50
  3.9 8.8 %collective-permute-start.4 = (bf16[16,4,32,256]{3,2,1,0:T(8,128)(2,1)S(1)}, bf16[16,4,32,256]{3,2,1,0:T(8,128)(2,1)}, u32[]{:S(2)}, u32[]{:S(2)}) collective-permute-start(bf16[16,4,32,256]{3,2,1,0:T(8,128)(2,1)S(1)} %bitcast.63), channel_id=1, source_target_pairs={{0,16},{16,0},{1,17},{17,1},{2,18},{18,2},{3,19},{19,3},{4,20},{20... | collective-permute-start | bytes 3145736 | tf_op jit(solution)/shard_map/ppermute | solution.py:23
  12.8 9.1 %all_to_all.25 = bf16[4,128,256]{2,1,0:T(8,128)(2,1)S(1)} all-to-all(bf16[4,128,256]{2,1,0:T(8,128)(2,1)S(1)} %broadcast_in_dim.12), channel_id=1, replica_groups=mesh['zh'=4,'x'=4,'core'=2,'y'=4,'zl'=4] {'y'}, dimensions={0} | all-to-all | bytes 524288 | tf_op jit(solution)/shard_map/all_to_all | solution.py:14
  21.9 1.9 %collective-permute-start.2 = (bf16[4,128,256]{2,1,0:T(8,128)(2,1)S(1)}, bf16[4,128,256]{2,1,0:T(8,128)(2,1)S(1)}, u32[]{:S(2)}, u32[]{:S(2)}) collective-permute-start(bf16[4,128,256]{2,1,0:T(8,128)(2,1)S(1)} %all_to_all.25), channel_id=1, source_target_pairs={{0,1},{1,2},{2,3},{3,128},{128,129},{129,130},{130,131},{131,256},... | collective-permute-start | bytes 786440 | tf_op jit(solution)/shard_map/ppermute | solution.py:32
  23.8 8.5 %collective-permute-start.1 = (bf16[4,128,256]{2,1,0:T(8,128)(2,1)S(1)}, bf16[4,128,256]{2,1,0:T(8,128)(2,1)S(1)}, u32[]{:S(2)}, u32[]{:S(2)}) collective-permute-start(bf16[4,128,256]{2,1,0:T(8,128)(2,1)S(1)} %all_to_all.25), channel_id=1, source_target_pairs={{0,2},{1,3},{2,128},{3,129},{128,130},{129,131},{130,256},{131,257... | collective-permute-start | bytes 786440 | tf_op jit(solution)/shard_map/ppermute | solution.py:32
  32.3 2.6 %collective-permute-start = (bf16[4,128,256]{2,1,0:T(8,128)(2,1)S(1)}, bf16[4,128,256]{2,1,0:T(8,128)(2,1)S(1)}, u32[]{:S(2)}, u32[]{:S(2)}) collective-permute-start(bf16[4,128,256]{2,1,0:T(8,128)(2,1)S(1)} %all_to_all.25), channel_id=1, source_target_pairs={{0,387},{1,0},{2,1},{3,2},{128,3},{129,128},{130,129},{131,130},{2... | collective-permute-start | bytes 786440 | tf_op jit(solution)/shard_map/ppermute | solution.py:32
  35.0 5.0 %collective-permute-done.1 = bf16[4,128,256]{2,1,0:T(8,128)(2,1)S(1)} collective-permute-done((bf16[4,128,256]{2,1,0:T(8,128)(2,1)S(1)}, bf16[4,128,256]{2,1,0:T(8,128)(2,1)S(1)}, u32[]{:S(2)}, u32[]{:S(2)}) %collective-permute-start.1) | collective-permute-done | bytes 262176 | tf_op jit(solution)/shard_map/ppermute | solution.py:32
  40.0 3.8 %collective-permute-done = bf16[4,128,256]{2,1,0:T(8,128)(2,1)S(1)} collective-permute-done((bf16[4,128,256]{2,1,0:T(8,128)(2,1)S(1)}, bf16[4,128,256]{2,1,0:T(8,128)(2,1)S(1)}, u32[]{:S(2)}, u32[]{:S(2)}) %collective-permute-start) | collective-permute-done | bytes 262176 | tf_op jit(solution)/shard_map/ppermute | solution.py:32
  43.9 1.9 %collective-permute-start.3 = (bf16[4,4,128,256]{3,2,0,1:T(8,128)(2,1)S(1)}, bf16[4,4,128,256]{3,2,0,1:T(8,128)(2,1)}, u32[]{:S(2)}, u32[]{:S(2)}) collective-permute-start(bf16[4,4,128,256]{3,2,0,1:T(8,128)(2,1)S(1)} %pad_maximum_fusion), channel_id=1, source_target_pairs={{0,16},{16,0},{1,17},{17,1},{2,18},{18,2},{3,19},{19,3},{4,20},{20... | collective-permute-start | bytes 3145736 | tf_op jit(solution)/shard_map/ppermute | solution.py:23
  46.7 2.7 %fusion.4 = bf16[16,4,32,256]{3,2,1,0:T(8,128)(2,1)} fusion(f32[4,4,4,32,256]{4,3,1,2,0:T(8,128)S(1)} %copy.35, bf16[16,4,32,256]{3,2,1,0:T(8,128)(2,1)} %collective-permute-done.4), kind=kLoop, calls=%fused_computation.11 | loop fusion | flops 1572864 | bytes 4194304 | tf_op jit(solution)/shard_map/convert_element_type | solution.py:62
  49.5 4.8 %all-to-all-start.1 = ((bf16[16,4,32,256]{3,2,1,0:T(8,128)(2,1)}), bf16[16,4,32,256]{3,2,1,0:T(8,128)(2,1)}, u32[]{:S(2)}, u32[]{:S(2)}) async-start(bf16[16,4,32,256]{3,2,1,0:T(8,128)(2,1)} %fusion.4), calls=%async_computation.1 | async-start | bytes 2097152 | tf_op jit(solution)/shard_map/all_to_all | solution.py:14
  55.6 1.6 %broadcast_select_fusion = (bf16[4,4,128,256]{3,2,0,1:T(8,128)(2,1)S(1)}, bf16[4,4,128,256]{3,2,0,1:T(8,128)(2,1)S(1)}) fusion(bf16[4,4,128,256]{3,2,0,1:T(8,128)(2,1)} %collective-permute-done.3, pred[]{:T(512)S(6)} %eq.9, bf16[1,4,128,256]{3,2,0,1:T(8,128)(2,1)} %bitcast.68, bf16[1,4,128,256]{3,2,0,1:T(8,128)(2,1)} %bitcast.70, ...), kind=kLoop, calls=%fused_computation.26 | loop fusion | flops 2621440 | bytes 4194305 | tf_op jit(solution)/shard_map/jit(_where)/select_n | solution.py:94
  57.2 13.3 %all-to-all-done.1 = bf16[16,4,32,256]{3,2,1,0:T(8,128)(2,1)} async-done(((bf16[16,4,32,256]{3,2,1,0:T(8,128)(2,1)}), bf16[16,4,32,256]{3,2,1,0:T(8,128)(2,1)}, u32[]{:S(2)}, u32[]{:S(2)}) %all-to-all-start.1) | async-done | bytes 1048608 | tf_op jit(solution)/shard_map/all_to_all | solution.py:14
  70.5 1.4 %convert_reduce_fusion = f32[4,32,256]{2,1,0:T(8,128)S(1)} fusion(bf16[16,4,32,256]{3,2,1,0:T(8,128)(2,1)} %all-to-all-done.1), kind=kLoop, calls=%fused_computation.12 | loop fusion | flops 1015808 | bytes 1179648 | tf_op jit(solution)/shard_map/reduce_sum | solution.py:70
  74.3 9.8 %all-to-all-start.2 = ((bf16[16,32,384]{2,1,0:T(8,128)(2,1)}), bf16[16,32,384]{2,1,0:T(8,128)(2,1)S(1)}, u32[]{:S(2)}, u32[]{:S(2)}) async-start(bf16[16,32,384]{2,1,0:T(8,128)(2,1)} %bitcast.62), calls=%async_computation.2 | async-start | bytes 786432 | tf_op jit(solution)/shard_map/all_to_all | solution.py:14
  84.0 1.1 fusion.2
  86.1 1.3 %convolution_convert_fusion.1 = bf16[192,512]{1,0:T(8,128)(2,1)} fusion(bf16[2048,512]{1,0:T(8,128)(2,1)S(1)} %bitcast.58, bf16[192,2048]{1,0:T(8,128)(2,1)S(1)} %copy-done.1, f32[2048]{0:T(1024)S(1)} %copy-done.5, f32[192]{0:T(256)S(1)} %add_rsqrt_fusion), kind=kOutput, calls=%fused_computation.24 | convolution fusion | flops 404324352 | bytes 3089152 | tf_op jit(solution)/shard_map/dot_general | solution.py:97
  87.4 1.2 fusion.12
  88.7 13.1 %all-to-all-done.2 = bf16[16,32,384]{2,1,0:T(8,128)(2,1)S(1)} async-done(((bf16[16,32,384]{2,1,0:T(8,128)(2,1)}), bf16[16,32,384]{2,1,0:T(8,128)(2,1)S(1)}, u32[]{:S(2)}, u32[]{:S(2)}) %all-to-all-start.2) | async-done | bytes 393248 | tf_op jit(solution)/shard_map/all_to_all | solution.py:14
  102.5 10.2 %all-to-all-start.3 = ((bf16[8,32,256]{2,1,0:T(8,128)(2,1)}), bf16[8,32,256]{2,1,0:T(8,128)(2,1)S(1)}, u32[]{:S(2)}, u32[]{:S(2)}) async-start(bf16[8,32,256]{2,1,0:T(8,128)(2,1)} %broadcast_in_dim.16), calls=%async_computation.3 | async-start | bytes 262144 | tf_op jit(solution)/shard_map/all_to_all | solution.py:14
  112.8 5.1 %all-to-all-done.3 = bf16[8,32,256]{2,1,0:T(8,128)(2,1)S(1)} async-done(((bf16[8,32,256]{2,1,0:T(8,128)(2,1)}), bf16[8,32,256]{2,1,0:T(8,128)(2,1)S(1)}, u32[]{:S(2)}, u32[]{:S(2)}) %all-to-all-start.3) | async-done | bytes 131104 | tf_op jit(solution)/shard_map/all_to_all | solution.py:14
  118.6 5.0 %all-to-all-start.4 = ((f32[32,8,128]{2,1,0:T(8,128)}), f32[32,8,128]{2,1,0:T(8,128)S(1)}, u32[]{:S(2)}, u32[]{:S(2)}) async-start(f32[32,8,128]{2,1,0:T(8,128)} %broadcast_in_dim.17), calls=%async_computation.4 | async-start | bytes 262144 | tf_op jit(solution)/shard_map/all_to_all | solution.py:14
  124.6 6.7 %all-to-all-done.4 = f32[32,8,128]{2,1,0:T(8,128)S(1)} async-done(((f32[32,8,128]{2,1,0:T(8,128)}), f32[32,8,128]{2,1,0:T(8,128)S(1)}, u32[]{:S(2)}, u32[]{:S(2)}) %all-to-all-start.4) | async-done | bytes 131104 | tf_op jit(solution)/shard_map/all_to_all | solution.py:14
  (54 shorter events, 9.0 us)
Async XLA Ops:
  0.6 1.4 %copy-start = (bf16[192,512]{1,0:T(8,128)(2,1)S(1)}, bf16[192,512]{1,0:T(8,128)(2,1)}, u32[]{:S(2)}) copy-start(bf16[192,512]{1,0:T(8,128)(2,1)} %param.13) | copy-start | bytes 589828
  3.8 8.9 %copy-start.7 = (f32[1,512]{1,0:T(1,128)S(1)}, f32[1,512]{1,0:T(1,128)}, u32[]{:S(2)}) copy-start(f32[1,512]{1,0:T(1,128)} %param.12) | copy-start | bytes 6148
  3.8 8.9 %copy-start.6 = (s32[128,512]{1,0:T(8,128)S(1)}, s32[128,512]{1,0:T(8,128)}, u32[]{:S(2)}) copy-start(s32[128,512]{1,0:T(8,128)} %param.11) | copy-start | bytes 786436
  3.9 42.8 %collective-permute-start.4 = (bf16[16,4,32,256]{3,2,1,0:T(8,128)(2,1)S(1)}, bf16[16,4,32,256]{3,2,1,0:T(8,128)(2,1)}, u32[]{:S(2)}, u32[]{:S(2)}) collective-permute-start(bf16[16,4,32,256]{3,2,1,0:T(8,128)(2,1)S(1)} %bitcast.63), channel_id=1, source_target_pairs={{0,16},{16,0},{1,17},{17,1},{2,18},{18,2},{3,19},{19,3},{4,20},{20... | collective-permute-start | bytes 3145736 | tf_op jit(solution)/shard_map/ppermute | solution.py:23
  12.8 33.1 %copy-start.1 = (bf16[192,2048]{1,0:T(8,128)(2,1)S(1)}, bf16[192,2048]{1,0:T(8,128)(2,1)}, u32[]{:S(2)}) copy-start(bf16[192,2048]{1,0:T(8,128)(2,1)} %param.9) | copy-start | bytes 2359300
  12.8 33.1 %copy-start.5 = (f32[2048]{0:T(1024)S(1)}, f32[2048]{0:T(1024)}, u32[]{:S(2)}) copy-start(f32[2048]{0:T(1024)} %param.10) | copy-start | bytes 24580
  21.9 13.1 %collective-permute-start.2 = (bf16[4,128,256]{2,1,0:T(8,128)(2,1)S(1)}, bf16[4,128,256]{2,1,0:T(8,128)(2,1)S(1)}, u32[]{:S(2)}, u32[]{:S(2)}) collective-permute-start(bf16[4,128,256]{2,1,0:T(8,128)(2,1)S(1)} %all_to_all.25), channel_id=1, source_target_pairs={{0,1},{1,2},{2,3},{3,128},{128,129},{129,130},{130,131},{131,256},... | collective-permute-start | bytes 786440 | tf_op jit(solution)/shard_map/ppermute | solution.py:32
  23.8 16.2 %collective-permute-start.1 = (bf16[4,128,256]{2,1,0:T(8,128)(2,1)S(1)}, bf16[4,128,256]{2,1,0:T(8,128)(2,1)S(1)}, u32[]{:S(2)}, u32[]{:S(2)}) collective-permute-start(bf16[4,128,256]{2,1,0:T(8,128)(2,1)S(1)} %all_to_all.25), channel_id=1, source_target_pairs={{0,2},{1,3},{2,128},{3,129},{128,130},{129,131},{130,256},{131,257... | collective-permute-start | bytes 786440 | tf_op jit(solution)/shard_map/ppermute | solution.py:32
  32.3 11.4 %collective-permute-start = (bf16[4,128,256]{2,1,0:T(8,128)(2,1)S(1)}, bf16[4,128,256]{2,1,0:T(8,128)(2,1)S(1)}, u32[]{:S(2)}, u32[]{:S(2)}) collective-permute-start(bf16[4,128,256]{2,1,0:T(8,128)(2,1)S(1)} %all_to_all.25), channel_id=1, source_target_pairs={{0,387},{1,0},{2,1},{3,2},{128,3},{129,128},{130,129},{131,130},{2... | collective-permute-start | bytes 786440 | tf_op jit(solution)/shard_map/ppermute | solution.py:32
  35.0 11.5 %copy-start.2 = (bf16[4,128,256]{2,1,0:T(8,128)(2,1)}, bf16[4,128,256]{2,1,0:T(8,128)(2,1)S(1)}, u32[]{:S(2)}) copy-start(bf16[4,128,256]{2,1,0:T(8,128)(2,1)S(1)} %collective-permute-done.2) | copy-start | bytes 786436
  40.0 6.4 %copy-start.3 = (bf16[4,128,256]{2,1,0:T(8,128)(2,1)}, bf16[4,128,256]{2,1,0:T(8,128)(2,1)S(1)}, u32[]{:S(2)}) copy-start(bf16[4,128,256]{2,1,0:T(8,128)(2,1)S(1)} %collective-permute-done.1) | copy-start | bytes 786436
  43.8 2.7 %copy-start.4 = (bf16[4,128,256]{2,1,0:T(8,128)(2,1)}, bf16[4,128,256]{2,1,0:T(8,128)(2,1)S(1)}, u32[]{:S(2)}) copy-start(bf16[4,128,256]{2,1,0:T(8,128)(2,1)S(1)} %collective-permute-done) | copy-start | bytes 786436
  43.9 11.7 %collective-permute-start.3 = (bf16[4,4,128,256]{3,2,0,1:T(8,128)(2,1)S(1)}, bf16[4,4,128,256]{3,2,0,1:T(8,128)(2,1)}, u32[]{:S(2)}, u32[]{:S(2)}) collective-permute-start(bf16[4,4,128,256]{3,2,0,1:T(8,128)(2,1)S(1)} %pad_maximum_fusion), channel_id=1, source_target_pairs={{0,16},{16,0},{1,17},{17,1},{2,18},{18,2},{3,19},{19,3},{4,20},{20... | collective-permute-start | bytes 3145736 | tf_op jit(solution)/shard_map/ppermute | solution.py:23
  49.5 21.0 %all-to-all-start.1 = ((bf16[16,4,32,256]{3,2,1,0:T(8,128)(2,1)}), bf16[16,4,32,256]{3,2,1,0:T(8,128)(2,1)}, u32[]{:S(2)}, u32[]{:S(2)}) async-start(bf16[16,4,32,256]{3,2,1,0:T(8,128)(2,1)} %fusion.4), calls=%async_computation.1 | async-start | bytes 2097152 | tf_op jit(solution)/shard_map/all_to_all | solution.py:14
  74.3 27.5 %all-to-all-start.2 = ((bf16[16,32,384]{2,1,0:T(8,128)(2,1)}), bf16[16,32,384]{2,1,0:T(8,128)(2,1)S(1)}, u32[]{:S(2)}, u32[]{:S(2)}) async-start(bf16[16,32,384]{2,1,0:T(8,128)(2,1)} %bitcast.62), calls=%async_computation.2 | async-start | bytes 786432 | tf_op jit(solution)/shard_map/all_to_all | solution.py:14
  102.5 15.5 %all-to-all-start.3 = ((bf16[8,32,256]{2,1,0:T(8,128)(2,1)}), bf16[8,32,256]{2,1,0:T(8,128)(2,1)S(1)}, u32[]{:S(2)}, u32[]{:S(2)}) async-start(bf16[8,32,256]{2,1,0:T(8,128)(2,1)} %broadcast_in_dim.16), calls=%async_computation.3 | async-start | bytes 262144 | tf_op jit(solution)/shard_map/all_to_all | solution.py:14
  118.6 12.7 %all-to-all-start.4 = ((f32[32,8,128]{2,1,0:T(8,128)}), f32[32,8,128]{2,1,0:T(8,128)S(1)}, u32[]{:S(2)}, u32[]{:S(2)}) async-start(f32[32,8,128]{2,1,0:T(8,128)} %broadcast_in_dim.17), calls=%async_computation.4 | async-start | bytes 262144 | tf_op jit(solution)/shard_map/all_to_all | solution.py:14

commit v2 on v1

v2 whole, which is shorter than its diff:
```python
import functools

import jax
import jax.numpy as jnp
from jax import lax
from jax.experimental import pallas as pl
from jax.experimental.pallas import tpu as pltpu
from jax.sharding import Mesh, PartitionSpec as P

eps = 1e-05
AXES = ("zh", "x", "core", "y", "zl")
SIZES = (4, 4, 2, 4, 4)
Z = ("zh", "zl")
DEVICES = 512
HALF = 256
f32, bf16 = jnp.float32, jnp.bfloat16
VMEM = pl.BlockSpec(memory_space=pltpu.VMEM)
SMEM = pl.BlockSpec(memory_space=pltpu.SMEM)
ANY = pl.BlockSpec(memory_space=pl.ANY)
PARAMS = pltpu.CompilerParams(vmem_limit_bytes=40 * 1024 * 1024)


def exchange(blocks, axes):
    return lax.all_to_all(blocks, axes, 0, 0, tiled=False)


def swap(block):
    return lax.ppermute(block, "core", [(0, 1), (1, 0)])


def along_y(block, step):
    return lax.ppermute(block, "y", [(y, (y + step) % 4) for y in range(4)])


def along_z(block, step):
    pairs = []
    for z in range(16):
        for x in range(4):
            for core in range(2):
                to = (z + step(x, core)) % 16
                pairs.append(
                    (((z // 4 * 4 + x) * 2 + core) * 4 + z % 4, ((to // 4 * 4 + x) * 2 + core) * 4 + to % 4)
                )
    return lax.ppermute(block, ("zh", "x", "core", "zl"), pairs)


def contract_rows(a, b):
    return lax.dot_general(a, b, (((0,), (0,)), ((), ())), preferred_element_type=f32)


def put_product(normed, grad, out, dtype):
    for k in range(8):
        part = contract_rows(normed[:, k * HALF : (k + 1) * HALF], grad)
        for sub in range(16):
            pair = jnp.concatenate(
                [part[sub * 8 : sub * 8 + 8], part[128 + sub * 8 : 136 + sub * 8]], axis=0
            )
            out[sub, :, k * HALF : (k + 1) * HALF] = pair.astype(dtype)


def norm_kernel(place, tokens, norm_gain, key_grad, normed, inv_rms, theirs):
    wide = tokens[...].astype(f32)
    inv = lax.rsqrt(jnp.mean(wide * wide, axis=1, keepdims=True) + eps)
    inv_rms[...] = jnp.broadcast_to(inv, inv_rms.shape)
    normed[...] = (wide * inv * norm_gain[...]).astype(bf16)
    start = pl.multiple_of((1 - place[0]) * HALF, HALF)
    put_product(normed, key_grad[:, pl.ds(start, HALF)], theirs, bf16)


def mine_kernel(place, normed, key_grad, mine):
    start = pl.multiple_of(place[0] * HALF, HALF)
    put_product(normed, key_grad[:, pl.ds(start, HALF)], mine, f32)


def pair_kernel(mine, got, rows, out):
    for sub in range(16):
        out[sub, :, :2048] = (mine[sub] + got[sub].astype(f32)).astype(bf16)
        own = rows[sub * 8 : sub * 8 + 8, :].astype(f32)
        out[sub, :, 2048:] = jnp.concatenate([own[:, :128], own[:, 128:]], axis=0).astype(bf16)


def square_kernel(place, square, out, shards, products):
    zl = place[3]
    for k in range(8):
        cols = slice(k * HALF, (k + 1) * HALF)
        total = square[0, :, cols].astype(f32)
        for sender in range(1, 16):
            total += square[sender, :, cols].astype(f32)
        shards[2 * k] = total[:8]
        shards[2 * k + 1] = total[8:]
    for sender in range(16):
        shard = sender // 4 * 4 + lax.rem(zl + sender % 4, 4)
        packed = square[sender, :, 2048:].astype(f32)
        rows = jnp.concatenate([packed[:8], packed[8:]], axis=1)
        products[shard] = shards[shard] * rows
    gain = lax.dot_general(
        jnp.ones((16, HALF), f32),
        products[...].reshape(128, HALF),
        (((1,), (1,)), ((), ())),
        preferred_element_type=f32,
        precision=lax.Precision.HIGHEST,
    )
    high = gain.astype(bf16).astype(f32)
    row = lax.broadcasted_iota(jnp.int32, (16, 128), 0)
    gains = jnp.where(row == 0, high, jnp.where(row == 1, gain - high, 0.0)).astype(bf16)
    for target in range(4):
        first = jnp.concatenate([shards[target], shards[4 + target]], axis=0).astype(bf16)
        second = jnp.concatenate([shards[8 + target], shards[12 + target]], axis=0).astype(bf16)
        for zh in range(4):
            z = zh * 4 + target
            out[z, :, :HALF] = first
            out[z, :, HALF : 2 * HALF] = second
            out[z, :, 2 * HALF :] = gains


def line_kernel(line, out):
    total = line[0].astype(f32)
    for sender in range(1, 16):
        total += line[sender].astype(f32)
    gain = total[0:1, 512:] + total[1:2, 512:]
    high = gain.astype(bf16).astype(f32)
    both = jnp.concatenate([high, gain - high], axis=1)
    row = lax.broadcasted_iota(jnp.int32, (8, HALF), 0)
    gains = jnp.where(row == 0, jnp.broadcast_to(both, (8, HALF)), 0.0)
    for y in range(4):
        rows = total[y % 2 * 8 : y % 2 * 8 + 8, y // 2 * HALF : (y // 2 + 1) * HALF]
        block = jnp.concatenate([rows, gains], axis=0).astype(bf16)
        for peer in range(8):
            out[y * 8 + peer] = block


def last_kernel(blocks, norm_gain, weight_grad, gain_grad):
    rows_of = []
    for sub in range(16):
        gains = None
        for core in range(2):
            block = blocks[sub * 2 + core].astype(f32)
            weight_grad[sub * 8 : sub * 8 + 8, core * HALF : (core + 1) * HALF] = block[:8] / DEVICES
            gain = block[8:9, :128] + block[8:9, 128:]
            gains = gain if gains is None else gains + gain
        rows_of.append(gains)
    sums = jnp.concatenate(rows_of, axis=0)
    lane = lax.broadcasted_iota(jnp.int32, (16, 128), 1)
    sub = lax.broadcasted_iota(jnp.int32, (16, 128), 0)
    spread = (
        lax.broadcasted_iota(jnp.int32, (128, 128), 0) % 8
        == lax.broadcasted_iota(jnp.int32, (128, 128), 1) % 8
    ).astype(f32)
    stacked = jnp.concatenate(
        [jnp.where(lane // 8 == shard, sums, 0.0) for shard in range(16)], axis=0
    )
    moved = lax.dot_general(
        stacked, spread, (((1,), (0,)), ((), ())), preferred_element_type=f32,
        precision=lax.Precision.HIGHEST,
    )
    for shard in range(16):
        block = moved[shard * 16 : shard * 16 + 16]
        gain_grad[shard : shard + 1, :] = jnp.sum(
            jnp.where(lane // 8 == sub, block, 0.0), axis=0, keepdims=True
        ) / (norm_gain[shard : shard + 1, :] * DEVICES)


def token_kernel(place, tokens, inv_rms, norm_gain, key_grad, *rest):
    pieces, (keys, tokens_grad, weight, sem) = rest[:8], rest[8:]
    core, y, zl = place[0], place[2], place[3]
    copies = []
    for step in range(4):
        for side in range(2):
            column = core * HALF if side == 0 else (1 - core) * HALF
            for j in range(4):
                row = (lax.rem(y + step, 4) * 4 + lax.rem(zl + j, 4)) * 128
                copies.append(
                    pltpu.make_async_copy(
                        pieces[step * 2 + side].at[j],
                        weight.at[pl.ds(pl.multiple_of(row, 128), 128), pl.ds(pl.multiple_of(column, HALF), HALF)],
                        sem.at[len(copies)],
                    )
                )
    for copy in copies:
        copy.start()
    for copy in copies:
        copy.wait()
    for rows in (slice(0, 96), slice(96, 192)):
        inv = inv_rms[rows, 0:1]
        unit = tokens[rows, :].astype(f32) * inv
        normed = (unit * norm_gain[...]).astype(bf16)
        keys[rows, :] = jnp.dot(normed, weight[...], preferred_element_type=f32).astype(bf16)
        scaled = norm_gain[...] * lax.dot_general(
            key_grad[rows, :], weight[...], (((1,), (1,)), ((), ())), preferred_element_type=f32
        )
        mean = jnp.mean(scaled * unit, axis=1, keepdims=True)
        tokens_grad[rows, :] = (inv * (scaled - unit * mean)).astype(bf16)


def call(kernel, outs, ins, args, scratch=(), flops=0, **kw):
    moved = sum(a.size * a.dtype.itemsize for a in args)
    return pl.pallas_call(
        kernel,
        out_shape=[jax.ShapeDtypeStruct(s, d) for s, d in outs],
        in_specs=ins,
        out_specs=[VMEM] * len(outs),
        scratch_shapes=list(scratch),
        compiler_params=PARAMS,
        cost_estimate=pl.CostEstimate(flops=flops, bytes_accessed=2 * moved, transcendentals=0),
    )(*args)


def local(tokens, norm_gain, weight_codes, block_scales, key_grad):
    core = lax.axis_index("core")
    place = jnp.stack(
        [core, lax.axis_index("x"), lax.axis_index("y"), lax.axis_index("zl")]
    ).astype(jnp.int32)
    gain_row = norm_gain.reshape(1, 2048)

    codes = lax.dynamic_slice_in_dim(weight_codes, core * HALF, HALF, 1)
    scales = lax.dynamic_slice_in_dim(block_scales, core * HALF, HALF, 1)
    shard = (codes.astype(f32) * scales).astype(bf16)
    gain_rows = along_z(shard, lambda x, core: (0, -1, -2, 1)[x])

    normed, inv_rms, theirs = call(
        norm_kernel,
        [((192, 2048), bf16), ((192, 128), f32), ((16, 16, 2048), bf16)],
        [SMEM, VMEM, VMEM, VMEM],
        (place, tokens, gain_row, key_grad),
        flops=2 * 192 * 2048 * 256,
    )
    got = swap(theirs)
    (mine,) = call(
        mine_kernel,
        [((16, 16, 2048), f32)],
        [SMEM, VMEM, VMEM],
        (place, normed, key_grad),
        flops=2 * 192 * 2048 * 256,
    )
    (pair,) = call(pair_kernel, [((16, 16, 2176), bf16)], [VMEM] * 3, (mine, got, gain_rows))
    square = exchange(pair, ("y", "x"))

    shard_late, _ = lax.optimization_barrier((shard, pair))
    above = along_z(shard_late, lambda x, core: -1)
    across = along_z(shard_late, lambda x, core: (2, -2)[core])
    below = along_z(shard_late, lambda x, core: 1)
    stack = jnp.stack([shard, above, across, below])

    (payload,) = call(
        square_kernel,
        [((16, 16, 640), bf16)],
        [SMEM, VMEM],
        (place, square),
        scratch=[pltpu.VMEM((16, 8, HALF), f32), pltpu.VMEM((16, 8, HALF), f32)],
    )
    line = exchange(payload, Z)

    stack_late, _ = lax.optimization_barrier((stack, payload))
    pieces = []
    for step in range(4):
        piece = stack if step == 0 else along_y(stack_late, -step)
        pieces += [piece, swap(piece)]
    (blocks,) = call(line_kernel, [((32, 16, HALF), bf16)], [VMEM], (line,))
    blocks = exchange(blocks, ("y", "x", "core"))
    keys, tokens_grad = call(
        token_kernel,
        [((192, 512), bf16), ((192, 2048), bf16)],
        [SMEM, VMEM, VMEM, VMEM, VMEM] + [ANY] * 8,
        (place, tokens, inv_rms, gain_row, key_grad, *pieces),
        scratch=[pltpu.VMEM((2048, 512), bf16), pltpu.SemaphoreType.DMA((32,))],
        flops=4 * 192 * 2048 * 512,
    )
    weight_grad, gain_grad = call(
        last_kernel,
        [((128, 512), f32), ((16, 128), f32)],
        [VMEM] * 2,
        (blocks, norm_gain.reshape(16, 128)),
    )
    return keys, tokens_grad, weight_grad, gain_grad.reshape(2048)


def solution(mesh):
    fine = Mesh(mesh.devices.reshape(SIZES), AXES)
    everyone = P(AXES, None)
    group = P(("y", "zl"), None)
    in_specs = (everyone, P(), group, group, everyone)
    out_specs = (everyone, everyone, group, P())
    return jax.shard_map(local, mesh=fine, in_specs=in_specs, out_specs=out_specs, check_vma=False)
```

time: 133 us -> 114 us (0.86)
  waiting for transfers between devices: 47 us -> 12.1 us
  blocking collectives: 9.05 us -> 30.5 us
  other arithmetic: 13.2 us -> 1.06 us
  Pallas kernels: 0 us -> 10.3 us
  matrix products: 4.6 us -> 0 us
  starting transfers between devices: 53.5 us -> 55.3 us
    all_to_all x4 -> x2, waiting for transfers between devices: 38.2 us -> 4.36 us  [exchange(): return lax.all_to_all(blocks, axes, 0, 0, tiled=False)]
    all_to_all x1, blocking collectives: 9.05 us -> 30.5 us  [exchange(): return lax.all_to_all(blocks, axes, 0, 0, tiled=False)]
    all_to_all x4 -> x2, starting transfers between devices: 29.7 us -> 12.4 us  [exchange(): return lax.all_to_all(blocks, axes, 0, 0, tiled=False)]
    ppermute x2 -> x5, starting transfers between devices: 10.7 us -> 23.3 us  [swap(): return lax.ppermute(block, 'core', [(0, 1), (1, 0)])]
    pallas_call x0 -> x7, Pallas kernels: none -> 10.3 us  [call(): pl.pallas_call(kernel, out_shape=[jax.ShapeDtypeStruct(s, d) for s, d in...]
    ppermute x3 -> x7, starting transfers between devices: 13 us -> 19.6 us  [the longest x4 11.3 us: along_z(): return lax.ppermute(block, ('zh', 'x', 'core', 'zl'), pairs)]
    dot_general x4 -> x0, matrix products: 4.6 us -> none  [the longest x2 2.29 us: product(): lax.dot_general(normed, columns(key_grad, which), (((0,), (0,)), ((), ())...]
    convert_element_type x4 -> x1, other arithmetic: 4.13 us -> 0.93 us  [local(): shard = (codes.astype(f32) * scales).astype(bf16)]
  transfers between devices with their start and end apart: 9 -> 14, of which waited for: 6 -> 4; matrix products, arithmetic and copies ran while one was open for 9% -> 1% of each run, Pallas kernels for 0% -> 6%
where the time goes in v2:
time: 114 us; the launch traced here: 113 us
  starting transfers between devices  55.3 us (49%)
  blocking collectives  30.5 us (27%)
  waiting for transfers between devices  12.1 us (11%)
  Pallas kernels  10.3 us (9%)
  local copies, waits for them, and re-layouts  2.79 us (2%)
    all_to_all x1, blocking collectives, exchange(): return lax.all_to_all(blocks, axes, 0, 0, tiled=False)  30.5 us
    ppermute x5, starting transfers between devices, swap(): return lax.ppermute(block, 'core', [(0, 1), (1, 0)])  23.3 us
    all_to_all x2, starting transfers between devices, exchange(): return lax.all_to_all(blocks, axes, 0, 0, tiled=False)  12.4 us
    ppermute x4, starting transfers between devices, along_z(): return lax.ppermute(block, ('zh', 'x', 'core', 'zl'), pairs)  11.3 us
    pallas_call x7, Pallas kernels, call(): pl.pallas_call(kernel, out_shape=[jax.ShapeDtypeStruct(s, d) for s, d in...  10.3 us
    ppermute x3, starting transfers between devices, along_y(): return lax.ppermute(block, 'y', [(y, (y + step) % 4) for y in range(4)])  8.26 us
    ppermute x4, waiting for transfers between devices, along_z(): return lax.ppermute(block, ('zh', 'x', 'core', 'zl'), pairs)  7.73 us
    all_to_all x2, waiting for transfers between devices, exchange(): return lax.all_to_all(blocks, axes, 0, 0, tiled=False)  4.36 us
  transfers between devices with their start and end apart: 14, of which 4 were waited for; matrix products, arithmetic and copies ran while one was open for 1% of the time, Pallas kernels for 6%

profile of v2, /device:TPU:1, one launch (start us, length us, event | category | flops | bytes accessed | tf_op | source)
XLA Modules:
  0.0 113.0 jit_solution(3335225938378795682)
XLA Ops:
  0.7 1.1 %copy-done.1 = bf16[192,2048]{1,0:T(8,128)(2,1)S(1)} copy-done((bf16[192,2048]{1,0:T(8,128)(2,1)S(1)}, bf16[192,2048]{1,0:T(8,128)(2,1)}, u32[]{:S(2)}) %copy-start.1) | copy-done | bytes 786456
  1.9 0.9 copy-done.3
  3.5 1.3 %shard_map.84 = (bf16[192,2048]{1,0:T(8,128)(2,1)S(1)}, f32[192,128]{1,0:T(8,128)S(1)}, bf16[16,16,2048]{2,1,0:T(8,128)(2,1)S(1)}) custom-call(s32[4]{0:T(128)S(1)} %pad_add_fusion.place, bf16[192,2048]{1,0:T(8,128)(2,1)S(1)} %copy-done.1, f32[1,2048]{1,0:T(1,128)S(1)} %bitcast.13, bf16[192,512]{1,0:T(8,128)(2,1)S(1)} %copy-done.3), custom_call_target="tpu_custom_call" | custom-call | flops 201326592 | bytes 1982496 | tf_op jit(solution)/shard_map/pallas_call | solution.py:197
  4.8 8.8 %collective-permute-start = (bf16[16,16,2048]{2,1,0:T(8,128)(2,1)S(1)}, bf16[16,16,2048]{2,1,0:T(8,128)(2,1)S(1)}, u32[]{:S(2)}, u32[]{:S(2)}) collective-permute-start(bf16[16,16,2048]{2,1,0:T(8,128)(2,1)S(1)} %get-tuple-element.15), channel_id=1, source_target_pairs={{0,16},{16,0},{1,17},{17,1},{2,18},{18,2},{3,19},{19,3},{4,20},{20... | collective-permute-start | bytes 3145736 | tf_op jit(solution)/shard_map/ppermute | solution.py:28
  13.6 0.9 multiply_convert_fusion
  15.2 1.0 shard_map.85.mine
  16.5 30.5 %all_to_all.15.square = bf16[16,16,2176]{2,1,0:T(8,128)(2,1)S(1)} all-to-all(bf16[16,16,2176]{2,1,0:T(8,128)(2,1)S(1)} %shard_map.86), channel_id=1, replica_groups=mesh['zh'=4,'x'=4,'core'=2,'y'=4,'zl'=4] {'y','x'}, dimensions={0} | all-to-all | bytes 2228224 | tf_op jit(solution)/shard_map/all_to_all | solution.py:24
  47.0 1.7 %shard_map.87 = bf16[16,16,640]{2,1,0:T(8,128)(2,1)} custom-call(s32[4]{0:T(128)S(1)} %pad_add_fusion.place, bf16[16,16,2176]{2,1,0:T(8,128)(2,1)S(1)} %all_to_all.15.square), custom_call_target="tpu_custom_call" | custom-call | bytes 2228256 | tf_op jit(solution)/shard_map/pallas_call | solution.py:197
  48.7 8.8 %all-to-all-start.1 = ((bf16[16,16,640]{2,1,0:T(8,128)(2,1)}), bf16[16,16,640]{2,1,0:T(8,128)(2,1)S(1)}, u32[]{:S(2)}, u32[]{:S(2)}) async-start(bf16[16,16,640]{2,1,0:T(8,128)(2,1)} %shard_map.87), calls=%async_computation.1 | async-start | bytes 655360 | tf_op jit(solution)/shard_map/all_to_all | solution.py:24
  57.5 3.3 %collective-permute-start.4 = (bf16[128,256]{1,0:T(8,128)(2,1)S(1)}, bf16[128,256]{1,0:T(8,128)(2,1)S(1)}, u32[]{:S(2)}, u32[]{:S(2)}) collective-permute-start(bf16[128,256]{1,0:T(8,128)(2,1)S(1)} %multiply_convert_fusion), channel_id=1, source_target_pairs={{0,1},{16,17},{32,33},{48,49},{64,65},{80,81},{96,97},{112,113},{1... | collective-permute-start | bytes 196616 | tf_op jit(solution)/shard_map/ppermute | solution.py:44
  60.7 4.3 %collective-permute-start.3 = (bf16[128,256]{1,0:T(8,128)(2,1)S(1)}, bf16[128,256]{1,0:T(8,128)(2,1)S(1)}, u32[]{:S(2)}, u32[]{:S(2)}) collective-permute-start(bf16[128,256]{1,0:T(8,128)(2,1)S(1)} %multiply_convert_fusion), channel_id=1, source_target_pairs={{0,2},{16,402},{32,34},{48,434},{64,66},{80,466},{96,98},{112,498}... | collective-permute-start | bytes 196616 | tf_op jit(solution)/shard_map/ppermute | solution.py:44
  65.1 3.1 %collective-permute-start.2 = (bf16[128,256]{1,0:T(8,128)(2,1)S(1)}, bf16[128,256]{1,0:T(8,128)(2,1)S(1)}, u32[]{:S(2)}, u32[]{:S(2)}) collective-permute-start(bf16[128,256]{1,0:T(8,128)(2,1)S(1)} %multiply_convert_fusion), channel_id=1, source_target_pairs={{0,387},{16,403},{32,419},{48,435},{64,451},{80,467},{96,483},{112... | collective-permute-start | bytes 196616 | tf_op jit(solution)/shard_map/ppermute | solution.py:44
  68.2 4.9 %collective-permute-done.4 = bf16[128,256]{1,0:T(8,128)(2,1)S(1)} collective-permute-done((bf16[128,256]{1,0:T(8,128)(2,1)S(1)}, bf16[128,256]{1,0:T(8,128)(2,1)S(1)}, u32[]{:S(2)}, u32[]{:S(2)}) %collective-permute-start.4) | collective-permute-done | bytes 65568 | tf_op jit(solution)/shard_map/ppermute | solution.py:44
  73.2 2.7 %collective-permute-done.2 = bf16[128,256]{1,0:T(8,128)(2,1)S(1)} collective-permute-done((bf16[128,256]{1,0:T(8,128)(2,1)S(1)}, bf16[128,256]{1,0:T(8,128)(2,1)S(1)}, u32[]{:S(2)}, u32[]{:S(2)}) %collective-permute-start.2) | collective-permute-done | bytes 65568 | tf_op jit(solution)/shard_map/ppermute | solution.py:44
  76.0 2.9 %collective-permute-start.6 = (bf16[4,128,256]{2,1,0:T(8,128)(2,1)S(1)}, bf16[4,128,256]{2,1,0:T(8,128)(2,1)S(1)}, u32[]{:S(2)}, u32[]{:S(2)}) collective-permute-start(bf16[4,128,256]{2,1,0:T(8,128)(2,1)S(1)} %pad_maximum_fusion.rest_0_), channel_id=1, source_target_pairs={{0,12},{4,0},{8,4},{12,8},{1,13},{5,1},{9,5},{13,9},{2,14},{6,2},{... | collective-permute-start | bytes 786440 | tf_op jit(solution)/shard_map/ppermute | solution.py:32
  78.9 3.4 %collective-permute-start.8 = (bf16[4,128,256]{2,1,0:T(8,128)(2,1)S(1)}, bf16[4,128,256]{2,1,0:T(8,128)(2,1)S(1)}, u32[]{:S(2)}, u32[]{:S(2)}) collective-permute-start(bf16[4,128,256]{2,1,0:T(8,128)(2,1)S(1)} %pad_maximum_fusion.rest_0_), channel_id=1, source_target_pairs={{0,8},{4,12},{8,0},{12,4},{1,9},{5,13},{9,1},{13,5},{2,10},{6,14},... | collective-permute-start | bytes 786440 | tf_op jit(solution)/shard_map/ppermute | solution.py:32
  82.3 2.0 %collective-permute-start.10 = (bf16[4,128,256]{2,1,0:T(8,128)(2,1)S(1)}, bf16[4,128,256]{2,1,0:T(8,128)(2,1)S(1)}, u32[]{:S(2)}, u32[]{:S(2)}) collective-permute-start(bf16[4,128,256]{2,1,0:T(8,128)(2,1)S(1)} %pad_maximum_fusion.rest_0_), channel_id=1, source_target_pairs={{0,4},{4,8},{8,12},{12,0},{1,5},{5,9},{9,13},{13,1},{2,6},{6,10},{... | collective-permute-start | bytes 786440 | tf_op jit(solution)/shard_map/ppermute | solution.py:32
  84.3 5.1 %collective-permute-start.5 = (bf16[4,128,256]{2,1,0:T(8,128)(2,1)S(1)}, bf16[4,128,256]{2,1,0:T(8,128)(2,1)S(1)}, u32[]{:S(2)}, u32[]{:S(2)}) collective-permute-start(bf16[4,128,256]{2,1,0:T(8,128)(2,1)S(1)} %pad_maximum_fusion.rest_0_), channel_id=1, source_target_pairs={{0,16},{16,0},{1,17},{17,1},{2,18},{18,2},{3,19},{19,3},{4,20},{20... | collective-permute-start | bytes 786440 | tf_op jit(solution)/shard_map/ppermute | solution.py:28
  89.3 2.1 %collective-permute-start.7 = (bf16[4,128,256]{2,1,0:T(8,128)(2,1)S(1)}, bf16[4,128,256]{2,1,0:T(8,128)(2,1)S(1)}, u32[]{:S(2)}, u32[]{:S(2)}) collective-permute-start(bf16[4,128,256]{2,1,0:T(8,128)(2,1)S(1)} %collective-permute-done.6.rest_2_), channel_id=1, source_target_pairs={{0,16},{16,0},{1,17},{17,1},{2,18},{18,2},{3,19},{19,3},{4,20},{20... | collective-permute-start | bytes 786440 | tf_op jit(solution)/shard_map/ppermute | solution.py:28
  91.5 4.5 %collective-permute-start.9 = (bf16[4,128,256]{2,1,0:T(8,128)(2,1)S(1)}, bf16[4,128,256]{2,1,0:T(8,128)(2,1)S(1)}, u32[]{:S(2)}, u32[]{:S(2)}) collective-permute-start(bf16[4,128,256]{2,1,0:T(8,128)(2,1)S(1)} %collective-permute-done.8.rest_4_), channel_id=1, source_target_pairs={{0,16},{16,0},{1,17},{17,1},{2,18},{18,2},{3,19},{19,3},{4,20},{20... | collective-permute-start | bytes 786440 | tf_op jit(solution)/shard_map/ppermute | solution.py:28
  96.0 2.8 %collective-permute-start.11 = (bf16[4,128,256]{2,1,0:T(8,128)(2,1)S(1)}, bf16[4,128,256]{2,1,0:T(8,128)(2,1)S(1)}, u32[]{:S(2)}, u32[]{:S(2)}) collective-permute-start(bf16[4,128,256]{2,1,0:T(8,128)(2,1)S(1)} %collective-permute-done.10.rest_6_), channel_id=1, source_target_pairs={{0,16},{16,0},{1,17},{17,1},{2,18},{18,2},{3,19},{19,3},{4,20},{20... | collective-permute-start | bytes 786440 | tf_op jit(solution)/shard_map/ppermute | solution.py:28
  99.6 3.7 %all-to-all-start.2 = ((bf16[32,16,256]{2,1,0:T(8,128)(2,1)}), bf16[32,16,256]{2,1,0:T(8,128)(2,1)S(1)}, u32[]{:S(2)}, u32[]{:S(2)}) async-start(bf16[32,16,256]{2,1,0:T(8,128)(2,1)} %shard_map.89), calls=%async_computation.2 | async-start | bytes 524288 | tf_op jit(solution)/shard_map/all_to_all | solution.py:24
  103.3 4.5 %shard_map.88 = (bf16[192,512]{1,0:T(8,128)(2,1)}, bf16[192,2048]{1,0:T(8,128)(2,1)}) custom-call(s32[4]{0:T(128)S(1)} %pad_add_fusion.place, bf16[192,2048]{1,0:T(8,128)(2,1)S(1)} %copy-done.2, f32[192,128]{1,0:T(8,128)S(1)} %get-tuple-element.13.inv_rms, f32[1,2048]{1,0:T(1,128)S(1)} %bitcast.14, bf16[192,512]{1,0:T(8,128)(2,1)S(1)} %copy-done.4, ...), custom_call_target="tpu_custom_call" | custom-call | flops 805306368 | bytes 6373408 | tf_op jit(solution)/shard_map/pallas_call | solution.py:197
  107.8 4.4 %all-to-all-done.2.blocks = bf16[32,16,256]{2,1,0:T(8,128)(2,1)S(1)} async-done(((bf16[32,16,256]{2,1,0:T(8,128)(2,1)}), bf16[32,16,256]{2,1,0:T(8,128)(2,1)S(1)}, u32[]{:S(2)}, u32[]{:S(2)}) %all-to-all-start.2) | async-done | bytes 262176 | tf_op jit(solution)/shard_map/all_to_all | solution.py:24
  (33 shorter events, 3.5 us)
Async XLA Ops:
  0.6 12.9 %copy-start = (f32[1,512]{1,0:T(1,128)S(1)}, f32[1,512]{1,0:T(1,128)}, u32[]{:S(2)}) copy-start(f32[1,512]{1,0:T(1,128)} %param.8) | copy-start | bytes 6148
  0.7 1.1 %copy-start.1 = (bf16[192,2048]{1,0:T(8,128)(2,1)S(1)}, bf16[192,2048]{1,0:T(8,128)(2,1)}, u32[]{:S(2)}) copy-start(bf16[192,2048]{1,0:T(8,128)(2,1)} %tokens.3) | copy-start | bytes 2359300
  1.9 0.9 copy-start.3
  2.8 0.7 copy-start.5
  3.5 11.7 %copy-start.4 = (bf16[192,512]{1,0:T(8,128)(2,1)S(1)}, bf16[192,512]{1,0:T(8,128)(2,1)}, u32[]{:S(2)}) copy-start(bf16[192,512]{1,0:T(8,128)(2,1)} %key_grad.5) | copy-start | bytes 589828
  4.8 11.5 %collective-permute-start = (bf16[16,16,2048]{2,1,0:T(8,128)(2,1)S(1)}, bf16[16,16,2048]{2,1,0:T(8,128)(2,1)S(1)}, u32[]{:S(2)}, u32[]{:S(2)}) collective-permute-start(bf16[16,16,2048]{2,1,0:T(8,128)(2,1)S(1)} %get-tuple-element.15), channel_id=1, source_target_pairs={{0,16},{16,0},{1,17},{17,1},{2,18},{18,2},{3,19},{19,3},{4,20},{20... | collective-permute-start | bytes 3145736 | tf_op jit(solution)/shard_map/ppermute | solution.py:28
  14.5 1.7 %collective-permute-start.1 = (bf16[128,256]{1,0:T(8,128)(2,1)S(1)}, bf16[128,256]{1,0:T(8,128)(2,1)S(1)}, u32[]{:S(2)}, u32[]{:S(2)}) collective-permute-start(bf16[128,256]{1,0:T(8,128)(2,1)S(1)} %multiply_convert_fusion), channel_id=1, source_target_pairs={{0,0},{16,16},{32,419},{48,435},{64,450},{80,466},{96,97},{112,113... | collective-permute-start | bytes 196616 | tf_op jit(solution)/shard_map/ppermute | solution.py:44
  47.0 21.1 %copy-start.7 = (s32[128,512]{1,0:T(8,128)S(1)}, s32[128,512]{1,0:T(8,128)}, u32[]{:S(2)}) copy-start(s32[128,512]{1,0:T(8,128)} %param.7) | copy-start | bytes 786436
  48.7 54.6 %copy-start.2 = (bf16[192,2048]{1,0:T(8,128)(2,1)S(1)}, bf16[192,2048]{1,0:T(8,128)(2,1)}, u32[]{:S(2)}) copy-start(bf16[192,2048]{1,0:T(8,128)(2,1)} %tokens.3) | copy-start | bytes 2359300
  48.7 54.6 %copy-start.6 = (f32[2048]{0:T(1024)S(1)}, f32[2048]{0:T(1024)}, u32[]{:S(2)}) copy-start(f32[2048]{0:T(1024)} %param.6) | copy-start | bytes 24580
  48.7 50.1 %all-to-all-start.1 = ((bf16[16,16,640]{2,1,0:T(8,128)(2,1)}), bf16[16,16,640]{2,1,0:T(8,128)(2,1)S(1)}, u32[]{:S(2)}, u32[]{:S(2)}) async-start(bf16[16,16,640]{2,1,0:T(8,128)(2,1)} %shard_map.87), calls=%async_computation.1 | async-start | bytes 655360 | tf_op jit(solution)/shard_map/all_to_all | solution.py:24
  57.5 15.6 %collective-permute-start.4 = (bf16[128,256]{1,0:T(8,128)(2,1)S(1)}, bf16[128,256]{1,0:T(8,128)(2,1)S(1)}, u32[]{:S(2)}, u32[]{:S(2)}) collective-permute-start(bf16[128,256]{1,0:T(8,128)(2,1)S(1)} %multiply_convert_fusion), channel_id=1, source_target_pairs={{0,1},{16,17},{32,33},{48,49},{64,65},{80,81},{96,97},{112,113},{1... | collective-permute-start | bytes 196616 | tf_op jit(solution)/shard_map/ppermute | solution.py:44
  60.7 12.5 %collective-permute-start.3 = (bf16[128,256]{1,0:T(8,128)(2,1)S(1)}, bf16[128,256]{1,0:T(8,128)(2,1)S(1)}, u32[]{:S(2)}, u32[]{:S(2)}) collective-permute-start(bf16[128,256]{1,0:T(8,128)(2,1)S(1)} %multiply_convert_fusion), channel_id=1, source_target_pairs={{0,2},{16,402},{32,34},{48,434},{64,66},{80,466},{96,98},{112,498}... | collective-permute-start | bytes 196616 | tf_op jit(solution)/shard_map/ppermute | solution.py:44
  65.1 10.9 %collective-permute-start.2 = (bf16[128,256]{1,0:T(8,128)(2,1)S(1)}, bf16[128,256]{1,0:T(8,128)(2,1)S(1)}, u32[]{:S(2)}, u32[]{:S(2)}) collective-permute-start(bf16[128,256]{1,0:T(8,128)(2,1)S(1)} %multiply_convert_fusion), channel_id=1, source_target_pairs={{0,387},{16,403},{32,419},{48,435},{64,451},{80,467},{96,483},{112... | collective-permute-start | bytes 196616 | tf_op jit(solution)/shard_map/ppermute | solution.py:44
  76.0 13.4 %collective-permute-start.6 = (bf16[4,128,256]{2,1,0:T(8,128)(2,1)S(1)}, bf16[4,128,256]{2,1,0:T(8,128)(2,1)S(1)}, u32[]{:S(2)}, u32[]{:S(2)}) collective-permute-start(bf16[4,128,256]{2,1,0:T(8,128)(2,1)S(1)} %pad_maximum_fusion.rest_0_), channel_id=1, source_target_pairs={{0,12},{4,0},{8,4},{12,8},{1,13},{5,1},{9,5},{13,9},{2,14},{6,2},{... | collective-permute-start | bytes 786440 | tf_op jit(solution)/shard_map/ppermute | solution.py:32
  78.9 12.6 %collective-permute-start.8 = (bf16[4,128,256]{2,1,0:T(8,128)(2,1)S(1)}, bf16[4,128,256]{2,1,0:T(8,128)(2,1)S(1)}, u32[]{:S(2)}, u32[]{:S(2)}) collective-permute-start(bf16[4,128,256]{2,1,0:T(8,128)(2,1)S(1)} %pad_maximum_fusion.rest_0_), channel_id=1, source_target_pairs={{0,8},{4,12},{8,0},{12,4},{1,9},{5,13},{9,1},{13,5},{2,10},{6,14},... | collective-permute-start | bytes 786440 | tf_op jit(solution)/shard_map/ppermute | solution.py:32
  82.3 13.7 %collective-permute-start.10 = (bf16[4,128,256]{2,1,0:T(8,128)(2,1)S(1)}, bf16[4,128,256]{2,1,0:T(8,128)(2,1)S(1)}, u32[]{:S(2)}, u32[]{:S(2)}) collective-permute-start(bf16[4,128,256]{2,1,0:T(8,128)(2,1)S(1)} %pad_maximum_fusion.rest_0_), channel_id=1, source_target_pairs={{0,4},{4,8},{8,12},{12,0},{1,5},{5,9},{9,13},{13,1},{2,6},{6,10},{... | collective-permute-start | bytes 786440 | tf_op jit(solution)/shard_map/ppermute | solution.py:32
  84.3 19.0 %collective-permute-start.5 = (bf16[4,128,256]{2,1,0:T(8,128)(2,1)S(1)}, bf16[4,128,256]{2,1,0:T(8,128)(2,1)S(1)}, u32[]{:S(2)}, u32[]{:S(2)}) collective-permute-start(bf16[4,128,256]{2,1,0:T(8,128)(2,1)S(1)} %pad_maximum_fusion.rest_0_), channel_id=1, source_target_pairs={{0,16},{16,0},{1,17},{17,1},{2,18},{18,2},{3,19},{19,3},{4,20},{20... | collective-permute-start | bytes 786440 | tf_op jit(solution)/shard_map/ppermute | solution.py:28
  89.3 13.9 %collective-permute-start.7 = (bf16[4,128,256]{2,1,0:T(8,128)(2,1)S(1)}, bf16[4,128,256]{2,1,0:T(8,128)(2,1)S(1)}, u32[]{:S(2)}, u32[]{:S(2)}) collective-permute-start(bf16[4,128,256]{2,1,0:T(8,128)(2,1)S(1)} %collective-permute-done.6.rest_2_), channel_id=1, source_target_pairs={{0,16},{16,0},{1,17},{17,1},{2,18},{18,2},{3,19},{19,3},{4,20},{20... | collective-permute-start | bytes 786440 | tf_op jit(solution)/shard_map/ppermute | solution.py:28
  91.5 11.8 %collective-permute-start.9 = (bf16[4,128,256]{2,1,0:T(8,128)(2,1)S(1)}, bf16[4,128,256]{2,1,0:T(8,128)(2,1)S(1)}, u32[]{:S(2)}, u32[]{:S(2)}) collective-permute-start(bf16[4,128,256]{2,1,0:T(8,128)(2,1)S(1)} %collective-permute-done.8.rest_4_), channel_id=1, source_target_pairs={{0,16},{16,0},{1,17},{17,1},{2,18},{18,2},{3,19},{19,3},{4,20},{20... | collective-permute-start | bytes 786440 | tf_op jit(solution)/shard_map/ppermute | solution.py:28
  96.0 7.3 %collective-permute-start.11 = (bf16[4,128,256]{2,1,0:T(8,128)(2,1)S(1)}, bf16[4,128,256]{2,1,0:T(8,128)(2,1)S(1)}, u32[]{:S(2)}, u32[]{:S(2)}) collective-permute-start(bf16[4,128,256]{2,1,0:T(8,128)(2,1)S(1)} %collective-permute-done.10.rest_6_), channel_id=1, source_target_pairs={{0,16},{16,0},{1,17},{17,1},{2,18},{18,2},{3,19},{19,3},{4,20},{20... | collective-permute-start | bytes 786440 | tf_op jit(solution)/shard_map/ppermute | solution.py:28
  99.6 12.6 %all-to-all-start.2 = ((bf16[32,16,256]{2,1,0:T(8,128)(2,1)}), bf16[32,16,256]{2,1,0:T(8,128)(2,1)S(1)}, u32[]{:S(2)}, u32[]{:S(2)}) async-start(bf16[32,16,256]{2,1,0:T(8,128)(2,1)} %shard_map.89), calls=%async_computation.2 | async-start | bytes 524288 | tf_op jit(solution)/shard_map/all_to_all | solution.py:24

commit v3 on v2

--- a/solution.py
+++ b/solution.py
@@ -17,7 +17,12 @@
 VMEM = pl.BlockSpec(memory_space=pltpu.VMEM)
 SMEM = pl.BlockSpec(memory_space=pltpu.SMEM)
 ANY = pl.BlockSpec(memory_space=pl.ANY)
+HBM = pl.BlockSpec(memory_space=pltpu.HBM)
 PARAMS = pltpu.CompilerParams(vmem_limit_bytes=40 * 1024 * 1024)
+
+
+def in_hbm(array):
+    return pltpu.with_memory_space_constraint(array, pltpu.HBM)
 
 
 def exchange(blocks, axes):
@@ -58,7 +63,17 @@
             out[sub, :, k * HALF : (k + 1) * HALF] = pair.astype(dtype)
 
 
-def norm_kernel(place, tokens, norm_gain, key_grad, normed, inv_rms, theirs):
+def norm_kernel(place, tokens_at, gain_at, grad_at, normed, inv_rms, theirs, tokens, norm_gain, key_grad, sem):
+    copies = [
+        pltpu.make_async_copy(source, target, sem.at[i])
+        for i, (source, target) in enumerate(
+            ((tokens_at, tokens), (gain_at, norm_gain), (grad_at, key_grad))
+        )
+    ]
+    for copy in copies:
+        copy.start()
+    for copy in copies:
+        copy.wait()
     wide = tokens[...].astype(f32)
     inv = lax.rsqrt(jnp.mean(wide * wide, axis=1, keepdims=True) + eps)
     inv_rms[...] = jnp.broadcast_to(inv, inv_rms.shape)
@@ -217,11 +232,18 @@
     shard = (codes.astype(f32) * scales).astype(bf16)
     gain_rows = along_z(shard, lambda x, core: (0, -1, -2, 1)[x])
 
+    tokens_first, _ = lax.optimization_barrier((tokens, shard))
     normed, inv_rms, theirs = call(
         norm_kernel,
         [((192, 2048), bf16), ((192, 128), f32), ((16, 16, 2048), bf16)],
-        [SMEM, VMEM, VMEM, VMEM],
-        (place, tokens, gain_row, key_grad),
+        [SMEM, HBM, HBM, HBM],
+        (place, in_hbm(tokens_first), in_hbm(gain_row), in_hbm(key_grad)),
+        scratch=[
+            pltpu.VMEM((192, 2048), bf16),
+            pltpu.VMEM((1, 2048), f32),
+            pltpu.VMEM((192, 512), bf16),
+            pltpu.SemaphoreType.DMA((3,)),
+        ],
         flops=2 * 192 * 2048 * 256,
     )
     got = swap(theirs)
@@ -239,6 +261,7 @@
     above = along_z(shard_late, lambda x, core: -1)
     across = along_z(shard_late, lambda x, core: (2, -2)[core])
     below = along_z(shard_late, lambda x, core: 1)
+    square, above, across, below = lax.optimization_barrier((square, above, across, below))
     stack = jnp.stack([shard, above, across, below])
 
     (payload,) = call(
@@ -255,6 +278,7 @@
     for step in range(4):
         piece = stack if step == 0 else along_y(stack_late, -step)
         pieces += [piece, swap(piece)]
+    line, *pieces = lax.optimization_barrier((line, *pieces))
     (blocks,) = call(line_kernel, [((32, 16, HALF), bf16)], [VMEM], (line,))
     blocks = exchange(blocks, ("y", "x", "core"))
     keys, tokens_grad = call(

time: 114 us -> 97.8 us (0.86)
  blocking collectives: 30.5 us -> 0 us
  starting transfers between devices: 55.3 us -> 71.2 us
  Pallas kernels: 10.3 us -> 12.5 us
  local copies, waits for them, and re-layouts: 2.79 us -> 0.68 us
  waiting for transfers between devices: 12.1 us -> 10.6 us
    all_to_all x1 -> x0, blocking collectives: 30.5 us -> none  [exchange(): return lax.all_to_all(blocks, axes, 0, 0, tiled=False)]
    all_to_all x2 -> x3, starting transfers between devices: 12.4 us -> 27.8 us  [exchange(): return lax.all_to_all(blocks, axes, 0, 0, tiled=False)]
    ppermute x4, waiting for transfers between devices: 7.73 us -> 4.02 us  [along_z(): return lax.ppermute(block, ('zh', 'x', 'core', 'zl'), pairs)]
    pallas_call x7, Pallas kernels: 10.3 us -> 12.5 us  [call(): pl.pallas_call(kernel, out_shape=[jax.ShapeDtypeStruct(s, d) for s, d in...]
    unnamed x16 -> x10, local copies, waits for them, and re-layouts: 2.78 us -> 0.68 us
    ppermute x5, waiting for transfers between devices: 0.01 us -> 1.64 us  [swap(): return lax.ppermute(block, 'core', [(0, 1), (1, 0)])]
    all_to_all x2 -> x3, waiting for transfers between devices: 4.36 us -> 4.96 us  [exchange(): return lax.all_to_all(blocks, axes, 0, 0, tiled=False)]
  transfers between devices with their start and end apart: 14 -> 15, of which waited for: 4 -> 5; matrix products, arithmetic and copies ran while one was open for 1% -> 0% of each run, Pallas kernels for 6% -> 6%
where the time goes in v3:
time: 97.8 us; the launch traced here: 97 us
  starting transfers between devices  71.2 us (73%)
  Pallas kernels  12.5 us (13%)
  waiting for transfers between devices  10.6 us (11%)
  other arithmetic  1.06 us (1%)
    all_to_all x3, starting transfers between devices, exchange(): return lax.all_to_all(blocks, axes, 0, 0, tiled=False)  27.8 us
    ppermute x5, starting transfers between devices, swap(): return lax.ppermute(block, 'core', [(0, 1), (1, 0)])  23.4 us
    pallas_call x7, Pallas kernels, call(): pl.pallas_call(kernel, out_shape=[jax.ShapeDtypeStruct(s, d) for s, d in...  12.5 us
    ppermute x4, starting transfers between devices, along_z(): return lax.ppermute(block, ('zh', 'x', 'core', 'zl'), pairs)  12.4 us
    ppermute x3, starting transfers between devices, along_y(): return lax.ppermute(block, 'y', [(y, (y + step) % 4) for y in range(4)])  7.61 us
    all_to_all x3, waiting for transfers between devices, exchange(): return lax.all_to_all(blocks, axes, 0, 0, tiled=False)  4.96 us
    ppermute x4, waiting for transfers between devices, along_z(): return lax.ppermute(block, ('zh', 'x', 'core', 'zl'), pairs)  4.02 us
  transfers between devices with their start and end apart: 15, of which 5 were waited for; matrix products, arithmetic and copies ran while one was open for 0% of the time, Pallas kernels for 6%

profile of v3, /device:TPU:1, one launch (start us, length us, event | category | flops | bytes accessed | tf_op | source)
XLA Modules:
  0.0 97.0 jit_solution(11778254116567021048)
XLA Ops:
  1.3 0.9 multiply_convert_fusion
  2.3 2.5 %shard_map.84 = (bf16[192,2048]{1,0:T(8,128)(2,1)S(1)}, f32[192,128]{1,0:T(8,128)S(1)}, bf16[16,16,2048]{2,1,0:T(8,128)(2,1)S(1)}) custom-call(s32[4]{0:T(128)S(1)} %pad_add_fusion.place, bf16[192,2048]{1,0:T(8,128)(2,1)} %tokens.1, f32[1,2048]{1,0:T(1,128)} %bitcast.13, bf16[192,512]{1,0:T(8,128)(2,1)} %key_grad.3), custom_call_target="tpu_custom_call" | custom-call | flops 201326592 | bytes 1982496 | tf_op jit(solution)/shard_map/pallas_call | solution.py:212
  4.8 8.8 %collective-permute-start = (bf16[16,16,2048]{2,1,0:T(8,128)(2,1)S(1)}, bf16[16,16,2048]{2,1,0:T(8,128)(2,1)S(1)}, u32[]{:S(2)}, u32[]{:S(2)}) collective-permute-start(bf16[16,16,2048]{2,1,0:T(8,128)(2,1)S(1)} %get-tuple-element.30), channel_id=1, source_target_pairs={{0,16},{16,0},{1,17},{17,1},{2,18},{18,2},{3,19},{19,3},{4,20},{20... | collective-permute-start | bytes 3145736 | tf_op jit(solution)/shard_map/ppermute | solution.py:33
  14.3 1.0 %shard_map.85.mine = f32[16,16,2048]{2,1,0:T(8,128)S(1)} custom-call(s32[4]{0:T(128)S(1)} %pad_add_fusion.place, bf16[192,2048]{1,0:T(8,128)(2,1)S(1)} %get-tuple-element.29.normed, bf16[192,512]{1,0:T(8,128)(2,1)S(1)} %copy-done.2), custom_call_target="tpu_custom_call" | custom-call | flops 201326592 | bytes 1966112 | tf_op jit(solution)/shard_map/pallas_call | solution.py:212
  15.9 1.2 %shard_map.86 = bf16[16,16,2176]{2,1,0:T(8,128)(2,1)} custom-call(f32[16,16,2048]{2,1,0:T(8,128)S(1)} %shard_map.85.mine, bf16[16,16,2048]{2,1,0:T(8,128)(2,1)S(1)} %collective-permute-done.got, bf16[128,256]{1,0:T(8,128)(2,1)S(1)} %collective-permute-done.1.rows), custom_call_target="tpu_custom_call" | custom-call | bytes 6422528 | tf_op jit(solution)/shard_map/pallas_call | solution.py:212
  17.1 13.5 %all-to-all-start = ((bf16[16,16,2176]{2,1,0:T(8,128)(2,1)}), bf16[16,16,2176]{2,1,0:T(8,128)(2,1)S(1)}, u32[]{:S(2)}, u32[]{:S(2)}) async-start(bf16[16,16,2176]{2,1,0:T(8,128)(2,1)} %shard_map.86), calls=%async_computation | async-start | bytes 2228224 | tf_op jit(solution)/shard_map/all_to_all | solution.py:29
  30.6 4.7 %collective-permute-start.2 = (bf16[128,256]{1,0:T(8,128)(2,1)S(1)}, bf16[128,256]{1,0:T(8,128)(2,1)S(1)}, u32[]{:S(2)}, u32[]{:S(2)}) collective-permute-start(bf16[128,256]{1,0:T(8,128)(2,1)S(1)} %multiply_convert_fusion), channel_id=1, source_target_pairs={{0,387},{16,403},{32,419},{48,435},{64,451},{80,467},{96,483},{112... | collective-permute-start | bytes 196616 | tf_op jit(solution)/shard_map/ppermute | solution.py:49
  35.3 3.7 %collective-permute-start.3 = (bf16[128,256]{1,0:T(8,128)(2,1)S(1)}, bf16[128,256]{1,0:T(8,128)(2,1)S(1)}, u32[]{:S(2)}, u32[]{:S(2)}) collective-permute-start(bf16[128,256]{1,0:T(8,128)(2,1)S(1)} %multiply_convert_fusion), channel_id=1, source_target_pairs={{0,2},{16,402},{32,34},{48,434},{64,66},{80,466},{96,98},{112,498}... | collective-permute-start | bytes 196616 | tf_op jit(solution)/shard_map/ppermute | solution.py:49
  39.0 3.4 %collective-permute-start.4 = (bf16[128,256]{1,0:T(8,128)(2,1)S(1)}, bf16[128,256]{1,0:T(8,128)(2,1)S(1)}, u32[]{:S(2)}, u32[]{:S(2)}) collective-permute-start(bf16[128,256]{1,0:T(8,128)(2,1)S(1)} %multiply_convert_fusion), channel_id=1, source_target_pairs={{0,1},{16,17},{32,33},{48,49},{64,65},{80,81},{96,97},{112,113},{1... | collective-permute-start | bytes 196616 | tf_op jit(solution)/shard_map/ppermute | solution.py:49
  42.4 4.0 %collective-permute-done.4 = bf16[128,256]{1,0:T(8,128)(2,1)S(1)} collective-permute-done((bf16[128,256]{1,0:T(8,128)(2,1)S(1)}, bf16[128,256]{1,0:T(8,128)(2,1)S(1)}, u32[]{:S(2)}, u32[]{:S(2)}) %collective-permute-start.4) | collective-permute-done | bytes 65568 | tf_op jit(solution)/shard_map/ppermute | solution.py:49
  47.0 1.7 %shard_map.87 = bf16[16,16,640]{2,1,0:T(8,128)(2,1)} custom-call(s32[4]{0:T(128)S(1)} %pad_add_fusion.place, bf16[16,16,2176]{2,1,0:T(8,128)(2,1)S(1)} %all-to-all-done.square), custom_call_target="tpu_custom_call" | custom-call | bytes 2228256 | tf_op jit(solution)/shard_map/pallas_call | solution.py:212
  48.6 8.8 %all-to-all-start.1 = ((bf16[16,16,640]{2,1,0:T(8,128)(2,1)}), bf16[16,16,640]{2,1,0:T(8,128)(2,1)S(1)}, u32[]{:S(2)}, u32[]{:S(2)}) async-start(bf16[16,16,640]{2,1,0:T(8,128)(2,1)} %shard_map.87), calls=%async_computation.1 | async-start | bytes 655360 | tf_op jit(solution)/shard_map/all_to_all | solution.py:29
  57.6 2.6 %collective-permute-start.6 = (bf16[4,128,256]{2,1,0:T(8,128)(2,1)S(1)}, bf16[4,128,256]{2,1,0:T(8,128)(2,1)S(1)}, u32[]{:S(2)}, u32[]{:S(2)}) collective-permute-start(bf16[4,128,256]{2,1,0:T(8,128)(2,1)S(1)} %pad_maximum_fusion.rest_0_), channel_id=1, source_target_pairs={{0,12},{4,0},{8,4},{12,8},{1,13},{5,1},{9,5},{13,9},{2,14},{6,2},{... | collective-permute-start | bytes 786440 | tf_op jit(solution)/shard_map/ppermute | solution.py:37
  60.2 2.5 %collective-permute-start.8 = (bf16[4,128,256]{2,1,0:T(8,128)(2,1)S(1)}, bf16[4,128,256]{2,1,0:T(8,128)(2,1)S(1)}, u32[]{:S(2)}, u32[]{:S(2)}) collective-permute-start(bf16[4,128,256]{2,1,0:T(8,128)(2,1)S(1)} %pad_maximum_fusion.rest_0_), channel_id=1, source_target_pairs={{0,8},{4,12},{8,0},{12,4},{1,9},{5,13},{9,1},{13,5},{2,10},{6,14},... | collective-permute-start | bytes 786440 | tf_op jit(solution)/shard_map/ppermute | solution.py:37
  62.7 2.5 %collective-permute-start.10 = (bf16[4,128,256]{2,1,0:T(8,128)(2,1)S(1)}, bf16[4,128,256]{2,1,0:T(8,128)(2,1)S(1)}, u32[]{:S(2)}, u32[]{:S(2)}) collective-permute-start(bf16[4,128,256]{2,1,0:T(8,128)(2,1)S(1)} %pad_maximum_fusion.rest_0_), channel_id=1, source_target_pairs={{0,4},{4,8},{8,12},{12,0},{1,5},{5,9},{9,13},{13,1},{2,6},{6,10},{... | collective-permute-start | bytes 786440 | tf_op jit(solution)/shard_map/ppermute | solution.py:37
  65.2 5.5 %collective-permute-start.5 = (bf16[4,128,256]{2,1,0:T(8,128)(2,1)S(1)}, bf16[4,128,256]{2,1,0:T(8,128)(2,1)S(1)}, u32[]{:S(2)}, u32[]{:S(2)}) collective-permute-start(bf16[4,128,256]{2,1,0:T(8,128)(2,1)S(1)} %pad_maximum_fusion.rest_0_), channel_id=1, source_target_pairs={{0,16},{16,0},{1,17},{17,1},{2,18},{18,2},{3,19},{19,3},{4,20},{20... | collective-permute-start | bytes 786440 | tf_op jit(solution)/shard_map/ppermute | solution.py:33
  70.8 2.2 %collective-permute-start.7 = (bf16[4,128,256]{2,1,0:T(8,128)(2,1)S(1)}, bf16[4,128,256]{2,1,0:T(8,128)(2,1)S(1)}, u32[]{:S(2)}, u32[]{:S(2)}) collective-permute-start(bf16[4,128,256]{2,1,0:T(8,128)(2,1)S(1)} %collective-permute-done.6.rest_2_), channel_id=1, source_target_pairs={{0,16},{16,0},{1,17},{17,1},{2,18},{18,2},{3,19},{19,3},{4,20},{20... | collective-permute-start | bytes 786440 | tf_op jit(solution)/shard_map/ppermute | solution.py:33
  73.0 4.5 %collective-permute-start.9 = (bf16[4,128,256]{2,1,0:T(8,128)(2,1)S(1)}, bf16[4,128,256]{2,1,0:T(8,128)(2,1)S(1)}, u32[]{:S(2)}, u32[]{:S(2)}) collective-permute-start(bf16[4,128,256]{2,1,0:T(8,128)(2,1)S(1)} %collective-permute-done.8.rest_4_), channel_id=1, source_target_pairs={{0,16},{16,0},{1,17},{17,1},{2,18},{18,2},{3,19},{19,3},{4,20},{20... | collective-permute-start | bytes 786440 | tf_op jit(solution)/shard_map/ppermute | solution.py:33
  77.5 2.4 %collective-permute-start.11 = (bf16[4,128,256]{2,1,0:T(8,128)(2,1)S(1)}, bf16[4,128,256]{2,1,0:T(8,128)(2,1)S(1)}, u32[]{:S(2)}, u32[]{:S(2)}) collective-permute-start(bf16[4,128,256]{2,1,0:T(8,128)(2,1)S(1)} %collective-permute-done.10.rest_6_), channel_id=1, source_target_pairs={{0,16},{16,0},{1,17},{17,1},{2,18},{18,2},{3,19},{19,3},{4,20},{20... | collective-permute-start | bytes 786440 | tf_op jit(solution)/shard_map/ppermute | solution.py:33
  79.9 1.1 %collective-permute-done.11.rest_7_ = bf16[4,128,256]{2,1,0:T(8,128)(2,1)S(1)} collective-permute-done((bf16[4,128,256]{2,1,0:T(8,128)(2,1)S(1)}, bf16[4,128,256]{2,1,0:T(8,128)(2,1)S(1)}, u32[]{:S(2)}, u32[]{:S(2)}) %collective-permute-start.11) | collective-permute-done | bytes 262176 | tf_op jit(solution)/shard_map/ppermute | solution.py:33
  81.8 5.5 %all-to-all-start.2 = ((bf16[32,16,256]{2,1,0:T(8,128)(2,1)}), bf16[32,16,256]{2,1,0:T(8,128)(2,1)S(1)}, u32[]{:S(2)}, u32[]{:S(2)}) async-start(bf16[32,16,256]{2,1,0:T(8,128)(2,1)} %shard_map.89), calls=%async_computation.2 | async-start | bytes 524288 | tf_op jit(solution)/shard_map/all_to_all | solution.py:29
  87.3 4.5 %shard_map.88 = (bf16[192,512]{1,0:T(8,128)(2,1)}, bf16[192,2048]{1,0:T(8,128)(2,1)}) custom-call(s32[4]{0:T(128)S(1)} %pad_add_fusion.place, bf16[192,2048]{1,0:T(8,128)(2,1)S(1)} %copy-done.1, f32[192,128]{1,0:T(8,128)S(1)} %get-tuple-element.28.inv_rms, f32[1,2048]{1,0:T(1,128)S(1)} %bitcast.14, bf16[192,512]{1,0:T(8,128)(2,1)S(1)} %copy-done.2, ...), custom_call_target="tpu_custom_call" | custom-call | flops 805306368 | bytes 6373408 | tf_op jit(solution)/shard_map/pallas_call | solution.py:212
  91.7 4.4 %all-to-all-done.2.blocks = bf16[32,16,256]{2,1,0:T(8,128)(2,1)S(1)} async-done(((bf16[32,16,256]{2,1,0:T(8,128)(2,1)}), bf16[32,16,256]{2,1,0:T(8,128)(2,1)S(1)}, u32[]{:S(2)}, u32[]{:S(2)}) %all-to-all-start.2) | async-done | bytes 262176 | tf_op jit(solution)/shard_map/all_to_all | solution.py:29
  96.2 0.9 shard_map.90
  (28 shorter events, 3.3 us)
Async XLA Ops:
  0.6 0.7 copy-start
  0.6 13.7 %copy-start.2 = (bf16[192,512]{1,0:T(8,128)(2,1)S(1)}, bf16[192,512]{1,0:T(8,128)(2,1)}, u32[]{:S(2)}) copy-start(bf16[192,512]{1,0:T(8,128)(2,1)} %key_grad.3) | copy-start | bytes 589828
  4.8 11.1 %collective-permute-start = (bf16[16,16,2048]{2,1,0:T(8,128)(2,1)S(1)}, bf16[16,16,2048]{2,1,0:T(8,128)(2,1)S(1)}, u32[]{:S(2)}, u32[]{:S(2)}) collective-permute-start(bf16[16,16,2048]{2,1,0:T(8,128)(2,1)S(1)} %get-tuple-element.30), channel_id=1, source_target_pairs={{0,16},{16,0},{1,17},{17,1},{2,18},{18,2},{3,19},{19,3},{4,20},{20... | collective-permute-start | bytes 3145736 | tf_op jit(solution)/shard_map/ppermute | solution.py:33
  13.6 1.7 %collective-permute-start.1 = (bf16[128,256]{1,0:T(8,128)(2,1)S(1)}, bf16[128,256]{1,0:T(8,128)(2,1)S(1)}, u32[]{:S(2)}, u32[]{:S(2)}) collective-permute-start(bf16[128,256]{1,0:T(8,128)(2,1)S(1)} %multiply_convert_fusion), channel_id=1, source_target_pairs={{0,0},{16,16},{32,419},{48,435},{64,450},{80,466},{96,97},{112,113... | collective-permute-start | bytes 196616 | tf_op jit(solution)/shard_map/ppermute | solution.py:49
  17.1 29.9 %all-to-all-start = ((bf16[16,16,2176]{2,1,0:T(8,128)(2,1)}), bf16[16,16,2176]{2,1,0:T(8,128)(2,1)S(1)}, u32[]{:S(2)}, u32[]{:S(2)}) async-start(bf16[16,16,2176]{2,1,0:T(8,128)(2,1)} %shard_map.86), calls=%async_computation | async-start | bytes 2228224 | tf_op jit(solution)/shard_map/all_to_all | solution.py:29
  30.6 26.9 %copy-start.4 = (s32[128,512]{1,0:T(8,128)S(1)}, s32[128,512]{1,0:T(8,128)}, u32[]{:S(2)}) copy-start(s32[128,512]{1,0:T(8,128)} %param.7) | copy-start | bytes 786436
  30.6 11.8 %collective-permute-start.2 = (bf16[128,256]{1,0:T(8,128)(2,1)S(1)}, bf16[128,256]{1,0:T(8,128)(2,1)S(1)}, u32[]{:S(2)}, u32[]{:S(2)}) collective-permute-start(bf16[128,256]{1,0:T(8,128)(2,1)S(1)} %multiply_convert_fusion), channel_id=1, source_target_pairs={{0,387},{16,403},{32,419},{48,435},{64,451},{80,467},{96,483},{112... | collective-permute-start | bytes 196616 | tf_op jit(solution)/shard_map/ppermute | solution.py:49
  35.3 7.1 %collective-permute-start.3 = (bf16[128,256]{1,0:T(8,128)(2,1)S(1)}, bf16[128,256]{1,0:T(8,128)(2,1)S(1)}, u32[]{:S(2)}, u32[]{:S(2)}) collective-permute-start(bf16[128,256]{1,0:T(8,128)(2,1)S(1)} %multiply_convert_fusion), channel_id=1, source_target_pairs={{0,2},{16,402},{32,34},{48,434},{64,66},{80,466},{96,98},{112,498}... | collective-permute-start | bytes 196616 | tf_op jit(solution)/shard_map/ppermute | solution.py:49
  39.0 7.4 %collective-permute-start.4 = (bf16[128,256]{1,0:T(8,128)(2,1)S(1)}, bf16[128,256]{1,0:T(8,128)(2,1)S(1)}, u32[]{:S(2)}, u32[]{:S(2)}) collective-permute-start(bf16[128,256]{1,0:T(8,128)(2,1)S(1)} %multiply_convert_fusion), channel_id=1, source_target_pairs={{0,1},{16,17},{32,33},{48,49},{64,65},{80,81},{96,97},{112,113},{1... | collective-permute-start | bytes 196616 | tf_op jit(solution)/shard_map/ppermute | solution.py:49
  48.6 38.6 %copy-start.1 = (bf16[192,2048]{1,0:T(8,128)(2,1)S(1)}, bf16[192,2048]{1,0:T(8,128)(2,1)}, u32[]{:S(2)}) copy-start(bf16[192,2048]{1,0:T(8,128)(2,1)} %tokens.1) | copy-start | bytes 2359300
  48.6 38.6 %copy-start.3 = (f32[2048]{0:T(1024)S(1)}, f32[2048]{0:T(1024)}, u32[]{:S(2)}) copy-start(f32[2048]{0:T(1024)} %param.6) | copy-start | bytes 24580
  48.6 32.4 %all-to-all-start.1 = ((bf16[16,16,640]{2,1,0:T(8,128)(2,1)}), bf16[16,16,640]{2,1,0:T(8,128)(2,1)S(1)}, u32[]{:S(2)}, u32[]{:S(2)}) async-start(bf16[16,16,640]{2,1,0:T(8,128)(2,1)} %shard_map.87), calls=%async_computation.1 | async-start | bytes 655360 | tf_op jit(solution)/shard_map/all_to_all | solution.py:29
  57.6 13.2 %collective-permute-start.6 = (bf16[4,128,256]{2,1,0:T(8,128)(2,1)S(1)}, bf16[4,128,256]{2,1,0:T(8,128)(2,1)S(1)}, u32[]{:S(2)}, u32[]{:S(2)}) collective-permute-start(bf16[4,128,256]{2,1,0:T(8,128)(2,1)S(1)} %pad_maximum_fusion.rest_0_), channel_id=1, source_target_pairs={{0,12},{4,0},{8,4},{12,8},{1,13},{5,1},{9,5},{13,9},{2,14},{6,2},{... | collective-permute-start | bytes 786440 | tf_op jit(solution)/shard_map/ppermute | solution.py:37
  60.2 12.7 %collective-permute-start.8 = (bf16[4,128,256]{2,1,0:T(8,128)(2,1)S(1)}, bf16[4,128,256]{2,1,0:T(8,128)(2,1)S(1)}, u32[]{:S(2)}, u32[]{:S(2)}) collective-permute-start(bf16[4,128,256]{2,1,0:T(8,128)(2,1)S(1)} %pad_maximum_fusion.rest_0_), channel_id=1, source_target_pairs={{0,8},{4,12},{8,0},{12,4},{1,9},{5,13},{9,1},{13,5},{2,10},{6,14},... | collective-permute-start | bytes 786440 | tf_op jit(solution)/shard_map/ppermute | solution.py:37
  62.7 14.8 %collective-permute-start.10 = (bf16[4,128,256]{2,1,0:T(8,128)(2,1)S(1)}, bf16[4,128,256]{2,1,0:T(8,128)(2,1)S(1)}, u32[]{:S(2)}, u32[]{:S(2)}) collective-permute-start(bf16[4,128,256]{2,1,0:T(8,128)(2,1)S(1)} %pad_maximum_fusion.rest_0_), channel_id=1, source_target_pairs={{0,4},{4,8},{8,12},{12,0},{1,5},{5,9},{9,13},{13,1},{2,6},{6,10},{... | collective-permute-start | bytes 786440 | tf_op jit(solution)/shard_map/ppermute | solution.py:37
  65.2 14.7 %collective-permute-start.5 = (bf16[4,128,256]{2,1,0:T(8,128)(2,1)S(1)}, bf16[4,128,256]{2,1,0:T(8,128)(2,1)S(1)}, u32[]{:S(2)}, u32[]{:S(2)}) collective-permute-start(bf16[4,128,256]{2,1,0:T(8,128)(2,1)S(1)} %pad_maximum_fusion.rest_0_), channel_id=1, source_target_pairs={{0,16},{16,0},{1,17},{17,1},{2,18},{18,2},{3,19},{19,3},{4,20},{20... | collective-permute-start | bytes 786440 | tf_op jit(solution)/shard_map/ppermute | solution.py:33
  70.8 9.1 %collective-permute-start.7 = (bf16[4,128,256]{2,1,0:T(8,128)(2,1)S(1)}, bf16[4,128,256]{2,1,0:T(8,128)(2,1)S(1)}, u32[]{:S(2)}, u32[]{:S(2)}) collective-permute-start(bf16[4,128,256]{2,1,0:T(8,128)(2,1)S(1)} %collective-permute-done.6.rest_2_), channel_id=1, source_target_pairs={{0,16},{16,0},{1,17},{17,1},{2,18},{18,2},{3,19},{19,3},{4,20},{20... | collective-permute-start | bytes 786440 | tf_op jit(solution)/shard_map/ppermute | solution.py:33
  73.0 6.9 %collective-permute-start.9 = (bf16[4,128,256]{2,1,0:T(8,128)(2,1)S(1)}, bf16[4,128,256]{2,1,0:T(8,128)(2,1)S(1)}, u32[]{:S(2)}, u32[]{:S(2)}) collective-permute-start(bf16[4,128,256]{2,1,0:T(8,128)(2,1)S(1)} %collective-permute-done.8.rest_4_), channel_id=1, source_target_pairs={{0,16},{16,0},{1,17},{17,1},{2,18},{18,2},{3,19},{19,3},{4,20},{20... | collective-permute-start | bytes 786440 | tf_op jit(solution)/shard_map/ppermute | solution.py:33
  77.5 3.5 %collective-permute-start.11 = (bf16[4,128,256]{2,1,0:T(8,128)(2,1)S(1)}, bf16[4,128,256]{2,1,0:T(8,128)(2,1)S(1)}, u32[]{:S(2)}, u32[]{:S(2)}) collective-permute-start(bf16[4,128,256]{2,1,0:T(8,128)(2,1)S(1)} %collective-permute-done.10.rest_6_), channel_id=1, source_target_pairs={{0,16},{16,0},{1,17},{17,1},{2,18},{18,2},{3,19},{19,3},{4,20},{20... | collective-permute-start | bytes 786440 | tf_op jit(solution)/shard_map/ppermute | solution.py:33
  81.8 14.4 %all-to-all-start.2 = ((bf16[32,16,256]{2,1,0:T(8,128)(2,1)}), bf16[32,16,256]{2,1,0:T(8,128)(2,1)S(1)}, u32[]{:S(2)}, u32[]{:S(2)}) async-start(bf16[32,16,256]{2,1,0:T(8,128)(2,1)} %shard_map.89), calls=%async_computation.2 | async-start | bytes 524288 | tf_op jit(solution)/shard_map/all_to_all | solution.py:29

commit v4 on v3

--- a/solution.py
+++ b/solution.py
@@ -54,13 +54,14 @@
 
 
 def put_product(normed, grad, out, dtype):
-    for k in range(8):
-        part = contract_rows(normed[:, k * HALF : (k + 1) * HALF], grad)
-        for sub in range(16):
-            pair = jnp.concatenate(
-                [part[sub * 8 : sub * 8 + 8], part[128 + sub * 8 : 136 + sub * 8]], axis=0
-            )
-            out[sub, :, k * HALF : (k + 1) * HALF] = pair.astype(dtype)
+    for part_at in range(8):
+        y, first = part_at // 2, part_at % 2 * 2
+        part = contract_rows(normed[:, part_at * HALF : (part_at + 1) * HALF], grad).astype(dtype)
+        for x in range(4):
+            for k in range(4):
+                row = k // 2 * 128 + x * 32 + k % 2 * 16
+                column = (first * 2 + k) * HALF
+                out[y * 4 + x, :, column : column + HALF] = part[row : row + 16]
 
 
 def norm_kernel(place, tokens_at, gain_at, grad_at, normed, inv_rms, theirs, tokens, norm_gain, key_grad, sem):
@@ -87,27 +88,29 @@
     put_product(normed, key_grad[:, pl.ds(start, HALF)], mine, f32)
 
 
-def pair_kernel(mine, got, rows, out):
-    for sub in range(16):
-        out[sub, :, :2048] = (mine[sub] + got[sub].astype(f32)).astype(bf16)
-        own = rows[sub * 8 : sub * 8 + 8, :].astype(f32)
-        out[sub, :, 2048:] = jnp.concatenate([own[:, :128], own[:, 128:]], axis=0).astype(bf16)
-
-
-def square_kernel(place, square, out, shards, products):
-    zl = place[3]
+def pair_kernel(mine, got, out):
+    for peer in range(16):
+        out[peer] = (mine[peer] + got[peer].astype(f32)).astype(bf16)
+
+
+def two_rows(value):
+    high = value.astype(bf16).astype(f32)
+    row = lax.broadcasted_iota(jnp.int32, (16, 128), 0)
+    return jnp.where(row == 0, high, jnp.where(row == 1, value - high, 0.0)).astype(bf16)
+
+
+def square_kernel(place, square, shard, above, across, below, out, shards, products):
+    x, zl = place[1], place[3]
     for k in range(8):
         cols = slice(k * HALF, (k + 1) * HALF)
         total = square[0, :, cols].astype(f32)
         for sender in range(1, 16):
             total += square[sender, :, cols].astype(f32)
-        shards[2 * k] = total[:8]
-        shards[2 * k + 1] = total[8:]
-    for sender in range(16):
-        shard = sender // 4 * 4 + lax.rem(zl + sender % 4, 4)
-        packed = square[sender, :, 2048:].astype(f32)
-        rows = jnp.concatenate([packed[:8], packed[8:]], axis=1)
-        products[shard] = shards[shard] * rows
+        shards[k // 2, k % 2 * 16 : k % 2 * 16 + 16] = total
+    for j, piece in enumerate((shard, above, across, below)):
+        which = lax.rem(zl + j, 4)
+        rows = piece[pl.ds(pl.multiple_of(x * 32, 32), 32), :].astype(f32)
+        products[which] = shards[which] * rows
     gain = lax.dot_general(
         jnp.ones((16, HALF), f32),
         products[...].reshape(128, HALF),
@@ -115,16 +118,13 @@
         preferred_element_type=f32,
         precision=lax.Precision.HIGHEST,
     )
-    high = gain.astype(bf16).astype(f32)
-    row = lax.broadcasted_iota(jnp.int32, (16, 128), 0)
-    gains = jnp.where(row == 0, high, jnp.where(row == 1, gain - high, 0.0)).astype(bf16)
+    gains = two_rows(gain)
     for target in range(4):
-        first = jnp.concatenate([shards[target], shards[4 + target]], axis=0).astype(bf16)
-        second = jnp.concatenate([shards[8 + target], shards[12 + target]], axis=0).astype(bf16)
+        rows = shards[target].astype(bf16)
         for zh in range(4):
             z = zh * 4 + target
-            out[z, :, :HALF] = first
-            out[z, :, HALF : 2 * HALF] = second
+            out[z, :, :HALF] = rows[:16]
+            out[z, :, HALF : 2 * HALF] = rows[16:]
             out[z, :, 2 * HALF :] = gains
 
 
@@ -132,47 +132,45 @@
     total = line[0].astype(f32)
     for sender in range(1, 16):
         total += line[sender].astype(f32)
-    gain = total[0:1, 512:] + total[1:2, 512:]
-    high = gain.astype(bf16).astype(f32)
-    both = jnp.concatenate([high, gain - high], axis=1)
-    row = lax.broadcasted_iota(jnp.int32, (8, HALF), 0)
-    gains = jnp.where(row == 0, jnp.broadcast_to(both, (8, HALF)), 0.0)
-    for y in range(4):
-        rows = total[y % 2 * 8 : y % 2 * 8 + 8, y // 2 * HALF : (y // 2 + 1) * HALF]
-        block = jnp.concatenate([rows, gains], axis=0).astype(bf16)
-        for peer in range(8):
-            out[y * 8 + peer] = block
-
-
-def last_kernel(blocks, norm_gain, weight_grad, gain_grad):
+    gains = two_rows(jnp.broadcast_to(total[0:1, 512:] + total[1:2, 512:], (16, 128)))
+    rows = total[:, :512].astype(bf16)
+    for peer in range(32):
+        out[peer, :, :512] = rows
+        out[peer, :, 512:] = gains
+
+
+def last_kernel(place, blocks, norm_gain, weight_grad, gain_grad):
+    y = place[2]
+    for x in range(4):
+        for core in range(2):
+            block = blocks[y * 8 + x * 2 + core].astype(f32) / DEVICES
+            for k in range(2):
+                weight_grad[x * 32 + k * 16 : x * 32 + k * 16 + 16, core * HALF : (core + 1) * HALF] = block[
+                    :, k * HALF : (k + 1) * HALF
+                ]
     rows_of = []
-    for sub in range(16):
-        gains = None
-        for core in range(2):
-            block = blocks[sub * 2 + core].astype(f32)
-            weight_grad[sub * 8 : sub * 8 + 8, core * HALF : (core + 1) * HALF] = block[:8] / DEVICES
-            gain = block[8:9, :128] + block[8:9, 128:]
-            gains = gain if gains is None else gains + gain
-        rows_of.append(gains)
+    for peer in range(16):
+        gains = blocks[peer * 2, :, 512:].astype(f32) + blocks[peer * 2 + 1, :, 512:].astype(f32)
+        rows_of.append(gains[0:1] + gains[1:2])
     sums = jnp.concatenate(rows_of, axis=0)
     lane = lax.broadcasted_iota(jnp.int32, (16, 128), 1)
-    sub = lax.broadcasted_iota(jnp.int32, (16, 128), 0)
+    peer = lax.broadcasted_iota(jnp.int32, (16, 128), 0)
     spread = (
-        lax.broadcasted_iota(jnp.int32, (128, 128), 0) % 8
-        == lax.broadcasted_iota(jnp.int32, (128, 128), 1) % 8
+        lax.broadcasted_iota(jnp.int32, (128, 128), 0) % 32
+        == lax.broadcasted_iota(jnp.int32, (128, 128), 1) % 32
     ).astype(f32)
-    stacked = jnp.concatenate(
-        [jnp.where(lane // 8 == shard, sums, 0.0) for shard in range(16)], axis=0
-    )
+    stacked = jnp.concatenate([jnp.where(lane // 32 == zl, sums, 0.0) for zl in range(4)], axis=0)
     moved = lax.dot_general(
         stacked, spread, (((1,), (0,)), ((), ())), preferred_element_type=f32,
         precision=lax.Precision.HIGHEST,
     )
-    for shard in range(16):
-        block = moved[shard * 16 : shard * 16 + 16]
-        gain_grad[shard : shard + 1, :] = jnp.sum(
-            jnp.where(lane // 8 == sub, block, 0.0), axis=0, keepdims=True
-        ) / (norm_gain[shard : shard + 1, :] * DEVICES)
+    for row in range(4):
+        for zl in range(4):
+            picked = jnp.where(peer == row * 4 + lane // 32, moved[zl * 16 : zl * 16 + 16], 0.0)
+            at = row * 4 + zl
+            gain_grad[at : at + 1, :] = jnp.sum(picked, axis=0, keepdims=True) / (
+                norm_gain[at : at + 1, :] * DEVICES
+            )
 
 
 def token_kernel(place, tokens, inv_rms, norm_gain, key_grad, *rest):
@@ -230,14 +228,11 @@
     codes = lax.dynamic_slice_in_dim(weight_codes, core * HALF, HALF, 1)
     scales = lax.dynamic_slice_in_dim(block_scales, core * HALF, HALF, 1)
     shard = (codes.astype(f32) * scales).astype(bf16)
-    gain_rows = along_z(shard, lambda x, core: (0, -1, -2, 1)[x])
-
-    tokens_first, _ = lax.optimization_barrier((tokens, shard))
     normed, inv_rms, theirs = call(
         norm_kernel,
         [((192, 2048), bf16), ((192, 128), f32), ((16, 16, 2048), bf16)],
         [SMEM, HBM, HBM, HBM],
-        (place, in_hbm(tokens_first), in_hbm(gain_row), in_hbm(key_grad)),
+        (place, in_hbm(tokens), in_hbm(gain_row), in_hbm(key_grad)),
         scratch=[
             pltpu.VMEM((192, 2048), bf16),
             pltpu.VMEM((1, 2048), f32),
@@ -254,32 +249,30 @@
         (place, normed, key_grad),
         flops=2 * 192 * 2048 * 256,
     )
-    (pair,) = call(pair_kernel, [((16, 16, 2176), bf16)], [VMEM] * 3, (mine, got, gain_rows))
+    (pair,) = call(pair_kernel, [((16, 16, 2048), bf16)], [VMEM] * 2, (mine, got))
     square = exchange(pair, ("y", "x"))
 
     shard_late, _ = lax.optimization_barrier((shard, pair))
     above = along_z(shard_late, lambda x, core: -1)
     across = along_z(shard_late, lambda x, core: (2, -2)[core])
     below = along_z(shard_late, lambda x, core: 1)
-    square, above, across, below = lax.optimization_barrier((square, above, across, below))
     stack = jnp.stack([shard, above, across, below])
 
     (payload,) = call(
         square_kernel,
         [((16, 16, 640), bf16)],
-        [SMEM, VMEM],
-        (place, square),
-        scratch=[pltpu.VMEM((16, 8, HALF), f32), pltpu.VMEM((16, 8, HALF), f32)],
+        [SMEM] + [VMEM] * 5,
+        (place, square, shard, above, across, below),
+        scratch=[pltpu.VMEM((4, 32, HALF), f32), pltpu.VMEM((4, 32, HALF), f32)],
     )
     line = exchange(payload, Z)
 
     stack_late, _ = lax.optimization_barrier((stack, payload))
-    pieces = []
-    for step in range(4):
-        piece = stack if step == 0 else along_y(stack_late, -step)
-        pieces += [piece, swap(piece)]
+    pieces = [stack] + [along_y(stack_late, -step) for step in range(1, 4)]
     line, *pieces = lax.optimization_barrier((line, *pieces))
-    (blocks,) = call(line_kernel, [((32, 16, HALF), bf16)], [VMEM], (line,))
+    (blocks,) = call(line_kernel, [((32, 16, 640), bf16)], [VMEM], (line,))
+    *late, _ = lax.optimization_barrier((*pieces, blocks))
+    pieces = [part for piece, other in zip(pieces, map(swap, late)) for part in (piece, other)]
     blocks = exchange(blocks, ("y", "x", "core"))
     keys, tokens_grad = call(
         token_kernel,
@@ -292,8 +285,8 @@
     weight_grad, gain_grad = call(
         last_kernel,
         [((128, 512), f32), ((16, 128), f32)],
-        [VMEM] * 2,
-        (blocks, norm_gain.reshape(16, 128)),
+        [SMEM, VMEM, VMEM],
+        (place, blocks, norm_gain.reshape(16, 128)),
     )
     return keys, tokens_grad, weight_grad, gain_grad.reshape(2048)
 

time: 97.8 us -> 94.4 us (0.965)
  starting transfers between devices: 71.2 us -> 60.7 us
  waiting for transfers between devices: 10.6 us -> 17.6 us
    ppermute x3, waiting for transfers between devices: 0.01 us -> 11.5 us  [along_y(): return lax.ppermute(block, 'y', [(y, (y + step) % 4) for y in range(4)])]
    all_to_all x3, starting transfers between devices: 27.8 us -> 21.5 us  [exchange(): return lax.all_to_all(blocks, axes, 0, 0, tiled=False)]
    ppermute x5, starting transfers between devices: 23.4 us -> 17.5 us  [swap(): return lax.ppermute(block, 'core', [(0, 1), (1, 0)])]
    all_to_all x3, waiting for transfers between devices: 4.96 us -> 0.01 us  [exchange(): return lax.all_to_all(blocks, axes, 0, 0, tiled=False)]
    ppermute x4 -> x3, starting transfers between devices: 12.4 us -> 14.6 us  [along_z(): return lax.ppermute(block, ('zh', 'x', 'core', 'zl'), pairs)]
    ppermute x4 -> x3, waiting for transfers between devices: 4.02 us -> 4.6 us  [along_z(): return lax.ppermute(block, ('zh', 'x', 'core', 'zl'), pairs)]
  transfers between devices with their start and end apart: 15 -> 14, of which waited for: 5 -> 6; matrix products, arithmetic and copies ran while one was open for 0% -> 0% of each run, Pallas kernels for 6% -> 6%
where the time goes in v4:
time: 94.4 us; the launch traced here: 93.6 us
  starting transfers between devices  60.7 us (64%)
  waiting for transfers between devices  17.6 us (19%)
  Pallas kernels  13.2 us (14%)
  local copies, waits for them, and re-layouts  0.96 us (1%)
    all_to_all x3, starting transfers between devices, exchange(): return lax.all_to_all(blocks, axes, 0, 0, tiled=False)  21.5 us
    ppermute x5, starting transfers between devices, swap(): return lax.ppermute(block, 'core', [(0, 1), (1, 0)])  17.5 us
    ppermute x3, starting transfers between devices, along_z(): return lax.ppermute(block, ('zh', 'x', 'core', 'zl'), pairs)  14.6 us
    pallas_call x7, Pallas kernels, call(): pl.pallas_call(kernel, out_shape=[jax.ShapeDtypeStruct(s, d) for s, d in...  13.2 us
    ppermute x3, waiting for transfers between devices, along_y(): return lax.ppermute(block, 'y', [(y, (y + step) % 4) for y in range(4)])  11.5 us
    ppermute x3, starting transfers between devices, along_y(): return lax.ppermute(block, 'y', [(y, (y + step) % 4) for y in range(4)])  7.2 us
    ppermute x3, waiting for transfers between devices, along_z(): return lax.ppermute(block, ('zh', 'x', 'core', 'zl'), pairs)  4.6 us
  transfers between devices with their start and end apart: 14, of which 6 were waited for; matrix products, arithmetic and copies ran while one was open for 0% of the time, Pallas kernels for 6%

profile of v4, /device:TPU:1, one launch (start us, length us, event | category | flops | bytes accessed | tf_op | source)
XLA Modules:
  0.0 93.6 jit_solution(14818087261553359659)
XLA Ops:
  0.7 2.5 %shard_map.84 = (bf16[192,2048]{1,0:T(8,128)(2,1)S(1)}, f32[192,128]{1,0:T(8,128)S(1)}, bf16[16,16,2048]{2,1,0:T(8,128)(2,1)S(1)}) custom-call(s32[4]{0:T(128)S(1)} %pad_add_fusion.place, bf16[192,2048]{1,0:T(8,128)(2,1)} %tokens.1, f32[1,2048]{1,0:T(1,128)} %bitcast.16, bf16[192,512]{1,0:T(8,128)(2,1)} %key_grad.3), custom_call_target="tpu_custom_call" | custom-call | flops 201326592 | bytes 1982496 | tf_op jit(solution)/shard_map/pallas_call | solution.py:210
  3.2 8.8 %collective-permute-start = (bf16[16,16,2048]{2,1,0:T(8,128)(2,1)S(1)}, bf16[16,16,2048]{2,1,0:T(8,128)(2,1)S(1)}, u32[]{:S(2)}, u32[]{:S(2)}) collective-permute-start(bf16[16,16,2048]{2,1,0:T(8,128)(2,1)S(1)} %get-tuple-element.24), channel_id=1, source_target_pairs={{0,16},{16,0},{1,17},{17,1},{2,18},{18,2},{3,19},{19,3},{4,20},{20... | collective-permute-start | bytes 3145736 | tf_op jit(solution)/shard_map/ppermute | solution.py:33
  13.0 1.0 %shard_map.85.mine = f32[16,16,2048]{2,1,0:T(8,128)S(1)} custom-call(s32[4]{0:T(128)S(1)} %pad_add_fusion.place, bf16[192,2048]{1,0:T(8,128)(2,1)S(1)} %get-tuple-element.23.normed, bf16[192,512]{1,0:T(8,128)(2,1)S(1)} %copy-done.2), custom_call_target="tpu_custom_call" | custom-call | flops 201326592 | bytes 1966112 | tf_op jit(solution)/shard_map/pallas_call | solution.py:210
  14.3 1.3 %shard_map.86 = bf16[16,16,2048]{2,1,0:T(8,128)(2,1)} custom-call(f32[16,16,2048]{2,1,0:T(8,128)S(1)} %shard_map.85.mine, bf16[16,16,2048]{2,1,0:T(8,128)(2,1)S(1)} %collective-permute-done.got), custom_call_target="tpu_custom_call" | custom-call | bytes 6291456 | tf_op jit(solution)/shard_map/pallas_call | solution.py:210
  15.6 3.8 %all-to-all-start = ((bf16[16,16,2048]{2,1,0:T(8,128)(2,1)}), bf16[16,16,2048]{2,1,0:T(8,128)(2,1)S(1)}, u32[]{:S(2)}, u32[]{:S(2)}) async-start(bf16[16,16,2048]{2,1,0:T(8,128)(2,1)} %shard_map.86), calls=%async_computation | async-start | bytes 2097152 | tf_op jit(solution)/shard_map/all_to_all | solution.py:29
  19.4 8.9 %collective-permute-start.1 = (bf16[128,256]{1,0:T(8,128)(2,1)S(1)}, bf16[128,256]{1,0:T(8,128)(2,1)S(1)}, u32[]{:S(2)}, u32[]{:S(2)}) collective-permute-start(bf16[128,256]{1,0:T(8,128)(2,1)S(1)} %multiply_convert_fusion.shard), channel_id=1, source_target_pairs={{0,387},{16,403},{32,419},{48,435},{64,451},{80,467},{96,483},{112... | collective-permute-start | bytes 196616 | tf_op jit(solution)/shard_map/ppermute | solution.py:49
  28.3 3.1 %collective-permute-start.2 = (bf16[128,256]{1,0:T(8,128)(2,1)S(1)}, bf16[128,256]{1,0:T(8,128)(2,1)S(1)}, u32[]{:S(2)}, u32[]{:S(2)}) collective-permute-start(bf16[128,256]{1,0:T(8,128)(2,1)S(1)} %multiply_convert_fusion.shard), channel_id=1, source_target_pairs={{0,2},{16,402},{32,34},{48,434},{64,66},{80,466},{96,98},{112,498}... | collective-permute-start | bytes 196616 | tf_op jit(solution)/shard_map/ppermute | solution.py:49
  31.4 2.6 %collective-permute-start.3 = (bf16[128,256]{1,0:T(8,128)(2,1)S(1)}, bf16[128,256]{1,0:T(8,128)(2,1)S(1)}, u32[]{:S(2)}, u32[]{:S(2)}) collective-permute-start(bf16[128,256]{1,0:T(8,128)(2,1)S(1)} %multiply_convert_fusion.shard), channel_id=1, source_target_pairs={{0,1},{16,17},{32,33},{48,49},{64,65},{80,81},{96,97},{112,113},{1... | collective-permute-start | bytes 196616 | tf_op jit(solution)/shard_map/ppermute | solution.py:49
  34.3 4.3 %collective-permute-done.3.below = bf16[128,256]{1,0:T(8,128)(2,1)S(1)} collective-permute-done((bf16[128,256]{1,0:T(8,128)(2,1)S(1)}, bf16[128,256]{1,0:T(8,128)(2,1)S(1)}, u32[]{:S(2)}, u32[]{:S(2)}) %collective-permute-start.3) | collective-permute-done | bytes 65568 | tf_op jit(solution)/shard_map/ppermute | solution.py:49
  38.7 1.7 %shard_map.87 = bf16[16,16,640]{2,1,0:T(8,128)(2,1)} custom-call(s32[4]{0:T(128)S(1)} %pad_add_fusion.place, bf16[16,16,2048]{2,1,0:T(8,128)(2,1)S(1)} %all-to-all-done.square, bf16[128,256]{1,0:T(8,128)(2,1)S(1)} %multiply_convert_fusion.shard, bf16[128,256]{1,0:T(8,128)(2,1)S(1)} %collective-permute-done.1.above, ...), custom_call_target="tpu_custom_call" | custom-call | bytes 2621472 | tf_op jit(solution)/shard_map/pallas_call | solution.py:210
  40.3 9.8 %all-to-all-start.1 = ((bf16[16,16,640]{2,1,0:T(8,128)(2,1)}), bf16[16,16,640]{2,1,0:T(8,128)(2,1)S(1)}, u32[]{:S(2)}, u32[]{:S(2)}) async-start(bf16[16,16,640]{2,1,0:T(8,128)(2,1)} %shard_map.87), calls=%async_computation.1 | async-start | bytes 655360 | tf_op jit(solution)/shard_map/all_to_all | solution.py:29
  50.2 2.5 %collective-permute-start.4 = (bf16[4,128,256]{2,1,0:T(8,128)(2,1)S(1)}, bf16[4,128,256]{2,1,0:T(8,128)(2,1)S(1)}, u32[]{:S(2)}, u32[]{:S(2)}) collective-permute-start(bf16[4,128,256]{2,1,0:T(8,128)(2,1)S(1)} %pad_maximum_fusion.rest_0_), channel_id=1, source_target_pairs={{0,12},{4,0},{8,4},{12,8},{1,13},{5,1},{9,5},{13,9},{2,14},{6,2},{... | collective-permute-start | bytes 786440 | tf_op jit(solution)/shard_map/ppermute | solution.py:37
  52.7 2.2 %collective-permute-start.5 = (bf16[4,128,256]{2,1,0:T(8,128)(2,1)S(1)}, bf16[4,128,256]{2,1,0:T(8,128)(2,1)S(1)}, u32[]{:S(2)}, u32[]{:S(2)}) collective-permute-start(bf16[4,128,256]{2,1,0:T(8,128)(2,1)S(1)} %pad_maximum_fusion.rest_0_), channel_id=1, source_target_pairs={{0,8},{4,12},{8,0},{12,4},{1,9},{5,13},{9,1},{13,5},{2,10},{6,14},... | collective-permute-start | bytes 786440 | tf_op jit(solution)/shard_map/ppermute | solution.py:37
  55.0 2.5 %collective-permute-start.6 = (bf16[4,128,256]{2,1,0:T(8,128)(2,1)S(1)}, bf16[4,128,256]{2,1,0:T(8,128)(2,1)S(1)}, u32[]{:S(2)}, u32[]{:S(2)}) collective-permute-start(bf16[4,128,256]{2,1,0:T(8,128)(2,1)S(1)} %pad_maximum_fusion.rest_0_), channel_id=1, source_target_pairs={{0,4},{4,8},{8,12},{12,0},{1,5},{5,9},{9,13},{13,1},{2,6},{6,10},{... | collective-permute-start | bytes 786440 | tf_op jit(solution)/shard_map/ppermute | solution.py:37
  57.5 4.2 %collective-permute-done.5.rest_4_ = bf16[4,128,256]{2,1,0:T(8,128)(2,1)S(1)} collective-permute-done((bf16[4,128,256]{2,1,0:T(8,128)(2,1)S(1)}, bf16[4,128,256]{2,1,0:T(8,128)(2,1)S(1)}, u32[]{:S(2)}, u32[]{:S(2)}) %collective-permute-start.5) | collective-permute-done | bytes 262176 | tf_op jit(solution)/shard_map/ppermute | solution.py:37
  61.6 7.4 %collective-permute-done.6.rest_6_ = bf16[4,128,256]{2,1,0:T(8,128)(2,1)S(1)} collective-permute-done((bf16[4,128,256]{2,1,0:T(8,128)(2,1)S(1)}, bf16[4,128,256]{2,1,0:T(8,128)(2,1)S(1)}, u32[]{:S(2)}, u32[]{:S(2)}) %collective-permute-start.6) | collective-permute-done | bytes 262176 | tf_op jit(solution)/shard_map/ppermute | solution.py:37
  69.9 7.9 %all-to-all-start.2 = ((bf16[32,16,640]{2,1,0:T(8,128)(2,1)}), bf16[32,16,640]{2,1,0:T(8,128)(2,1)S(1)}, u32[]{:S(2)}, u32[]{:S(2)}) async-start(bf16[32,16,640]{2,1,0:T(8,128)(2,1)} %shard_map.88), calls=%async_computation.2 | async-start | bytes 1310720 | tf_op jit(solution)/shard_map/all_to_all | solution.py:29
  77.9 2.1 %collective-permute-start.7 = (bf16[4,128,256]{2,1,0:T(8,128)(2,1)S(1)}, bf16[4,128,256]{2,1,0:T(8,128)(2,1)S(1)}, u32[]{:S(2)}, u32[]{:S(2)}) collective-permute-start(bf16[4,128,256]{2,1,0:T(8,128)(2,1)S(1)} %pad_maximum_fusion.rest_0_), channel_id=1, source_target_pairs={{0,16},{16,0},{1,17},{17,1},{2,18},{18,2},{3,19},{19,3},{4,20},{20... | collective-permute-start | bytes 786440 | tf_op jit(solution)/shard_map/ppermute | solution.py:33
  80.0 2.2 %collective-permute-start.8 = (bf16[4,128,256]{2,1,0:T(8,128)(2,1)S(1)}, bf16[4,128,256]{2,1,0:T(8,128)(2,1)S(1)}, u32[]{:S(2)}, u32[]{:S(2)}) collective-permute-start(bf16[4,128,256]{2,1,0:T(8,128)(2,1)S(1)} %collective-permute-done.4.rest_2_), channel_id=1, source_target_pairs={{0,16},{16,0},{1,17},{17,1},{2,18},{18,2},{3,19},{19,3},{4,20},{20... | collective-permute-start | bytes 786440 | tf_op jit(solution)/shard_map/ppermute | solution.py:33
  82.2 2.1 %collective-permute-start.9 = (bf16[4,128,256]{2,1,0:T(8,128)(2,1)S(1)}, bf16[4,128,256]{2,1,0:T(8,128)(2,1)S(1)}, u32[]{:S(2)}, u32[]{:S(2)}) collective-permute-start(bf16[4,128,256]{2,1,0:T(8,128)(2,1)S(1)} %collective-permute-done.5.rest_4_), channel_id=1, source_target_pairs={{0,16},{16,0},{1,17},{17,1},{2,18},{18,2},{3,19},{19,3},{4,20},{20... | collective-permute-start | bytes 786440 | tf_op jit(solution)/shard_map/ppermute | solution.py:33
  84.3 2.2 %collective-permute-start.10 = (bf16[4,128,256]{2,1,0:T(8,128)(2,1)S(1)}, bf16[4,128,256]{2,1,0:T(8,128)(2,1)S(1)}, u32[]{:S(2)}, u32[]{:S(2)}) collective-permute-start(bf16[4,128,256]{2,1,0:T(8,128)(2,1)S(1)} %collective-permute-done.6.rest_6_), channel_id=1, source_target_pairs={{0,16},{16,0},{1,17},{17,1},{2,18},{18,2},{3,19},{19,3},{4,20},{20... | collective-permute-start | bytes 786440 | tf_op jit(solution)/shard_map/ppermute | solution.py:33
  86.6 1.2 %collective-permute-done.10.rest_7_ = bf16[4,128,256]{2,1,0:T(8,128)(2,1)S(1)} collective-permute-done((bf16[4,128,256]{2,1,0:T(8,128)(2,1)S(1)}, bf16[4,128,256]{2,1,0:T(8,128)(2,1)S(1)}, u32[]{:S(2)}, u32[]{:S(2)}) %collective-permute-start.10) | collective-permute-done | bytes 262176 | tf_op jit(solution)/shard_map/ppermute | solution.py:33
  87.8 4.5 %shard_map.89 = (bf16[192,512]{1,0:T(8,128)(2,1)}, bf16[192,2048]{1,0:T(8,128)(2,1)}) custom-call(s32[4]{0:T(128)S(1)} %pad_add_fusion.place, bf16[192,2048]{1,0:T(8,128)(2,1)S(1)} %copy-done.1, f32[192,128]{1,0:T(8,128)S(1)} %get-tuple-element.22.inv_rms, f32[1,2048]{1,0:T(1,128)S(1)} %bitcast.17, bf16[192,512]{1,0:T(8,128)(2,1)S(1)} %copy-done.3, ...), custom_call_target="tpu_custom_call" | custom-call | flops 805306368 | bytes 6373408 | tf_op jit(solution)/shard_map/pallas_call | solution.py:210
  92.3 1.4 %shard_map.90 = (f32[128,512]{1,0:T(8,128)}, f32[16,128]{1,0:T(8,128)}) custom-call(s32[4]{0:T(128)S(1)} %pad_add_fusion.place, bf16[32,16,640]{2,1,0:T(8,128)(2,1)S(1)} %all-to-all-done.2.blocks, f32[16,128]{1,0:T(8,128)S(1)} %bitcast.18), custom_call_target="tpu_custom_call" | custom-call | bytes 1327136 | tf_op jit(solution)/shard_map/pallas_call | solution.py:210
  (28 shorter events, 2.6 us)
Async XLA Ops:
  0.6 18.7 %copy-start = (f32[1,512]{1,0:T(1,128)S(1)}, f32[1,512]{1,0:T(1,128)}, u32[]{:S(2)}) copy-start(f32[1,512]{1,0:T(1,128)} %param.8) | copy-start | bytes 6148
  3.2 11.1 %collective-permute-start = (bf16[16,16,2048]{2,1,0:T(8,128)(2,1)S(1)}, bf16[16,16,2048]{2,1,0:T(8,128)(2,1)S(1)}, u32[]{:S(2)}, u32[]{:S(2)}) collective-permute-start(bf16[16,16,2048]{2,1,0:T(8,128)(2,1)S(1)} %get-tuple-element.24), channel_id=1, source_target_pairs={{0,16},{16,0},{1,17},{17,1},{2,18},{18,2},{3,19},{19,3},{4,20},{20... | collective-permute-start | bytes 3145736 | tf_op jit(solution)/shard_map/ppermute | solution.py:33
  12.0 0.9 copy-start.2
  15.6 3.8 %copy-start.5 = (s32[128,512]{1,0:T(8,128)S(1)}, s32[128,512]{1,0:T(8,128)}, u32[]{:S(2)}) copy-start(s32[128,512]{1,0:T(8,128)} %param.7) | copy-start | bytes 786436
  15.6 23.1 %all-to-all-start = ((bf16[16,16,2048]{2,1,0:T(8,128)(2,1)}), bf16[16,16,2048]{2,1,0:T(8,128)(2,1)S(1)}, u32[]{:S(2)}, u32[]{:S(2)}) async-start(bf16[16,16,2048]{2,1,0:T(8,128)(2,1)} %shard_map.86), calls=%async_computation | async-start | bytes 2097152 | tf_op jit(solution)/shard_map/all_to_all | solution.py:29
  19.4 14.6 %collective-permute-start.1 = (bf16[128,256]{1,0:T(8,128)(2,1)S(1)}, bf16[128,256]{1,0:T(8,128)(2,1)S(1)}, u32[]{:S(2)}, u32[]{:S(2)}) collective-permute-start(bf16[128,256]{1,0:T(8,128)(2,1)S(1)} %multiply_convert_fusion.shard), channel_id=1, source_target_pairs={{0,387},{16,403},{32,419},{48,435},{64,451},{80,467},{96,483},{112... | collective-permute-start | bytes 196616 | tf_op jit(solution)/shard_map/ppermute | solution.py:49
  28.3 6.0 %collective-permute-start.2 = (bf16[128,256]{1,0:T(8,128)(2,1)S(1)}, bf16[128,256]{1,0:T(8,128)(2,1)S(1)}, u32[]{:S(2)}, u32[]{:S(2)}) collective-permute-start(bf16[128,256]{1,0:T(8,128)(2,1)S(1)} %multiply_convert_fusion.shard), channel_id=1, source_target_pairs={{0,2},{16,402},{32,34},{48,434},{64,66},{80,466},{96,98},{112,498}... | collective-permute-start | bytes 196616 | tf_op jit(solution)/shard_map/ppermute | solution.py:49
  31.4 7.3 %collective-permute-start.3 = (bf16[128,256]{1,0:T(8,128)(2,1)S(1)}, bf16[128,256]{1,0:T(8,128)(2,1)S(1)}, u32[]{:S(2)}, u32[]{:S(2)}) collective-permute-start(bf16[128,256]{1,0:T(8,128)(2,1)S(1)} %multiply_convert_fusion.shard), channel_id=1, source_target_pairs={{0,1},{16,17},{32,33},{48,49},{64,65},{80,81},{96,97},{112,113},{1... | collective-permute-start | bytes 196616 | tf_op jit(solution)/shard_map/ppermute | solution.py:49
  40.3 47.4 %copy-start.1 = (bf16[192,2048]{1,0:T(8,128)(2,1)S(1)}, bf16[192,2048]{1,0:T(8,128)(2,1)}, u32[]{:S(2)}) copy-start(bf16[192,2048]{1,0:T(8,128)(2,1)} %tokens.1) | copy-start | bytes 2359300
  40.3 47.4 %copy-start.3 = (bf16[192,512]{1,0:T(8,128)(2,1)S(1)}, bf16[192,512]{1,0:T(8,128)(2,1)}, u32[]{:S(2)}) copy-start(bf16[192,512]{1,0:T(8,128)(2,1)} %key_grad.3) | copy-start | bytes 589828
  40.3 47.4 %copy-start.4 = (f32[2048]{0:T(1024)S(1)}, f32[2048]{0:T(1024)}, u32[]{:S(2)}) copy-start(f32[2048]{0:T(1024)} %param.6) | copy-start | bytes 24580
  40.3 28.7 %all-to-all-start.1 = ((bf16[16,16,640]{2,1,0:T(8,128)(2,1)}), bf16[16,16,640]{2,1,0:T(8,128)(2,1)S(1)}, u32[]{:S(2)}, u32[]{:S(2)}) async-start(bf16[16,16,640]{2,1,0:T(8,128)(2,1)} %shard_map.87), calls=%async_computation.1 | async-start | bytes 655360 | tf_op jit(solution)/shard_map/all_to_all | solution.py:29
  50.2 7.2 %collective-permute-start.4 = (bf16[4,128,256]{2,1,0:T(8,128)(2,1)S(1)}, bf16[4,128,256]{2,1,0:T(8,128)(2,1)S(1)}, u32[]{:S(2)}, u32[]{:S(2)}) collective-permute-start(bf16[4,128,256]{2,1,0:T(8,128)(2,1)S(1)} %pad_maximum_fusion.rest_0_), channel_id=1, source_target_pairs={{0,12},{4,0},{8,4},{12,8},{1,13},{5,1},{9,5},{13,9},{2,14},{6,2},{... | collective-permute-start | bytes 786440 | tf_op jit(solution)/shard_map/ppermute | solution.py:37
  52.7 8.9 %collective-permute-start.5 = (bf16[4,128,256]{2,1,0:T(8,128)(2,1)S(1)}, bf16[4,128,256]{2,1,0:T(8,128)(2,1)S(1)}, u32[]{:S(2)}, u32[]{:S(2)}) collective-permute-start(bf16[4,128,256]{2,1,0:T(8,128)(2,1)S(1)} %pad_maximum_fusion.rest_0_), channel_id=1, source_target_pairs={{0,8},{4,12},{8,0},{12,4},{1,9},{5,13},{9,1},{13,5},{2,10},{6,14},... | collective-permute-start | bytes 786440 | tf_op jit(solution)/shard_map/ppermute | solution.py:37
  55.0 14.0 %collective-permute-start.6 = (bf16[4,128,256]{2,1,0:T(8,128)(2,1)S(1)}, bf16[4,128,256]{2,1,0:T(8,128)(2,1)S(1)}, u32[]{:S(2)}, u32[]{:S(2)}) collective-permute-start(bf16[4,128,256]{2,1,0:T(8,128)(2,1)S(1)} %pad_maximum_fusion.rest_0_), channel_id=1, source_target_pairs={{0,4},{4,8},{8,12},{12,0},{1,5},{5,9},{9,13},{13,1},{2,6},{6,10},{... | collective-permute-start | bytes 786440 | tf_op jit(solution)/shard_map/ppermute | solution.py:37
  69.9 22.3 %all-to-all-start.2 = ((bf16[32,16,640]{2,1,0:T(8,128)(2,1)}), bf16[32,16,640]{2,1,0:T(8,128)(2,1)S(1)}, u32[]{:S(2)}, u32[]{:S(2)}) async-start(bf16[32,16,640]{2,1,0:T(8,128)(2,1)} %shard_map.88), calls=%async_computation.2 | async-start | bytes 1310720 | tf_op jit(solution)/shard_map/all_to_all | solution.py:29
  77.9 8.7 %collective-permute-start.7 = (bf16[4,128,256]{2,1,0:T(8,128)(2,1)S(1)}, bf16[4,128,256]{2,1,0:T(8,128)(2,1)S(1)}, u32[]{:S(2)}, u32[]{:S(2)}) collective-permute-start(bf16[4,128,256]{2,1,0:T(8,128)(2,1)S(1)} %pad_maximum_fusion.rest_0_), channel_id=1, source_target_pairs={{0,16},{16,0},{1,17},{17,1},{2,18},{18,2},{3,19},{19,3},{4,20},{20... | collective-permute-start | bytes 786440 | tf_op jit(solution)/shard_map/ppermute | solution.py:33
  80.0 6.5 %collective-permute-start.8 = (bf16[4,128,256]{2,1,0:T(8,128)(2,1)S(1)}, bf16[4,128,256]{2,1,0:T(8,128)(2,1)S(1)}, u32[]{:S(2)}, u32[]{:S(2)}) collective-permute-start(bf16[4,128,256]{2,1,0:T(8,128)(2,1)S(1)} %collective-permute-done.4.rest_2_), channel_id=1, source_target_pairs={{0,16},{16,0},{1,17},{17,1},{2,18},{18,2},{3,19},{19,3},{4,20},{20... | collective-permute-start | bytes 786440 | tf_op jit(solution)/shard_map/ppermute | solution.py:33
  82.2 4.4 %collective-permute-start.9 = (bf16[4,128,256]{2,1,0:T(8,128)(2,1)S(1)}, bf16[4,128,256]{2,1,0:T(8,128)(2,1)S(1)}, u32[]{:S(2)}, u32[]{:S(2)}) collective-permute-start(bf16[4,128,256]{2,1,0:T(8,128)(2,1)S(1)} %collective-permute-done.5.rest_4_), channel_id=1, source_target_pairs={{0,16},{16,0},{1,17},{17,1},{2,18},{18,2},{3,19},{19,3},{4,20},{20... | collective-permute-start | bytes 786440 | tf_op jit(solution)/shard_map/ppermute | solution.py:33
  84.3 3.4 %collective-permute-start.10 = (bf16[4,128,256]{2,1,0:T(8,128)(2,1)S(1)}, bf16[4,128,256]{2,1,0:T(8,128)(2,1)S(1)}, u32[]{:S(2)}, u32[]{:S(2)}) collective-permute-start(bf16[4,128,256]{2,1,0:T(8,128)(2,1)S(1)} %collective-permute-done.6.rest_6_), channel_id=1, source_target_pairs={{0,16},{16,0},{1,17},{17,1},{2,18},{18,2},{3,19},{19,3},{4,20},{20... | collective-permute-start | bytes 786440 | tf_op jit(solution)/shard_map/ppermute | solution.py:33

commit v5 on v4

--- a/solution.py
+++ b/solution.py
@@ -65,20 +65,22 @@
 
 
 def norm_kernel(place, tokens_at, gain_at, grad_at, normed, inv_rms, theirs, tokens, norm_gain, key_grad, sem):
+    quarters = [slice(i * 48, i * 48 + 48) for i in range(4)]
+    copies = [(gain_at, norm_gain)] + [(tokens_at.at[rows], tokens.at[rows]) for rows in quarters]
     copies = [
         pltpu.make_async_copy(source, target, sem.at[i])
-        for i, (source, target) in enumerate(
-            ((tokens_at, tokens), (gain_at, norm_gain), (grad_at, key_grad))
-        )
+        for i, (source, target) in enumerate(copies + [(grad_at, key_grad)])
     ]
     for copy in copies:
         copy.start()
-    for copy in copies:
+    copies[0].wait()
+    for copy, rows in zip(copies[1:], quarters):
         copy.wait()
-    wide = tokens[...].astype(f32)
-    inv = lax.rsqrt(jnp.mean(wide * wide, axis=1, keepdims=True) + eps)
-    inv_rms[...] = jnp.broadcast_to(inv, inv_rms.shape)
-    normed[...] = (wide * inv * norm_gain[...]).astype(bf16)
+        wide = tokens[rows, :].astype(f32)
+        inv = lax.rsqrt(jnp.mean(wide * wide, axis=1, keepdims=True) + eps)
+        inv_rms[rows, :] = jnp.broadcast_to(inv, (48, 128))
+        normed[rows, :] = (wide * inv * norm_gain[...]).astype(bf16)
+    copies[5].wait()
     start = pl.multiple_of((1 - place[0]) * HALF, HALF)
     put_product(normed, key_grad[:, pl.ds(start, HALF)], theirs, bf16)
 
@@ -237,7 +239,7 @@
             pltpu.VMEM((192, 2048), bf16),
             pltpu.VMEM((1, 2048), f32),
             pltpu.VMEM((192, 512), bf16),
-            pltpu.SemaphoreType.DMA((3,)),
+            pltpu.SemaphoreType.DMA((6,)),
         ],
         flops=2 * 192 * 2048 * 256,
     )
@@ -268,11 +270,13 @@
     line = exchange(payload, Z)
 
     stack_late, _ = lax.optimization_barrier((stack, payload))
-    pieces = [stack] + [along_y(stack_late, -step) for step in range(1, 4)]
-    line, *pieces = lax.optimization_barrier((line, *pieces))
+    own = stack_late
+    one, two, three = (along_y(stack_late, -step) for step in (1, 2, 3))
+    own_other, one_other = swap(own), swap(one)
+    line, own_other, one_other, two, three = lax.optimization_barrier((line, own_other, one_other, two, three))
     (blocks,) = call(line_kernel, [((32, 16, 640), bf16)], [VMEM], (line,))
-    *late, _ = lax.optimization_barrier((*pieces, blocks))
-    pieces = [part for piece, other in zip(pieces, map(swap, late)) for part in (piece, other)]
+    two_late, three_late, _ = lax.optimization_barrier((two, three, blocks))
+    pieces = (own, own_other, one, one_other, two, swap(two_late), three, swap(three_late))
     blocks = exchange(blocks, ("y", "x", "core"))
     keys, tokens_grad = call(
         token_kernel,

time: 94.4 us -> 94.7 us (level)
    all_to_all x3, starting transfers between devices: 21.5 us -> 17.9 us  [exchange(): return lax.all_to_all(blocks, axes, 0, 0, tiled=False)]
    all_to_all x3, waiting for transfers between devices: 0.01 us -> 2.84 us  [exchange(): return lax.all_to_all(blocks, axes, 0, 0, tiled=False)]
    ppermute x5, starting transfers between devices: 17.5 us -> 19.8 us  [swap(): return lax.ppermute(block, 'core', [(0, 1), (1, 0)])]
    ppermute x3, waiting for transfers between devices: 11.5 us -> 9.49 us  [along_y(): return lax.ppermute(block, 'y', [(y, (y + step) % 4) for y in range(4)])]
  transfers between devices with their start and end apart: 14 -> 14, of which waited for: 6 -> 7; matrix products, arithmetic and copies ran while one was open for 0% -> 0% of each run, Pallas kernels for 6% -> 6%
where the time goes in v5:
time: 94.7 us; the launch traced here: 94 us
  starting transfers between devices  60.1 us (63%)
  waiting for transfers between devices  18.5 us (20%)
  Pallas kernels  13.4 us (14%)
  local copies, waits for them, and re-layouts  0.96 us (1%)
    ppermute x5, starting transfers between devices, swap(): return lax.ppermute(block, 'core', [(0, 1), (1, 0)])  19.8 us
    all_to_all x3, starting transfers between devices, exchange(): return lax.all_to_all(blocks, axes, 0, 0, tiled=False)  17.9 us
    ppermute x3, starting transfers between devices, along_z(): return lax.ppermute(block, ('zh', 'x', 'core', 'zl'), pairs)  14.6 us
    pallas_call x7, Pallas kernels, call(): pl.pallas_call(kernel, out_shape=[jax.ShapeDtypeStruct(s, d) for s, d in...  13.4 us
    ppermute x3, waiting for transfers between devices, along_y(): return lax.ppermute(block, 'y', [(y, (y + step) % 4) for y in range(4)])  9.49 us
    ppermute x3, starting transfers between devices, along_y(): return lax.ppermute(block, 'y', [(y, (y + step) % 4) for y in range(4)])  7.76 us
    ppermute x3, waiting for transfers between devices, along_z(): return lax.ppermute(block, ('zh', 'x', 'core', 'zl'), pairs)  4.6 us
    all_to_all x3, waiting for transfers between devices, exchange(): return lax.all_to_all(blocks, axes, 0, 0, tiled=False)  2.84 us
  transfers between devices with their start and end apart: 14, of which 7 were waited for; matrix products, arithmetic and copies ran while one was open for 0% of the time, Pallas kernels for 6%

profile of v5, /device:TPU:1, one launch (start us, length us, event | category | flops | bytes accessed | tf_op | source)
XLA Modules:
  0.0 94.0 jit_solution(12890762072195176672)
XLA Ops:
  0.7 2.6 %shard_map.84 = (bf16[192,2048]{1,0:T(8,128)(2,1)S(1)}, f32[192,128]{1,0:T(8,128)S(1)}, bf16[16,16,2048]{2,1,0:T(8,128)(2,1)S(1)}) custom-call(s32[4]{0:T(128)S(1)} %pad_add_fusion.place, bf16[192,2048]{1,0:T(8,128)(2,1)} %tokens.1, f32[1,2048]{1,0:T(1,128)} %bitcast.16, bf16[192,512]{1,0:T(8,128)(2,1)} %key_grad.3), custom_call_target="tpu_custom_call" | custom-call | flops 201326592 | bytes 1982496 | tf_op jit(solution)/shard_map/pallas_call | solution.py:212
  3.4 8.8 %collective-permute-start = (bf16[16,16,2048]{2,1,0:T(8,128)(2,1)S(1)}, bf16[16,16,2048]{2,1,0:T(8,128)(2,1)S(1)}, u32[]{:S(2)}, u32[]{:S(2)}) collective-permute-start(bf16[16,16,2048]{2,1,0:T(8,128)(2,1)S(1)} %get-tuple-element.22), channel_id=1, source_target_pairs={{0,16},{16,0},{1,17},{17,1},{2,18},{18,2},{3,19},{19,3},{4,20},{20... | collective-permute-start | bytes 3145736 | tf_op jit(solution)/shard_map/ppermute | solution.py:33
  14.4 1.3 %shard_map.86 = bf16[16,16,2048]{2,1,0:T(8,128)(2,1)} custom-call(f32[16,16,2048]{2,1,0:T(8,128)S(1)} %shard_map.85.mine, bf16[16,16,2048]{2,1,0:T(8,128)(2,1)S(1)} %collective-permute-done.got), custom_call_target="tpu_custom_call" | custom-call | bytes 6291456 | tf_op jit(solution)/shard_map/pallas_call | solution.py:212
  15.7 3.8 %all-to-all-start = ((bf16[16,16,2048]{2,1,0:T(8,128)(2,1)}), bf16[16,16,2048]{2,1,0:T(8,128)(2,1)S(1)}, u32[]{:S(2)}, u32[]{:S(2)}) async-start(bf16[16,16,2048]{2,1,0:T(8,128)(2,1)} %shard_map.86), calls=%async_computation | async-start | bytes 2097152 | tf_op jit(solution)/shard_map/all_to_all | solution.py:29
  19.6 8.9 %collective-permute-start.1 = (bf16[128,256]{1,0:T(8,128)(2,1)S(1)}, bf16[128,256]{1,0:T(8,128)(2,1)S(1)}, u32[]{:S(2)}, u32[]{:S(2)}) collective-permute-start(bf16[128,256]{1,0:T(8,128)(2,1)S(1)} %multiply_convert_fusion.shard), channel_id=1, source_target_pairs={{0,387},{16,403},{32,419},{48,435},{64,451},{80,467},{96,483},{112... | collective-permute-start | bytes 196616 | tf_op jit(solution)/shard_map/ppermute | solution.py:49
  28.4 3.1 %collective-permute-start.2 = (bf16[128,256]{1,0:T(8,128)(2,1)S(1)}, bf16[128,256]{1,0:T(8,128)(2,1)S(1)}, u32[]{:S(2)}, u32[]{:S(2)}) collective-permute-start(bf16[128,256]{1,0:T(8,128)(2,1)S(1)} %multiply_convert_fusion.shard), channel_id=1, source_target_pairs={{0,2},{16,402},{32,34},{48,434},{64,66},{80,466},{96,98},{112,498}... | collective-permute-start | bytes 196616 | tf_op jit(solution)/shard_map/ppermute | solution.py:49
  31.5 2.6 %collective-permute-start.3 = (bf16[128,256]{1,0:T(8,128)(2,1)S(1)}, bf16[128,256]{1,0:T(8,128)(2,1)S(1)}, u32[]{:S(2)}, u32[]{:S(2)}) collective-permute-start(bf16[128,256]{1,0:T(8,128)(2,1)S(1)} %multiply_convert_fusion.shard), channel_id=1, source_target_pairs={{0,1},{16,17},{32,33},{48,49},{64,65},{80,81},{96,97},{112,113},{1... | collective-permute-start | bytes 196616 | tf_op jit(solution)/shard_map/ppermute | solution.py:49
  34.5 4.3 %collective-permute-done.3.below = bf16[128,256]{1,0:T(8,128)(2,1)S(1)} collective-permute-done((bf16[128,256]{1,0:T(8,128)(2,1)S(1)}, bf16[128,256]{1,0:T(8,128)(2,1)S(1)}, u32[]{:S(2)}, u32[]{:S(2)}) %collective-permute-start.3) | collective-permute-done | bytes 65568 | tf_op jit(solution)/shard_map/ppermute | solution.py:49
  38.8 1.7 %shard_map.87 = bf16[16,16,640]{2,1,0:T(8,128)(2,1)} custom-call(s32[4]{0:T(128)S(1)} %pad_add_fusion.place, bf16[16,16,2048]{2,1,0:T(8,128)(2,1)S(1)} %all-to-all-done.square, bf16[128,256]{1,0:T(8,128)(2,1)S(1)} %multiply_convert_fusion.shard, bf16[128,256]{1,0:T(8,128)(2,1)S(1)} %collective-permute-done.1.above, ...), custom_call_target="tpu_custom_call" | custom-call | bytes 2621472 | tf_op jit(solution)/shard_map/pallas_call | solution.py:212
  40.5 9.8 %all-to-all-start.1 = ((bf16[16,16,640]{2,1,0:T(8,128)(2,1)}), bf16[16,16,640]{2,1,0:T(8,128)(2,1)S(1)}, u32[]{:S(2)}, u32[]{:S(2)}) async-start(bf16[16,16,640]{2,1,0:T(8,128)(2,1)} %shard_map.87), calls=%async_computation.1 | async-start | bytes 655360 | tf_op jit(solution)/shard_map/all_to_all | solution.py:29
  50.4 2.5 %collective-permute-start.5 = (bf16[4,128,256]{2,1,0:T(8,128)(2,1)S(1)}, bf16[4,128,256]{2,1,0:T(8,128)(2,1)S(1)}, u32[]{:S(2)}, u32[]{:S(2)}) collective-permute-start(bf16[4,128,256]{2,1,0:T(8,128)(2,1)S(1)} %pad_maximum_fusion.rest_0_), channel_id=1, source_target_pairs={{0,12},{4,0},{8,4},{12,8},{1,13},{5,1},{9,5},{13,9},{2,14},{6,2},{... | collective-permute-start | bytes 786440 | tf_op jit(solution)/shard_map/ppermute | solution.py:37
  52.9 4.2 %collective-permute-start.4 = (bf16[4,128,256]{2,1,0:T(8,128)(2,1)S(1)}, bf16[4,128,256]{2,1,0:T(8,128)(2,1)S(1)}, u32[]{:S(2)}, u32[]{:S(2)}) collective-permute-start(bf16[4,128,256]{2,1,0:T(8,128)(2,1)S(1)} %pad_maximum_fusion.rest_0_), channel_id=1, source_target_pairs={{0,16},{16,0},{1,17},{17,1},{2,18},{18,2},{3,19},{19,3},{4,20},{20... | collective-permute-start | bytes 786440 | tf_op jit(solution)/shard_map/ppermute | solution.py:33
  57.1 2.2 %collective-permute-start.7 = (bf16[4,128,256]{2,1,0:T(8,128)(2,1)S(1)}, bf16[4,128,256]{2,1,0:T(8,128)(2,1)S(1)}, u32[]{:S(2)}, u32[]{:S(2)}) collective-permute-start(bf16[4,128,256]{2,1,0:T(8,128)(2,1)S(1)} %pad_maximum_fusion.rest_0_), channel_id=1, source_target_pairs={{0,8},{4,12},{8,0},{12,4},{1,9},{5,13},{9,1},{13,5},{2,10},{6,14},... | collective-permute-start | bytes 786440 | tf_op jit(solution)/shard_map/ppermute | solution.py:37
  59.4 3.0 %collective-permute-start.8 = (bf16[4,128,256]{2,1,0:T(8,128)(2,1)S(1)}, bf16[4,128,256]{2,1,0:T(8,128)(2,1)S(1)}, u32[]{:S(2)}, u32[]{:S(2)}) collective-permute-start(bf16[4,128,256]{2,1,0:T(8,128)(2,1)S(1)} %pad_maximum_fusion.rest_0_), channel_id=1, source_target_pairs={{0,4},{4,8},{8,12},{12,0},{1,5},{5,9},{9,13},{13,1},{2,6},{6,10},{... | collective-permute-start | bytes 786440 | tf_op jit(solution)/shard_map/ppermute | solution.py:37
  62.4 2.5 %collective-permute-start.6 = (bf16[4,128,256]{2,1,0:T(8,128)(2,1)S(1)}, bf16[4,128,256]{2,1,0:T(8,128)(2,1)S(1)}, u32[]{:S(2)}, u32[]{:S(2)}) collective-permute-start(bf16[4,128,256]{2,1,0:T(8,128)(2,1)S(1)} %collective-permute-done.5.rest_2_), channel_id=1, source_target_pairs={{0,16},{16,0},{1,17},{17,1},{2,18},{18,2},{3,19},{19,3},{4,20},{20... | collective-permute-start | bytes 786440 | tf_op jit(solution)/shard_map/ppermute | solution.py:33
  64.9 3.6 %collective-permute-done.7.rest_4_ = bf16[4,128,256]{2,1,0:T(8,128)(2,1)S(1)} collective-permute-done((bf16[4,128,256]{2,1,0:T(8,128)(2,1)S(1)}, bf16[4,128,256]{2,1,0:T(8,128)(2,1)S(1)}, u32[]{:S(2)}, u32[]{:S(2)}) %collective-permute-start.7) | collective-permute-done | bytes 262176 | tf_op jit(solution)/shard_map/ppermute | solution.py:37
  68.5 5.9 %collective-permute-done.8.rest_6_ = bf16[4,128,256]{2,1,0:T(8,128)(2,1)S(1)} collective-permute-done((bf16[4,128,256]{2,1,0:T(8,128)(2,1)S(1)}, bf16[4,128,256]{2,1,0:T(8,128)(2,1)S(1)}, u32[]{:S(2)}, u32[]{:S(2)}) %collective-permute-start.8) | collective-permute-done | bytes 262176 | tf_op jit(solution)/shard_map/ppermute | solution.py:37
  75.4 4.3 %all-to-all-start.2 = ((bf16[32,16,640]{2,1,0:T(8,128)(2,1)}), bf16[32,16,640]{2,1,0:T(8,128)(2,1)S(1)}, u32[]{:S(2)}, u32[]{:S(2)}) async-start(bf16[32,16,640]{2,1,0:T(8,128)(2,1)} %shard_map.88), calls=%async_computation.2 | async-start | bytes 1310720 | tf_op jit(solution)/shard_map/all_to_all | solution.py:29
  79.7 2.1 %collective-permute-start.10 = (bf16[4,128,256]{2,1,0:T(8,128)(2,1)S(1)}, bf16[4,128,256]{2,1,0:T(8,128)(2,1)S(1)}, u32[]{:S(2)}, u32[]{:S(2)}) collective-permute-start(bf16[4,128,256]{2,1,0:T(8,128)(2,1)S(1)} %collective-permute-done.8.rest_6_), channel_id=1, source_target_pairs={{0,16},{16,0},{1,17},{17,1},{2,18},{18,2},{3,19},{19,3},{4,20},{20... | collective-permute-start | bytes 786440 | tf_op jit(solution)/shard_map/ppermute | solution.py:33
  81.8 2.2 %collective-permute-start.9 = (bf16[4,128,256]{2,1,0:T(8,128)(2,1)S(1)}, bf16[4,128,256]{2,1,0:T(8,128)(2,1)S(1)}, u32[]{:S(2)}, u32[]{:S(2)}) collective-permute-start(bf16[4,128,256]{2,1,0:T(8,128)(2,1)S(1)} %collective-permute-done.7.rest_4_), channel_id=1, source_target_pairs={{0,16},{16,0},{1,17},{17,1},{2,18},{18,2},{3,19},{19,3},{4,20},{20... | collective-permute-start | bytes 786440 | tf_op jit(solution)/shard_map/ppermute | solution.py:33
  84.0 1.2 %collective-permute-done.9.rest_5_ = bf16[4,128,256]{2,1,0:T(8,128)(2,1)S(1)} collective-permute-done((bf16[4,128,256]{2,1,0:T(8,128)(2,1)S(1)}, bf16[4,128,256]{2,1,0:T(8,128)(2,1)S(1)}, u32[]{:S(2)}, u32[]{:S(2)}) %collective-permute-start.9) | collective-permute-done | bytes 262176 | tf_op jit(solution)/shard_map/ppermute | solution.py:33
  85.3 4.5 %shard_map.89 = (bf16[192,512]{1,0:T(8,128)(2,1)}, bf16[192,2048]{1,0:T(8,128)(2,1)}) custom-call(s32[4]{0:T(128)S(1)} %pad_add_fusion.place, bf16[192,2048]{1,0:T(8,128)(2,1)S(1)} %copy-done.1, f32[192,128]{1,0:T(8,128)S(1)} %get-tuple-element.20.inv_rms, f32[1,2048]{1,0:T(1,128)S(1)} %bitcast.17, bf16[192,512]{1,0:T(8,128)(2,1)S(1)} %copy-done.3, ...), custom_call_target="tpu_custom_call" | custom-call | flops 805306368 | bytes 6373408 | tf_op jit(solution)/shard_map/pallas_call | solution.py:212
  89.8 2.8 %all-to-all-done.2.blocks = bf16[32,16,640]{2,1,0:T(8,128)(2,1)S(1)} async-done(((bf16[32,16,640]{2,1,0:T(8,128)(2,1)}), bf16[32,16,640]{2,1,0:T(8,128)(2,1)S(1)}, u32[]{:S(2)}, u32[]{:S(2)}) %all-to-all-start.2) | async-done | bytes 655392 | tf_op jit(solution)/shard_map/all_to_all | solution.py:29
  92.6 1.4 %shard_map.90 = (f32[128,512]{1,0:T(8,128)}, f32[16,128]{1,0:T(8,128)}) custom-call(s32[4]{0:T(128)S(1)} %pad_add_fusion.place, bf16[32,16,640]{2,1,0:T(8,128)(2,1)S(1)} %all-to-all-done.2.blocks, f32[16,128]{1,0:T(8,128)S(1)} %bitcast.18), custom_call_target="tpu_custom_call" | custom-call | bytes 1327136 | tf_op jit(solution)/shard_map/pallas_call | solution.py:212
  (28 shorter events, 3.6 us)
Async XLA Ops:
  0.6 18.9 %copy-start = (f32[1,512]{1,0:T(1,128)S(1)}, f32[1,512]{1,0:T(1,128)}, u32[]{:S(2)}) copy-start(f32[1,512]{1,0:T(1,128)} %param.8) | copy-start | bytes 6148
  3.4 11.1 %collective-permute-start = (bf16[16,16,2048]{2,1,0:T(8,128)(2,1)S(1)}, bf16[16,16,2048]{2,1,0:T(8,128)(2,1)S(1)}, u32[]{:S(2)}, u32[]{:S(2)}) collective-permute-start(bf16[16,16,2048]{2,1,0:T(8,128)(2,1)S(1)} %get-tuple-element.22), channel_id=1, source_target_pairs={{0,16},{16,0},{1,17},{17,1},{2,18},{18,2},{3,19},{19,3},{4,20},{20... | collective-permute-start | bytes 3145736 | tf_op jit(solution)/shard_map/ppermute | solution.py:33
  12.2 0.9 copy-start.2
  15.7 3.8 %copy-start.5 = (s32[128,512]{1,0:T(8,128)S(1)}, s32[128,512]{1,0:T(8,128)}, u32[]{:S(2)}) copy-start(s32[128,512]{1,0:T(8,128)} %param.7) | copy-start | bytes 786436
  15.7 23.1 %all-to-all-start = ((bf16[16,16,2048]{2,1,0:T(8,128)(2,1)}), bf16[16,16,2048]{2,1,0:T(8,128)(2,1)S(1)}, u32[]{:S(2)}, u32[]{:S(2)}) async-start(bf16[16,16,2048]{2,1,0:T(8,128)(2,1)} %shard_map.86), calls=%async_computation | async-start | bytes 2097152 | tf_op jit(solution)/shard_map/all_to_all | solution.py:29
  19.6 14.6 %collective-permute-start.1 = (bf16[128,256]{1,0:T(8,128)(2,1)S(1)}, bf16[128,256]{1,0:T(8,128)(2,1)S(1)}, u32[]{:S(2)}, u32[]{:S(2)}) collective-permute-start(bf16[128,256]{1,0:T(8,128)(2,1)S(1)} %multiply_convert_fusion.shard), channel_id=1, source_target_pairs={{0,387},{16,403},{32,419},{48,435},{64,451},{80,467},{96,483},{112... | collective-permute-start | bytes 196616 | tf_op jit(solution)/shard_map/ppermute | solution.py:49
  28.4 6.0 %collective-permute-start.2 = (bf16[128,256]{1,0:T(8,128)(2,1)S(1)}, bf16[128,256]{1,0:T(8,128)(2,1)S(1)}, u32[]{:S(2)}, u32[]{:S(2)}) collective-permute-start(bf16[128,256]{1,0:T(8,128)(2,1)S(1)} %multiply_convert_fusion.shard), channel_id=1, source_target_pairs={{0,2},{16,402},{32,34},{48,434},{64,66},{80,466},{96,98},{112,498}... | collective-permute-start | bytes 196616 | tf_op jit(solution)/shard_map/ppermute | solution.py:49
  31.5 7.3 %collective-permute-start.3 = (bf16[128,256]{1,0:T(8,128)(2,1)S(1)}, bf16[128,256]{1,0:T(8,128)(2,1)S(1)}, u32[]{:S(2)}, u32[]{:S(2)}) collective-permute-start(bf16[128,256]{1,0:T(8,128)(2,1)S(1)} %multiply_convert_fusion.shard), channel_id=1, source_target_pairs={{0,1},{16,17},{32,33},{48,49},{64,65},{80,81},{96,97},{112,113},{1... | collective-permute-start | bytes 196616 | tf_op jit(solution)/shard_map/ppermute | solution.py:49
  40.5 44.8 %copy-start.1 = (bf16[192,2048]{1,0:T(8,128)(2,1)S(1)}, bf16[192,2048]{1,0:T(8,128)(2,1)}, u32[]{:S(2)}) copy-start(bf16[192,2048]{1,0:T(8,128)(2,1)} %tokens.1) | copy-start | bytes 2359300
  40.5 44.8 %copy-start.3 = (bf16[192,512]{1,0:T(8,128)(2,1)S(1)}, bf16[192,512]{1,0:T(8,128)(2,1)}, u32[]{:S(2)}) copy-start(bf16[192,512]{1,0:T(8,128)(2,1)} %key_grad.3) | copy-start | bytes 589828
  40.5 44.8 %copy-start.4 = (f32[2048]{0:T(1024)S(1)}, f32[2048]{0:T(1024)}, u32[]{:S(2)}) copy-start(f32[2048]{0:T(1024)} %param.6) | copy-start | bytes 24580
  40.5 33.9 %all-to-all-start.1 = ((bf16[16,16,640]{2,1,0:T(8,128)(2,1)}), bf16[16,16,640]{2,1,0:T(8,128)(2,1)S(1)}, u32[]{:S(2)}, u32[]{:S(2)}) async-start(bf16[16,16,640]{2,1,0:T(8,128)(2,1)} %shard_map.87), calls=%async_computation.1 | async-start | bytes 655360 | tf_op jit(solution)/shard_map/all_to_all | solution.py:29
  50.4 12.0 %collective-permute-start.5 = (bf16[4,128,256]{2,1,0:T(8,128)(2,1)S(1)}, bf16[4,128,256]{2,1,0:T(8,128)(2,1)S(1)}, u32[]{:S(2)}, u32[]{:S(2)}) collective-permute-start(bf16[4,128,256]{2,1,0:T(8,128)(2,1)S(1)} %pad_maximum_fusion.rest_0_), channel_id=1, source_target_pairs={{0,12},{4,0},{8,4},{12,8},{1,13},{5,1},{9,5},{13,9},{2,14},{6,2},{... | collective-permute-start | bytes 786440 | tf_op jit(solution)/shard_map/ppermute | solution.py:37
  52.9 12.1 %collective-permute-start.4 = (bf16[4,128,256]{2,1,0:T(8,128)(2,1)S(1)}, bf16[4,128,256]{2,1,0:T(8,128)(2,1)S(1)}, u32[]{:S(2)}, u32[]{:S(2)}) collective-permute-start(bf16[4,128,256]{2,1,0:T(8,128)(2,1)S(1)} %pad_maximum_fusion.rest_0_), channel_id=1, source_target_pairs={{0,16},{16,0},{1,17},{17,1},{2,18},{18,2},{3,19},{19,3},{4,20},{20... | collective-permute-start | bytes 786440 | tf_op jit(solution)/shard_map/ppermute | solution.py:33
  57.1 11.4 %collective-permute-start.7 = (bf16[4,128,256]{2,1,0:T(8,128)(2,1)S(1)}, bf16[4,128,256]{2,1,0:T(8,128)(2,1)S(1)}, u32[]{:S(2)}, u32[]{:S(2)}) collective-permute-start(bf16[4,128,256]{2,1,0:T(8,128)(2,1)S(1)} %pad_maximum_fusion.rest_0_), channel_id=1, source_target_pairs={{0,8},{4,12},{8,0},{12,4},{1,9},{5,13},{9,1},{13,5},{2,10},{6,14},... | collective-permute-start | bytes 786440 | tf_op jit(solution)/shard_map/ppermute | solution.py:37
  59.4 15.0 %collective-permute-start.8 = (bf16[4,128,256]{2,1,0:T(8,128)(2,1)S(1)}, bf16[4,128,256]{2,1,0:T(8,128)(2,1)S(1)}, u32[]{:S(2)}, u32[]{:S(2)}) collective-permute-start(bf16[4,128,256]{2,1,0:T(8,128)(2,1)S(1)} %pad_maximum_fusion.rest_0_), channel_id=1, source_target_pairs={{0,4},{4,8},{8,12},{12,0},{1,5},{5,9},{9,13},{13,1},{2,6},{6,10},{... | collective-permute-start | bytes 786440 | tf_op jit(solution)/shard_map/ppermute | solution.py:37
  62.4 12.0 %collective-permute-start.6 = (bf16[4,128,256]{2,1,0:T(8,128)(2,1)S(1)}, bf16[4,128,256]{2,1,0:T(8,128)(2,1)S(1)}, u32[]{:S(2)}, u32[]{:S(2)}) collective-permute-start(bf16[4,128,256]{2,1,0:T(8,128)(2,1)S(1)} %collective-permute-done.5.rest_2_), channel_id=1, source_target_pairs={{0,16},{16,0},{1,17},{17,1},{2,18},{18,2},{3,19},{19,3},{4,20},{20... | collective-permute-start | bytes 786440 | tf_op jit(solution)/shard_map/ppermute | solution.py:33
  75.4 17.2 %all-to-all-start.2 = ((bf16[32,16,640]{2,1,0:T(8,128)(2,1)}), bf16[32,16,640]{2,1,0:T(8,128)(2,1)S(1)}, u32[]{:S(2)}, u32[]{:S(2)}) async-start(bf16[32,16,640]{2,1,0:T(8,128)(2,1)} %shard_map.88), calls=%async_computation.2 | async-start | bytes 1310720 | tf_op jit(solution)/shard_map/all_to_all | solution.py:29
  79.7 4.3 %collective-permute-start.10 = (bf16[4,128,256]{2,1,0:T(8,128)(2,1)S(1)}, bf16[4,128,256]{2,1,0:T(8,128)(2,1)S(1)}, u32[]{:S(2)}, u32[]{:S(2)}) collective-permute-start(bf16[4,128,256]{2,1,0:T(8,128)(2,1)S(1)} %collective-permute-done.8.rest_6_), channel_id=1, source_target_pairs={{0,16},{16,0},{1,17},{17,1},{2,18},{18,2},{3,19},{19,3},{4,20},{20... | collective-permute-start | bytes 786440 | tf_op jit(solution)/shard_map/ppermute | solution.py:33
  81.8 3.4 %collective-permute-start.9 = (bf16[4,128,256]{2,1,0:T(8,128)(2,1)S(1)}, bf16[4,128,256]{2,1,0:T(8,128)(2,1)S(1)}, u32[]{:S(2)}, u32[]{:S(2)}) collective-permute-start(bf16[4,128,256]{2,1,0:T(8,128)(2,1)S(1)} %collective-permute-done.7.rest_4_), channel_id=1, source_target_pairs={{0,16},{16,0},{1,17},{17,1},{2,18},{18,2},{3,19},{19,3},{4,20},{20... | collective-permute-start | bytes 786440 | tf_op jit(solution)/shard_map/ppermute | solution.py:33

commit v6 on v5

--- a/solution.py
+++ b/solution.py
@@ -10,7 +10,6 @@
 eps = 1e-05
 AXES = ("zh", "x", "core", "y", "zl")
 SIZES = (4, 4, 2, 4, 4)
-Z = ("zh", "zl")
 DEVICES = 512
 HALF = 256
 f32, bf16 = jnp.float32, jnp.bfloat16
@@ -123,20 +122,18 @@
     gains = two_rows(gain)
     for target in range(4):
         rows = shards[target].astype(bf16)
-        for zh in range(4):
-            z = zh * 4 + target
-            out[z, :, :HALF] = rows[:16]
-            out[z, :, HALF : 2 * HALF] = rows[16:]
-            out[z, :, 2 * HALF :] = gains
+        out[target, :, :HALF] = rows[:16]
+        out[target, :, HALF : 2 * HALF] = rows[16:]
+        out[target, :, 2 * HALF :] = gains
 
 
 def line_kernel(line, out):
     total = line[0].astype(f32)
-    for sender in range(1, 16):
+    for sender in range(1, 4):
         total += line[sender].astype(f32)
     gains = two_rows(jnp.broadcast_to(total[0:1, 512:] + total[1:2, 512:], (16, 128)))
     rows = total[:, :512].astype(bf16)
-    for peer in range(32):
+    for peer in range(out.shape[0]):
         out[peer, :, :512] = rows
         out[peer, :, 512:] = gains
 
@@ -176,7 +173,7 @@
 
 
 def token_kernel(place, tokens, inv_rms, norm_gain, key_grad, *rest):
-    pieces, (keys, tokens_grad, weight, sem) = rest[:8], rest[8:]
+    pieces, (keys, tokens_grad, weight, sem) = rest[:4], rest[4:]
     core, y, zl = place[0], place[2], place[3]
     copies = []
     for step in range(4):
@@ -186,7 +183,7 @@
                 row = (lax.rem(y + step, 4) * 4 + lax.rem(zl + j, 4)) * 128
                 copies.append(
                     pltpu.make_async_copy(
-                        pieces[step * 2 + side].at[j],
+                        pieces[side * 2 + step // 2].at[step % 2 * 4 + j],
                         weight.at[pl.ds(pl.multiple_of(row, 128), 128), pl.ds(pl.multiple_of(column, HALF), HALF)],
                         sem.at[len(copies)],
                     )
@@ -262,30 +259,31 @@
 
     (payload,) = call(
         square_kernel,
-        [((16, 16, 640), bf16)],
+        [((4, 16, 640), bf16)],
         [SMEM] + [VMEM] * 5,
         (place, square, shard, above, across, below),
         scratch=[pltpu.VMEM((4, 32, HALF), f32), pltpu.VMEM((4, 32, HALF), f32)],
     )
-    line = exchange(payload, Z)
-
+    near = exchange(payload, "zl")
     stack_late, _ = lax.optimization_barrier((stack, payload))
-    own = stack_late
     one, two, three = (along_y(stack_late, -step) for step in (1, 2, 3))
-    own_other, one_other = swap(own), swap(one)
-    line, own_other, one_other, two, three = lax.optimization_barrier((line, own_other, one_other, two, three))
-    (blocks,) = call(line_kernel, [((32, 16, 640), bf16)], [VMEM], (line,))
-    two_late, three_late, _ = lax.optimization_barrier((two, three, blocks))
-    pieces = (own, own_other, one, one_other, two, swap(two_late), three, swap(three_late))
+    (near_sum,) = call(line_kernel, [((4, 16, 640), bf16)], [VMEM], (near,))
+    far = exchange(near_sum, "zh")
+    halves = jnp.concatenate([stack, one], axis=0), jnp.concatenate([two, three], axis=0)
+    far, *halves = lax.optimization_barrier((far, *halves))
+    (blocks,) = call(line_kernel, [((32, 16, 640), bf16)], [VMEM], (far,))
+    *halves_late, _ = lax.optimization_barrier((*halves, blocks))
+    pieces = (*halves, *map(swap, halves_late))
     blocks = exchange(blocks, ("y", "x", "core"))
     keys, tokens_grad = call(
         token_kernel,
         [((192, 512), bf16), ((192, 2048), bf16)],
-        [SMEM, VMEM, VMEM, VMEM, VMEM] + [ANY] * 8,
+        [SMEM, VMEM, VMEM, VMEM, VMEM] + [ANY] * 4,
         (place, tokens, inv_rms, gain_row, key_grad, *pieces),
         scratch=[pltpu.VMEM((2048, 512), bf16), pltpu.SemaphoreType.DMA((32,))],
         flops=4 * 192 * 2048 * 512,
     )
+    blocks, keys, tokens_grad = lax.optimization_barrier((blocks, keys, tokens_grad))
     weight_grad, gain_grad = call(
         last_kernel,
         [((128, 512), f32), ((16, 128), f32)],

time: 94.7 us -> 98.8 us (1.043)
  waiting for transfers between devices: 18.5 us -> 21.5 us
    all_to_all x3 -> x4, waiting for transfers between devices: 2.84 us -> 10.8 us  [exchange(): return lax.all_to_all(blocks, axes, 0, 0, tiled=False)]
    ppermute x5 -> x3, starting transfers between devices: 19.8 us -> 13.1 us  [swap(): return lax.ppermute(block, 'core', [(0, 1), (1, 0)])]
    all_to_all x3 -> x4, starting transfers between devices: 17.9 us -> 23.4 us  [exchange(): return lax.all_to_all(blocks, axes, 0, 0, tiled=False)]
    ppermute x3, waiting for transfers between devices: 9.49 us -> 4.16 us  [along_y(): return lax.ppermute(block, 'y', [(y, (y + step) % 4) for y in range(4)])]
    ppermute x3, starting transfers between devices: 7.76 us -> 9.53 us  [along_y(): return lax.ppermute(block, 'y', [(y, (y + step) % 4) for y in range(4)])]
    pallas_call x7 -> x8, Pallas kernels: 13.4 us -> 13.9 us  [call(): pl.pallas_call(kernel, out_shape=[jax.ShapeDtypeStruct(s, d) for s, d in...]
  transfers between devices with their start and end apart: 14 -> 13, of which waited for: 7 -> 7; matrix products, arithmetic and copies ran while one was open for 0% -> 0% of each run, Pallas kernels for 6% -> 6%
where the time goes in v6:
time: 98.8 us; the launch traced here: 98.1 us
  starting transfers between devices  60.6 us (61%)
  waiting for transfers between devices  21.5 us (22%)
  Pallas kernels  13.9 us (14%)
  local copies, waits for them, and re-layouts  1 us (1%)
    all_to_all x4, starting transfers between devices, exchange(): return lax.all_to_all(blocks, axes, 0, 0, tiled=False)  23.4 us
    ppermute x3, starting transfers between devices, along_z(): return lax.ppermute(block, ('zh', 'x', 'core', 'zl'), pairs)  14.6 us
    pallas_call x8, Pallas kernels, call(): pl.pallas_call(kernel, out_shape=[jax.ShapeDtypeStruct(s, d) for s, d in...  13.9 us
    ppermute x3, starting transfers between devices, swap(): return lax.ppermute(block, 'core', [(0, 1), (1, 0)])  13.1 us
    all_to_all x4, waiting for transfers between devices, exchange(): return lax.all_to_all(blocks, axes, 0, 0, tiled=False)  10.8 us
    ppermute x3, starting transfers between devices, along_y(): return lax.ppermute(block, 'y', [(y, (y + step) % 4) for y in range(4)])  9.53 us
    ppermute x3, waiting for transfers between devices, along_z(): return lax.ppermute(block, ('zh', 'x', 'core', 'zl'), pairs)  4.59 us
    ppermute x3, waiting for transfers between devices, along_y(): return lax.ppermute(block, 'y', [(y, (y + step) % 4) for y in range(4)])  4.16 us
  transfers between devices with their start and end apart: 13, of which 7 were waited for; matrix products, arithmetic and copies ran while one was open for 0% of the time, Pallas kernels for 6%

profile of v6, /device:TPU:1, one launch (start us, length us, event | category | flops | bytes accessed | tf_op | source)
XLA Modules:
  0.0 98.1 jit_solution(3281297715306301464)
XLA Ops:
  0.7 2.6 %shard_map.84 = (bf16[192,2048]{1,0:T(8,128)(2,1)S(1)}, f32[192,128]{1,0:T(8,128)S(1)}, bf16[16,16,2048]{2,1,0:T(8,128)(2,1)S(1)}) custom-call(s32[4]{0:T(128)S(1)} %pad_add_fusion.place, bf16[192,2048]{1,0:T(8,128)(2,1)} %tokens.1, f32[1,2048]{1,0:T(1,128)} %bitcast.20, bf16[192,512]{1,0:T(8,128)(2,1)} %key_grad.3), custom_call_target="tpu_custom_call" | custom-call | flops 201326592 | bytes 1982496 | tf_op jit(solution)/shard_map/pallas_call | solution.py:209
  3.4 8.8 %collective-permute-start = (bf16[16,16,2048]{2,1,0:T(8,128)(2,1)S(1)}, bf16[16,16,2048]{2,1,0:T(8,128)(2,1)S(1)}, u32[]{:S(2)}, u32[]{:S(2)}) collective-permute-start(bf16[16,16,2048]{2,1,0:T(8,128)(2,1)S(1)} %get-tuple-element.22), channel_id=1, source_target_pairs={{0,16},{16,0},{1,17},{17,1},{2,18},{18,2},{3,19},{19,3},{4,20},{20... | collective-permute-start | bytes 3145736 | tf_op jit(solution)/shard_map/ppermute | solution.py:32
  13.1 1.0 %shard_map.85.mine = f32[16,16,2048]{2,1,0:T(8,128)S(1)} custom-call(s32[4]{0:T(128)S(1)} %pad_add_fusion.place, bf16[192,2048]{1,0:T(8,128)(2,1)S(1)} %get-tuple-element.21.normed, bf16[192,512]{1,0:T(8,128)(2,1)S(1)} %copy-done.2), custom_call_target="tpu_custom_call" | custom-call | flops 201326592 | bytes 1966112 | tf_op jit(solution)/shard_map/pallas_call | solution.py:209
  14.4 1.3 %shard_map.86 = bf16[16,16,2048]{2,1,0:T(8,128)(2,1)} custom-call(f32[16,16,2048]{2,1,0:T(8,128)S(1)} %shard_map.85.mine, bf16[16,16,2048]{2,1,0:T(8,128)(2,1)S(1)} %collective-permute-done.got), custom_call_target="tpu_custom_call" | custom-call | bytes 6291456 | tf_op jit(solution)/shard_map/pallas_call | solution.py:209
  15.7 3.8 %all-to-all-start = ((bf16[16,16,2048]{2,1,0:T(8,128)(2,1)}), bf16[16,16,2048]{2,1,0:T(8,128)(2,1)S(1)}, u32[]{:S(2)}, u32[]{:S(2)}) async-start(bf16[16,16,2048]{2,1,0:T(8,128)(2,1)} %shard_map.86), calls=%async_computation | async-start | bytes 2097152 | tf_op jit(solution)/shard_map/all_to_all | solution.py:28
  19.6 8.9 %collective-permute-start.1 = (bf16[128,256]{1,0:T(8,128)(2,1)S(1)}, bf16[128,256]{1,0:T(8,128)(2,1)S(1)}, u32[]{:S(2)}, u32[]{:S(2)}) collective-permute-start(bf16[128,256]{1,0:T(8,128)(2,1)S(1)} %get-tuple-element.23.shard), channel_id=1, source_target_pairs={{0,387},{16,403},{32,419},{48,435},{64,451},{80,467},{96,483},{112... | collective-permute-start | bytes 196616 | tf_op jit(solution)/shard_map/ppermute | solution.py:48
  28.5 3.1 %collective-permute-start.2 = (bf16[128,256]{1,0:T(8,128)(2,1)S(1)}, bf16[128,256]{1,0:T(8,128)(2,1)S(1)}, u32[]{:S(2)}, u32[]{:S(2)}) collective-permute-start(bf16[128,256]{1,0:T(8,128)(2,1)S(1)} %get-tuple-element.23.shard), channel_id=1, source_target_pairs={{0,2},{16,402},{32,34},{48,434},{64,66},{80,466},{96,98},{112,498}... | collective-permute-start | bytes 196616 | tf_op jit(solution)/shard_map/ppermute | solution.py:48
  31.5 2.6 %collective-permute-start.3 = (bf16[128,256]{1,0:T(8,128)(2,1)S(1)}, bf16[128,256]{1,0:T(8,128)(2,1)S(1)}, u32[]{:S(2)}, u32[]{:S(2)}) collective-permute-start(bf16[128,256]{1,0:T(8,128)(2,1)S(1)} %get-tuple-element.23.shard), channel_id=1, source_target_pairs={{0,1},{16,17},{32,33},{48,49},{64,65},{80,81},{96,97},{112,113},{1... | collective-permute-start | bytes 196616 | tf_op jit(solution)/shard_map/ppermute | solution.py:48
  34.5 4.3 %collective-permute-done.3.below = bf16[128,256]{1,0:T(8,128)(2,1)S(1)} collective-permute-done((bf16[128,256]{1,0:T(8,128)(2,1)S(1)}, bf16[128,256]{1,0:T(8,128)(2,1)S(1)}, u32[]{:S(2)}, u32[]{:S(2)}) %collective-permute-start.3) | collective-permute-done | bytes 65568 | tf_op jit(solution)/shard_map/ppermute | solution.py:48
  38.8 1.6 %shard_map.87 = bf16[4,16,640]{2,1,0:T(8,128)(2,1)} custom-call(s32[4]{0:T(128)S(1)} %pad_add_fusion.place, bf16[16,16,2048]{2,1,0:T(8,128)(2,1)S(1)} %all-to-all-done.square, bf16[128,256]{1,0:T(8,128)(2,1)S(1)} %get-tuple-element.23.shard, bf16[128,256]{1,0:T(8,128)(2,1)S(1)} %collective-permute-done.1.above, ...), custom_call_target="tpu_custom_call" | custom-call | bytes 2621472 | tf_op jit(solution)/shard_map/pallas_call | solution.py:209
  40.4 3.3 %all-to-all-start.1 = ((bf16[4,16,640]{2,1,0:T(8,128)(2,1)}), bf16[4,16,640]{2,1,0:T(8,128)(2,1)S(1)}, u32[]{:S(2)}, u32[]{:S(2)}) async-start(bf16[4,16,640]{2,1,0:T(8,128)(2,1)} %shard_map.87), calls=%async_computation.1 | async-start | bytes 163840 | tf_op jit(solution)/shard_map/all_to_all | solution.py:28
  43.8 4.6 %collective-permute-start.4 = (bf16[4,128,256]{2,1,0:T(8,128)(2,1)S(1)}, bf16[4,128,256]{2,1,0:T(8,128)(2,1)S(1)}, u32[]{:S(2)}, u32[]{:S(2)}) collective-permute-start(bf16[4,128,256]{2,1,0:T(8,128)(2,1)S(1)} %pad_maximum_fusion.1), channel_id=1, source_target_pairs={{0,12},{4,0},{8,4},{12,8},{1,13},{5,1},{9,5},{13,9},{2,14},{6,2},{... | collective-permute-start | bytes 786440 | tf_op jit(solution)/shard_map/ppermute | solution.py:36
  48.4 2.5 %collective-permute-start.5 = (bf16[4,128,256]{2,1,0:T(8,128)(2,1)S(1)}, bf16[4,128,256]{2,1,0:T(8,128)(2,1)S(1)}, u32[]{:S(2)}, u32[]{:S(2)}) collective-permute-start(bf16[4,128,256]{2,1,0:T(8,128)(2,1)S(1)} %pad_maximum_fusion.1), channel_id=1, source_target_pairs={{0,8},{4,12},{8,0},{12,4},{1,9},{5,13},{9,1},{13,5},{2,10},{6,14},... | collective-permute-start | bytes 786440 | tf_op jit(solution)/shard_map/ppermute | solution.py:36
  50.9 2.5 %collective-permute-start.6 = (bf16[4,128,256]{2,1,0:T(8,128)(2,1)S(1)}, bf16[4,128,256]{2,1,0:T(8,128)(2,1)S(1)}, u32[]{:S(2)}, u32[]{:S(2)}) collective-permute-start(bf16[4,128,256]{2,1,0:T(8,128)(2,1)S(1)} %pad_maximum_fusion.1), channel_id=1, source_target_pairs={{0,4},{4,8},{8,12},{12,0},{1,5},{5,9},{9,13},{13,1},{2,6},{6,10},{... | collective-permute-start | bytes 786440 | tf_op jit(solution)/shard_map/ppermute | solution.py:36
  54.0 7.4 %all-to-all-start.2 = ((bf16[4,16,640]{2,1,0:T(8,128)(2,1)}), bf16[4,16,640]{2,1,0:T(8,128)(2,1)S(1)}, u32[]{:S(2)}, u32[]{:S(2)}) async-start(bf16[4,16,640]{2,1,0:T(8,128)(2,1)} %shard_map.88), calls=%async_computation.2 | async-start | bytes 163840 | tf_op jit(solution)/shard_map/all_to_all | solution.py:28
  61.5 4.2 %collective-permute-done.6 = bf16[4,128,256]{2,1,0:T(8,128)(2,1)S(1)} collective-permute-done((bf16[4,128,256]{2,1,0:T(8,128)(2,1)S(1)}, bf16[4,128,256]{2,1,0:T(8,128)(2,1)S(1)}, u32[]{:S(2)}, u32[]{:S(2)}) %collective-permute-start.6) | collective-permute-done | bytes 262176 | tf_op jit(solution)/shard_map/ppermute | solution.py:36
  65.7 8.3 %all-to-all-done.2.line = bf16[4,16,640]{2,1,0:T(8,128)(2,1)S(1)} async-done(((bf16[4,16,640]{2,1,0:T(8,128)(2,1)}), bf16[4,16,640]{2,1,0:T(8,128)(2,1)S(1)}, u32[]{:S(2)}, u32[]{:S(2)}) %all-to-all-start.2) | async-done | bytes 81952 | tf_op jit(solution)/shard_map/all_to_all | solution.py:28
  74.9 8.9 %all-to-all-start.3 = ((bf16[32,16,640]{2,1,0:T(8,128)(2,1)}), bf16[32,16,640]{2,1,0:T(8,128)(2,1)S(1)}, u32[]{:S(2)}, u32[]{:S(2)}) async-start(bf16[32,16,640]{2,1,0:T(8,128)(2,1)} %shard_map.89), calls=%async_computation.3 | async-start | bytes 1310720 | tf_op jit(solution)/shard_map/all_to_all | solution.py:28
  83.8 2.1 %collective-permute-start.7 = (bf16[8,128,256]{2,1,0:T(8,128)(2,1)S(1)}, bf16[8,128,256]{2,1,0:T(8,128)(2,1)S(1)}, u32[]{:S(2)}, u32[]{:S(2)}) collective-permute-start(bf16[8,128,256]{2,1,0:T(8,128)(2,1)S(1)} %constant_dynamic-update-slice_fusion.rest_0_), channel_id=1, source_target_pairs={{0,16},{16,0},{1,17},{17,1},{2,18},{18,2},{3,19},{19,3},{4,20},{20... | collective-permute-start | bytes 1572872 | tf_op jit(solution)/shard_map/ppermute | solution.py:32
  86.0 2.2 %collective-permute-start.8 = (bf16[8,128,256]{2,1,0:T(8,128)(2,1)S(1)}, bf16[8,128,256]{2,1,0:T(8,128)(2,1)S(1)}, u32[]{:S(2)}, u32[]{:S(2)}) collective-permute-start(bf16[8,128,256]{2,1,0:T(8,128)(2,1)S(1)} %pad_maximum_fusion.rest_1_), channel_id=1, source_target_pairs={{0,16},{16,0},{1,17},{17,1},{2,18},{18,2},{3,19},{19,3},{4,20},{20... | collective-permute-start | bytes 1572872 | tf_op jit(solution)/shard_map/ppermute | solution.py:32
  88.2 1.6 %collective-permute-done.8.rest_3_ = bf16[8,128,256]{2,1,0:T(8,128)(2,1)S(1)} collective-permute-done((bf16[8,128,256]{2,1,0:T(8,128)(2,1)S(1)}, bf16[8,128,256]{2,1,0:T(8,128)(2,1)S(1)}, u32[]{:S(2)}, u32[]{:S(2)}) %collective-permute-start.8) | collective-permute-done | bytes 524320 | tf_op jit(solution)/shard_map/ppermute | solution.py:32
  89.8 4.5 %shard_map.90 = (bf16[192,512]{1,0:T(8,128)(2,1)}, bf16[192,2048]{1,0:T(8,128)(2,1)}) custom-call(s32[4]{0:T(128)S(1)} %pad_add_fusion.place, bf16[192,2048]{1,0:T(8,128)(2,1)S(1)} %copy-done.1, f32[192,128]{1,0:T(8,128)S(1)} %get-tuple-element.26.inv_rms, f32[1,2048]{1,0:T(1,128)S(1)} %bitcast.21, bf16[192,512]{1,0:T(8,128)(2,1)S(1)} %copy-done.3, ...), custom_call_target="tpu_custom_call" | custom-call | flops 805306368 | bytes 6373408 | tf_op jit(solution)/shard_map/pallas_call | solution.py:209
  94.2 2.5 %all-to-all-done.3.blocks = bf16[32,16,640]{2,1,0:T(8,128)(2,1)S(1)} async-done(((bf16[32,16,640]{2,1,0:T(8,128)(2,1)}), bf16[32,16,640]{2,1,0:T(8,128)(2,1)S(1)}, u32[]{:S(2)}, u32[]{:S(2)}) %all-to-all-start.3) | async-done | bytes 655392 | tf_op jit(solution)/shard_map/all_to_all | solution.py:28
  96.7 1.4 %shard_map.91 = (f32[128,512]{1,0:T(8,128)}, f32[16,128]{1,0:T(8,128)}) custom-call(s32[4]{0:T(128)S(1)} %pad_add_fusion.place, bf16[32,16,640]{2,1,0:T(8,128)(2,1)S(1)} %all-to-all-done.3.blocks, f32[16,128]{1,0:T(8,128)S(1)} %bitcast.22), custom_call_target="tpu_custom_call" | custom-call | bytes 1327136 | tf_op jit(solution)/shard_map/pallas_call | solution.py:209
  (31 shorter events, 3.3 us)
Async XLA Ops:
  0.6 18.9 %copy-start = (f32[1,512]{1,0:T(1,128)S(1)}, f32[1,512]{1,0:T(1,128)}, u32[]{:S(2)}) copy-start(f32[1,512]{1,0:T(1,128)} %param.8) | copy-start | bytes 6148
  3.4 11.1 %collective-permute-start = (bf16[16,16,2048]{2,1,0:T(8,128)(2,1)S(1)}, bf16[16,16,2048]{2,1,0:T(8,128)(2,1)S(1)}, u32[]{:S(2)}, u32[]{:S(2)}) collective-permute-start(bf16[16,16,2048]{2,1,0:T(8,128)(2,1)S(1)} %get-tuple-element.22), channel_id=1, source_target_pairs={{0,16},{16,0},{1,17},{17,1},{2,18},{18,2},{3,19},{19,3},{4,20},{20... | collective-permute-start | bytes 3145736 | tf_op jit(solution)/shard_map/ppermute | solution.py:32
  12.2 0.9 copy-start.2
  15.7 3.8 %copy-start.5 = (s32[128,512]{1,0:T(8,128)S(1)}, s32[128,512]{1,0:T(8,128)}, u32[]{:S(2)}) copy-start(s32[128,512]{1,0:T(8,128)} %param.7) | copy-start | bytes 786436
  15.7 23.1 %all-to-all-start = ((bf16[16,16,2048]{2,1,0:T(8,128)(2,1)}), bf16[16,16,2048]{2,1,0:T(8,128)(2,1)S(1)}, u32[]{:S(2)}, u32[]{:S(2)}) async-start(bf16[16,16,2048]{2,1,0:T(8,128)(2,1)} %shard_map.86), calls=%async_computation | async-start | bytes 2097152 | tf_op jit(solution)/shard_map/all_to_all | solution.py:28
  19.6 14.6 %collective-permute-start.1 = (bf16[128,256]{1,0:T(8,128)(2,1)S(1)}, bf16[128,256]{1,0:T(8,128)(2,1)S(1)}, u32[]{:S(2)}, u32[]{:S(2)}) collective-permute-start(bf16[128,256]{1,0:T(8,128)(2,1)S(1)} %get-tuple-element.23.shard), channel_id=1, source_target_pairs={{0,387},{16,403},{32,419},{48,435},{64,451},{80,467},{96,483},{112... | collective-permute-start | bytes 196616 | tf_op jit(solution)/shard_map/ppermute | solution.py:48
  28.5 6.0 %collective-permute-start.2 = (bf16[128,256]{1,0:T(8,128)(2,1)S(1)}, bf16[128,256]{1,0:T(8,128)(2,1)S(1)}, u32[]{:S(2)}, u32[]{:S(2)}) collective-permute-start(bf16[128,256]{1,0:T(8,128)(2,1)S(1)} %get-tuple-element.23.shard), channel_id=1, source_target_pairs={{0,2},{16,402},{32,34},{48,434},{64,66},{80,466},{96,98},{112,498}... | collective-permute-start | bytes 196616 | tf_op jit(solution)/shard_map/ppermute | solution.py:48
  31.5 7.3 %collective-permute-start.3 = (bf16[128,256]{1,0:T(8,128)(2,1)S(1)}, bf16[128,256]{1,0:T(8,128)(2,1)S(1)}, u32[]{:S(2)}, u32[]{:S(2)}) collective-permute-start(bf16[128,256]{1,0:T(8,128)(2,1)S(1)} %get-tuple-element.23.shard), channel_id=1, source_target_pairs={{0,1},{16,17},{32,33},{48,49},{64,65},{80,81},{96,97},{112,113},{1... | collective-permute-start | bytes 196616 | tf_op jit(solution)/shard_map/ppermute | solution.py:48
  40.4 13.0 %all-to-all-start.1 = ((bf16[4,16,640]{2,1,0:T(8,128)(2,1)}), bf16[4,16,640]{2,1,0:T(8,128)(2,1)S(1)}, u32[]{:S(2)}, u32[]{:S(2)}) async-start(bf16[4,16,640]{2,1,0:T(8,128)(2,1)} %shard_map.87), calls=%async_computation.1 | async-start | bytes 163840 | tf_op jit(solution)/shard_map/all_to_all | solution.py:28
  43.8 46.0 %copy-start.1 = (bf16[192,2048]{1,0:T(8,128)(2,1)S(1)}, bf16[192,2048]{1,0:T(8,128)(2,1)}, u32[]{:S(2)}) copy-start(bf16[192,2048]{1,0:T(8,128)(2,1)} %tokens.1) | copy-start | bytes 2359300
  43.8 46.0 %copy-start.3 = (bf16[192,512]{1,0:T(8,128)(2,1)S(1)}, bf16[192,512]{1,0:T(8,128)(2,1)}, u32[]{:S(2)}) copy-start(bf16[192,512]{1,0:T(8,128)(2,1)} %key_grad.3) | copy-start | bytes 589828
  43.8 46.0 %copy-start.4 = (f32[2048]{0:T(1024)S(1)}, f32[2048]{0:T(1024)}, u32[]{:S(2)}) copy-start(f32[2048]{0:T(1024)} %param.6) | copy-start | bytes 24580
  43.8 17.6 %collective-permute-start.4 = (bf16[4,128,256]{2,1,0:T(8,128)(2,1)S(1)}, bf16[4,128,256]{2,1,0:T(8,128)(2,1)S(1)}, u32[]{:S(2)}, u32[]{:S(2)}) collective-permute-start(bf16[4,128,256]{2,1,0:T(8,128)(2,1)S(1)} %pad_maximum_fusion.1), channel_id=1, source_target_pairs={{0,12},{4,0},{8,4},{12,8},{1,13},{5,1},{9,5},{13,9},{2,14},{6,2},{... | collective-permute-start | bytes 786440 | tf_op jit(solution)/shard_map/ppermute | solution.py:36
  48.4 13.1 %collective-permute-start.5 = (bf16[4,128,256]{2,1,0:T(8,128)(2,1)S(1)}, bf16[4,128,256]{2,1,0:T(8,128)(2,1)S(1)}, u32[]{:S(2)}, u32[]{:S(2)}) collective-permute-start(bf16[4,128,256]{2,1,0:T(8,128)(2,1)S(1)} %pad_maximum_fusion.1), channel_id=1, source_target_pairs={{0,8},{4,12},{8,0},{12,4},{1,9},{5,13},{9,1},{13,5},{2,10},{6,14},... | collective-permute-start | bytes 786440 | tf_op jit(solution)/shard_map/ppermute | solution.py:36
  50.9 14.8 %collective-permute-start.6 = (bf16[4,128,256]{2,1,0:T(8,128)(2,1)S(1)}, bf16[4,128,256]{2,1,0:T(8,128)(2,1)S(1)}, u32[]{:S(2)}, u32[]{:S(2)}) collective-permute-start(bf16[4,128,256]{2,1,0:T(8,128)(2,1)S(1)} %pad_maximum_fusion.1), channel_id=1, source_target_pairs={{0,4},{4,8},{8,12},{12,0},{1,5},{5,9},{9,13},{13,1},{2,6},{6,10},{... | collective-permute-start | bytes 786440 | tf_op jit(solution)/shard_map/ppermute | solution.py:36
  54.0 20.0 %all-to-all-start.2 = ((bf16[4,16,640]{2,1,0:T(8,128)(2,1)}), bf16[4,16,640]{2,1,0:T(8,128)(2,1)S(1)}, u32[]{:S(2)}, u32[]{:S(2)}) async-start(bf16[4,16,640]{2,1,0:T(8,128)(2,1)} %shard_map.88), calls=%async_computation.2 | async-start | bytes 163840 | tf_op jit(solution)/shard_map/all_to_all | solution.py:28
  74.9 21.8 %all-to-all-start.3 = ((bf16[32,16,640]{2,1,0:T(8,128)(2,1)}), bf16[32,16,640]{2,1,0:T(8,128)(2,1)S(1)}, u32[]{:S(2)}, u32[]{:S(2)}) async-start(bf16[32,16,640]{2,1,0:T(8,128)(2,1)} %shard_map.89), calls=%async_computation.3 | async-start | bytes 1310720 | tf_op jit(solution)/shard_map/all_to_all | solution.py:28
  83.8 4.3 %collective-permute-start.7 = (bf16[8,128,256]{2,1,0:T(8,128)(2,1)S(1)}, bf16[8,128,256]{2,1,0:T(8,128)(2,1)S(1)}, u32[]{:S(2)}, u32[]{:S(2)}) collective-permute-start(bf16[8,128,256]{2,1,0:T(8,128)(2,1)S(1)} %constant_dynamic-update-slice_fusion.rest_0_), channel_id=1, source_target_pairs={{0,16},{16,0},{1,17},{17,1},{2,18},{18,2},{3,19},{19,3},{4,20},{20... | collective-permute-start | bytes 1572872 | tf_op jit(solution)/shard_map/ppermute | solution.py:32
  86.0 3.8 %collective-permute-start.8 = (bf16[8,128,256]{2,1,0:T(8,128)(2,1)S(1)}, bf16[8,128,256]{2,1,0:T(8,128)(2,1)S(1)}, u32[]{:S(2)}, u32[]{:S(2)}) collective-permute-start(bf16[8,128,256]{2,1,0:T(8,128)(2,1)S(1)} %pad_maximum_fusion.rest_1_), channel_id=1, source_target_pairs={{0,16},{16,0},{1,17},{17,1},{2,18},{18,2},{3,19},{19,3},{4,20},{20... | collective-permute-start | bytes 1572872 | tf_op jit(solution)/shard_map/ppermute | solution.py:32

commit v7 on v6

--- a/solution.py
+++ b/solution.py
@@ -122,14 +122,16 @@
     gains = two_rows(gain)
     for target in range(4):
         rows = shards[target].astype(bf16)
-        out[target, :, :HALF] = rows[:16]
-        out[target, :, HALF : 2 * HALF] = rows[16:]
-        out[target, :, 2 * HALF :] = gains
+        for zh in range(4):
+            z = zh * 4 + target
+            out[z, :, :HALF] = rows[:16]
+            out[z, :, HALF : 2 * HALF] = rows[16:]
+            out[z, :, 2 * HALF :] = gains
 
 
 def line_kernel(line, out):
     total = line[0].astype(f32)
-    for sender in range(1, 4):
+    for sender in range(1, 16):
         total += line[sender].astype(f32)
     gains = two_rows(jnp.broadcast_to(total[0:1, 512:] + total[1:2, 512:], (16, 128)))
     rows = total[:, :512].astype(bf16)
@@ -259,19 +261,17 @@
 
     (payload,) = call(
         square_kernel,
-        [((4, 16, 640), bf16)],
+        [((16, 16, 640), bf16)],
         [SMEM] + [VMEM] * 5,
         (place, square, shard, above, across, below),
         scratch=[pltpu.VMEM((4, 32, HALF), f32), pltpu.VMEM((4, 32, HALF), f32)],
     )
-    near = exchange(payload, "zl")
+    line = exchange(payload, ("zh", "zl"))
     stack_late, _ = lax.optimization_barrier((stack, payload))
     one, two, three = (along_y(stack_late, -step) for step in (1, 2, 3))
-    (near_sum,) = call(line_kernel, [((4, 16, 640), bf16)], [VMEM], (near,))
-    far = exchange(near_sum, "zh")
     halves = jnp.concatenate([stack, one], axis=0), jnp.concatenate([two, three], axis=0)
-    far, *halves = lax.optimization_barrier((far, *halves))
-    (blocks,) = call(line_kernel, [((32, 16, 640), bf16)], [VMEM], (far,))
+    line, *halves = lax.optimization_barrier((line, *halves))
+    (blocks,) = call(line_kernel, [((32, 16, 640), bf16)], [VMEM], (line,))
     *halves_late, _ = lax.optimization_barrier((*halves, blocks))
     pieces = (*halves, *map(swap, halves_late))
     blocks = exchange(blocks, ("y", "x", "core"))

time: 98.8 us -> 92.8 us (0.939)
  starting transfers between devices: 60.6 us -> 56.2 us
  waiting for transfers between devices: 21.5 us -> 20.5 us
    all_to_all x4 -> x3, waiting for transfers between devices: 10.8 us -> 2.48 us  [exchange(): return lax.all_to_all(blocks, axes, 0, 0, tiled=False)]
    ppermute x3, waiting for transfers between devices: 4.16 us -> 11.5 us  [along_y(): return lax.ppermute(block, 'y', [(y, (y + step) % 4) for y in range(4)])]
    ppermute x3, starting transfers between devices: 9.53 us -> 7.33 us  [along_y(): return lax.ppermute(block, 'y', [(y, (y + step) % 4) for y in range(4)])]
    all_to_all x4 -> x3, starting transfers between devices: 23.4 us -> 21.2 us  [exchange(): return lax.all_to_all(blocks, axes, 0, 0, tiled=False)]
    pallas_call x8 -> x7, Pallas kernels: 13.9 us -> 13.4 us  [call(): pl.pallas_call(kernel, out_shape=[jax.ShapeDtypeStruct(s, d) for s, d in...]
  transfers between devices with their start and end apart: 13 -> 12, of which waited for: 7 -> 7; matrix products, arithmetic and copies ran while one was open for 0% -> 0% of each run, Pallas kernels for 6% -> 6%
where the time goes in v7:
time: 92.8 us; the launch traced here: 92.1 us
  starting transfers between devices  56.2 us (61%)
  waiting for transfers between devices  20.5 us (22%)
  Pallas kernels  13.4 us (14%)
  local copies, waits for them, and re-layouts  1 us (1%)
    all_to_all x3, starting transfers between devices, exchange(): return lax.all_to_all(blocks, axes, 0, 0, tiled=False)  21.2 us
    ppermute x3, starting transfers between devices, along_z(): return lax.ppermute(block, ('zh', 'x', 'core', 'zl'), pairs)  14.6 us
    pallas_call x7, Pallas kernels, call(): pl.pallas_call(kernel, out_shape=[jax.ShapeDtypeStruct(s, d) for s, d in...  13.4 us
    ppermute x3, starting transfers between devices, swap(): return lax.ppermute(block, 'core', [(0, 1), (1, 0)])  13.1 us
    ppermute x3, waiting for transfers between devices, along_y(): return lax.ppermute(block, 'y', [(y, (y + step) % 4) for y in range(4)])  11.5 us
    ppermute x3, starting transfers between devices, along_y(): return lax.ppermute(block, 'y', [(y, (y + step) % 4) for y in range(4)])  7.33 us
    ppermute x3, waiting for transfers between devices, along_z(): return lax.ppermute(block, ('zh', 'x', 'core', 'zl'), pairs)  4.6 us
    all_to_all x3, waiting for transfers between devices, exchange(): return lax.all_to_all(blocks, axes, 0, 0, tiled=False)  2.48 us
  transfers between devices with their start and end apart: 12, of which 7 were waited for; matrix products, arithmetic and copies ran while one was open for 0% of the time, Pallas kernels for 6%

profile of v7, /device:TPU:1, one launch (start us, length us, event | category | flops | bytes accessed | tf_op | source)
XLA Modules:
  0.0 92.1 jit_solution(12714488406433204729)
XLA Ops:
  0.7 2.6 %shard_map.84 = (bf16[192,2048]{1,0:T(8,128)(2,1)S(1)}, f32[192,128]{1,0:T(8,128)S(1)}, bf16[16,16,2048]{2,1,0:T(8,128)(2,1)S(1)}) custom-call(s32[4]{0:T(128)S(1)} %pad_add_fusion.place, bf16[192,2048]{1,0:T(8,128)(2,1)} %tokens.1, f32[1,2048]{1,0:T(1,128)} %bitcast.20, bf16[192,512]{1,0:T(8,128)(2,1)} %key_grad.3), custom_call_target="tpu_custom_call" | custom-call | flops 201326592 | bytes 1982496 | tf_op jit(solution)/shard_map/pallas_call | solution.py:211
  3.4 8.8 %collective-permute-start = (bf16[16,16,2048]{2,1,0:T(8,128)(2,1)S(1)}, bf16[16,16,2048]{2,1,0:T(8,128)(2,1)S(1)}, u32[]{:S(2)}, u32[]{:S(2)}) collective-permute-start(bf16[16,16,2048]{2,1,0:T(8,128)(2,1)S(1)} %get-tuple-element.22), channel_id=1, source_target_pairs={{0,16},{16,0},{1,17},{17,1},{2,18},{18,2},{3,19},{19,3},{4,20},{20... | collective-permute-start | bytes 3145736 | tf_op jit(solution)/shard_map/ppermute | solution.py:32
  13.1 1.0 %shard_map.85.mine = f32[16,16,2048]{2,1,0:T(8,128)S(1)} custom-call(s32[4]{0:T(128)S(1)} %pad_add_fusion.place, bf16[192,2048]{1,0:T(8,128)(2,1)S(1)} %get-tuple-element.21.normed, bf16[192,512]{1,0:T(8,128)(2,1)S(1)} %copy-done.2), custom_call_target="tpu_custom_call" | custom-call | flops 201326592 | bytes 1966112 | tf_op jit(solution)/shard_map/pallas_call | solution.py:211
  14.4 1.3 %shard_map.86 = bf16[16,16,2048]{2,1,0:T(8,128)(2,1)} custom-call(f32[16,16,2048]{2,1,0:T(8,128)S(1)} %shard_map.85.mine, bf16[16,16,2048]{2,1,0:T(8,128)(2,1)S(1)} %collective-permute-done.got), custom_call_target="tpu_custom_call" | custom-call | bytes 6291456 | tf_op jit(solution)/shard_map/pallas_call | solution.py:211
  15.7 3.8 %all-to-all-start = ((bf16[16,16,2048]{2,1,0:T(8,128)(2,1)}), bf16[16,16,2048]{2,1,0:T(8,128)(2,1)S(1)}, u32[]{:S(2)}, u32[]{:S(2)}) async-start(bf16[16,16,2048]{2,1,0:T(8,128)(2,1)} %shard_map.86), calls=%async_computation | async-start | bytes 2097152 | tf_op jit(solution)/shard_map/all_to_all | solution.py:28
  19.6 8.9 %collective-permute-start.1 = (bf16[128,256]{1,0:T(8,128)(2,1)S(1)}, bf16[128,256]{1,0:T(8,128)(2,1)S(1)}, u32[]{:S(2)}, u32[]{:S(2)}) collective-permute-start(bf16[128,256]{1,0:T(8,128)(2,1)S(1)} %get-tuple-element.23.shard), channel_id=1, source_target_pairs={{0,387},{16,403},{32,419},{48,435},{64,451},{80,467},{96,483},{112... | collective-permute-start | bytes 196616 | tf_op jit(solution)/shard_map/ppermute | solution.py:48
  28.4 3.1 %collective-permute-start.2 = (bf16[128,256]{1,0:T(8,128)(2,1)S(1)}, bf16[128,256]{1,0:T(8,128)(2,1)S(1)}, u32[]{:S(2)}, u32[]{:S(2)}) collective-permute-start(bf16[128,256]{1,0:T(8,128)(2,1)S(1)} %get-tuple-element.23.shard), channel_id=1, source_target_pairs={{0,2},{16,402},{32,34},{48,434},{64,66},{80,466},{96,98},{112,498}... | collective-permute-start | bytes 196616 | tf_op jit(solution)/shard_map/ppermute | solution.py:48
  31.5 2.6 %collective-permute-start.3 = (bf16[128,256]{1,0:T(8,128)(2,1)S(1)}, bf16[128,256]{1,0:T(8,128)(2,1)S(1)}, u32[]{:S(2)}, u32[]{:S(2)}) collective-permute-start(bf16[128,256]{1,0:T(8,128)(2,1)S(1)} %get-tuple-element.23.shard), channel_id=1, source_target_pairs={{0,1},{16,17},{32,33},{48,49},{64,65},{80,81},{96,97},{112,113},{1... | collective-permute-start | bytes 196616 | tf_op jit(solution)/shard_map/ppermute | solution.py:48
  34.4 4.3 %collective-permute-done.3.below = bf16[128,256]{1,0:T(8,128)(2,1)S(1)} collective-permute-done((bf16[128,256]{1,0:T(8,128)(2,1)S(1)}, bf16[128,256]{1,0:T(8,128)(2,1)S(1)}, u32[]{:S(2)}, u32[]{:S(2)}) %collective-permute-start.3) | collective-permute-done | bytes 65568 | tf_op jit(solution)/shard_map/ppermute | solution.py:48
  38.8 1.7 %shard_map.87 = bf16[16,16,640]{2,1,0:T(8,128)(2,1)} custom-call(s32[4]{0:T(128)S(1)} %pad_add_fusion.place, bf16[16,16,2048]{2,1,0:T(8,128)(2,1)S(1)} %all-to-all-done.square, bf16[128,256]{1,0:T(8,128)(2,1)S(1)} %get-tuple-element.23.shard, bf16[128,256]{1,0:T(8,128)(2,1)S(1)} %collective-permute-done.1.above, ...), custom_call_target="tpu_custom_call" | custom-call | bytes 2621472 | tf_op jit(solution)/shard_map/pallas_call | solution.py:211
  40.5 9.7 %all-to-all-start.1 = ((bf16[16,16,640]{2,1,0:T(8,128)(2,1)}), bf16[16,16,640]{2,1,0:T(8,128)(2,1)S(1)}, u32[]{:S(2)}, u32[]{:S(2)}) async-start(bf16[16,16,640]{2,1,0:T(8,128)(2,1)} %shard_map.87), calls=%async_computation.1 | async-start | bytes 655360 | tf_op jit(solution)/shard_map/all_to_all | solution.py:28
  50.3 2.6 %collective-permute-start.4 = (bf16[4,128,256]{2,1,0:T(8,128)(2,1)S(1)}, bf16[4,128,256]{2,1,0:T(8,128)(2,1)S(1)}, u32[]{:S(2)}, u32[]{:S(2)}) collective-permute-start(bf16[4,128,256]{2,1,0:T(8,128)(2,1)S(1)} %pad_maximum_fusion.1), channel_id=1, source_target_pairs={{0,12},{4,0},{8,4},{12,8},{1,13},{5,1},{9,5},{13,9},{2,14},{6,2},{... | collective-permute-start | bytes 786440 | tf_op jit(solution)/shard_map/ppermute | solution.py:36
  52.9 2.2 %collective-permute-start.5 = (bf16[4,128,256]{2,1,0:T(8,128)(2,1)S(1)}, bf16[4,128,256]{2,1,0:T(8,128)(2,1)S(1)}, u32[]{:S(2)}, u32[]{:S(2)}) collective-permute-start(bf16[4,128,256]{2,1,0:T(8,128)(2,1)S(1)} %pad_maximum_fusion.1), channel_id=1, source_target_pairs={{0,8},{4,12},{8,0},{12,4},{1,9},{5,13},{9,1},{13,5},{2,10},{6,14},... | collective-permute-start | bytes 786440 | tf_op jit(solution)/shard_map/ppermute | solution.py:36
  55.1 2.5 %collective-permute-start.6 = (bf16[4,128,256]{2,1,0:T(8,128)(2,1)S(1)}, bf16[4,128,256]{2,1,0:T(8,128)(2,1)S(1)}, u32[]{:S(2)}, u32[]{:S(2)}) collective-permute-start(bf16[4,128,256]{2,1,0:T(8,128)(2,1)S(1)} %pad_maximum_fusion.1), channel_id=1, source_target_pairs={{0,4},{4,8},{8,12},{12,0},{1,5},{5,9},{9,13},{13,1},{2,6},{6,10},{... | collective-permute-start | bytes 786440 | tf_op jit(solution)/shard_map/ppermute | solution.py:36
  57.7 4.1 %collective-permute-done.5 = bf16[4,128,256]{2,1,0:T(8,128)(2,1)S(1)} collective-permute-done((bf16[4,128,256]{2,1,0:T(8,128)(2,1)S(1)}, bf16[4,128,256]{2,1,0:T(8,128)(2,1)S(1)}, u32[]{:S(2)}, u32[]{:S(2)}) %collective-permute-start.5) | collective-permute-done | bytes 262176 | tf_op jit(solution)/shard_map/ppermute | solution.py:36
  61.8 7.4 %collective-permute-done.6 = bf16[4,128,256]{2,1,0:T(8,128)(2,1)S(1)} collective-permute-done((bf16[4,128,256]{2,1,0:T(8,128)(2,1)S(1)}, bf16[4,128,256]{2,1,0:T(8,128)(2,1)S(1)}, u32[]{:S(2)}, u32[]{:S(2)}) %collective-permute-start.6) | collective-permute-done | bytes 262176 | tf_op jit(solution)/shard_map/ppermute | solution.py:36
  69.2 0.9 %shard_map.88 = bf16[32,16,640]{2,1,0:T(8,128)(2,1)} custom-call(bf16[16,16,640]{2,1,0:T(8,128)(2,1)S(1)} %all-to-all-done.1.line), custom_call_target="tpu_custom_call" | custom-call | bytes 655360 | tf_op jit(solution)/shard_map/pallas_call | solution.py:211
  70.1 7.7 %all-to-all-start.2 = ((bf16[32,16,640]{2,1,0:T(8,128)(2,1)}), bf16[32,16,640]{2,1,0:T(8,128)(2,1)S(1)}, u32[]{:S(2)}, u32[]{:S(2)}) async-start(bf16[32,16,640]{2,1,0:T(8,128)(2,1)} %shard_map.88), calls=%async_computation.2 | async-start | bytes 1310720 | tf_op jit(solution)/shard_map/all_to_all | solution.py:28
  77.8 2.1 %collective-permute-start.7 = (bf16[8,128,256]{2,1,0:T(8,128)(2,1)S(1)}, bf16[8,128,256]{2,1,0:T(8,128)(2,1)S(1)}, u32[]{:S(2)}, u32[]{:S(2)}) collective-permute-start(bf16[8,128,256]{2,1,0:T(8,128)(2,1)S(1)} %constant_dynamic-update-slice_fusion.rest_0_), channel_id=1, source_target_pairs={{0,16},{16,0},{1,17},{17,1},{2,18},{18,2},{3,19},{19,3},{4,20},{20... | collective-permute-start | bytes 1572872 | tf_op jit(solution)/shard_map/ppermute | solution.py:32
  80.0 2.2 %collective-permute-start.8 = (bf16[8,128,256]{2,1,0:T(8,128)(2,1)S(1)}, bf16[8,128,256]{2,1,0:T(8,128)(2,1)S(1)}, u32[]{:S(2)}, u32[]{:S(2)}) collective-permute-start(bf16[8,128,256]{2,1,0:T(8,128)(2,1)S(1)} %pad_maximum_fusion.rest_1_), channel_id=1, source_target_pairs={{0,16},{16,0},{1,17},{17,1},{2,18},{18,2},{3,19},{19,3},{4,20},{20... | collective-permute-start | bytes 1572872 | tf_op jit(solution)/shard_map/ppermute | solution.py:32
  82.2 1.6 %collective-permute-done.8.rest_3_ = bf16[8,128,256]{2,1,0:T(8,128)(2,1)S(1)} collective-permute-done((bf16[8,128,256]{2,1,0:T(8,128)(2,1)S(1)}, bf16[8,128,256]{2,1,0:T(8,128)(2,1)S(1)}, u32[]{:S(2)}, u32[]{:S(2)}) %collective-permute-start.8) | collective-permute-done | bytes 524320 | tf_op jit(solution)/shard_map/ppermute | solution.py:32
  83.8 4.5 %shard_map.89 = (bf16[192,512]{1,0:T(8,128)(2,1)}, bf16[192,2048]{1,0:T(8,128)(2,1)}) custom-call(s32[4]{0:T(128)S(1)} %pad_add_fusion.place, bf16[192,2048]{1,0:T(8,128)(2,1)S(1)} %copy-done.1, f32[192,128]{1,0:T(8,128)S(1)} %get-tuple-element.26.inv_rms, f32[1,2048]{1,0:T(1,128)S(1)} %bitcast.21, bf16[192,512]{1,0:T(8,128)(2,1)S(1)} %copy-done.3, ...), custom_call_target="tpu_custom_call" | custom-call | flops 805306368 | bytes 6373408 | tf_op jit(solution)/shard_map/pallas_call | solution.py:211
  88.3 2.5 %all-to-all-done.2.blocks = bf16[32,16,640]{2,1,0:T(8,128)(2,1)S(1)} async-done(((bf16[32,16,640]{2,1,0:T(8,128)(2,1)}), bf16[32,16,640]{2,1,0:T(8,128)(2,1)S(1)}, u32[]{:S(2)}, u32[]{:S(2)}) %all-to-all-start.2) | async-done | bytes 655392 | tf_op jit(solution)/shard_map/all_to_all | solution.py:28
  90.8 1.4 %shard_map.90 = (f32[128,512]{1,0:T(8,128)}, f32[16,128]{1,0:T(8,128)}) custom-call(s32[4]{0:T(128)S(1)} %pad_add_fusion.place, bf16[32,16,640]{2,1,0:T(8,128)(2,1)S(1)} %all-to-all-done.2.blocks, f32[16,128]{1,0:T(8,128)S(1)} %bitcast.22), custom_call_target="tpu_custom_call" | custom-call | bytes 1327136 | tf_op jit(solution)/shard_map/pallas_call | solution.py:211
  (28 shorter events, 1.8 us)
Async XLA Ops:
  0.6 18.9 %copy-start = (f32[1,512]{1,0:T(1,128)S(1)}, f32[1,512]{1,0:T(1,128)}, u32[]{:S(2)}) copy-start(f32[1,512]{1,0:T(1,128)} %param.8) | copy-start | bytes 6148
  3.4 11.1 %collective-permute-start = (bf16[16,16,2048]{2,1,0:T(8,128)(2,1)S(1)}, bf16[16,16,2048]{2,1,0:T(8,128)(2,1)S(1)}, u32[]{:S(2)}, u32[]{:S(2)}) collective-permute-start(bf16[16,16,2048]{2,1,0:T(8,128)(2,1)S(1)} %get-tuple-element.22), channel_id=1, source_target_pairs={{0,16},{16,0},{1,17},{17,1},{2,18},{18,2},{3,19},{19,3},{4,20},{20... | collective-permute-start | bytes 3145736 | tf_op jit(solution)/shard_map/ppermute | solution.py:32
  12.2 0.9 %copy-start.2 = (bf16[192,512]{1,0:T(8,128)(2,1)S(1)}, bf16[192,512]{1,0:T(8,128)(2,1)}, u32[]{:S(2)}) copy-start(bf16[192,512]{1,0:T(8,128)(2,1)} %key_grad.3) | copy-start | bytes 589828
  15.7 3.8 %copy-start.5 = (s32[128,512]{1,0:T(8,128)S(1)}, s32[128,512]{1,0:T(8,128)}, u32[]{:S(2)}) copy-start(s32[128,512]{1,0:T(8,128)} %param.7) | copy-start | bytes 786436
  15.7 23.1 %all-to-all-start = ((bf16[16,16,2048]{2,1,0:T(8,128)(2,1)}), bf16[16,16,2048]{2,1,0:T(8,128)(2,1)S(1)}, u32[]{:S(2)}, u32[]{:S(2)}) async-start(bf16[16,16,2048]{2,1,0:T(8,128)(2,1)} %shard_map.86), calls=%async_computation | async-start | bytes 2097152 | tf_op jit(solution)/shard_map/all_to_all | solution.py:28
  19.6 14.6 %collective-permute-start.1 = (bf16[128,256]{1,0:T(8,128)(2,1)S(1)}, bf16[128,256]{1,0:T(8,128)(2,1)S(1)}, u32[]{:S(2)}, u32[]{:S(2)}) collective-permute-start(bf16[128,256]{1,0:T(8,128)(2,1)S(1)} %get-tuple-element.23.shard), channel_id=1, source_target_pairs={{0,387},{16,403},{32,419},{48,435},{64,451},{80,467},{96,483},{112... | collective-permute-start | bytes 196616 | tf_op jit(solution)/shard_map/ppermute | solution.py:48
  28.4 6.0 %collective-permute-start.2 = (bf16[128,256]{1,0:T(8,128)(2,1)S(1)}, bf16[128,256]{1,0:T(8,128)(2,1)S(1)}, u32[]{:S(2)}, u32[]{:S(2)}) collective-permute-start(bf16[128,256]{1,0:T(8,128)(2,1)S(1)} %get-tuple-element.23.shard), channel_id=1, source_target_pairs={{0,2},{16,402},{32,34},{48,434},{64,66},{80,466},{96,98},{112,498}... | collective-permute-start | bytes 196616 | tf_op jit(solution)/shard_map/ppermute | solution.py:48
  31.5 7.3 %collective-permute-start.3 = (bf16[128,256]{1,0:T(8,128)(2,1)S(1)}, bf16[128,256]{1,0:T(8,128)(2,1)S(1)}, u32[]{:S(2)}, u32[]{:S(2)}) collective-permute-start(bf16[128,256]{1,0:T(8,128)(2,1)S(1)} %get-tuple-element.23.shard), channel_id=1, source_target_pairs={{0,1},{16,17},{32,33},{48,49},{64,65},{80,81},{96,97},{112,113},{1... | collective-permute-start | bytes 196616 | tf_op jit(solution)/shard_map/ppermute | solution.py:48
  40.5 28.7 %all-to-all-start.1 = ((bf16[16,16,640]{2,1,0:T(8,128)(2,1)}), bf16[16,16,640]{2,1,0:T(8,128)(2,1)S(1)}, u32[]{:S(2)}, u32[]{:S(2)}) async-start(bf16[16,16,640]{2,1,0:T(8,128)(2,1)} %shard_map.87), calls=%async_computation.1 | async-start | bytes 655360 | tf_op jit(solution)/shard_map/all_to_all | solution.py:28
  50.2 33.6 %copy-start.1 = (bf16[192,2048]{1,0:T(8,128)(2,1)S(1)}, bf16[192,2048]{1,0:T(8,128)(2,1)}, u32[]{:S(2)}) copy-start(bf16[192,2048]{1,0:T(8,128)(2,1)} %tokens.1) | copy-start | bytes 2359300
  50.2 33.6 %copy-start.3 = (bf16[192,512]{1,0:T(8,128)(2,1)S(1)}, bf16[192,512]{1,0:T(8,128)(2,1)}, u32[]{:S(2)}) copy-start(bf16[192,512]{1,0:T(8,128)(2,1)} %key_grad.3) | copy-start | bytes 589828
  50.2 33.6 %copy-start.4 = (f32[2048]{0:T(1024)S(1)}, f32[2048]{0:T(1024)}, u32[]{:S(2)}) copy-start(f32[2048]{0:T(1024)} %param.6) | copy-start | bytes 24580
  50.3 7.4 %collective-permute-start.4 = (bf16[4,128,256]{2,1,0:T(8,128)(2,1)S(1)}, bf16[4,128,256]{2,1,0:T(8,128)(2,1)S(1)}, u32[]{:S(2)}, u32[]{:S(2)}) collective-permute-start(bf16[4,128,256]{2,1,0:T(8,128)(2,1)S(1)} %pad_maximum_fusion.1), channel_id=1, source_target_pairs={{0,12},{4,0},{8,4},{12,8},{1,13},{5,1},{9,5},{13,9},{2,14},{6,2},{... | collective-permute-start | bytes 786440 | tf_op jit(solution)/shard_map/ppermute | solution.py:36
  52.9 8.9 %collective-permute-start.5 = (bf16[4,128,256]{2,1,0:T(8,128)(2,1)S(1)}, bf16[4,128,256]{2,1,0:T(8,128)(2,1)S(1)}, u32[]{:S(2)}, u32[]{:S(2)}) collective-permute-start(bf16[4,128,256]{2,1,0:T(8,128)(2,1)S(1)} %pad_maximum_fusion.1), channel_id=1, source_target_pairs={{0,8},{4,12},{8,0},{12,4},{1,9},{5,13},{9,1},{13,5},{2,10},{6,14},... | collective-permute-start | bytes 786440 | tf_op jit(solution)/shard_map/ppermute | solution.py:36
  55.1 14.0 %collective-permute-start.6 = (bf16[4,128,256]{2,1,0:T(8,128)(2,1)S(1)}, bf16[4,128,256]{2,1,0:T(8,128)(2,1)S(1)}, u32[]{:S(2)}, u32[]{:S(2)}) collective-permute-start(bf16[4,128,256]{2,1,0:T(8,128)(2,1)S(1)} %pad_maximum_fusion.1), channel_id=1, source_target_pairs={{0,4},{4,8},{8,12},{12,0},{1,5},{5,9},{9,13},{13,1},{2,6},{6,10},{... | collective-permute-start | bytes 786440 | tf_op jit(solution)/shard_map/ppermute | solution.py:36
  70.1 20.6 %all-to-all-start.2 = ((bf16[32,16,640]{2,1,0:T(8,128)(2,1)}), bf16[32,16,640]{2,1,0:T(8,128)(2,1)S(1)}, u32[]{:S(2)}, u32[]{:S(2)}) async-start(bf16[32,16,640]{2,1,0:T(8,128)(2,1)} %shard_map.88), calls=%async_computation.2 | async-start | bytes 1310720 | tf_op jit(solution)/shard_map/all_to_all | solution.py:28
  77.8 4.3 %collective-permute-start.7 = (bf16[8,128,256]{2,1,0:T(8,128)(2,1)S(1)}, bf16[8,128,256]{2,1,0:T(8,128)(2,1)S(1)}, u32[]{:S(2)}, u32[]{:S(2)}) collective-permute-start(bf16[8,128,256]{2,1,0:T(8,128)(2,1)S(1)} %constant_dynamic-update-slice_fusion.rest_0_), channel_id=1, source_target_pairs={{0,16},{16,0},{1,17},{17,1},{2,18},{18,2},{3,19},{19,3},{4,20},{20... | collective-permute-start | bytes 1572872 | tf_op jit(solution)/shard_map/ppermute | solution.py:32
  80.0 3.8 %collective-permute-start.8 = (bf16[8,128,256]{2,1,0:T(8,128)(2,1)S(1)}, bf16[8,128,256]{2,1,0:T(8,128)(2,1)S(1)}, u32[]{:S(2)}, u32[]{:S(2)}) collective-permute-start(bf16[8,128,256]{2,1,0:T(8,128)(2,1)S(1)} %pad_maximum_fusion.rest_1_), channel_id=1, source_target_pairs={{0,16},{16,0},{1,17},{17,1},{2,18},{18,2},{3,19},{19,3},{4,20},{20... | collective-permute-start | bytes 1572872 | tf_op jit(solution)/shard_map/ppermute | solution.py:32

commit v8 on v7

--- a/solution.py
+++ b/solution.py
@@ -89,18 +89,31 @@
     put_product(normed, key_grad[:, pl.ds(start, HALF)], mine, f32)
 
 
-def pair_kernel(mine, got, out):
-    for peer in range(16):
-        out[peer] = (mine[peer] + got[peer].astype(f32)).astype(bf16)
+def copy_out(pairs, sem):
+    copies = [pltpu.make_async_copy(source, target, sem.at[i]) for i, (source, target) in enumerate(pairs)]
+    for copy in copies:
+        copy.start()
+    return copies
+
+
+def pair_kernel(mine, got, out, held, sem):
+    copies = []
+    for part in range(4):
+        peers = slice(part * 4, part * 4 + 4)
+        for peer in range(part * 4, part * 4 + 4):
+            held[peer] = (mine[peer] + got[peer].astype(f32)).astype(bf16)
+        copies += copy_out([(held.at[peers], out.at[peers])], sem.at[pl.ds(part, 1)])
+    for copy in copies:
+        copy.wait()
 
 
 def two_rows(value):
     high = value.astype(bf16).astype(f32)
-    row = lax.broadcasted_iota(jnp.int32, (16, 128), 0)
+    row = lax.broadcasted_iota(jnp.int32, (8, 128), 0)
     return jnp.where(row == 0, high, jnp.where(row == 1, value - high, 0.0)).astype(bf16)
 
 
-def square_kernel(place, square, shard, above, across, below, out, shards, products):
+def square_kernel(place, square, shard, above, across, below, out, shards, products, held, sem):
     x, zl = place[1], place[3]
     for k in range(8):
         cols = slice(k * HALF, (k + 1) * HALF)
@@ -113,7 +126,7 @@
         rows = piece[pl.ds(pl.multiple_of(x * 32, 32), 32), :].astype(f32)
         products[which] = shards[which] * rows
     gain = lax.dot_general(
-        jnp.ones((16, HALF), f32),
+        jnp.ones((8, HALF), f32),
         products[...].reshape(128, HALF),
         (((1,), (1,)), ((), ())),
         preferred_element_type=f32,
@@ -121,23 +134,24 @@
     )
     gains = two_rows(gain)
     for target in range(4):
-        rows = shards[target].astype(bf16)
-        for zh in range(4):
-            z = zh * 4 + target
-            out[z, :, :HALF] = rows[:16]
-            out[z, :, HALF : 2 * HALF] = rows[16:]
-            out[z, :, 2 * HALF :] = gains
-
-
-def line_kernel(line, out):
+        for k in range(4):
+            held[target, :, k * HALF : (k + 1) * HALF] = shards[target, k * 8 : k * 8 + 8].astype(bf16)
+        held[target, :, 4 * HALF :] = gains
+    for copy in copy_out([(held, out.at[zh * 4 : zh * 4 + 4]) for zh in range(4)], sem):
+        copy.wait()
+
+
+def line_kernel(line, out, held, sem):
     total = line[0].astype(f32)
     for sender in range(1, 16):
         total += line[sender].astype(f32)
-    gains = two_rows(jnp.broadcast_to(total[0:1, 512:] + total[1:2, 512:], (16, 128)))
-    rows = total[:, :512].astype(bf16)
-    for peer in range(out.shape[0]):
-        out[peer, :, :512] = rows
-        out[peer, :, 512:] = gains
+    gains = two_rows(jnp.broadcast_to(total[0:1, 4 * HALF :] + total[1:2, 4 * HALF :], (8, 128)))
+    rows = total[:, : 4 * HALF].astype(bf16)
+    for peer in range(8):
+        held[peer, :, : 4 * HALF] = rows
+        held[peer, :, 4 * HALF :] = gains
+    for copy in copy_out([(held, out.at[y * 8 : y * 8 + 8]) for y in range(4)], sem):
+        copy.wait()
 
 
 def last_kernel(place, blocks, norm_gain, weight_grad, gain_grad):
@@ -145,13 +159,12 @@
     for x in range(4):
         for core in range(2):
             block = blocks[y * 8 + x * 2 + core].astype(f32) / DEVICES
-            for k in range(2):
-                weight_grad[x * 32 + k * 16 : x * 32 + k * 16 + 16, core * HALF : (core + 1) * HALF] = block[
-                    :, k * HALF : (k + 1) * HALF
-                ]
+            for k in range(4):
+                at = x * 32 + k * 8
+                weight_grad[at : at + 8, core * HALF : (core + 1) * HALF] = block[:, k * HALF : (k + 1) * HALF]
     rows_of = []
     for peer in range(16):
-        gains = blocks[peer * 2, :, 512:].astype(f32) + blocks[peer * 2 + 1, :, 512:].astype(f32)
+        gains = blocks[peer * 2, :, 4 * HALF :].astype(f32) + blocks[peer * 2 + 1, :, 4 * HALF :].astype(f32)
         rows_of.append(gains[0:1] + gains[1:2])
     sums = jnp.concatenate(rows_of, axis=0)
     lane = lax.broadcasted_iota(jnp.int32, (16, 128), 1)
@@ -206,13 +219,13 @@
         tokens_grad[rows, :] = (inv * (scaled - unit * mean)).astype(bf16)
 
 
-def call(kernel, outs, ins, args, scratch=(), flops=0, **kw):
+def call(kernel, outs, ins, args, scratch=(), flops=0, out_specs=None):
     moved = sum(a.size * a.dtype.itemsize for a in args)
     return pl.pallas_call(
         kernel,
         out_shape=[jax.ShapeDtypeStruct(s, d) for s, d in outs],
         in_specs=ins,
-        out_specs=[VMEM] * len(outs),
+        out_specs=out_specs or [VMEM] * len(outs),
         scratch_shapes=list(scratch),
         compiler_params=PARAMS,
         cost_estimate=pl.CostEstimate(flops=flops, bytes_accessed=2 * moved, transcendentals=0),
@@ -250,7 +263,7 @@
         (place, normed, key_grad),
         flops=2 * 192 * 2048 * 256,
     )
-    (pair,) = call(pair_kernel, [((16, 16, 2048), bf16)], [VMEM] * 2, (mine, got))
+    (pair,) = call(pair_kernel, [((16, 16, 2048), bf16)], [VMEM] * 2, (mine, got), scratch=[pltpu.VMEM((16, 16, 2048), bf16), pltpu.SemaphoreType.DMA((4,))], out_specs=[ANY])
     square = exchange(pair, ("y", "x"))
 
     shard_late, _ = lax.optimization_barrier((shard, pair))
@@ -261,17 +274,30 @@
 
     (payload,) = call(
         square_kernel,
-        [((16, 16, 640), bf16)],
+        [((16, 8, 1152), bf16)],
         [SMEM] + [VMEM] * 5,
         (place, square, shard, above, across, below),
-        scratch=[pltpu.VMEM((4, 32, HALF), f32), pltpu.VMEM((4, 32, HALF), f32)],
+        scratch=[
+            pltpu.VMEM((4, 32, HALF), f32),
+            pltpu.VMEM((4, 32, HALF), f32),
+            pltpu.VMEM((4, 8, 1152), bf16),
+            pltpu.SemaphoreType.DMA((4,)),
+        ],
+        out_specs=[ANY],
     )
     line = exchange(payload, ("zh", "zl"))
     stack_late, _ = lax.optimization_barrier((stack, payload))
     one, two, three = (along_y(stack_late, -step) for step in (1, 2, 3))
     halves = jnp.concatenate([stack, one], axis=0), jnp.concatenate([two, three], axis=0)
     line, *halves = lax.optimization_barrier((line, *halves))
-    (blocks,) = call(line_kernel, [((32, 16, 640), bf16)], [VMEM], (line,))
+    (blocks,) = call(
+        line_kernel,
+        [((32, 8, 1152), bf16)],
+        [VMEM],
+        (line,),
+        scratch=[pltpu.VMEM((8, 8, 1152), bf16), pltpu.SemaphoreType.DMA((4,))],
+        out_specs=[ANY],
+    )
     *halves_late, _ = lax.optimization_barrier((*halves, blocks))
     pieces = (*halves, *map(swap, halves_late))
     blocks = exchange(blocks, ("y", "x", "core"))

time: 92.8 us -> 95.3 us (1.027)
  waiting for transfers between devices: 20.5 us -> 23.2 us
  starting transfers between devices: 56.2 us -> 55.1 us
    all_to_all x3, waiting for transfers between devices: 2.48 us -> 6.82 us  [exchange(): return lax.all_to_all(blocks, axes, 0, 0, tiled=False)]
    all_to_all x3, starting transfers between devices: 21.2 us -> 18.9 us  [exchange(): return lax.all_to_all(blocks, axes, 0, 0, tiled=False)]
    ppermute x3, waiting for transfers between devices: 1.9 us -> 0.3 us  [swap(): return lax.ppermute(block, 'core', [(0, 1), (1, 0)])]
    ppermute x3, starting transfers between devices: 13.1 us -> 14.3 us  [swap(): return lax.ppermute(block, 'core', [(0, 1), (1, 0)])]
  transfers between devices with their start and end apart: 12 -> 12, of which waited for: 7 -> 6; matrix products, arithmetic and copies ran while one was open for 0% -> 0% of each run, Pallas kernels for 6% -> 7%
where the time goes in v8:
time: 95.3 us; the launch traced here: 94.6 us
  starting transfers between devices  55.1 us (58%)
  waiting for transfers between devices  23.2 us (24%)
  Pallas kernels  14.1 us (15%)
  local copies, waits for them, and re-layouts  1.01 us (1%)
  between operations  0.97 us (1%)
    all_to_all x3, starting transfers between devices, exchange(): return lax.all_to_all(blocks, axes, 0, 0, tiled=False)  18.9 us
    ppermute x3, starting transfers between devices, along_z(): return lax.ppermute(block, ('zh', 'x', 'core', 'zl'), pairs)  14.6 us
    ppermute x3, starting transfers between devices, swap(): return lax.ppermute(block, 'core', [(0, 1), (1, 0)])  14.3 us
    pallas_call x7, Pallas kernels, call(): pl.pallas_call(kernel, out_shape=[jax.ShapeDtypeStruct(s, d) for s, d in...  14.1 us
    ppermute x3, waiting for transfers between devices, along_y(): return lax.ppermute(block, 'y', [(y, (y + step) % 4) for y in range(4)])  11.5 us
    ppermute x3, starting transfers between devices, along_y(): return lax.ppermute(block, 'y', [(y, (y + step) % 4) for y in range(4)])  7.33 us
    all_to_all x3, waiting for transfers between devices, exchange(): return lax.all_to_all(blocks, axes, 0, 0, tiled=False)  6.82 us
    ppermute x3, waiting for transfers between devices, along_z(): return lax.ppermute(block, ('zh', 'x', 'core', 'zl'), pairs)  4.6 us
  transfers between devices with their start and end apart: 12, of which 6 were waited for; matrix products, arithmetic and copies ran while one was open for 0% of the time, Pallas kernels for 7%

profile of v8, /device:TPU:1, one launch (start us, length us, event | category | flops | bytes accessed | tf_op | source)
XLA Modules:
  0.0 94.6 jit_solution(17882114173676480198)
XLA Ops:
  0.7 2.6 %shard_map.84 = (bf16[192,2048]{1,0:T(8,128)(2,1)S(1)}, f32[192,128]{1,0:T(8,128)S(1)}, bf16[16,16,2048]{2,1,0:T(8,128)(2,1)S(1)}) custom-call(s32[4]{0:T(128)S(1)} %pad_add_fusion.place, bf16[192,2048]{1,0:T(8,128)(2,1)} %tokens.1, f32[1,2048]{1,0:T(1,128)} %bitcast.20, bf16[192,512]{1,0:T(8,128)(2,1)} %key_grad.3), custom_call_target="tpu_custom_call" | custom-call | flops 201326592 | bytes 1982496 | tf_op jit(solution)/shard_map/pallas_call | solution.py:224
  3.4 8.8 %collective-permute-start = (bf16[16,16,2048]{2,1,0:T(8,128)(2,1)S(1)}, bf16[16,16,2048]{2,1,0:T(8,128)(2,1)S(1)}, u32[]{:S(2)}, u32[]{:S(2)}) collective-permute-start(bf16[16,16,2048]{2,1,0:T(8,128)(2,1)S(1)} %get-tuple-element.22), channel_id=1, source_target_pairs={{0,16},{16,0},{1,17},{17,1},{2,18},{18,2},{3,19},{19,3},{4,20},{20... | collective-permute-start | bytes 3145736 | tf_op jit(solution)/shard_map/ppermute | solution.py:32
  12.2 0.9 copy-done.2
  13.1 1.0 %shard_map.85.mine = f32[16,16,2048]{2,1,0:T(8,128)S(1)} custom-call(s32[4]{0:T(128)S(1)} %pad_add_fusion.place, bf16[192,2048]{1,0:T(8,128)(2,1)S(1)} %get-tuple-element.21.normed, bf16[192,512]{1,0:T(8,128)(2,1)S(1)} %copy-done.2), custom_call_target="tpu_custom_call" | custom-call | flops 201326592 | bytes 1966112 | tf_op jit(solution)/shard_map/pallas_call | solution.py:224
  14.4 1.1 %shard_map.86 = bf16[16,16,2048]{2,1,0:T(8,128)(2,1)} custom-call(f32[16,16,2048]{2,1,0:T(8,128)S(1)} %shard_map.85.mine, bf16[16,16,2048]{2,1,0:T(8,128)(2,1)S(1)} %collective-permute-done.got), custom_call_target="tpu_custom_call" | custom-call | bytes 6291456 | tf_op jit(solution)/shard_map/pallas_call | solution.py:224
  15.6 3.8 %all-to-all-start = ((bf16[16,16,2048]{2,1,0:T(8,128)(2,1)}), bf16[16,16,2048]{2,1,0:T(8,128)(2,1)S(1)}, u32[]{:S(2)}, u32[]{:S(2)}) async-start(bf16[16,16,2048]{2,1,0:T(8,128)(2,1)} %shard_map.86), calls=%async_computation | async-start | bytes 2097152 | tf_op jit(solution)/shard_map/all_to_all | solution.py:28
  19.4 8.9 %collective-permute-start.1 = (bf16[128,256]{1,0:T(8,128)(2,1)S(1)}, bf16[128,256]{1,0:T(8,128)(2,1)S(1)}, u32[]{:S(2)}, u32[]{:S(2)}) collective-permute-start(bf16[128,256]{1,0:T(8,128)(2,1)S(1)} %get-tuple-element.23.shard), channel_id=1, source_target_pairs={{0,387},{16,403},{32,419},{48,435},{64,451},{80,467},{96,483},{112... | collective-permute-start | bytes 196616 | tf_op jit(solution)/shard_map/ppermute | solution.py:48
  28.3 3.1 %collective-permute-start.2 = (bf16[128,256]{1,0:T(8,128)(2,1)S(1)}, bf16[128,256]{1,0:T(8,128)(2,1)S(1)}, u32[]{:S(2)}, u32[]{:S(2)}) collective-permute-start(bf16[128,256]{1,0:T(8,128)(2,1)S(1)} %get-tuple-element.23.shard), channel_id=1, source_target_pairs={{0,2},{16,402},{32,34},{48,434},{64,66},{80,466},{96,98},{112,498}... | collective-permute-start | bytes 196616 | tf_op jit(solution)/shard_map/ppermute | solution.py:48
  31.4 2.6 %collective-permute-start.3 = (bf16[128,256]{1,0:T(8,128)(2,1)S(1)}, bf16[128,256]{1,0:T(8,128)(2,1)S(1)}, u32[]{:S(2)}, u32[]{:S(2)}) collective-permute-start(bf16[128,256]{1,0:T(8,128)(2,1)S(1)} %get-tuple-element.23.shard), channel_id=1, source_target_pairs={{0,1},{16,17},{32,33},{48,49},{64,65},{80,81},{96,97},{112,113},{1... | collective-permute-start | bytes 196616 | tf_op jit(solution)/shard_map/ppermute | solution.py:48
  34.3 4.3 %collective-permute-done.3.below = bf16[128,256]{1,0:T(8,128)(2,1)S(1)} collective-permute-done((bf16[128,256]{1,0:T(8,128)(2,1)S(1)}, bf16[128,256]{1,0:T(8,128)(2,1)S(1)}, u32[]{:S(2)}, u32[]{:S(2)}) %collective-permute-start.3) | collective-permute-done | bytes 65568 | tf_op jit(solution)/shard_map/ppermute | solution.py:48
  38.7 1.7 %shard_map.87 = bf16[16,8,1152]{2,1,0:T(8,128)(2,1)} custom-call(s32[4]{0:T(128)S(1)} %pad_add_fusion.place, bf16[16,16,2048]{2,1,0:T(8,128)(2,1)S(1)} %all-to-all-done.square, bf16[128,256]{1,0:T(8,128)(2,1)S(1)} %get-tuple-element.23.shard, bf16[128,256]{1,0:T(8,128)(2,1)S(1)} %collective-permute-done.1.above, ...), custom_call_target="tpu_custom_call" | custom-call | bytes 2621472 | tf_op jit(solution)/shard_map/pallas_call | solution.py:224
  40.3 9.7 %all-to-all-start.1 = ((bf16[16,8,1152]{2,1,0:T(8,128)(2,1)}), bf16[16,8,1152]{2,1,0:T(8,128)(2,1)S(1)}, u32[]{:S(2)}, u32[]{:S(2)}) async-start(bf16[16,8,1152]{2,1,0:T(8,128)(2,1)} %shard_map.87), calls=%async_computation.1 | async-start | bytes 589824 | tf_op jit(solution)/shard_map/all_to_all | solution.py:28
  50.1 2.6 %collective-permute-start.4 = (bf16[4,128,256]{2,1,0:T(8,128)(2,1)S(1)}, bf16[4,128,256]{2,1,0:T(8,128)(2,1)S(1)}, u32[]{:S(2)}, u32[]{:S(2)}) collective-permute-start(bf16[4,128,256]{2,1,0:T(8,128)(2,1)S(1)} %pad_maximum_fusion.1), channel_id=1, source_target_pairs={{0,12},{4,0},{8,4},{12,8},{1,13},{5,1},{9,5},{13,9},{2,14},{6,2},{... | collective-permute-start | bytes 786440 | tf_op jit(solution)/shard_map/ppermute | solution.py:36
  52.8 2.2 %collective-permute-start.5 = (bf16[4,128,256]{2,1,0:T(8,128)(2,1)S(1)}, bf16[4,128,256]{2,1,0:T(8,128)(2,1)S(1)}, u32[]{:S(2)}, u32[]{:S(2)}) collective-permute-start(bf16[4,128,256]{2,1,0:T(8,128)(2,1)S(1)} %pad_maximum_fusion.1), channel_id=1, source_target_pairs={{0,8},{4,12},{8,0},{12,4},{1,9},{5,13},{9,1},{13,5},{2,10},{6,14},... | collective-permute-start | bytes 786440 | tf_op jit(solution)/shard_map/ppermute | solution.py:36
  55.0 2.5 %collective-permute-start.6 = (bf16[4,128,256]{2,1,0:T(8,128)(2,1)S(1)}, bf16[4,128,256]{2,1,0:T(8,128)(2,1)S(1)}, u32[]{:S(2)}, u32[]{:S(2)}) collective-permute-start(bf16[4,128,256]{2,1,0:T(8,128)(2,1)S(1)} %pad_maximum_fusion.1), channel_id=1, source_target_pairs={{0,4},{4,8},{8,12},{12,0},{1,5},{5,9},{9,13},{13,1},{2,6},{6,10},{... | collective-permute-start | bytes 786440 | tf_op jit(solution)/shard_map/ppermute | solution.py:36
  57.6 4.1 %collective-permute-done.5 = bf16[4,128,256]{2,1,0:T(8,128)(2,1)S(1)} collective-permute-done((bf16[4,128,256]{2,1,0:T(8,128)(2,1)S(1)}, bf16[4,128,256]{2,1,0:T(8,128)(2,1)S(1)}, u32[]{:S(2)}, u32[]{:S(2)}) %collective-permute-start.5) | collective-permute-done | bytes 262176 | tf_op jit(solution)/shard_map/ppermute | solution.py:36
  61.7 7.4 %collective-permute-done.6 = bf16[4,128,256]{2,1,0:T(8,128)(2,1)S(1)} collective-permute-done((bf16[4,128,256]{2,1,0:T(8,128)(2,1)S(1)}, bf16[4,128,256]{2,1,0:T(8,128)(2,1)S(1)}, u32[]{:S(2)}, u32[]{:S(2)}) %collective-permute-start.6) | collective-permute-done | bytes 262176 | tf_op jit(solution)/shard_map/ppermute | solution.py:36
  69.1 0.9 shard_map.88
  70.0 3.6 %collective-permute-start.7 = (bf16[8,128,256]{2,1,0:T(8,128)(2,1)S(1)}, bf16[8,128,256]{2,1,0:T(8,128)(2,1)S(1)}, u32[]{:S(2)}, u32[]{:S(2)}) collective-permute-start(bf16[8,128,256]{2,1,0:T(8,128)(2,1)S(1)} %constant_dynamic-update-slice_fusion.rest_0_), channel_id=1, source_target_pairs={{0,16},{16,0},{1,17},{17,1},{2,18},{18,2},{3,19},{19,3},{4,20},{20... | collective-permute-start | bytes 1572872 | tf_op jit(solution)/shard_map/ppermute | solution.py:32
  73.6 1.9 %collective-permute-start.8 = (bf16[8,128,256]{2,1,0:T(8,128)(2,1)S(1)}, bf16[8,128,256]{2,1,0:T(8,128)(2,1)}, u32[]{:S(2)}, u32[]{:S(2)}) collective-permute-start(bf16[8,128,256]{2,1,0:T(8,128)(2,1)S(1)} %pad_maximum_fusion.rest_1_), channel_id=1, source_target_pairs={{0,16},{16,0},{1,17},{17,1},{2,18},{18,2},{3,19},{19,3},{4,20},{20... | collective-permute-start | bytes 1572872 | tf_op jit(solution)/shard_map/ppermute | solution.py:32
  75.5 5.4 %all-to-all-start.2 = ((bf16[32,8,1152]{2,1,0:T(8,128)(2,1)}), bf16[32,8,1152]{2,1,0:T(8,128)(2,1)S(1)}, u32[]{:S(2)}, u32[]{:S(2)}) async-start(bf16[32,8,1152]{2,1,0:T(8,128)(2,1)} %shard_map.88), calls=%async_computation.2 | async-start | bytes 1179648 | tf_op jit(solution)/shard_map/all_to_all | solution.py:28
  81.0 5.4 %shard_map.89 = (bf16[192,512]{1,0:T(8,128)(2,1)}, bf16[192,2048]{1,0:T(8,128)(2,1)}) custom-call(s32[4]{0:T(128)S(1)} %pad_add_fusion.place, bf16[192,2048]{1,0:T(8,128)(2,1)S(1)} %copy-done.1, f32[192,128]{1,0:T(8,128)S(1)} %get-tuple-element.26.inv_rms, f32[1,2048]{1,0:T(1,128)S(1)} %bitcast.21, bf16[192,512]{1,0:T(8,128)(2,1)S(1)} %copy-done.3, ...), custom_call_target="tpu_custom_call" | custom-call | flops 805306368 | bytes 6373408 | tf_op jit(solution)/shard_map/pallas_call | solution.py:224
  86.4 6.8 %all-to-all-done.2.blocks = bf16[32,8,1152]{2,1,0:T(8,128)(2,1)S(1)} async-done(((bf16[32,8,1152]{2,1,0:T(8,128)(2,1)}), bf16[32,8,1152]{2,1,0:T(8,128)(2,1)S(1)}, u32[]{:S(2)}, u32[]{:S(2)}) %all-to-all-start.2) | async-done | bytes 589856 | tf_op jit(solution)/shard_map/all_to_all | solution.py:28
  93.2 1.3 %shard_map.90 = (f32[128,512]{1,0:T(8,128)}, f32[16,128]{1,0:T(8,128)}) custom-call(s32[4]{0:T(128)S(1)} %pad_add_fusion.place, bf16[32,8,1152]{2,1,0:T(8,128)(2,1)S(1)} %all-to-all-done.2.blocks, f32[16,128]{1,0:T(8,128)S(1)} %bitcast.22), custom_call_target="tpu_custom_call" | custom-call | bytes 1196064 | tf_op jit(solution)/shard_map/pallas_call | solution.py:224
  (28 shorter events, 0.8 us)
Async XLA Ops:
  0.6 18.7 %copy-start = (f32[1,512]{1,0:T(1,128)S(1)}, f32[1,512]{1,0:T(1,128)}, u32[]{:S(2)}) copy-start(f32[1,512]{1,0:T(1,128)} %param.8) | copy-start | bytes 6148
  3.4 11.1 %collective-permute-start = (bf16[16,16,2048]{2,1,0:T(8,128)(2,1)S(1)}, bf16[16,16,2048]{2,1,0:T(8,128)(2,1)S(1)}, u32[]{:S(2)}, u32[]{:S(2)}) collective-permute-start(bf16[16,16,2048]{2,1,0:T(8,128)(2,1)S(1)} %get-tuple-element.22), channel_id=1, source_target_pairs={{0,16},{16,0},{1,17},{17,1},{2,18},{18,2},{3,19},{19,3},{4,20},{20... | collective-permute-start | bytes 3145736 | tf_op jit(solution)/shard_map/ppermute | solution.py:32
  12.2 0.9 copy-start.2
  15.5 3.9 %copy-start.5 = (s32[128,512]{1,0:T(8,128)S(1)}, s32[128,512]{1,0:T(8,128)}, u32[]{:S(2)}) copy-start(s32[128,512]{1,0:T(8,128)} %param.7) | copy-start | bytes 786436
  15.6 23.1 %all-to-all-start = ((bf16[16,16,2048]{2,1,0:T(8,128)(2,1)}), bf16[16,16,2048]{2,1,0:T(8,128)(2,1)S(1)}, u32[]{:S(2)}, u32[]{:S(2)}) async-start(bf16[16,16,2048]{2,1,0:T(8,128)(2,1)} %shard_map.86), calls=%async_computation | async-start | bytes 2097152 | tf_op jit(solution)/shard_map/all_to_all | solution.py:28
  19.4 14.6 %collective-permute-start.1 = (bf16[128,256]{1,0:T(8,128)(2,1)S(1)}, bf16[128,256]{1,0:T(8,128)(2,1)S(1)}, u32[]{:S(2)}, u32[]{:S(2)}) collective-permute-start(bf16[128,256]{1,0:T(8,128)(2,1)S(1)} %get-tuple-element.23.shard), channel_id=1, source_target_pairs={{0,387},{16,403},{32,419},{48,435},{64,451},{80,467},{96,483},{112... | collective-permute-start | bytes 196616 | tf_op jit(solution)/shard_map/ppermute | solution.py:48
  28.3 6.0 %collective-permute-start.2 = (bf16[128,256]{1,0:T(8,128)(2,1)S(1)}, bf16[128,256]{1,0:T(8,128)(2,1)S(1)}, u32[]{:S(2)}, u32[]{:S(2)}) collective-permute-start(bf16[128,256]{1,0:T(8,128)(2,1)S(1)} %get-tuple-element.23.shard), channel_id=1, source_target_pairs={{0,2},{16,402},{32,34},{48,434},{64,66},{80,466},{96,98},{112,498}... | collective-permute-start | bytes 196616 | tf_op jit(solution)/shard_map/ppermute | solution.py:48
  31.4 7.3 %collective-permute-start.3 = (bf16[128,256]{1,0:T(8,128)(2,1)S(1)}, bf16[128,256]{1,0:T(8,128)(2,1)S(1)}, u32[]{:S(2)}, u32[]{:S(2)}) collective-permute-start(bf16[128,256]{1,0:T(8,128)(2,1)S(1)} %get-tuple-element.23.shard), channel_id=1, source_target_pairs={{0,1},{16,17},{32,33},{48,49},{64,65},{80,81},{96,97},{112,113},{1... | collective-permute-start | bytes 196616 | tf_op jit(solution)/shard_map/ppermute | solution.py:48
  40.3 28.8 %all-to-all-start.1 = ((bf16[16,8,1152]{2,1,0:T(8,128)(2,1)}), bf16[16,8,1152]{2,1,0:T(8,128)(2,1)S(1)}, u32[]{:S(2)}, u32[]{:S(2)}) async-start(bf16[16,8,1152]{2,1,0:T(8,128)(2,1)} %shard_map.87), calls=%async_computation.1 | async-start | bytes 589824 | tf_op jit(solution)/shard_map/all_to_all | solution.py:28
  50.1 30.9 %copy-start.1 = (bf16[192,2048]{1,0:T(8,128)(2,1)S(1)}, bf16[192,2048]{1,0:T(8,128)(2,1)}, u32[]{:S(2)}) copy-start(bf16[192,2048]{1,0:T(8,128)(2,1)} %tokens.1) | copy-start | bytes 2359300
  50.1 30.9 %copy-start.3 = (bf16[192,512]{1,0:T(8,128)(2,1)S(1)}, bf16[192,512]{1,0:T(8,128)(2,1)}, u32[]{:S(2)}) copy-start(bf16[192,512]{1,0:T(8,128)(2,1)} %key_grad.3) | copy-start | bytes 589828
  50.1 30.9 %copy-start.4 = (f32[2048]{0:T(1024)S(1)}, f32[2048]{0:T(1024)}, u32[]{:S(2)}) copy-start(f32[2048]{0:T(1024)} %param.6) | copy-start | bytes 24580
  50.1 7.4 %collective-permute-start.4 = (bf16[4,128,256]{2,1,0:T(8,128)(2,1)S(1)}, bf16[4,128,256]{2,1,0:T(8,128)(2,1)S(1)}, u32[]{:S(2)}, u32[]{:S(2)}) collective-permute-start(bf16[4,128,256]{2,1,0:T(8,128)(2,1)S(1)} %pad_maximum_fusion.1), channel_id=1, source_target_pairs={{0,12},{4,0},{8,4},{12,8},{1,13},{5,1},{9,5},{13,9},{2,14},{6,2},{... | collective-permute-start | bytes 786440 | tf_op jit(solution)/shard_map/ppermute | solution.py:36
  52.8 8.9 %collective-permute-start.5 = (bf16[4,128,256]{2,1,0:T(8,128)(2,1)S(1)}, bf16[4,128,256]{2,1,0:T(8,128)(2,1)S(1)}, u32[]{:S(2)}, u32[]{:S(2)}) collective-permute-start(bf16[4,128,256]{2,1,0:T(8,128)(2,1)S(1)} %pad_maximum_fusion.1), channel_id=1, source_target_pairs={{0,8},{4,12},{8,0},{12,4},{1,9},{5,13},{9,1},{13,5},{2,10},{6,14},... | collective-permute-start | bytes 786440 | tf_op jit(solution)/shard_map/ppermute | solution.py:36
  55.0 14.0 %collective-permute-start.6 = (bf16[4,128,256]{2,1,0:T(8,128)(2,1)S(1)}, bf16[4,128,256]{2,1,0:T(8,128)(2,1)S(1)}, u32[]{:S(2)}, u32[]{:S(2)}) collective-permute-start(bf16[4,128,256]{2,1,0:T(8,128)(2,1)S(1)} %pad_maximum_fusion.1), channel_id=1, source_target_pairs={{0,4},{4,8},{8,12},{12,0},{1,5},{5,9},{9,13},{13,1},{2,6},{6,10},{... | collective-permute-start | bytes 786440 | tf_op jit(solution)/shard_map/ppermute | solution.py:36
  70.0 11.0 %collective-permute-start.7 = (bf16[8,128,256]{2,1,0:T(8,128)(2,1)S(1)}, bf16[8,128,256]{2,1,0:T(8,128)(2,1)S(1)}, u32[]{:S(2)}, u32[]{:S(2)}) collective-permute-start(bf16[8,128,256]{2,1,0:T(8,128)(2,1)S(1)} %constant_dynamic-update-slice_fusion.rest_0_), channel_id=1, source_target_pairs={{0,16},{16,0},{1,17},{17,1},{2,18},{18,2},{3,19},{19,3},{4,20},{20... | collective-permute-start | bytes 1572872 | tf_op jit(solution)/shard_map/ppermute | solution.py:32
  73.6 7.4 %collective-permute-start.8 = (bf16[8,128,256]{2,1,0:T(8,128)(2,1)S(1)}, bf16[8,128,256]{2,1,0:T(8,128)(2,1)}, u32[]{:S(2)}, u32[]{:S(2)}) collective-permute-start(bf16[8,128,256]{2,1,0:T(8,128)(2,1)S(1)} %pad_maximum_fusion.rest_1_), channel_id=1, source_target_pairs={{0,16},{16,0},{1,17},{17,1},{2,18},{18,2},{3,19},{19,3},{4,20},{20... | collective-permute-start | bytes 1572872 | tf_op jit(solution)/shard_map/ppermute | solution.py:32
  75.5 17.7 %all-to-all-start.2 = ((bf16[32,8,1152]{2,1,0:T(8,128)(2,1)}), bf16[32,8,1152]{2,1,0:T(8,128)(2,1)S(1)}, u32[]{:S(2)}, u32[]{:S(2)}) async-start(bf16[32,8,1152]{2,1,0:T(8,128)(2,1)} %shard_map.88), calls=%async_computation.2 | async-start | bytes 1179648 | tf_op jit(solution)/shard_map/all_to_all | solution.py:28

commit v9 on v8

--- a/solution.py
+++ b/solution.py
@@ -288,8 +288,8 @@
     line = exchange(payload, ("zh", "zl"))
     stack_late, _ = lax.optimization_barrier((stack, payload))
     one, two, three = (along_y(stack_late, -step) for step in (1, 2, 3))
-    halves = jnp.concatenate([stack, one], axis=0), jnp.concatenate([two, three], axis=0)
-    line, *halves = lax.optimization_barrier((line, *halves))
+    near = jnp.concatenate([stack, one], axis=0)
+    line, near, three = lax.optimization_barrier((line, near, three))
     (blocks,) = call(
         line_kernel,
         [((32, 8, 1152), bf16)],
@@ -298,8 +298,9 @@
         scratch=[pltpu.VMEM((8, 8, 1152), bf16), pltpu.SemaphoreType.DMA((4,))],
         out_specs=[ANY],
     )
-    *halves_late, _ = lax.optimization_barrier((*halves, blocks))
-    pieces = (*halves, *map(swap, halves_late))
+    near_late, two, _ = lax.optimization_barrier((near, two, blocks))
+    far = jnp.concatenate([two, three], axis=0)
+    pieces = (near, far, swap(near_late), swap(far))
     blocks = exchange(blocks, ("y", "x", "core"))
     keys, tokens_grad = call(
         token_kernel,
@@ -307,7 +308,6 @@
         [SMEM, VMEM, VMEM, VMEM, VMEM] + [ANY] * 4,
         (place, tokens, inv_rms, gain_row, key_grad, *pieces),
         scratch=[pltpu.VMEM((2048, 512), bf16), pltpu.SemaphoreType.DMA((32,))],
-        flops=4 * 192 * 2048 * 512,
     )
     blocks, keys, tokens_grad = lax.optimization_barrier((blocks, keys, tokens_grad))
     weight_grad, gain_grad = call(

time: 95.3 us -> 90.4 us (0.949)
  waiting for transfers between devices: 23.2 us -> 13.3 us
  starting transfers between devices: 55.1 us -> 61.1 us
    ppermute x3, waiting for transfers between devices: 11.5 us -> 3.27 us  [along_y(): return lax.ppermute(block, 'y', [(y, (y + step) % 4) for y in range(4)])]
    all_to_all x3, starting transfers between devices: 18.9 us -> 25.5 us  [exchange(): return lax.all_to_all(blocks, axes, 0, 0, tiled=False)]
    all_to_all x3, waiting for transfers between devices: 6.82 us -> 3.49 us  [exchange(): return lax.all_to_all(blocks, axes, 0, 0, tiled=False)]
    ppermute x3, waiting for transfers between devices: 0.3 us -> 1.9 us  [swap(): return lax.ppermute(block, 'core', [(0, 1), (1, 0)])]
    ppermute x3, starting transfers between devices: 14.3 us -> 13.1 us  [swap(): return lax.ppermute(block, 'core', [(0, 1), (1, 0)])]
  transfers between devices with their start and end apart: 12 -> 12, of which waited for: 6 -> 7; matrix products, arithmetic and copies ran while one was open for 0% -> 0% of each run, Pallas kernels for 7% -> 7%
where the time goes in v9:
time: 90.4 us; the launch traced here: 89.7 us
  starting transfers between devices  61.1 us (68%)
  waiting for transfers between devices  13.3 us (15%)
  Pallas kernels  13.2 us (15%)
  local copies, waits for them, and re-layouts  1.05 us (1%)
  between operations  0.96 us (1%)
    all_to_all x3, starting transfers between devices, exchange(): return lax.all_to_all(blocks, axes, 0, 0, tiled=False)  25.5 us
    ppermute x3, starting transfers between devices, along_z(): return lax.ppermute(block, ('zh', 'x', 'core', 'zl'), pairs)  14.6 us
    pallas_call x7, Pallas kernels, call(): pl.pallas_call(kernel, out_shape=[jax.ShapeDtypeStruct(s, d) for s, d in...  13.2 us
    ppermute x3, starting transfers between devices, swap(): return lax.ppermute(block, 'core', [(0, 1), (1, 0)])  13.1 us
    ppermute x3, starting transfers between devices, along_y(): return lax.ppermute(block, 'y', [(y, (y + step) % 4) for y in range(4)])  7.9 us
    ppermute x3, waiting for transfers between devices, along_z(): return lax.ppermute(block, ('zh', 'x', 'core', 'zl'), pairs)  4.6 us
    all_to_all x3, waiting for transfers between devices, exchange(): return lax.all_to_all(blocks, axes, 0, 0, tiled=False)  3.49 us
    ppermute x3, waiting for transfers between devices, along_y(): return lax.ppermute(block, 'y', [(y, (y + step) % 4) for y in range(4)])  3.27 us
  transfers between devices with their start and end apart: 12, of which 7 were waited for; matrix products, arithmetic and copies ran while one was open for 0% of the time, Pallas kernels for 7%

profile of v9, /device:TPU:1, one launch (start us, length us, event | category | flops | bytes accessed | tf_op | source)
XLA Modules:
  0.0 89.7 jit_solution(12242428175530574562)
XLA Ops:
  0.7 2.6 %shard_map.84 = (bf16[192,2048]{1,0:T(8,128)(2,1)S(1)}, f32[192,128]{1,0:T(8,128)S(1)}, bf16[16,16,2048]{2,1,0:T(8,128)(2,1)S(1)}) custom-call(s32[4]{0:T(128)S(1)} %pad_add_fusion.place, bf16[192,2048]{1,0:T(8,128)(2,1)} %tokens.1, f32[1,2048]{1,0:T(1,128)} %bitcast.20, bf16[192,512]{1,0:T(8,128)(2,1)} %key_grad.3), custom_call_target="tpu_custom_call" | custom-call | flops 201326592 | bytes 1982496 | tf_op jit(solution)/shard_map/pallas_call | solution.py:224
  3.4 8.8 %collective-permute-start = (bf16[16,16,2048]{2,1,0:T(8,128)(2,1)S(1)}, bf16[16,16,2048]{2,1,0:T(8,128)(2,1)S(1)}, u32[]{:S(2)}, u32[]{:S(2)}) collective-permute-start(bf16[16,16,2048]{2,1,0:T(8,128)(2,1)S(1)} %get-tuple-element.22), channel_id=1, source_target_pairs={{0,16},{16,0},{1,17},{17,1},{2,18},{18,2},{3,19},{19,3},{4,20},{20... | collective-permute-start | bytes 3145736 | tf_op jit(solution)/shard_map/ppermute | solution.py:32
  12.2 0.9 %copy-done.2 = bf16[192,512]{1,0:T(8,128)(2,1)S(1)} copy-done((bf16[192,512]{1,0:T(8,128)(2,1)S(1)}, bf16[192,512]{1,0:T(8,128)(2,1)}, u32[]{:S(2)}) %copy-start.2) | copy-done | bytes 196632
  13.1 1.0 %shard_map.85.mine = f32[16,16,2048]{2,1,0:T(8,128)S(1)} custom-call(s32[4]{0:T(128)S(1)} %pad_add_fusion.place, bf16[192,2048]{1,0:T(8,128)(2,1)S(1)} %get-tuple-element.21.normed, bf16[192,512]{1,0:T(8,128)(2,1)S(1)} %copy-done.2), custom_call_target="tpu_custom_call" | custom-call | flops 201326592 | bytes 1966112 | tf_op jit(solution)/shard_map/pallas_call | solution.py:224
  14.4 1.1 %shard_map.86 = bf16[16,16,2048]{2,1,0:T(8,128)(2,1)} custom-call(f32[16,16,2048]{2,1,0:T(8,128)S(1)} %shard_map.85.mine, bf16[16,16,2048]{2,1,0:T(8,128)(2,1)S(1)} %collective-permute-done.got), custom_call_target="tpu_custom_call" | custom-call | bytes 6291456 | tf_op jit(solution)/shard_map/pallas_call | solution.py:224
  15.6 3.8 %all-to-all-start = ((bf16[16,16,2048]{2,1,0:T(8,128)(2,1)}), bf16[16,16,2048]{2,1,0:T(8,128)(2,1)S(1)}, u32[]{:S(2)}, u32[]{:S(2)}) async-start(bf16[16,16,2048]{2,1,0:T(8,128)(2,1)} %shard_map.86), calls=%async_computation | async-start | bytes 2097152 | tf_op jit(solution)/shard_map/all_to_all | solution.py:28
  19.4 8.9 %collective-permute-start.1 = (bf16[128,256]{1,0:T(8,128)(2,1)S(1)}, bf16[128,256]{1,0:T(8,128)(2,1)S(1)}, u32[]{:S(2)}, u32[]{:S(2)}) collective-permute-start(bf16[128,256]{1,0:T(8,128)(2,1)S(1)} %get-tuple-element.23.shard), channel_id=1, source_target_pairs={{0,387},{16,403},{32,419},{48,435},{64,451},{80,467},{96,483},{112... | collective-permute-start | bytes 196616 | tf_op jit(solution)/shard_map/ppermute | solution.py:48
  28.3 3.1 %collective-permute-start.2 = (bf16[128,256]{1,0:T(8,128)(2,1)S(1)}, bf16[128,256]{1,0:T(8,128)(2,1)S(1)}, u32[]{:S(2)}, u32[]{:S(2)}) collective-permute-start(bf16[128,256]{1,0:T(8,128)(2,1)S(1)} %get-tuple-element.23.shard), channel_id=1, source_target_pairs={{0,2},{16,402},{32,34},{48,434},{64,66},{80,466},{96,98},{112,498}... | collective-permute-start | bytes 196616 | tf_op jit(solution)/shard_map/ppermute | solution.py:48
  31.4 2.6 %collective-permute-start.3 = (bf16[128,256]{1,0:T(8,128)(2,1)S(1)}, bf16[128,256]{1,0:T(8,128)(2,1)S(1)}, u32[]{:S(2)}, u32[]{:S(2)}) collective-permute-start(bf16[128,256]{1,0:T(8,128)(2,1)S(1)} %get-tuple-element.23.shard), channel_id=1, source_target_pairs={{0,1},{16,17},{32,33},{48,49},{64,65},{80,81},{96,97},{112,113},{1... | collective-permute-start | bytes 196616 | tf_op jit(solution)/shard_map/ppermute | solution.py:48
  34.3 4.3 %collective-permute-done.3.below = bf16[128,256]{1,0:T(8,128)(2,1)S(1)} collective-permute-done((bf16[128,256]{1,0:T(8,128)(2,1)S(1)}, bf16[128,256]{1,0:T(8,128)(2,1)S(1)}, u32[]{:S(2)}, u32[]{:S(2)}) %collective-permute-start.3) | collective-permute-done | bytes 65568 | tf_op jit(solution)/shard_map/ppermute | solution.py:48
  38.7 1.7 %shard_map.87 = bf16[16,8,1152]{2,1,0:T(8,128)(2,1)} custom-call(s32[4]{0:T(128)S(1)} %pad_add_fusion.place, bf16[16,16,2048]{2,1,0:T(8,128)(2,1)S(1)} %all-to-all-done.square, bf16[128,256]{1,0:T(8,128)(2,1)S(1)} %get-tuple-element.23.shard, bf16[128,256]{1,0:T(8,128)(2,1)S(1)} %collective-permute-done.1.above, ...), custom_call_target="tpu_custom_call" | custom-call | bytes 2621472 | tf_op jit(solution)/shard_map/pallas_call | solution.py:224
  40.3 9.7 %all-to-all-start.1 = ((bf16[16,8,1152]{2,1,0:T(8,128)(2,1)}), bf16[16,8,1152]{2,1,0:T(8,128)(2,1)S(1)}, u32[]{:S(2)}, u32[]{:S(2)}) async-start(bf16[16,8,1152]{2,1,0:T(8,128)(2,1)} %shard_map.87), calls=%async_computation.1 | async-start | bytes 589824 | tf_op jit(solution)/shard_map/all_to_all | solution.py:28
  50.1 2.6 %collective-permute-start.4 = (bf16[4,128,256]{2,1,0:T(8,128)(2,1)S(1)}, bf16[4,128,256]{2,1,0:T(8,128)(2,1)S(1)}, u32[]{:S(2)}, u32[]{:S(2)}) collective-permute-start(bf16[4,128,256]{2,1,0:T(8,128)(2,1)S(1)} %pad_maximum_fusion), channel_id=1, source_target_pairs={{0,12},{4,0},{8,4},{12,8},{1,13},{5,1},{9,5},{13,9},{2,14},{6,2},{... | collective-permute-start | bytes 786440 | tf_op jit(solution)/shard_map/ppermute | solution.py:36
  52.8 2.8 %collective-permute-start.5 = (bf16[4,128,256]{2,1,0:T(8,128)(2,1)S(1)}, bf16[4,128,256]{2,1,0:T(8,128)(2,1)S(1)}, u32[]{:S(2)}, u32[]{:S(2)}) collective-permute-start(bf16[4,128,256]{2,1,0:T(8,128)(2,1)S(1)} %pad_maximum_fusion), channel_id=1, source_target_pairs={{0,4},{4,8},{8,12},{12,0},{1,5},{5,9},{9,13},{13,1},{2,6},{6,10},{... | collective-permute-start | bytes 786440 | tf_op jit(solution)/shard_map/ppermute | solution.py:36
  55.6 2.5 %collective-permute-start.6 = (bf16[4,128,256]{2,1,0:T(8,128)(2,1)S(1)}, bf16[4,128,256]{2,1,0:T(8,128)(2,1)S(1)}, u32[]{:S(2)}, u32[]{:S(2)}) collective-permute-start(bf16[4,128,256]{2,1,0:T(8,128)(2,1)S(1)} %pad_maximum_fusion), channel_id=1, source_target_pairs={{0,8},{4,12},{8,0},{12,4},{1,9},{5,13},{9,1},{13,5},{2,10},{6,14},... | collective-permute-start | bytes 786440 | tf_op jit(solution)/shard_map/ppermute | solution.py:36
  58.1 3.3 %collective-permute-done.5 = bf16[4,128,256]{2,1,0:T(8,128)(2,1)S(1)} collective-permute-done((bf16[4,128,256]{2,1,0:T(8,128)(2,1)S(1)}, bf16[4,128,256]{2,1,0:T(8,128)(2,1)S(1)}, u32[]{:S(2)}, u32[]{:S(2)}) %collective-permute-start.5) | collective-permute-done | bytes 262176 | tf_op jit(solution)/shard_map/ppermute | solution.py:36
  61.4 1.7 %all-to-all-done.1.line = bf16[16,8,1152]{2,1,0:T(8,128)(2,1)S(1)} async-done(((bf16[16,8,1152]{2,1,0:T(8,128)(2,1)}), bf16[16,8,1152]{2,1,0:T(8,128)(2,1)S(1)}, u32[]{:S(2)}, u32[]{:S(2)}) %all-to-all-start.1) | async-done | bytes 294944 | tf_op jit(solution)/shard_map/all_to_all | solution.py:28
  64.1 12.0 %all-to-all-start.2 = ((bf16[32,8,1152]{2,1,0:T(8,128)(2,1)}), bf16[32,8,1152]{2,1,0:T(8,128)(2,1)S(1)}, u32[]{:S(2)}, u32[]{:S(2)}) async-start(bf16[32,8,1152]{2,1,0:T(8,128)(2,1)} %shard_map.88), calls=%async_computation.2 | async-start | bytes 1179648 | tf_op jit(solution)/shard_map/all_to_all | solution.py:28
  76.2 2.1 %collective-permute-start.8 = (bf16[8,128,256]{2,1,0:T(8,128)(2,1)S(1)}, bf16[8,128,256]{2,1,0:T(8,128)(2,1)S(1)}, u32[]{:S(2)}, u32[]{:S(2)}) collective-permute-start(bf16[8,128,256]{2,1,0:T(8,128)(2,1)S(1)} %constant_dynamic-update-slice_fusion.5.rest_1_), channel_id=1, source_target_pairs={{0,16},{16,0},{1,17},{17,1},{2,18},{18,2},{3,19},{19,3},{4,20},{20... | collective-permute-start | bytes 1572872 | tf_op jit(solution)/shard_map/ppermute | solution.py:32
  78.3 2.2 %collective-permute-start.7 = (bf16[8,128,256]{2,1,0:T(8,128)(2,1)S(1)}, bf16[8,128,256]{2,1,0:T(8,128)(2,1)S(1)}, u32[]{:S(2)}, u32[]{:S(2)}) collective-permute-start(bf16[8,128,256]{2,1,0:T(8,128)(2,1)S(1)} %constant_dynamic-update-slice_fusion.rest_0_), channel_id=1, source_target_pairs={{0,16},{16,0},{1,17},{17,1},{2,18},{18,2},{3,19},{19,3},{4,20},{20... | collective-permute-start | bytes 1572872 | tf_op jit(solution)/shard_map/ppermute | solution.py:32
  80.5 1.6 %collective-permute-done.7.rest_2_ = bf16[8,128,256]{2,1,0:T(8,128)(2,1)S(1)} collective-permute-done((bf16[8,128,256]{2,1,0:T(8,128)(2,1)S(1)}, bf16[8,128,256]{2,1,0:T(8,128)(2,1)S(1)}, u32[]{:S(2)}, u32[]{:S(2)}) %collective-permute-start.7) | collective-permute-done | bytes 524320 | tf_op jit(solution)/shard_map/ppermute | solution.py:32
  82.2 4.5 %shard_map.89 = (bf16[192,512]{1,0:T(8,128)(2,1)}, bf16[192,2048]{1,0:T(8,128)(2,1)}) custom-call(s32[4]{0:T(128)S(1)} %pad_add_fusion.place, bf16[192,2048]{1,0:T(8,128)(2,1)S(1)} %copy-done.1, f32[192,128]{1,0:T(8,128)S(1)} %get-tuple-element.26.inv_rms, f32[1,2048]{1,0:T(1,128)S(1)} %bitcast.21, bf16[192,512]{1,0:T(8,128)(2,1)S(1)} %copy-done.3, ...), custom_call_target="tpu_custom_call" | custom-call | bytes 6373408 | tf_op jit(solution)/shard_map/pallas_call | solution.py:224
  86.6 1.8 %all-to-all-done.2.blocks = bf16[32,8,1152]{2,1,0:T(8,128)(2,1)S(1)} async-done(((bf16[32,8,1152]{2,1,0:T(8,128)(2,1)}), bf16[32,8,1152]{2,1,0:T(8,128)(2,1)S(1)}, u32[]{:S(2)}, u32[]{:S(2)}) %all-to-all-start.2) | async-done | bytes 589856 | tf_op jit(solution)/shard_map/all_to_all | solution.py:28
  88.4 1.4 %shard_map.90 = (f32[128,512]{1,0:T(8,128)}, f32[16,128]{1,0:T(8,128)}) custom-call(s32[4]{0:T(128)S(1)} %pad_add_fusion.place, bf16[32,8,1152]{2,1,0:T(8,128)(2,1)S(1)} %all-to-all-done.2.blocks, f32[16,128]{1,0:T(8,128)S(1)} %bitcast.22), custom_call_target="tpu_custom_call" | custom-call | bytes 1196064 | tf_op jit(solution)/shard_map/pallas_call | solution.py:224
  (29 shorter events, 1.7 us)
Async XLA Ops:
  0.6 18.7 %copy-start = (f32[1,512]{1,0:T(1,128)S(1)}, f32[1,512]{1,0:T(1,128)}, u32[]{:S(2)}) copy-start(f32[1,512]{1,0:T(1,128)} %param.8) | copy-start | bytes 6148
  3.4 11.1 %collective-permute-start = (bf16[16,16,2048]{2,1,0:T(8,128)(2,1)S(1)}, bf16[16,16,2048]{2,1,0:T(8,128)(2,1)S(1)}, u32[]{:S(2)}, u32[]{:S(2)}) collective-permute-start(bf16[16,16,2048]{2,1,0:T(8,128)(2,1)S(1)} %get-tuple-element.22), channel_id=1, source_target_pairs={{0,16},{16,0},{1,17},{17,1},{2,18},{18,2},{3,19},{19,3},{4,20},{20... | collective-permute-start | bytes 3145736 | tf_op jit(solution)/shard_map/ppermute | solution.py:32
  12.2 0.9 %copy-start.2 = (bf16[192,512]{1,0:T(8,128)(2,1)S(1)}, bf16[192,512]{1,0:T(8,128)(2,1)}, u32[]{:S(2)}) copy-start(bf16[192,512]{1,0:T(8,128)(2,1)} %key_grad.3) | copy-start | bytes 589828
  15.5 3.9 %copy-start.5 = (s32[128,512]{1,0:T(8,128)S(1)}, s32[128,512]{1,0:T(8,128)}, u32[]{:S(2)}) copy-start(s32[128,512]{1,0:T(8,128)} %param.7) | copy-start | bytes 786436
  15.6 23.1 %all-to-all-start = ((bf16[16,16,2048]{2,1,0:T(8,128)(2,1)}), bf16[16,16,2048]{2,1,0:T(8,128)(2,1)S(1)}, u32[]{:S(2)}, u32[]{:S(2)}) async-start(bf16[16,16,2048]{2,1,0:T(8,128)(2,1)} %shard_map.86), calls=%async_computation | async-start | bytes 2097152 | tf_op jit(solution)/shard_map/all_to_all | solution.py:28
  19.4 14.6 %collective-permute-start.1 = (bf16[128,256]{1,0:T(8,128)(2,1)S(1)}, bf16[128,256]{1,0:T(8,128)(2,1)S(1)}, u32[]{:S(2)}, u32[]{:S(2)}) collective-permute-start(bf16[128,256]{1,0:T(8,128)(2,1)S(1)} %get-tuple-element.23.shard), channel_id=1, source_target_pairs={{0,387},{16,403},{32,419},{48,435},{64,451},{80,467},{96,483},{112... | collective-permute-start | bytes 196616 | tf_op jit(solution)/shard_map/ppermute | solution.py:48
  28.3 6.0 %collective-permute-start.2 = (bf16[128,256]{1,0:T(8,128)(2,1)S(1)}, bf16[128,256]{1,0:T(8,128)(2,1)S(1)}, u32[]{:S(2)}, u32[]{:S(2)}) collective-permute-start(bf16[128,256]{1,0:T(8,128)(2,1)S(1)} %get-tuple-element.23.shard), channel_id=1, source_target_pairs={{0,2},{16,402},{32,34},{48,434},{64,66},{80,466},{96,98},{112,498}... | collective-permute-start | bytes 196616 | tf_op jit(solution)/shard_map/ppermute | solution.py:48
  31.4 7.3 %collective-permute-start.3 = (bf16[128,256]{1,0:T(8,128)(2,1)S(1)}, bf16[128,256]{1,0:T(8,128)(2,1)S(1)}, u32[]{:S(2)}, u32[]{:S(2)}) collective-permute-start(bf16[128,256]{1,0:T(8,128)(2,1)S(1)} %get-tuple-element.23.shard), channel_id=1, source_target_pairs={{0,1},{16,17},{32,33},{48,49},{64,65},{80,81},{96,97},{112,113},{1... | collective-permute-start | bytes 196616 | tf_op jit(solution)/shard_map/ppermute | solution.py:48
  40.3 22.8 %all-to-all-start.1 = ((bf16[16,8,1152]{2,1,0:T(8,128)(2,1)}), bf16[16,8,1152]{2,1,0:T(8,128)(2,1)S(1)}, u32[]{:S(2)}, u32[]{:S(2)}) async-start(bf16[16,8,1152]{2,1,0:T(8,128)(2,1)} %shard_map.87), calls=%async_computation.1 | async-start | bytes 589824 | tf_op jit(solution)/shard_map/all_to_all | solution.py:28
  50.1 32.0 %copy-start.1 = (bf16[192,2048]{1,0:T(8,128)(2,1)S(1)}, bf16[192,2048]{1,0:T(8,128)(2,1)}, u32[]{:S(2)}) copy-start(bf16[192,2048]{1,0:T(8,128)(2,1)} %tokens.1) | copy-start | bytes 2359300
  50.1 32.0 %copy-start.3 = (bf16[192,512]{1,0:T(8,128)(2,1)S(1)}, bf16[192,512]{1,0:T(8,128)(2,1)}, u32[]{:S(2)}) copy-start(bf16[192,512]{1,0:T(8,128)(2,1)} %key_grad.3) | copy-start | bytes 589828
  50.1 32.0 %copy-start.4 = (f32[2048]{0:T(1024)S(1)}, f32[2048]{0:T(1024)}, u32[]{:S(2)}) copy-start(f32[2048]{0:T(1024)} %param.6) | copy-start | bytes 24580
  50.1 8.0 %collective-permute-start.4 = (bf16[4,128,256]{2,1,0:T(8,128)(2,1)S(1)}, bf16[4,128,256]{2,1,0:T(8,128)(2,1)S(1)}, u32[]{:S(2)}, u32[]{:S(2)}) collective-permute-start(bf16[4,128,256]{2,1,0:T(8,128)(2,1)S(1)} %pad_maximum_fusion), channel_id=1, source_target_pairs={{0,12},{4,0},{8,4},{12,8},{1,13},{5,1},{9,5},{13,9},{2,14},{6,2},{... | collective-permute-start | bytes 786440 | tf_op jit(solution)/shard_map/ppermute | solution.py:36
  52.8 8.6 %collective-permute-start.5 = (bf16[4,128,256]{2,1,0:T(8,128)(2,1)S(1)}, bf16[4,128,256]{2,1,0:T(8,128)(2,1)S(1)}, u32[]{:S(2)}, u32[]{:S(2)}) collective-permute-start(bf16[4,128,256]{2,1,0:T(8,128)(2,1)S(1)} %pad_maximum_fusion), channel_id=1, source_target_pairs={{0,4},{4,8},{8,12},{12,0},{1,5},{5,9},{9,13},{13,1},{2,6},{6,10},{... | collective-permute-start | bytes 786440 | tf_op jit(solution)/shard_map/ppermute | solution.py:36
  55.6 20.5 %collective-permute-start.6 = (bf16[4,128,256]{2,1,0:T(8,128)(2,1)S(1)}, bf16[4,128,256]{2,1,0:T(8,128)(2,1)S(1)}, u32[]{:S(2)}, u32[]{:S(2)}) collective-permute-start(bf16[4,128,256]{2,1,0:T(8,128)(2,1)S(1)} %pad_maximum_fusion), channel_id=1, source_target_pairs={{0,8},{4,12},{8,0},{12,4},{1,9},{5,13},{9,1},{13,5},{2,10},{6,14},... | collective-permute-start | bytes 786440 | tf_op jit(solution)/shard_map/ppermute | solution.py:36
  64.1 24.3 %all-to-all-start.2 = ((bf16[32,8,1152]{2,1,0:T(8,128)(2,1)}), bf16[32,8,1152]{2,1,0:T(8,128)(2,1)S(1)}, u32[]{:S(2)}, u32[]{:S(2)}) async-start(bf16[32,8,1152]{2,1,0:T(8,128)(2,1)} %shard_map.88), calls=%async_computation.2 | async-start | bytes 1179648 | tf_op jit(solution)/shard_map/all_to_all | solution.py:28
  76.2 4.3 %collective-permute-start.8 = (bf16[8,128,256]{2,1,0:T(8,128)(2,1)S(1)}, bf16[8,128,256]{2,1,0:T(8,128)(2,1)S(1)}, u32[]{:S(2)}, u32[]{:S(2)}) collective-permute-start(bf16[8,128,256]{2,1,0:T(8,128)(2,1)S(1)} %constant_dynamic-update-slice_fusion.5.rest_1_), channel_id=1, source_target_pairs={{0,16},{16,0},{1,17},{17,1},{2,18},{18,2},{3,19},{19,3},{4,20},{20... | collective-permute-start | bytes 1572872 | tf_op jit(solution)/shard_map/ppermute | solution.py:32
  78.3 3.8 %collective-permute-start.7 = (bf16[8,128,256]{2,1,0:T(8,128)(2,1)S(1)}, bf16[8,128,256]{2,1,0:T(8,128)(2,1)S(1)}, u32[]{:S(2)}, u32[]{:S(2)}) collective-permute-start(bf16[8,128,256]{2,1,0:T(8,128)(2,1)S(1)} %constant_dynamic-update-slice_fusion.rest_0_), channel_id=1, source_target_pairs={{0,16},{16,0},{1,17},{17,1},{2,18},{18,2},{3,19},{19,3},{4,20},{20... | collective-permute-start | bytes 1572872 | tf_op jit(solution)/shard_map/ppermute | solution.py:32

commit v10 on v9

--- a/solution.py
+++ b/solution.py
@@ -188,25 +188,15 @@
 
 
 def token_kernel(place, tokens, inv_rms, norm_gain, key_grad, *rest):
-    pieces, (keys, tokens_grad, weight, sem) = rest[:4], rest[4:]
+    pieces, (keys, tokens_grad, weight) = rest[:4], rest[4:]
     core, y, zl = place[0], place[2], place[3]
-    copies = []
-    for step in range(4):
-        for side in range(2):
-            column = core * HALF if side == 0 else (1 - core) * HALF
+    for side in range(2):
+        column = core * HALF if side == 0 else (1 - core) * HALF
+        columns = pl.ds(pl.multiple_of(column, HALF), HALF)
+        for step in range(4):
             for j in range(4):
                 row = (lax.rem(y + step, 4) * 4 + lax.rem(zl + j, 4)) * 128
-                copies.append(
-                    pltpu.make_async_copy(
-                        pieces[side * 2 + step // 2].at[step % 2 * 4 + j],
-                        weight.at[pl.ds(pl.multiple_of(row, 128), 128), pl.ds(pl.multiple_of(column, HALF), HALF)],
-                        sem.at[len(copies)],
-                    )
-                )
-    for copy in copies:
-        copy.start()
-    for copy in copies:
-        copy.wait()
+                weight[pl.ds(pl.multiple_of(row, 128), 128), columns] = pieces[side * 2 + step // 2][step % 2 * 4 + j]
     for rows in (slice(0, 96), slice(96, 192)):
         inv = inv_rms[rows, 0:1]
         unit = tokens[rows, :].astype(f32) * inv
@@ -289,7 +279,7 @@
     stack_late, _ = lax.optimization_barrier((stack, payload))
     one, two, three = (along_y(stack_late, -step) for step in (1, 2, 3))
     near = jnp.concatenate([stack, one], axis=0)
-    line, near, three = lax.optimization_barrier((line, near, three))
+    line, near = lax.optimization_barrier((line, near))
     (blocks,) = call(
         line_kernel,
         [((32, 8, 1152), bf16)],
@@ -298,16 +288,16 @@
         scratch=[pltpu.VMEM((8, 8, 1152), bf16), pltpu.SemaphoreType.DMA((4,))],
         out_specs=[ANY],
     )
-    near_late, two, _ = lax.optimization_barrier((near, two, blocks))
+    near_late, two, three, _ = lax.optimization_barrier((near, two, three, blocks))
     far = jnp.concatenate([two, three], axis=0)
     pieces = (near, far, swap(near_late), swap(far))
     blocks = exchange(blocks, ("y", "x", "core"))
     keys, tokens_grad = call(
         token_kernel,
         [((192, 512), bf16), ((192, 2048), bf16)],
-        [SMEM, VMEM, VMEM, VMEM, VMEM] + [ANY] * 4,
+        [SMEM] + [VMEM] * 8,
         (place, tokens, inv_rms, gain_row, key_grad, *pieces),
-        scratch=[pltpu.VMEM((2048, 512), bf16), pltpu.SemaphoreType.DMA((32,))],
+        scratch=[pltpu.VMEM((2048, 512), bf16)],
     )
     blocks, keys, tokens_grad = lax.optimization_barrier((blocks, keys, tokens_grad))
     weight_grad, gain_grad = call(

time: 90.4 us -> 90.4 us (level)
  waiting for transfers between devices: 13.3 us -> 14.3 us
    all_to_all x3, waiting for transfers between devices: 3.49 us -> 7.8 us  [exchange(): return lax.all_to_all(blocks, axes, 0, 0, tiled=False)]
    ppermute x3, waiting for transfers between devices: 3.27 us -> 0.01 us  [along_y(): return lax.ppermute(block, 'y', [(y, (y + step) % 4) for y in range(4)])]
  transfers between devices with their start and end apart: 12 -> 12, of which waited for: 7 -> 6; matrix products, arithmetic and copies ran while one was open for 0% -> 0% of each run, Pallas kernels for 7% -> 7%
where the time goes in v10:
time: 90.4 us; the launch traced here: 89.7 us
  starting transfers between devices  60.6 us (67%)
  waiting for transfers between devices  14.3 us (16%)
  Pallas kernels  12.7 us (14%)
  local copies, waits for them, and re-layouts  1.05 us (1%)
  between operations  0.96 us (1%)
    all_to_all x3, starting transfers between devices, exchange(): return lax.all_to_all(blocks, axes, 0, 0, tiled=False)  25.5 us
    ppermute x3, starting transfers between devices, along_z(): return lax.ppermute(block, ('zh', 'x', 'core', 'zl'), pairs)  14.6 us
    ppermute x3, starting transfers between devices, swap(): return lax.ppermute(block, 'core', [(0, 1), (1, 0)])  13.1 us
    pallas_call x7, Pallas kernels, call(): pl.pallas_call(kernel, out_shape=[jax.ShapeDtypeStruct(s, d) for s, d in...  12.7 us
    all_to_all x3, waiting for transfers between devices, exchange(): return lax.all_to_all(blocks, axes, 0, 0, tiled=False)  7.8 us
    ppermute x3, starting transfers between devices, along_y(): return lax.ppermute(block, 'y', [(y, (y + step) % 4) for y in range(4)])  7.33 us
    ppermute x3, waiting for transfers between devices, along_z(): return lax.ppermute(block, ('zh', 'x', 'core', 'zl'), pairs)  4.6 us
    ppermute x3, waiting for transfers between devices, swap(): return lax.ppermute(block, 'core', [(0, 1), (1, 0)])  1.9 us
  transfers between devices with their start and end apart: 12, of which 6 were waited for; matrix products, arithmetic and copies ran while one was open for 0% of the time, Pallas kernels for 7%

profile of v10, /device:TPU:1, one launch (start us, length us, event | category | flops | bytes accessed | tf_op | source)
XLA Modules:
  0.0 89.7 jit_solution(1763317025493184795)
XLA Ops:
  0.7 2.6 %shard_map.84 = (bf16[192,2048]{1,0:T(8,128)(2,1)S(1)}, f32[192,128]{1,0:T(8,128)S(1)}, bf16[16,16,2048]{2,1,0:T(8,128)(2,1)S(1)}) custom-call(s32[4]{0:T(128)S(1)} %pad_add_fusion.place, bf16[192,2048]{1,0:T(8,128)(2,1)} %tokens.1, f32[1,2048]{1,0:T(1,128)} %bitcast.20, bf16[192,512]{1,0:T(8,128)(2,1)} %key_grad.3), custom_call_target="tpu_custom_call" | custom-call | flops 201326592 | bytes 1982496 | tf_op jit(solution)/shard_map/pallas_call | solution.py:214
  3.4 8.8 %collective-permute-start = (bf16[16,16,2048]{2,1,0:T(8,128)(2,1)S(1)}, bf16[16,16,2048]{2,1,0:T(8,128)(2,1)S(1)}, u32[]{:S(2)}, u32[]{:S(2)}) collective-permute-start(bf16[16,16,2048]{2,1,0:T(8,128)(2,1)S(1)} %get-tuple-element.22), channel_id=1, source_target_pairs={{0,16},{16,0},{1,17},{17,1},{2,18},{18,2},{3,19},{19,3},{4,20},{20... | collective-permute-start | bytes 3145736 | tf_op jit(solution)/shard_map/ppermute | solution.py:32
  12.2 0.9 %copy-done.2 = bf16[192,512]{1,0:T(8,128)(2,1)S(1)} copy-done((bf16[192,512]{1,0:T(8,128)(2,1)S(1)}, bf16[192,512]{1,0:T(8,128)(2,1)}, u32[]{:S(2)}) %copy-start.2) | copy-done | bytes 196632
  13.1 1.0 %shard_map.85.mine = f32[16,16,2048]{2,1,0:T(8,128)S(1)} custom-call(s32[4]{0:T(128)S(1)} %pad_add_fusion.place, bf16[192,2048]{1,0:T(8,128)(2,1)S(1)} %get-tuple-element.21.normed, bf16[192,512]{1,0:T(8,128)(2,1)S(1)} %copy-done.2), custom_call_target="tpu_custom_call" | custom-call | flops 201326592 | bytes 1966112 | tf_op jit(solution)/shard_map/pallas_call | solution.py:214
  14.4 1.1 %shard_map.86 = bf16[16,16,2048]{2,1,0:T(8,128)(2,1)} custom-call(f32[16,16,2048]{2,1,0:T(8,128)S(1)} %shard_map.85.mine, bf16[16,16,2048]{2,1,0:T(8,128)(2,1)S(1)} %collective-permute-done.got), custom_call_target="tpu_custom_call" | custom-call | bytes 6291456 | tf_op jit(solution)/shard_map/pallas_call | solution.py:214
  15.6 3.8 %all-to-all-start = ((bf16[16,16,2048]{2,1,0:T(8,128)(2,1)}), bf16[16,16,2048]{2,1,0:T(8,128)(2,1)S(1)}, u32[]{:S(2)}, u32[]{:S(2)}) async-start(bf16[16,16,2048]{2,1,0:T(8,128)(2,1)} %shard_map.86), calls=%async_computation | async-start | bytes 2097152 | tf_op jit(solution)/shard_map/all_to_all | solution.py:28
  19.4 8.9 %collective-permute-start.1 = (bf16[128,256]{1,0:T(8,128)(2,1)S(1)}, bf16[128,256]{1,0:T(8,128)(2,1)S(1)}, u32[]{:S(2)}, u32[]{:S(2)}) collective-permute-start(bf16[128,256]{1,0:T(8,128)(2,1)S(1)} %get-tuple-element.23.shard), channel_id=1, source_target_pairs={{0,387},{16,403},{32,419},{48,435},{64,451},{80,467},{96,483},{112... | collective-permute-start | bytes 196616 | tf_op jit(solution)/shard_map/ppermute | solution.py:48
  28.3 3.1 %collective-permute-start.2 = (bf16[128,256]{1,0:T(8,128)(2,1)S(1)}, bf16[128,256]{1,0:T(8,128)(2,1)S(1)}, u32[]{:S(2)}, u32[]{:S(2)}) collective-permute-start(bf16[128,256]{1,0:T(8,128)(2,1)S(1)} %get-tuple-element.23.shard), channel_id=1, source_target_pairs={{0,2},{16,402},{32,34},{48,434},{64,66},{80,466},{96,98},{112,498}... | collective-permute-start | bytes 196616 | tf_op jit(solution)/shard_map/ppermute | solution.py:48
  31.4 2.6 %collective-permute-start.3 = (bf16[128,256]{1,0:T(8,128)(2,1)S(1)}, bf16[128,256]{1,0:T(8,128)(2,1)S(1)}, u32[]{:S(2)}, u32[]{:S(2)}) collective-permute-start(bf16[128,256]{1,0:T(8,128)(2,1)S(1)} %get-tuple-element.23.shard), channel_id=1, source_target_pairs={{0,1},{16,17},{32,33},{48,49},{64,65},{80,81},{96,97},{112,113},{1... | collective-permute-start | bytes 196616 | tf_op jit(solution)/shard_map/ppermute | solution.py:48
  34.3 4.3 %collective-permute-done.3.below = bf16[128,256]{1,0:T(8,128)(2,1)S(1)} collective-permute-done((bf16[128,256]{1,0:T(8,128)(2,1)S(1)}, bf16[128,256]{1,0:T(8,128)(2,1)S(1)}, u32[]{:S(2)}, u32[]{:S(2)}) %collective-permute-start.3) | collective-permute-done | bytes 65568 | tf_op jit(solution)/shard_map/ppermute | solution.py:48
  38.7 1.7 %shard_map.87 = bf16[16,8,1152]{2,1,0:T(8,128)(2,1)} custom-call(s32[4]{0:T(128)S(1)} %pad_add_fusion.place, bf16[16,16,2048]{2,1,0:T(8,128)(2,1)S(1)} %all-to-all-done.square, bf16[128,256]{1,0:T(8,128)(2,1)S(1)} %get-tuple-element.23.shard, bf16[128,256]{1,0:T(8,128)(2,1)S(1)} %collective-permute-done.1.above, ...), custom_call_target="tpu_custom_call" | custom-call | bytes 2621472 | tf_op jit(solution)/shard_map/pallas_call | solution.py:214
  40.3 9.7 %all-to-all-start.1 = ((bf16[16,8,1152]{2,1,0:T(8,128)(2,1)}), bf16[16,8,1152]{2,1,0:T(8,128)(2,1)S(1)}, u32[]{:S(2)}, u32[]{:S(2)}) async-start(bf16[16,8,1152]{2,1,0:T(8,128)(2,1)} %shard_map.87), calls=%async_computation.1 | async-start | bytes 589824 | tf_op jit(solution)/shard_map/all_to_all | solution.py:28
  50.1 2.6 %collective-permute-start.4 = (bf16[4,128,256]{2,1,0:T(8,128)(2,1)S(1)}, bf16[4,128,256]{2,1,0:T(8,128)(2,1)S(1)}, u32[]{:S(2)}, u32[]{:S(2)}) collective-permute-start(bf16[4,128,256]{2,1,0:T(8,128)(2,1)S(1)} %pad_maximum_fusion), channel_id=1, source_target_pairs={{0,12},{4,0},{8,4},{12,8},{1,13},{5,1},{9,5},{13,9},{2,14},{6,2},{... | collective-permute-start | bytes 786440 | tf_op jit(solution)/shard_map/ppermute | solution.py:36
  52.8 2.2 %collective-permute-start.5 = (bf16[4,128,256]{2,1,0:T(8,128)(2,1)S(1)}, bf16[4,128,256]{2,1,0:T(8,128)(2,1)S(1)}, u32[]{:S(2)}, u32[]{:S(2)}) collective-permute-start(bf16[4,128,256]{2,1,0:T(8,128)(2,1)S(1)} %pad_maximum_fusion), channel_id=1, source_target_pairs={{0,8},{4,12},{8,0},{12,4},{1,9},{5,13},{9,1},{13,5},{2,10},{6,14},... | collective-permute-start | bytes 786440 | tf_op jit(solution)/shard_map/ppermute | solution.py:36
  55.0 2.5 %collective-permute-start.6 = (bf16[4,128,256]{2,1,0:T(8,128)(2,1)S(1)}, bf16[4,128,256]{2,1,0:T(8,128)(2,1)S(1)}, u32[]{:S(2)}, u32[]{:S(2)}) collective-permute-start(bf16[4,128,256]{2,1,0:T(8,128)(2,1)S(1)} %pad_maximum_fusion), channel_id=1, source_target_pairs={{0,4},{4,8},{8,12},{12,0},{1,5},{5,9},{9,13},{13,1},{2,6},{6,10},{... | collective-permute-start | bytes 786440 | tf_op jit(solution)/shard_map/ppermute | solution.py:36
  57.6 5.6 %all-to-all-done.1.line = bf16[16,8,1152]{2,1,0:T(8,128)(2,1)S(1)} async-done(((bf16[16,8,1152]{2,1,0:T(8,128)(2,1)}), bf16[16,8,1152]{2,1,0:T(8,128)(2,1)S(1)}, u32[]{:S(2)}, u32[]{:S(2)}) %all-to-all-start.1) | async-done | bytes 294944 | tf_op jit(solution)/shard_map/all_to_all | solution.py:28
  63.1 0.9 %shard_map.88 = bf16[32,8,1152]{2,1,0:T(8,128)(2,1)} custom-call(bf16[16,8,1152]{2,1,0:T(8,128)(2,1)S(1)} %all-to-all-done.1.line), custom_call_target="tpu_custom_call" | custom-call | bytes 589824 | tf_op jit(solution)/shard_map/pallas_call | solution.py:214
  64.1 12.0 %all-to-all-start.2 = ((bf16[32,8,1152]{2,1,0:T(8,128)(2,1)}), bf16[32,8,1152]{2,1,0:T(8,128)(2,1)S(1)}, u32[]{:S(2)}, u32[]{:S(2)}) async-start(bf16[32,8,1152]{2,1,0:T(8,128)(2,1)} %shard_map.88), calls=%async_computation.2 | async-start | bytes 1179648 | tf_op jit(solution)/shard_map/all_to_all | solution.py:28
  76.2 2.1 %collective-permute-start.8 = (bf16[8,128,256]{2,1,0:T(8,128)(2,1)S(1)}, bf16[8,128,256]{2,1,0:T(8,128)(2,1)S(1)}, u32[]{:S(2)}, u32[]{:S(2)}) collective-permute-start(bf16[8,128,256]{2,1,0:T(8,128)(2,1)S(1)} %constant_dynamic-update-slice_fusion.5.rest_1_), channel_id=1, source_target_pairs={{0,16},{16,0},{1,17},{17,1},{2,18},{18,2},{3,19},{19,3},{4,20},{20... | collective-permute-start | bytes 1572872 | tf_op jit(solution)/shard_map/ppermute | solution.py:32
  78.3 2.2 %collective-permute-start.7 = (bf16[8,128,256]{2,1,0:T(8,128)(2,1)S(1)}, bf16[8,128,256]{2,1,0:T(8,128)(2,1)S(1)}, u32[]{:S(2)}, u32[]{:S(2)}) collective-permute-start(bf16[8,128,256]{2,1,0:T(8,128)(2,1)S(1)} %constant_dynamic-update-slice_fusion.rest_0_), channel_id=1, source_target_pairs={{0,16},{16,0},{1,17},{17,1},{2,18},{18,2},{3,19},{19,3},{4,20},{20... | collective-permute-start | bytes 1572872 | tf_op jit(solution)/shard_map/ppermute | solution.py:32
  80.5 1.6 %collective-permute-done.7.rest_2_ = bf16[8,128,256]{2,1,0:T(8,128)(2,1)S(1)} collective-permute-done((bf16[8,128,256]{2,1,0:T(8,128)(2,1)S(1)}, bf16[8,128,256]{2,1,0:T(8,128)(2,1)S(1)}, u32[]{:S(2)}, u32[]{:S(2)}) %collective-permute-start.7) | collective-permute-done | bytes 524320 | tf_op jit(solution)/shard_map/ppermute | solution.py:32
  82.2 4.0 %shard_map.89 = (bf16[192,512]{1,0:T(8,128)(2,1)}, bf16[192,2048]{1,0:T(8,128)(2,1)}) custom-call(s32[4]{0:T(128)S(1)} %pad_add_fusion.place, bf16[192,2048]{1,0:T(8,128)(2,1)S(1)} %copy-done.1, f32[192,128]{1,0:T(8,128)S(1)} %get-tuple-element.26.inv_rms, f32[1,2048]{1,0:T(1,128)S(1)} %bitcast.21, bf16[192,512]{1,0:T(8,128)(2,1)S(1)} %copy-done.3, ...), custom_call_target="tpu_custom_call" | custom-call | bytes 6373408 | tf_op jit(solution)/shard_map/pallas_call | solution.py:214
  86.1 2.2 %all-to-all-done.2.blocks = bf16[32,8,1152]{2,1,0:T(8,128)(2,1)S(1)} async-done(((bf16[32,8,1152]{2,1,0:T(8,128)(2,1)}), bf16[32,8,1152]{2,1,0:T(8,128)(2,1)S(1)}, u32[]{:S(2)}, u32[]{:S(2)}) %all-to-all-start.2) | async-done | bytes 589856 | tf_op jit(solution)/shard_map/all_to_all | solution.py:28
  88.4 1.4 %shard_map.90 = (f32[128,512]{1,0:T(8,128)}, f32[16,128]{1,0:T(8,128)}) custom-call(s32[4]{0:T(128)S(1)} %pad_add_fusion.place, bf16[32,8,1152]{2,1,0:T(8,128)(2,1)S(1)} %all-to-all-done.2.blocks, f32[16,128]{1,0:T(8,128)S(1)} %bitcast.22), custom_call_target="tpu_custom_call" | custom-call | bytes 1196064 | tf_op jit(solution)/shard_map/pallas_call | solution.py:214
  (29 shorter events, 0.8 us)
Async XLA Ops:
  0.6 18.7 %copy-start = (f32[1,512]{1,0:T(1,128)S(1)}, f32[1,512]{1,0:T(1,128)}, u32[]{:S(2)}) copy-start(f32[1,512]{1,0:T(1,128)} %param.8) | copy-start | bytes 6148
  3.4 11.1 %collective-permute-start = (bf16[16,16,2048]{2,1,0:T(8,128)(2,1)S(1)}, bf16[16,16,2048]{2,1,0:T(8,128)(2,1)S(1)}, u32[]{:S(2)}, u32[]{:S(2)}) collective-permute-start(bf16[16,16,2048]{2,1,0:T(8,128)(2,1)S(1)} %get-tuple-element.22), channel_id=1, source_target_pairs={{0,16},{16,0},{1,17},{17,1},{2,18},{18,2},{3,19},{19,3},{4,20},{20... | collective-permute-start | bytes 3145736 | tf_op jit(solution)/shard_map/ppermute | solution.py:32
  12.2 0.9 %copy-start.2 = (bf16[192,512]{1,0:T(8,128)(2,1)S(1)}, bf16[192,512]{1,0:T(8,128)(2,1)}, u32[]{:S(2)}) copy-start(bf16[192,512]{1,0:T(8,128)(2,1)} %key_grad.3) | copy-start | bytes 589828
  15.5 3.9 %copy-start.5 = (s32[128,512]{1,0:T(8,128)S(1)}, s32[128,512]{1,0:T(8,128)}, u32[]{:S(2)}) copy-start(s32[128,512]{1,0:T(8,128)} %param.7) | copy-start | bytes 786436
  15.6 23.1 %all-to-all-start = ((bf16[16,16,2048]{2,1,0:T(8,128)(2,1)}), bf16[16,16,2048]{2,1,0:T(8,128)(2,1)S(1)}, u32[]{:S(2)}, u32[]{:S(2)}) async-start(bf16[16,16,2048]{2,1,0:T(8,128)(2,1)} %shard_map.86), calls=%async_computation | async-start | bytes 2097152 | tf_op jit(solution)/shard_map/all_to_all | solution.py:28
  19.4 14.6 %collective-permute-start.1 = (bf16[128,256]{1,0:T(8,128)(2,1)S(1)}, bf16[128,256]{1,0:T(8,128)(2,1)S(1)}, u32[]{:S(2)}, u32[]{:S(2)}) collective-permute-start(bf16[128,256]{1,0:T(8,128)(2,1)S(1)} %get-tuple-element.23.shard), channel_id=1, source_target_pairs={{0,387},{16,403},{32,419},{48,435},{64,451},{80,467},{96,483},{112... | collective-permute-start | bytes 196616 | tf_op jit(solution)/shard_map/ppermute | solution.py:48
  28.3 6.0 %collective-permute-start.2 = (bf16[128,256]{1,0:T(8,128)(2,1)S(1)}, bf16[128,256]{1,0:T(8,128)(2,1)S(1)}, u32[]{:S(2)}, u32[]{:S(2)}) collective-permute-start(bf16[128,256]{1,0:T(8,128)(2,1)S(1)} %get-tuple-element.23.shard), channel_id=1, source_target_pairs={{0,2},{16,402},{32,34},{48,434},{64,66},{80,466},{96,98},{112,498}... | collective-permute-start | bytes 196616 | tf_op jit(solution)/shard_map/ppermute | solution.py:48
  31.4 7.3 %collective-permute-start.3 = (bf16[128,256]{1,0:T(8,128)(2,1)S(1)}, bf16[128,256]{1,0:T(8,128)(2,1)S(1)}, u32[]{:S(2)}, u32[]{:S(2)}) collective-permute-start(bf16[128,256]{1,0:T(8,128)(2,1)S(1)} %get-tuple-element.23.shard), channel_id=1, source_target_pairs={{0,1},{16,17},{32,33},{48,49},{64,65},{80,81},{96,97},{112,113},{1... | collective-permute-start | bytes 196616 | tf_op jit(solution)/shard_map/ppermute | solution.py:48
  40.3 22.8 %all-to-all-start.1 = ((bf16[16,8,1152]{2,1,0:T(8,128)(2,1)}), bf16[16,8,1152]{2,1,0:T(8,128)(2,1)S(1)}, u32[]{:S(2)}, u32[]{:S(2)}) async-start(bf16[16,8,1152]{2,1,0:T(8,128)(2,1)} %shard_map.87), calls=%async_computation.1 | async-start | bytes 589824 | tf_op jit(solution)/shard_map/all_to_all | solution.py:28
  50.1 32.1 %copy-start.1 = (bf16[192,2048]{1,0:T(8,128)(2,1)S(1)}, bf16[192,2048]{1,0:T(8,128)(2,1)}, u32[]{:S(2)}) copy-start(bf16[192,2048]{1,0:T(8,128)(2,1)} %tokens.1) | copy-start | bytes 2359300
  50.1 32.0 %copy-start.3 = (bf16[192,512]{1,0:T(8,128)(2,1)S(1)}, bf16[192,512]{1,0:T(8,128)(2,1)}, u32[]{:S(2)}) copy-start(bf16[192,512]{1,0:T(8,128)(2,1)} %key_grad.3) | copy-start | bytes 589828
  50.1 32.0 %copy-start.4 = (f32[2048]{0:T(1024)S(1)}, f32[2048]{0:T(1024)}, u32[]{:S(2)}) copy-start(f32[2048]{0:T(1024)} %param.6) | copy-start | bytes 24580
  50.1 7.4 %collective-permute-start.4 = (bf16[4,128,256]{2,1,0:T(8,128)(2,1)S(1)}, bf16[4,128,256]{2,1,0:T(8,128)(2,1)S(1)}, u32[]{:S(2)}, u32[]{:S(2)}) collective-permute-start(bf16[4,128,256]{2,1,0:T(8,128)(2,1)S(1)} %pad_maximum_fusion), channel_id=1, source_target_pairs={{0,12},{4,0},{8,4},{12,8},{1,13},{5,1},{9,5},{13,9},{2,14},{6,2},{... | collective-permute-start | bytes 786440 | tf_op jit(solution)/shard_map/ppermute | solution.py:36
  52.8 23.3 %collective-permute-start.5 = (bf16[4,128,256]{2,1,0:T(8,128)(2,1)S(1)}, bf16[4,128,256]{2,1,0:T(8,128)(2,1)S(1)}, u32[]{:S(2)}, u32[]{:S(2)}) collective-permute-start(bf16[4,128,256]{2,1,0:T(8,128)(2,1)S(1)} %pad_maximum_fusion), channel_id=1, source_target_pairs={{0,8},{4,12},{8,0},{12,4},{1,9},{5,13},{9,1},{13,5},{2,10},{6,14},... | collective-permute-start | bytes 786440 | tf_op jit(solution)/shard_map/ppermute | solution.py:36
  55.0 21.1 %collective-permute-start.6 = (bf16[4,128,256]{2,1,0:T(8,128)(2,1)S(1)}, bf16[4,128,256]{2,1,0:T(8,128)(2,1)S(1)}, u32[]{:S(2)}, u32[]{:S(2)}) collective-permute-start(bf16[4,128,256]{2,1,0:T(8,128)(2,1)S(1)} %pad_maximum_fusion), channel_id=1, source_target_pairs={{0,4},{4,8},{8,12},{12,0},{1,5},{5,9},{9,13},{13,1},{2,6},{6,10},{... | collective-permute-start | bytes 786440 | tf_op jit(solution)/shard_map/ppermute | solution.py:36
  64.1 24.3 %all-to-all-start.2 = ((bf16[32,8,1152]{2,1,0:T(8,128)(2,1)}), bf16[32,8,1152]{2,1,0:T(8,128)(2,1)S(1)}, u32[]{:S(2)}, u32[]{:S(2)}) async-start(bf16[32,8,1152]{2,1,0:T(8,128)(2,1)} %shard_map.88), calls=%async_computation.2 | async-start | bytes 1179648 | tf_op jit(solution)/shard_map/all_to_all | solution.py:28
  76.2 4.3 %collective-permute-start.8 = (bf16[8,128,256]{2,1,0:T(8,128)(2,1)S(1)}, bf16[8,128,256]{2,1,0:T(8,128)(2,1)S(1)}, u32[]{:S(2)}, u32[]{:S(2)}) collective-permute-start(bf16[8,128,256]{2,1,0:T(8,128)(2,1)S(1)} %constant_dynamic-update-slice_fusion.5.rest_1_), channel_id=1, source_target_pairs={{0,16},{16,0},{1,17},{17,1},{2,18},{18,2},{3,19},{19,3},{4,20},{20... | collective-permute-start | bytes 1572872 | tf_op jit(solution)/shard_map/ppermute | solution.py:32
  78.3 3.8 %collective-permute-start.7 = (bf16[8,128,256]{2,1,0:T(8,128)(2,1)S(1)}, bf16[8,128,256]{2,1,0:T(8,128)(2,1)S(1)}, u32[]{:S(2)}, u32[]{:S(2)}) collective-permute-start(bf16[8,128,256]{2,1,0:T(8,128)(2,1)S(1)} %constant_dynamic-update-slice_fusion.rest_0_), channel_id=1, source_target_pairs={{0,16},{16,0},{1,17},{17,1},{2,18},{18,2},{3,19},{19,3},{4,20},{20... | collective-permute-start | bytes 1572872 | tf_op jit(solution)/shard_map/ppermute | solution.py:32

commit v11 on v10

--- a/solution.py
+++ b/solution.py
@@ -137,7 +137,7 @@
         for k in range(4):
             held[target, :, k * HALF : (k + 1) * HALF] = shards[target, k * 8 : k * 8 + 8].astype(bf16)
         held[target, :, 4 * HALF :] = gains
-    for copy in copy_out([(held, out.at[zh * 4 : zh * 4 + 4]) for zh in range(4)], sem):
+    for copy in copy_out([(held.at[z // 4], out.at[z]) for z in range(16)], sem):
         copy.wait()
 
 
@@ -158,13 +158,14 @@
     y = place[2]
     for x in range(4):
         for core in range(2):
-            block = blocks[y * 8 + x * 2 + core].astype(f32) / DEVICES
+            block = blocks[x * 8 + core * 4 + y].astype(f32) / DEVICES
             for k in range(4):
                 at = x * 32 + k * 8
                 weight_grad[at : at + 8, core * HALF : (core + 1) * HALF] = block[:, k * HALF : (k + 1) * HALF]
     rows_of = []
     for peer in range(16):
-        gains = blocks[peer * 2, :, 4 * HALF :].astype(f32) + blocks[peer * 2 + 1, :, 4 * HALF :].astype(f32)
+        first = peer % 4 * 8 + peer // 4
+        gains = blocks[first, :, 4 * HALF :].astype(f32) + blocks[first + 4, :, 4 * HALF :].astype(f32)
         rows_of.append(gains[0:1] + gains[1:2])
     sums = jnp.concatenate(rows_of, axis=0)
     lane = lax.broadcasted_iota(jnp.int32, (16, 128), 1)
@@ -271,11 +272,11 @@
             pltpu.VMEM((4, 32, HALF), f32),
             pltpu.VMEM((4, 32, HALF), f32),
             pltpu.VMEM((4, 8, 1152), bf16),
-            pltpu.SemaphoreType.DMA((4,)),
+            pltpu.SemaphoreType.DMA((16,)),
         ],
         out_specs=[ANY],
     )
-    line = exchange(payload, ("zh", "zl"))
+    line = exchange(payload, ("zl", "zh"))
     stack_late, _ = lax.optimization_barrier((stack, payload))
     one, two, three = (along_y(stack_late, -step) for step in (1, 2, 3))
     near = jnp.concatenate([stack, one], axis=0)
@@ -291,7 +292,7 @@
     near_late, two, three, _ = lax.optimization_barrier((near, two, three, blocks))
     far = jnp.concatenate([two, three], axis=0)
     pieces = (near, far, swap(near_late), swap(far))
-    blocks = exchange(blocks, ("y", "x", "core"))
+    blocks = exchange(blocks, ("x", "core", "y"))
     keys, tokens_grad = call(
         token_kernel,
         [((192, 512), bf16), ((192, 2048), bf16)],

time: 90.4 us -> 91.1 us (level)
  the two profiles are of different devices: /device:TPU:1 before, /device:TPU:32 now
where the time goes in v11:
time: 91.1 us; the launch traced here: 90.4 us
  starting transfers between devices  54.9 us (60%)
  waiting for transfers between devices  20.6 us (23%)
  Pallas kernels  12.8 us (14%)
  local copies, waits for them, and re-layouts  1.04 us (1%)
  between operations  0.93 us (1%)
    all_to_all x3, starting transfers between devices, exchange(): return lax.all_to_all(blocks, axes, 0, 0, tiled=False)  28 us
    pallas_call x7, Pallas kernels, call(): pl.pallas_call(kernel, out_shape=[jax.ShapeDtypeStruct(s, d) for s, d in...  12.8 us
    ppermute x3, starting transfers between devices, along_z(): return lax.ppermute(block, ('zh', 'x', 'core', 'zl'), pairs)  12.2 us
    all_to_all x3, waiting for transfers between devices, exchange(): return lax.all_to_all(blocks, axes, 0, 0, tiled=False)  10.5 us
    ppermute x3, starting transfers between devices, along_y(): return lax.ppermute(block, 'y', [(y, (y + step) % 4) for y in range(4)])  8.39 us
    ppermute x3, starting transfers between devices, swap(): return lax.ppermute(block, 'core', [(0, 1), (1, 0)])  6.25 us
    ppermute x3, waiting for transfers between devices, along_z(): return lax.ppermute(block, ('zh', 'x', 'core', 'zl'), pairs)  5.33 us
    ppermute x3, waiting for transfers between devices, along_y(): return lax.ppermute(block, 'y', [(y, (y + step) % 4) for y in range(4)])  2.44 us
  transfers between devices with their start and end apart: 12, of which 8 were waited for; matrix products, arithmetic and copies ran while one was open for 0% of the time, Pallas kernels for 7%

profile of v11, /device:TPU:32, one launch (start us, length us, event | category | flops | bytes accessed | tf_op | source)
XLA Modules:
  0.0 90.4 jit_solution(12088155331688407952)
XLA Ops:
  0.7 2.6 %shard_map.84 = (bf16[192,2048]{1,0:T(8,128)(2,1)S(1)}, f32[192,128]{1,0:T(8,128)S(1)}, bf16[16,16,2048]{2,1,0:T(8,128)(2,1)S(1)}) custom-call(s32[4]{0:T(128)S(1)} %pad_add_fusion.place, bf16[192,2048]{1,0:T(8,128)(2,1)} %tokens.1, f32[1,2048]{1,0:T(1,128)} %bitcast.20, bf16[192,512]{1,0:T(8,128)(2,1)} %key_grad.3), custom_call_target="tpu_custom_call" | custom-call | flops 201326592 | bytes 1982496 | tf_op jit(solution)/shard_map/pallas_call | solution.py:215
  3.4 1.9 %collective-permute-start = (bf16[16,16,2048]{2,1,0:T(8,128)(2,1)S(1)}, bf16[16,16,2048]{2,1,0:T(8,128)(2,1)S(1)}, u32[]{:S(2)}, u32[]{:S(2)}) collective-permute-start(bf16[16,16,2048]{2,1,0:T(8,128)(2,1)S(1)} %get-tuple-element.22), channel_id=1, source_target_pairs={{0,16},{16,0},{1,17},{17,1},{2,18},{18,2},{3,19},{19,3},{4,20},{20... | collective-permute-start | bytes 3145736 | tf_op jit(solution)/shard_map/ppermute | solution.py:32
  6.2 1.0 %shard_map.85.mine = f32[16,16,2048]{2,1,0:T(8,128)S(1)} custom-call(s32[4]{0:T(128)S(1)} %pad_add_fusion.place, bf16[192,2048]{1,0:T(8,128)(2,1)S(1)} %get-tuple-element.21.normed, bf16[192,512]{1,0:T(8,128)(2,1)S(1)} %copy-done.2), custom_call_target="tpu_custom_call" | custom-call | flops 201326592 | bytes 1966112 | tf_op jit(solution)/shard_map/pallas_call | solution.py:215
  7.9 1.1 %shard_map.86 = bf16[16,16,2048]{2,1,0:T(8,128)(2,1)} custom-call(f32[16,16,2048]{2,1,0:T(8,128)S(1)} %shard_map.85.mine, bf16[16,16,2048]{2,1,0:T(8,128)(2,1)S(1)} %collective-permute-done.got), custom_call_target="tpu_custom_call" | custom-call | bytes 6291456 | tf_op jit(solution)/shard_map/pallas_call | solution.py:215
  9.1 7.2 %all-to-all-start = ((bf16[16,16,2048]{2,1,0:T(8,128)(2,1)}), bf16[16,16,2048]{2,1,0:T(8,128)(2,1)S(1)}, u32[]{:S(2)}, u32[]{:S(2)}) async-start(bf16[16,16,2048]{2,1,0:T(8,128)(2,1)} %shard_map.86), calls=%async_computation | async-start | bytes 2097152 | tf_op jit(solution)/shard_map/all_to_all | solution.py:28
  16.3 4.0 %collective-permute-start.1 = (bf16[128,256]{1,0:T(8,128)(2,1)S(1)}, bf16[128,256]{1,0:T(8,128)(2,1)S(1)}, u32[]{:S(2)}, u32[]{:S(2)}) collective-permute-start(bf16[128,256]{1,0:T(8,128)(2,1)S(1)} %get-tuple-element.23.shard), channel_id=1, source_target_pairs={{0,387},{16,403},{32,419},{48,435},{64,451},{80,467},{96,483},{112... | collective-permute-start | bytes 196616 | tf_op jit(solution)/shard_map/ppermute | solution.py:48
  20.3 3.2 %collective-permute-start.2 = (bf16[128,256]{1,0:T(8,128)(2,1)S(1)}, bf16[128,256]{1,0:T(8,128)(2,1)S(1)}, u32[]{:S(2)}, u32[]{:S(2)}) collective-permute-start(bf16[128,256]{1,0:T(8,128)(2,1)S(1)} %get-tuple-element.23.shard), channel_id=1, source_target_pairs={{0,2},{16,402},{32,34},{48,434},{64,66},{80,466},{96,98},{112,498}... | collective-permute-start | bytes 196616 | tf_op jit(solution)/shard_map/ppermute | solution.py:48
  23.5 5.0 %collective-permute-start.3 = (bf16[128,256]{1,0:T(8,128)(2,1)S(1)}, bf16[128,256]{1,0:T(8,128)(2,1)S(1)}, u32[]{:S(2)}, u32[]{:S(2)}) collective-permute-start(bf16[128,256]{1,0:T(8,128)(2,1)S(1)} %get-tuple-element.23.shard), channel_id=1, source_target_pairs={{0,1},{16,17},{32,33},{48,49},{64,65},{80,81},{96,97},{112,113},{1... | collective-permute-start | bytes 196616 | tf_op jit(solution)/shard_map/ppermute | solution.py:48
  28.6 3.9 %collective-permute-done.2.across = bf16[128,256]{1,0:T(8,128)(2,1)S(1)} collective-permute-done((bf16[128,256]{1,0:T(8,128)(2,1)S(1)}, bf16[128,256]{1,0:T(8,128)(2,1)S(1)}, u32[]{:S(2)}, u32[]{:S(2)}) %collective-permute-start.2) | collective-permute-done | bytes 65568 | tf_op jit(solution)/shard_map/ppermute | solution.py:48
  32.5 1.4 %collective-permute-done.3.below = bf16[128,256]{1,0:T(8,128)(2,1)S(1)} collective-permute-done((bf16[128,256]{1,0:T(8,128)(2,1)S(1)}, bf16[128,256]{1,0:T(8,128)(2,1)S(1)}, u32[]{:S(2)}, u32[]{:S(2)}) %collective-permute-start.3) | collective-permute-done | bytes 65568 | tf_op jit(solution)/shard_map/ppermute | solution.py:48
  34.0 1.8 %shard_map.87 = bf16[16,8,1152]{2,1,0:T(8,128)(2,1)} custom-call(s32[4]{0:T(128)S(1)} %pad_add_fusion.place, bf16[16,16,2048]{2,1,0:T(8,128)(2,1)S(1)} %all-to-all-done.square, bf16[128,256]{1,0:T(8,128)(2,1)S(1)} %get-tuple-element.23.shard, bf16[128,256]{1,0:T(8,128)(2,1)S(1)} %collective-permute-done.1.above, ...), custom_call_target="tpu_custom_call" | custom-call | bytes 2621472 | tf_op jit(solution)/shard_map/pallas_call | solution.py:215
  35.8 15.2 %all-to-all-start.1 = ((bf16[16,8,1152]{2,1,0:T(8,128)(2,1)}), bf16[16,8,1152]{2,1,0:T(8,128)(2,1)S(1)}, u32[]{:S(2)}, u32[]{:S(2)}) async-start(bf16[16,8,1152]{2,1,0:T(8,128)(2,1)} %shard_map.87), calls=%async_computation.1 | async-start | bytes 589824 | tf_op jit(solution)/shard_map/all_to_all | solution.py:28
  51.1 2.5 %collective-permute-start.4 = (bf16[4,128,256]{2,1,0:T(8,128)(2,1)S(1)}, bf16[4,128,256]{2,1,0:T(8,128)(2,1)S(1)}, u32[]{:S(2)}, u32[]{:S(2)}) collective-permute-start(bf16[4,128,256]{2,1,0:T(8,128)(2,1)S(1)} %pad_maximum_fusion), channel_id=1, source_target_pairs={{0,12},{4,0},{8,4},{12,8},{1,13},{5,1},{9,5},{13,9},{2,14},{6,2},{... | collective-permute-start | bytes 786440 | tf_op jit(solution)/shard_map/ppermute | solution.py:36
  53.7 2.5 %collective-permute-start.5 = (bf16[4,128,256]{2,1,0:T(8,128)(2,1)S(1)}, bf16[4,128,256]{2,1,0:T(8,128)(2,1)S(1)}, u32[]{:S(2)}, u32[]{:S(2)}) collective-permute-start(bf16[4,128,256]{2,1,0:T(8,128)(2,1)S(1)} %pad_maximum_fusion), channel_id=1, source_target_pairs={{0,8},{4,12},{8,0},{12,4},{1,9},{5,13},{9,1},{13,5},{2,10},{6,14},... | collective-permute-start | bytes 786440 | tf_op jit(solution)/shard_map/ppermute | solution.py:36
  56.2 3.3 %collective-permute-start.6 = (bf16[4,128,256]{2,1,0:T(8,128)(2,1)S(1)}, bf16[4,128,256]{2,1,0:T(8,128)(2,1)S(1)}, u32[]{:S(2)}, u32[]{:S(2)}) collective-permute-start(bf16[4,128,256]{2,1,0:T(8,128)(2,1)S(1)} %pad_maximum_fusion), channel_id=1, source_target_pairs={{0,4},{4,8},{8,12},{12,0},{1,5},{5,9},{9,13},{13,1},{2,6},{6,10},{... | collective-permute-start | bytes 786440 | tf_op jit(solution)/shard_map/ppermute | solution.py:36
  59.6 2.4 %collective-permute-done.4 = bf16[4,128,256]{2,1,0:T(8,128)(2,1)S(1)} collective-permute-done((bf16[4,128,256]{2,1,0:T(8,128)(2,1)S(1)}, bf16[4,128,256]{2,1,0:T(8,128)(2,1)S(1)}, u32[]{:S(2)}, u32[]{:S(2)}) %collective-permute-start.4) | collective-permute-done | bytes 262176 | tf_op jit(solution)/shard_map/ppermute | solution.py:36
  62.0 8.0 %all-to-all-done.1.line = bf16[16,8,1152]{2,1,0:T(8,128)(2,1)S(1)} async-done(((bf16[16,8,1152]{2,1,0:T(8,128)(2,1)}), bf16[16,8,1152]{2,1,0:T(8,128)(2,1)S(1)}, u32[]{:S(2)}, u32[]{:S(2)}) %all-to-all-start.1) | async-done | bytes 294944 | tf_op jit(solution)/shard_map/all_to_all | solution.py:28
  71.0 5.6 %all-to-all-start.2 = ((bf16[32,8,1152]{2,1,0:T(8,128)(2,1)}), bf16[32,8,1152]{2,1,0:T(8,128)(2,1)S(1)}, u32[]{:S(2)}, u32[]{:S(2)}) async-start(bf16[32,8,1152]{2,1,0:T(8,128)(2,1)} %shard_map.88), calls=%async_computation.2 | async-start | bytes 1179648 | tf_op jit(solution)/shard_map/all_to_all | solution.py:28
  76.7 2.2 %collective-permute-start.8 = (bf16[8,128,256]{2,1,0:T(8,128)(2,1)S(1)}, bf16[8,128,256]{2,1,0:T(8,128)(2,1)S(1)}, u32[]{:S(2)}, u32[]{:S(2)}) collective-permute-start(bf16[8,128,256]{2,1,0:T(8,128)(2,1)S(1)} %constant_dynamic-update-slice_fusion.5.rest_1_), channel_id=1, source_target_pairs={{0,16},{16,0},{1,17},{17,1},{2,18},{18,2},{3,19},{19,3},{4,20},{20... | collective-permute-start | bytes 1572872 | tf_op jit(solution)/shard_map/ppermute | solution.py:32
  78.9 2.1 %collective-permute-start.7 = (bf16[8,128,256]{2,1,0:T(8,128)(2,1)S(1)}, bf16[8,128,256]{2,1,0:T(8,128)(2,1)S(1)}, u32[]{:S(2)}, u32[]{:S(2)}) collective-permute-start(bf16[8,128,256]{2,1,0:T(8,128)(2,1)S(1)} %constant_dynamic-update-slice_fusion.rest_0_), channel_id=1, source_target_pairs={{0,16},{16,0},{1,17},{17,1},{2,18},{18,2},{3,19},{19,3},{4,20},{20... | collective-permute-start | bytes 1572872 | tf_op jit(solution)/shard_map/ppermute | solution.py:32
  81.1 1.6 %collective-permute-done.7.rest_2_ = bf16[8,128,256]{2,1,0:T(8,128)(2,1)S(1)} collective-permute-done((bf16[8,128,256]{2,1,0:T(8,128)(2,1)S(1)}, bf16[8,128,256]{2,1,0:T(8,128)(2,1)S(1)}, u32[]{:S(2)}, u32[]{:S(2)}) %collective-permute-start.7) | collective-permute-done | bytes 524320 | tf_op jit(solution)/shard_map/ppermute | solution.py:32
  82.7 4.0 %shard_map.89 = (bf16[192,512]{1,0:T(8,128)(2,1)}, bf16[192,2048]{1,0:T(8,128)(2,1)}) custom-call(s32[4]{0:T(128)S(1)} %pad_add_fusion.place, bf16[192,2048]{1,0:T(8,128)(2,1)S(1)} %copy-done.1, f32[192,128]{1,0:T(8,128)S(1)} %get-tuple-element.26.inv_rms, f32[1,2048]{1,0:T(1,128)S(1)} %bitcast.21, bf16[192,512]{1,0:T(8,128)(2,1)S(1)} %copy-done.3, ...), custom_call_target="tpu_custom_call" | custom-call | bytes 6373408 | tf_op jit(solution)/shard_map/pallas_call | solution.py:215
  86.7 2.4 %all-to-all-done.2.blocks = bf16[32,8,1152]{2,1,0:T(8,128)(2,1)S(1)} async-done(((bf16[32,8,1152]{2,1,0:T(8,128)(2,1)}), bf16[32,8,1152]{2,1,0:T(8,128)(2,1)S(1)}, u32[]{:S(2)}, u32[]{:S(2)}) %all-to-all-start.2) | async-done | bytes 589856 | tf_op jit(solution)/shard_map/all_to_all | solution.py:28
  89.1 1.4 %shard_map.90 = (f32[128,512]{1,0:T(8,128)}, f32[16,128]{1,0:T(8,128)}) custom-call(s32[4]{0:T(128)S(1)} %pad_add_fusion.place, bf16[32,8,1152]{2,1,0:T(8,128)(2,1)S(1)} %all-to-all-done.2.blocks, f32[16,128]{1,0:T(8,128)S(1)} %bitcast.22), custom_call_target="tpu_custom_call" | custom-call | bytes 1196064 | tf_op jit(solution)/shard_map/pallas_call | solution.py:215
  (29 shorter events, 2.9 us)
Async XLA Ops:
  0.6 15.6 %copy-start = (f32[1,512]{1,0:T(1,128)S(1)}, f32[1,512]{1,0:T(1,128)}, u32[]{:S(2)}) copy-start(f32[1,512]{1,0:T(1,128)} %param.8) | copy-start | bytes 6148
  3.4 4.6 %collective-permute-start = (bf16[16,16,2048]{2,1,0:T(8,128)(2,1)S(1)}, bf16[16,16,2048]{2,1,0:T(8,128)(2,1)S(1)}, u32[]{:S(2)}, u32[]{:S(2)}) collective-permute-start(bf16[16,16,2048]{2,1,0:T(8,128)(2,1)S(1)} %get-tuple-element.22), channel_id=1, source_target_pairs={{0,16},{16,0},{1,17},{17,1},{2,18},{18,2},{3,19},{19,3},{4,20},{20... | collective-permute-start | bytes 3145736 | tf_op jit(solution)/shard_map/ppermute | solution.py:32
  5.3 0.9 %copy-start.2 = (bf16[192,512]{1,0:T(8,128)(2,1)S(1)}, bf16[192,512]{1,0:T(8,128)(2,1)}, u32[]{:S(2)}) copy-start(bf16[192,512]{1,0:T(8,128)(2,1)} %key_grad.3) | copy-start | bytes 589828
  9.0 7.2 %copy-start.5 = (s32[128,512]{1,0:T(8,128)S(1)}, s32[128,512]{1,0:T(8,128)}, u32[]{:S(2)}) copy-start(s32[128,512]{1,0:T(8,128)} %param.7) | copy-start | bytes 786436
  9.1 25.0 %all-to-all-start = ((bf16[16,16,2048]{2,1,0:T(8,128)(2,1)}), bf16[16,16,2048]{2,1,0:T(8,128)(2,1)S(1)}, u32[]{:S(2)}, u32[]{:S(2)}) async-start(bf16[16,16,2048]{2,1,0:T(8,128)(2,1)} %shard_map.86), calls=%async_computation | async-start | bytes 2097152 | tf_op jit(solution)/shard_map/all_to_all | solution.py:28
  16.3 12.3 %collective-permute-start.1 = (bf16[128,256]{1,0:T(8,128)(2,1)S(1)}, bf16[128,256]{1,0:T(8,128)(2,1)S(1)}, u32[]{:S(2)}, u32[]{:S(2)}) collective-permute-start(bf16[128,256]{1,0:T(8,128)(2,1)S(1)} %get-tuple-element.23.shard), channel_id=1, source_target_pairs={{0,387},{16,403},{32,419},{48,435},{64,451},{80,467},{96,483},{112... | collective-permute-start | bytes 196616 | tf_op jit(solution)/shard_map/ppermute | solution.py:48
  20.3 12.2 %collective-permute-start.2 = (bf16[128,256]{1,0:T(8,128)(2,1)S(1)}, bf16[128,256]{1,0:T(8,128)(2,1)S(1)}, u32[]{:S(2)}, u32[]{:S(2)}) collective-permute-start(bf16[128,256]{1,0:T(8,128)(2,1)S(1)} %get-tuple-element.23.shard), channel_id=1, source_target_pairs={{0,2},{16,402},{32,34},{48,434},{64,66},{80,466},{96,98},{112,498}... | collective-permute-start | bytes 196616 | tf_op jit(solution)/shard_map/ppermute | solution.py:48
  23.5 10.4 %collective-permute-start.3 = (bf16[128,256]{1,0:T(8,128)(2,1)S(1)}, bf16[128,256]{1,0:T(8,128)(2,1)S(1)}, u32[]{:S(2)}, u32[]{:S(2)}) collective-permute-start(bf16[128,256]{1,0:T(8,128)(2,1)S(1)} %get-tuple-element.23.shard), channel_id=1, source_target_pairs={{0,1},{16,17},{32,33},{48,49},{64,65},{80,81},{96,97},{112,113},{1... | collective-permute-start | bytes 196616 | tf_op jit(solution)/shard_map/ppermute | solution.py:48
  35.8 34.2 %all-to-all-start.1 = ((bf16[16,8,1152]{2,1,0:T(8,128)(2,1)}), bf16[16,8,1152]{2,1,0:T(8,128)(2,1)S(1)}, u32[]{:S(2)}, u32[]{:S(2)}) async-start(bf16[16,8,1152]{2,1,0:T(8,128)(2,1)} %shard_map.87), calls=%async_computation.1 | async-start | bytes 589824 | tf_op jit(solution)/shard_map/all_to_all | solution.py:28
  51.1 31.6 %copy-start.1 = (bf16[192,2048]{1,0:T(8,128)(2,1)S(1)}, bf16[192,2048]{1,0:T(8,128)(2,1)}, u32[]{:S(2)}) copy-start(bf16[192,2048]{1,0:T(8,128)(2,1)} %tokens.1) | copy-start | bytes 2359300
  51.1 31.6 %copy-start.3 = (bf16[192,512]{1,0:T(8,128)(2,1)S(1)}, bf16[192,512]{1,0:T(8,128)(2,1)}, u32[]{:S(2)}) copy-start(bf16[192,512]{1,0:T(8,128)(2,1)} %key_grad.3) | copy-start | bytes 589828
  51.1 31.6 %copy-start.4 = (f32[2048]{0:T(1024)S(1)}, f32[2048]{0:T(1024)}, u32[]{:S(2)}) copy-start(f32[2048]{0:T(1024)} %param.6) | copy-start | bytes 24580
  51.1 10.9 %collective-permute-start.4 = (bf16[4,128,256]{2,1,0:T(8,128)(2,1)S(1)}, bf16[4,128,256]{2,1,0:T(8,128)(2,1)S(1)}, u32[]{:S(2)}, u32[]{:S(2)}) collective-permute-start(bf16[4,128,256]{2,1,0:T(8,128)(2,1)S(1)} %pad_maximum_fusion), channel_id=1, source_target_pairs={{0,12},{4,0},{8,4},{12,8},{1,13},{5,1},{9,5},{13,9},{2,14},{6,2},{... | collective-permute-start | bytes 786440 | tf_op jit(solution)/shard_map/ppermute | solution.py:36
  53.7 22.9 %collective-permute-start.5 = (bf16[4,128,256]{2,1,0:T(8,128)(2,1)S(1)}, bf16[4,128,256]{2,1,0:T(8,128)(2,1)S(1)}, u32[]{:S(2)}, u32[]{:S(2)}) collective-permute-start(bf16[4,128,256]{2,1,0:T(8,128)(2,1)S(1)} %pad_maximum_fusion), channel_id=1, source_target_pairs={{0,8},{4,12},{8,0},{12,4},{1,9},{5,13},{9,1},{13,5},{2,10},{6,14},... | collective-permute-start | bytes 786440 | tf_op jit(solution)/shard_map/ppermute | solution.py:36
  56.2 20.4 %collective-permute-start.6 = (bf16[4,128,256]{2,1,0:T(8,128)(2,1)S(1)}, bf16[4,128,256]{2,1,0:T(8,128)(2,1)S(1)}, u32[]{:S(2)}, u32[]{:S(2)}) collective-permute-start(bf16[4,128,256]{2,1,0:T(8,128)(2,1)S(1)} %pad_maximum_fusion), channel_id=1, source_target_pairs={{0,4},{4,8},{8,12},{12,0},{1,5},{5,9},{9,13},{13,1},{2,6},{6,10},{... | collective-permute-start | bytes 786440 | tf_op jit(solution)/shard_map/ppermute | solution.py:36
  71.0 18.1 %all-to-all-start.2 = ((bf16[32,8,1152]{2,1,0:T(8,128)(2,1)}), bf16[32,8,1152]{2,1,0:T(8,128)(2,1)S(1)}, u32[]{:S(2)}, u32[]{:S(2)}) async-start(bf16[32,8,1152]{2,1,0:T(8,128)(2,1)} %shard_map.88), calls=%async_computation.2 | async-start | bytes 1179648 | tf_op jit(solution)/shard_map/all_to_all | solution.py:28
  76.7 4.3 %collective-permute-start.8 = (bf16[8,128,256]{2,1,0:T(8,128)(2,1)S(1)}, bf16[8,128,256]{2,1,0:T(8,128)(2,1)S(1)}, u32[]{:S(2)}, u32[]{:S(2)}) collective-permute-start(bf16[8,128,256]{2,1,0:T(8,128)(2,1)S(1)} %constant_dynamic-update-slice_fusion.5.rest_1_), channel_id=1, source_target_pairs={{0,16},{16,0},{1,17},{17,1},{2,18},{18,2},{3,19},{19,3},{4,20},{20... | collective-permute-start | bytes 1572872 | tf_op jit(solution)/shard_map/ppermute | solution.py:32
  78.9 3.8 %collective-permute-start.7 = (bf16[8,128,256]{2,1,0:T(8,128)(2,1)S(1)}, bf16[8,128,256]{2,1,0:T(8,128)(2,1)S(1)}, u32[]{:S(2)}, u32[]{:S(2)}) collective-permute-start(bf16[8,128,256]{2,1,0:T(8,128)(2,1)S(1)} %constant_dynamic-update-slice_fusion.rest_0_), channel_id=1, source_target_pairs={{0,16},{16,0},{1,17},{17,1},{2,18},{18,2},{3,19},{19,3},{4,20},{20... | collective-permute-start | bytes 1572872 | tf_op jit(solution)/shard_map/ppermute | solution.py:32

commit v12 on v10

--- a/solution.py
+++ b/solution.py
@@ -125,12 +125,12 @@
         which = lax.rem(zl + j, 4)
         rows = piece[pl.ds(pl.multiple_of(x * 32, 32), 32), :].astype(f32)
         products[which] = shards[which] * rows
-    gain = lax.dot_general(
-        jnp.ones((8, HALF), f32),
-        products[...].reshape(128, HALF),
-        (((1,), (1,)), ((), ())),
-        preferred_element_type=f32,
-        precision=lax.Precision.HIGHEST,
+    exact = products[...].reshape(128, HALF)
+    high = exact.astype(bf16)
+    low = (exact - high.astype(f32)).astype(bf16)
+    ones = jnp.ones((8, HALF), bf16)
+    gain = sum(
+        lax.dot_general(ones, part, (((1,), (1,)), ((), ())), preferred_element_type=f32) for part in (high, low)
     )
     gains = two_rows(gain)
     for target in range(4):
@@ -154,37 +154,36 @@
         copy.wait()
 
 
-def last_kernel(place, blocks, norm_gain, weight_grad, gain_grad):
+def last_kernel(place, blocks, norm_gain, weight_grad, gain_grad, held, sem):
     y = place[2]
+    copies = []
     for x in range(4):
         for core in range(2):
-            block = blocks[y * 8 + x * 2 + core].astype(f32) / DEVICES
+            block = blocks[y * 8 + x * 2 + core, :, : 4 * HALF].astype(f32) / DEVICES
             for k in range(4):
                 at = x * 32 + k * 8
-                weight_grad[at : at + 8, core * HALF : (core + 1) * HALF] = block[:, k * HALF : (k + 1) * HALF]
-    rows_of = []
-    for peer in range(16):
-        gains = blocks[peer * 2, :, 4 * HALF :].astype(f32) + blocks[peer * 2 + 1, :, 4 * HALF :].astype(f32)
-        rows_of.append(gains[0:1] + gains[1:2])
-    sums = jnp.concatenate(rows_of, axis=0)
-    lane = lax.broadcasted_iota(jnp.int32, (16, 128), 1)
-    peer = lax.broadcasted_iota(jnp.int32, (16, 128), 0)
+                held[at : at + 8, core * HALF : (core + 1) * HALF] = block[:, k * HALF : (k + 1) * HALF]
+        rows = slice(x * 32, x * 32 + 32)
+        copies += copy_out([(held.at[rows], weight_grad.at[rows])], sem.at[pl.ds(x, 1)])
+    sums = blocks[:, :, 4 * HALF :].astype(f32).reshape(256, 128)
+    lane = lax.broadcasted_iota(jnp.int32, (256, 128), 1) // 32
+    own_x = lax.broadcasted_iota(jnp.int32, (64, 128), 0) // 16 == lax.broadcasted_iota(jnp.int32, (64, 128), 1) // 32
     spread = (
         lax.broadcasted_iota(jnp.int32, (128, 128), 0) % 32
         == lax.broadcasted_iota(jnp.int32, (128, 128), 1) % 32
-    ).astype(f32)
-    stacked = jnp.concatenate([jnp.where(lane // 32 == zl, sums, 0.0) for zl in range(4)], axis=0)
-    moved = lax.dot_general(
-        stacked, spread, (((1,), (0,)), ((), ())), preferred_element_type=f32,
-        precision=lax.Precision.HIGHEST,
-    )
-    for row in range(4):
-        for zl in range(4):
-            picked = jnp.where(peer == row * 4 + lane // 32, moved[zl * 16 : zl * 16 + 16], 0.0)
+    ).astype(f32).astype(bf16)
+    for zl in range(4):
+        moved = jnp.dot(
+            jnp.where(lane == zl, sums, 0.0).astype(bf16), spread, preferred_element_type=f32
+        )
+        for row in range(4):
+            picked = jnp.where(own_x, moved[row * 64 : row * 64 + 64], 0.0)
             at = row * 4 + zl
             gain_grad[at : at + 1, :] = jnp.sum(picked, axis=0, keepdims=True) / (
                 norm_gain[at : at + 1, :] * DEVICES
             )
+    for copy in copies:
+        copy.wait()
 
 
 def token_kernel(place, tokens, inv_rms, norm_gain, key_grad, *rest):
@@ -305,6 +304,8 @@
         [((128, 512), f32), ((16, 128), f32)],
         [SMEM, VMEM, VMEM],
         (place, blocks, norm_gain.reshape(16, 128)),
+        scratch=[pltpu.VMEM((128, 512), f32), pltpu.SemaphoreType.DMA((4,))],
+        out_specs=[ANY, VMEM],
     )
     return keys, tokens_grad, weight_grad, gain_grad.reshape(2048)
 

time: 90.4 us -> 91 us (level)
  no operation moved by 1% of the time
where the time goes in v12:
time: 91 us; the launch traced here: 90.3 us
  starting transfers between devices  60.6 us (67%)
  waiting for transfers between devices  14.3 us (16%)
  Pallas kernels  13.3 us (15%)
  local copies, waits for them, and re-layouts  1.05 us (1%)
  between operations  0.96 us (1%)
    all_to_all x3, starting transfers between devices, exchange(): return lax.all_to_all(blocks, axes, 0, 0, tiled=False)  25.5 us
    ppermute x3, starting transfers between devices, along_z(): return lax.ppermute(block, ('zh', 'x', 'core', 'zl'), pairs)  14.6 us
    pallas_call x7, Pallas kernels, call(): pl.pallas_call(kernel, out_shape=[jax.ShapeDtypeStruct(s, d) for s, d in...  13.3 us
    ppermute x3, starting transfers between devices, swap(): return lax.ppermute(block, 'core', [(0, 1), (1, 0)])  13.1 us
    all_to_all x3, waiting for transfers between devices, exchange(): return lax.all_to_all(blocks, axes, 0, 0, tiled=False)  7.8 us
    ppermute x3, starting transfers between devices, along_y(): return lax.ppermute(block, 'y', [(y, (y + step) % 4) for y in range(4)])  7.33 us
    ppermute x3, waiting for transfers between devices, along_z(): return lax.ppermute(block, ('zh', 'x', 'core', 'zl'), pairs)  4.6 us
    ppermute x3, waiting for transfers between devices, swap(): return lax.ppermute(block, 'core', [(0, 1), (1, 0)])  1.9 us
  transfers between devices with their start and end apart: 12, of which 6 were waited for; matrix products, arithmetic and copies ran while one was open for 0% of the time, Pallas kernels for 7%

profile of v12, /device:TPU:1, one launch (start us, length us, event | category | flops | bytes accessed | tf_op | source)
XLA Modules:
  0.0 90.3 jit_solution(9421701199137165804)
XLA Ops:
  0.7 2.6 %shard_map.84 = (bf16[192,2048]{1,0:T(8,128)(2,1)S(1)}, f32[192,128]{1,0:T(8,128)S(1)}, bf16[16,16,2048]{2,1,0:T(8,128)(2,1)S(1)}) custom-call(s32[4]{0:T(128)S(1)} %pad_add_fusion.place, bf16[192,2048]{1,0:T(8,128)(2,1)} %tokens.1, f32[1,2048]{1,0:T(1,128)} %bitcast.20, bf16[192,512]{1,0:T(8,128)(2,1)} %key_grad.3), custom_call_target="tpu_custom_call" | custom-call | flops 201326592 | bytes 1982496 | tf_op jit(solution)/shard_map/pallas_call | solution.py:213
  3.4 8.8 %collective-permute-start = (bf16[16,16,2048]{2,1,0:T(8,128)(2,1)S(1)}, bf16[16,16,2048]{2,1,0:T(8,128)(2,1)S(1)}, u32[]{:S(2)}, u32[]{:S(2)}) collective-permute-start(bf16[16,16,2048]{2,1,0:T(8,128)(2,1)S(1)} %get-tuple-element.22), channel_id=1, source_target_pairs={{0,16},{16,0},{1,17},{17,1},{2,18},{18,2},{3,19},{19,3},{4,20},{20... | collective-permute-start | bytes 3145736 | tf_op jit(solution)/shard_map/ppermute | solution.py:32
  12.2 0.9 %copy-done.2 = bf16[192,512]{1,0:T(8,128)(2,1)S(1)} copy-done((bf16[192,512]{1,0:T(8,128)(2,1)S(1)}, bf16[192,512]{1,0:T(8,128)(2,1)}, u32[]{:S(2)}) %copy-start.2) | copy-done | bytes 196632
  13.1 1.0 %shard_map.85.mine = f32[16,16,2048]{2,1,0:T(8,128)S(1)} custom-call(s32[4]{0:T(128)S(1)} %pad_add_fusion.place, bf16[192,2048]{1,0:T(8,128)(2,1)S(1)} %get-tuple-element.21.normed, bf16[192,512]{1,0:T(8,128)(2,1)S(1)} %copy-done.2), custom_call_target="tpu_custom_call" | custom-call | flops 201326592 | bytes 1966112 | tf_op jit(solution)/shard_map/pallas_call | solution.py:213
  14.4 1.1 %shard_map.86 = bf16[16,16,2048]{2,1,0:T(8,128)(2,1)} custom-call(f32[16,16,2048]{2,1,0:T(8,128)S(1)} %shard_map.85.mine, bf16[16,16,2048]{2,1,0:T(8,128)(2,1)S(1)} %collective-permute-done.got), custom_call_target="tpu_custom_call" | custom-call | bytes 6291456 | tf_op jit(solution)/shard_map/pallas_call | solution.py:213
  15.6 3.8 %all-to-all-start = ((bf16[16,16,2048]{2,1,0:T(8,128)(2,1)}), bf16[16,16,2048]{2,1,0:T(8,128)(2,1)S(1)}, u32[]{:S(2)}, u32[]{:S(2)}) async-start(bf16[16,16,2048]{2,1,0:T(8,128)(2,1)} %shard_map.86), calls=%async_computation | async-start | bytes 2097152 | tf_op jit(solution)/shard_map/all_to_all | solution.py:28
  19.4 8.9 %collective-permute-start.1 = (bf16[128,256]{1,0:T(8,128)(2,1)S(1)}, bf16[128,256]{1,0:T(8,128)(2,1)S(1)}, u32[]{:S(2)}, u32[]{:S(2)}) collective-permute-start(bf16[128,256]{1,0:T(8,128)(2,1)S(1)} %get-tuple-element.23.shard), channel_id=1, source_target_pairs={{0,387},{16,403},{32,419},{48,435},{64,451},{80,467},{96,483},{112... | collective-permute-start | bytes 196616 | tf_op jit(solution)/shard_map/ppermute | solution.py:48
  28.3 3.1 %collective-permute-start.2 = (bf16[128,256]{1,0:T(8,128)(2,1)S(1)}, bf16[128,256]{1,0:T(8,128)(2,1)S(1)}, u32[]{:S(2)}, u32[]{:S(2)}) collective-permute-start(bf16[128,256]{1,0:T(8,128)(2,1)S(1)} %get-tuple-element.23.shard), channel_id=1, source_target_pairs={{0,2},{16,402},{32,34},{48,434},{64,66},{80,466},{96,98},{112,498}... | collective-permute-start | bytes 196616 | tf_op jit(solution)/shard_map/ppermute | solution.py:48
  31.4 2.6 %collective-permute-start.3 = (bf16[128,256]{1,0:T(8,128)(2,1)S(1)}, bf16[128,256]{1,0:T(8,128)(2,1)S(1)}, u32[]{:S(2)}, u32[]{:S(2)}) collective-permute-start(bf16[128,256]{1,0:T(8,128)(2,1)S(1)} %get-tuple-element.23.shard), channel_id=1, source_target_pairs={{0,1},{16,17},{32,33},{48,49},{64,65},{80,81},{96,97},{112,113},{1... | collective-permute-start | bytes 196616 | tf_op jit(solution)/shard_map/ppermute | solution.py:48
  34.3 4.3 %collective-permute-done.3.below = bf16[128,256]{1,0:T(8,128)(2,1)S(1)} collective-permute-done((bf16[128,256]{1,0:T(8,128)(2,1)S(1)}, bf16[128,256]{1,0:T(8,128)(2,1)S(1)}, u32[]{:S(2)}, u32[]{:S(2)}) %collective-permute-start.3) | collective-permute-done | bytes 65568 | tf_op jit(solution)/shard_map/ppermute | solution.py:48
  38.7 1.6 %shard_map.87 = bf16[16,8,1152]{2,1,0:T(8,128)(2,1)} custom-call(s32[4]{0:T(128)S(1)} %pad_add_fusion.place, bf16[16,16,2048]{2,1,0:T(8,128)(2,1)S(1)} %all-to-all-done.square, bf16[128,256]{1,0:T(8,128)(2,1)S(1)} %get-tuple-element.23.shard, bf16[128,256]{1,0:T(8,128)(2,1)S(1)} %collective-permute-done.1.above, ...), custom_call_target="tpu_custom_call" | custom-call | bytes 2621472 | tf_op jit(solution)/shard_map/pallas_call | solution.py:213
  40.3 9.7 %all-to-all-start.1 = ((bf16[16,8,1152]{2,1,0:T(8,128)(2,1)}), bf16[16,8,1152]{2,1,0:T(8,128)(2,1)S(1)}, u32[]{:S(2)}, u32[]{:S(2)}) async-start(bf16[16,8,1152]{2,1,0:T(8,128)(2,1)} %shard_map.87), calls=%async_computation.1 | async-start | bytes 589824 | tf_op jit(solution)/shard_map/all_to_all | solution.py:28
  50.1 2.6 %collective-permute-start.4 = (bf16[4,128,256]{2,1,0:T(8,128)(2,1)S(1)}, bf16[4,128,256]{2,1,0:T(8,128)(2,1)S(1)}, u32[]{:S(2)}, u32[]{:S(2)}) collective-permute-start(bf16[4,128,256]{2,1,0:T(8,128)(2,1)S(1)} %pad_maximum_fusion), channel_id=1, source_target_pairs={{0,12},{4,0},{8,4},{12,8},{1,13},{5,1},{9,5},{13,9},{2,14},{6,2},{... | collective-permute-start | bytes 786440 | tf_op jit(solution)/shard_map/ppermute | solution.py:36
  52.7 2.2 %collective-permute-start.5 = (bf16[4,128,256]{2,1,0:T(8,128)(2,1)S(1)}, bf16[4,128,256]{2,1,0:T(8,128)(2,1)S(1)}, u32[]{:S(2)}, u32[]{:S(2)}) collective-permute-start(bf16[4,128,256]{2,1,0:T(8,128)(2,1)S(1)} %pad_maximum_fusion), channel_id=1, source_target_pairs={{0,8},{4,12},{8,0},{12,4},{1,9},{5,13},{9,1},{13,5},{2,10},{6,14},... | collective-permute-start | bytes 786440 | tf_op jit(solution)/shard_map/ppermute | solution.py:36
  55.0 2.5 %collective-permute-start.6 = (bf16[4,128,256]{2,1,0:T(8,128)(2,1)S(1)}, bf16[4,128,256]{2,1,0:T(8,128)(2,1)S(1)}, u32[]{:S(2)}, u32[]{:S(2)}) collective-permute-start(bf16[4,128,256]{2,1,0:T(8,128)(2,1)S(1)} %pad_maximum_fusion), channel_id=1, source_target_pairs={{0,4},{4,8},{8,12},{12,0},{1,5},{5,9},{9,13},{13,1},{2,6},{6,10},{... | collective-permute-start | bytes 786440 | tf_op jit(solution)/shard_map/ppermute | solution.py:36
  57.5 5.6 %all-to-all-done.1.line = bf16[16,8,1152]{2,1,0:T(8,128)(2,1)S(1)} async-done(((bf16[16,8,1152]{2,1,0:T(8,128)(2,1)}), bf16[16,8,1152]{2,1,0:T(8,128)(2,1)S(1)}, u32[]{:S(2)}, u32[]{:S(2)}) %all-to-all-start.1) | async-done | bytes 294944 | tf_op jit(solution)/shard_map/all_to_all | solution.py:28
  63.1 0.9 %shard_map.88 = bf16[32,8,1152]{2,1,0:T(8,128)(2,1)} custom-call(bf16[16,8,1152]{2,1,0:T(8,128)(2,1)S(1)} %all-to-all-done.1.line), custom_call_target="tpu_custom_call" | custom-call | bytes 589824 | tf_op jit(solution)/shard_map/pallas_call | solution.py:213
  64.0 12.0 %all-to-all-start.2 = ((bf16[32,8,1152]{2,1,0:T(8,128)(2,1)}), bf16[32,8,1152]{2,1,0:T(8,128)(2,1)S(1)}, u32[]{:S(2)}, u32[]{:S(2)}) async-start(bf16[32,8,1152]{2,1,0:T(8,128)(2,1)} %shard_map.88), calls=%async_computation.2 | async-start | bytes 1179648 | tf_op jit(solution)/shard_map/all_to_all | solution.py:28
  76.1 2.1 %collective-permute-start.8 = (bf16[8,128,256]{2,1,0:T(8,128)(2,1)S(1)}, bf16[8,128,256]{2,1,0:T(8,128)(2,1)S(1)}, u32[]{:S(2)}, u32[]{:S(2)}) collective-permute-start(bf16[8,128,256]{2,1,0:T(8,128)(2,1)S(1)} %constant_dynamic-update-slice_fusion.5.rest_1_), channel_id=1, source_target_pairs={{0,16},{16,0},{1,17},{17,1},{2,18},{18,2},{3,19},{19,3},{4,20},{20... | collective-permute-start | bytes 1572872 | tf_op jit(solution)/shard_map/ppermute | solution.py:32
  78.3 2.2 %collective-permute-start.7 = (bf16[8,128,256]{2,1,0:T(8,128)(2,1)S(1)}, bf16[8,128,256]{2,1,0:T(8,128)(2,1)S(1)}, u32[]{:S(2)}, u32[]{:S(2)}) collective-permute-start(bf16[8,128,256]{2,1,0:T(8,128)(2,1)S(1)} %constant_dynamic-update-slice_fusion.rest_0_), channel_id=1, source_target_pairs={{0,16},{16,0},{1,17},{17,1},{2,18},{18,2},{3,19},{19,3},{4,20},{20... | collective-permute-start | bytes 1572872 | tf_op jit(solution)/shard_map/ppermute | solution.py:32
  80.5 1.6 %collective-permute-done.7.rest_2_ = bf16[8,128,256]{2,1,0:T(8,128)(2,1)S(1)} collective-permute-done((bf16[8,128,256]{2,1,0:T(8,128)(2,1)S(1)}, bf16[8,128,256]{2,1,0:T(8,128)(2,1)S(1)}, u32[]{:S(2)}, u32[]{:S(2)}) %collective-permute-start.7) | collective-permute-done | bytes 524320 | tf_op jit(solution)/shard_map/ppermute | solution.py:32
  82.1 4.0 %shard_map.89 = (bf16[192,512]{1,0:T(8,128)(2,1)}, bf16[192,2048]{1,0:T(8,128)(2,1)}) custom-call(s32[4]{0:T(128)S(1)} %pad_add_fusion.place, bf16[192,2048]{1,0:T(8,128)(2,1)S(1)} %copy-done.1, f32[192,128]{1,0:T(8,128)S(1)} %get-tuple-element.26.inv_rms, f32[1,2048]{1,0:T(1,128)S(1)} %bitcast.21, bf16[192,512]{1,0:T(8,128)(2,1)S(1)} %copy-done.3, ...), custom_call_target="tpu_custom_call" | custom-call | bytes 6373408 | tf_op jit(solution)/shard_map/pallas_call | solution.py:213
  86.1 2.2 %all-to-all-done.2.blocks = bf16[32,8,1152]{2,1,0:T(8,128)(2,1)S(1)} async-done(((bf16[32,8,1152]{2,1,0:T(8,128)(2,1)}), bf16[32,8,1152]{2,1,0:T(8,128)(2,1)S(1)}, u32[]{:S(2)}, u32[]{:S(2)}) %all-to-all-start.2) | async-done | bytes 589856 | tf_op jit(solution)/shard_map/all_to_all | solution.py:28
  88.3 2.0 %shard_map.90 = (f32[128,512]{1,0:T(8,128)}, f32[16,128]{1,0:T(8,128)}) custom-call(s32[4]{0:T(128)S(1)} %pad_add_fusion.place, bf16[32,8,1152]{2,1,0:T(8,128)(2,1)S(1)} %all-to-all-done.2.blocks, f32[16,128]{1,0:T(8,128)S(1)} %bitcast.22), custom_call_target="tpu_custom_call" | custom-call | bytes 1196064 | tf_op jit(solution)/shard_map/pallas_call | solution.py:213
  (29 shorter events, 0.8 us)
Async XLA Ops:
  0.6 18.7 %copy-start = (f32[1,512]{1,0:T(1,128)S(1)}, f32[1,512]{1,0:T(1,128)}, u32[]{:S(2)}) copy-start(f32[1,512]{1,0:T(1,128)} %param.8) | copy-start | bytes 6148
  3.4 11.1 %collective-permute-start = (bf16[16,16,2048]{2,1,0:T(8,128)(2,1)S(1)}, bf16[16,16,2048]{2,1,0:T(8,128)(2,1)S(1)}, u32[]{:S(2)}, u32[]{:S(2)}) collective-permute-start(bf16[16,16,2048]{2,1,0:T(8,128)(2,1)S(1)} %get-tuple-element.22), channel_id=1, source_target_pairs={{0,16},{16,0},{1,17},{17,1},{2,18},{18,2},{3,19},{19,3},{4,20},{20... | collective-permute-start | bytes 3145736 | tf_op jit(solution)/shard_map/ppermute | solution.py:32
  12.2 0.9 %copy-start.2 = (bf16[192,512]{1,0:T(8,128)(2,1)S(1)}, bf16[192,512]{1,0:T(8,128)(2,1)}, u32[]{:S(2)}) copy-start(bf16[192,512]{1,0:T(8,128)(2,1)} %key_grad.3) | copy-start | bytes 589828
  15.5 3.9 %copy-start.5 = (s32[128,512]{1,0:T(8,128)S(1)}, s32[128,512]{1,0:T(8,128)}, u32[]{:S(2)}) copy-start(s32[128,512]{1,0:T(8,128)} %param.7) | copy-start | bytes 786436
  15.6 23.1 %all-to-all-start = ((bf16[16,16,2048]{2,1,0:T(8,128)(2,1)}), bf16[16,16,2048]{2,1,0:T(8,128)(2,1)S(1)}, u32[]{:S(2)}, u32[]{:S(2)}) async-start(bf16[16,16,2048]{2,1,0:T(8,128)(2,1)} %shard_map.86), calls=%async_computation | async-start | bytes 2097152 | tf_op jit(solution)/shard_map/all_to_all | solution.py:28
  19.4 14.6 %collective-permute-start.1 = (bf16[128,256]{1,0:T(8,128)(2,1)S(1)}, bf16[128,256]{1,0:T(8,128)(2,1)S(1)}, u32[]{:S(2)}, u32[]{:S(2)}) collective-permute-start(bf16[128,256]{1,0:T(8,128)(2,1)S(1)} %get-tuple-element.23.shard), channel_id=1, source_target_pairs={{0,387},{16,403},{32,419},{48,435},{64,451},{80,467},{96,483},{112... | collective-permute-start | bytes 196616 | tf_op jit(solution)/shard_map/ppermute | solution.py:48
  28.3 6.0 %collective-permute-start.2 = (bf16[128,256]{1,0:T(8,128)(2,1)S(1)}, bf16[128,256]{1,0:T(8,128)(2,1)S(1)}, u32[]{:S(2)}, u32[]{:S(2)}) collective-permute-start(bf16[128,256]{1,0:T(8,128)(2,1)S(1)} %get-tuple-element.23.shard), channel_id=1, source_target_pairs={{0,2},{16,402},{32,34},{48,434},{64,66},{80,466},{96,98},{112,498}... | collective-permute-start | bytes 196616 | tf_op jit(solution)/shard_map/ppermute | solution.py:48
  31.4 7.3 %collective-permute-start.3 = (bf16[128,256]{1,0:T(8,128)(2,1)S(1)}, bf16[128,256]{1,0:T(8,128)(2,1)S(1)}, u32[]{:S(2)}, u32[]{:S(2)}) collective-permute-start(bf16[128,256]{1,0:T(8,128)(2,1)S(1)} %get-tuple-element.23.shard), channel_id=1, source_target_pairs={{0,1},{16,17},{32,33},{48,49},{64,65},{80,81},{96,97},{112,113},{1... | collective-permute-start | bytes 196616 | tf_op jit(solution)/shard_map/ppermute | solution.py:48
  40.3 22.8 %all-to-all-start.1 = ((bf16[16,8,1152]{2,1,0:T(8,128)(2,1)}), bf16[16,8,1152]{2,1,0:T(8,128)(2,1)S(1)}, u32[]{:S(2)}, u32[]{:S(2)}) async-start(bf16[16,8,1152]{2,1,0:T(8,128)(2,1)} %shard_map.87), calls=%async_computation.1 | async-start | bytes 589824 | tf_op jit(solution)/shard_map/all_to_all | solution.py:28
  50.0 32.1 %copy-start.1 = (bf16[192,2048]{1,0:T(8,128)(2,1)S(1)}, bf16[192,2048]{1,0:T(8,128)(2,1)}, u32[]{:S(2)}) copy-start(bf16[192,2048]{1,0:T(8,128)(2,1)} %tokens.1) | copy-start | bytes 2359300
  50.0 32.0 %copy-start.3 = (bf16[192,512]{1,0:T(8,128)(2,1)S(1)}, bf16[192,512]{1,0:T(8,128)(2,1)}, u32[]{:S(2)}) copy-start(bf16[192,512]{1,0:T(8,128)(2,1)} %key_grad.3) | copy-start | bytes 589828
  50.1 32.0 %copy-start.4 = (f32[2048]{0:T(1024)S(1)}, f32[2048]{0:T(1024)}, u32[]{:S(2)}) copy-start(f32[2048]{0:T(1024)} %param.6) | copy-start | bytes 24580
  50.1 7.4 %collective-permute-start.4 = (bf16[4,128,256]{2,1,0:T(8,128)(2,1)S(1)}, bf16[4,128,256]{2,1,0:T(8,128)(2,1)S(1)}, u32[]{:S(2)}, u32[]{:S(2)}) collective-permute-start(bf16[4,128,256]{2,1,0:T(8,128)(2,1)S(1)} %pad_maximum_fusion), channel_id=1, source_target_pairs={{0,12},{4,0},{8,4},{12,8},{1,13},{5,1},{9,5},{13,9},{2,14},{6,2},{... | collective-permute-start | bytes 786440 | tf_op jit(solution)/shard_map/ppermute | solution.py:36
  52.7 23.3 %collective-permute-start.5 = (bf16[4,128,256]{2,1,0:T(8,128)(2,1)S(1)}, bf16[4,128,256]{2,1,0:T(8,128)(2,1)S(1)}, u32[]{:S(2)}, u32[]{:S(2)}) collective-permute-start(bf16[4,128,256]{2,1,0:T(8,128)(2,1)S(1)} %pad_maximum_fusion), channel_id=1, source_target_pairs={{0,8},{4,12},{8,0},{12,4},{1,9},{5,13},{9,1},{13,5},{2,10},{6,14},... | collective-permute-start | bytes 786440 | tf_op jit(solution)/shard_map/ppermute | solution.py:36
  55.0 21.1 %collective-permute-start.6 = (bf16[4,128,256]{2,1,0:T(8,128)(2,1)S(1)}, bf16[4,128,256]{2,1,0:T(8,128)(2,1)S(1)}, u32[]{:S(2)}, u32[]{:S(2)}) collective-permute-start(bf16[4,128,256]{2,1,0:T(8,128)(2,1)S(1)} %pad_maximum_fusion), channel_id=1, source_target_pairs={{0,4},{4,8},{8,12},{12,0},{1,5},{5,9},{9,13},{13,1},{2,6},{6,10},{... | collective-permute-start | bytes 786440 | tf_op jit(solution)/shard_map/ppermute | solution.py:36
  64.0 24.3 %all-to-all-start.2 = ((bf16[32,8,1152]{2,1,0:T(8,128)(2,1)}), bf16[32,8,1152]{2,1,0:T(8,128)(2,1)S(1)}, u32[]{:S(2)}, u32[]{:S(2)}) async-start(bf16[32,8,1152]{2,1,0:T(8,128)(2,1)} %shard_map.88), calls=%async_computation.2 | async-start | bytes 1179648 | tf_op jit(solution)/shard_map/all_to_all | solution.py:28
  76.1 4.3 %collective-permute-start.8 = (bf16[8,128,256]{2,1,0:T(8,128)(2,1)S(1)}, bf16[8,128,256]{2,1,0:T(8,128)(2,1)S(1)}, u32[]{:S(2)}, u32[]{:S(2)}) collective-permute-start(bf16[8,128,256]{2,1,0:T(8,128)(2,1)S(1)} %constant_dynamic-update-slice_fusion.5.rest_1_), channel_id=1, source_target_pairs={{0,16},{16,0},{1,17},{17,1},{2,18},{18,2},{3,19},{19,3},{4,20},{20... | collective-permute-start | bytes 1572872 | tf_op jit(solution)/shard_map/ppermute | solution.py:32
  78.3 3.8 %collective-permute-start.7 = (bf16[8,128,256]{2,1,0:T(8,128)(2,1)S(1)}, bf16[8,128,256]{2,1,0:T(8,128)(2,1)S(1)}, u32[]{:S(2)}, u32[]{:S(2)}) collective-permute-start(bf16[8,128,256]{2,1,0:T(8,128)(2,1)S(1)} %constant_dynamic-update-slice_fusion.rest_0_), channel_id=1, source_target_pairs={{0,16},{16,0},{1,17},{17,1},{2,18},{18,2},{3,19},{19,3},{4,20},{20... | collective-permute-start | bytes 1572872 | tf_op jit(solution)/shard_map/ppermute | solution.py:32

commit v13 on v10

--- a/solution.py
+++ b/solution.py
@@ -125,12 +125,12 @@
         which = lax.rem(zl + j, 4)
         rows = piece[pl.ds(pl.multiple_of(x * 32, 32), 32), :].astype(f32)
         products[which] = shards[which] * rows
-    gain = lax.dot_general(
-        jnp.ones((8, HALF), f32),
-        products[...].reshape(128, HALF),
-        (((1,), (1,)), ((), ())),
-        preferred_element_type=f32,
-        precision=lax.Precision.HIGHEST,
+    exact = products[...].reshape(128, HALF)
+    high = exact.astype(bf16)
+    low = (exact - high.astype(f32)).astype(bf16)
+    ones = jnp.ones((8, HALF), bf16)
+    gain = sum(
+        lax.dot_general(ones, part, (((1,), (1,)), ((), ())), preferred_element_type=f32) for part in (high, low)
     )
     gains = two_rows(gain)
     for target in range(4):
@@ -154,14 +154,17 @@
         copy.wait()
 
 
-def last_kernel(place, blocks, norm_gain, weight_grad, gain_grad):
+def last_kernel(place, blocks, norm_gain, weight_grad, gain_grad, held, sem):
     y = place[2]
+    copies = []
     for x in range(4):
         for core in range(2):
-            block = blocks[y * 8 + x * 2 + core].astype(f32) / DEVICES
+            block = blocks[y * 8 + x * 2 + core, :, : 4 * HALF].astype(f32) / DEVICES
             for k in range(4):
                 at = x * 32 + k * 8
-                weight_grad[at : at + 8, core * HALF : (core + 1) * HALF] = block[:, k * HALF : (k + 1) * HALF]
+                held[at : at + 8, core * HALF : (core + 1) * HALF] = block[:, k * HALF : (k + 1) * HALF]
+        rows = slice(x * 32, x * 32 + 32)
+        copies += copy_out([(held.at[rows], weight_grad.at[rows])], sem.at[pl.ds(x, 1)])
     rows_of = []
     for peer in range(16):
         gains = blocks[peer * 2, :, 4 * HALF :].astype(f32) + blocks[peer * 2 + 1, :, 4 * HALF :].astype(f32)
@@ -185,6 +188,8 @@
             gain_grad[at : at + 1, :] = jnp.sum(picked, axis=0, keepdims=True) / (
                 norm_gain[at : at + 1, :] * DEVICES
             )
+    for copy in copies:
+        copy.wait()
 
 
 def token_kernel(place, tokens, inv_rms, norm_gain, key_grad, *rest):
@@ -305,6 +310,8 @@
         [((128, 512), f32), ((16, 128), f32)],
         [SMEM, VMEM, VMEM],
         (place, blocks, norm_gain.reshape(16, 128)),
+        scratch=[pltpu.VMEM((128, 512), f32), pltpu.SemaphoreType.DMA((4,))],
+        out_specs=[ANY, VMEM],
     )
     return keys, tokens_grad, weight_grad, gain_grad.reshape(2048)
 

time: 90.4 us -> 90.9 us (level)
  no operation moved by 1% of the time
where the time goes in v13:
time: 90.9 us; the launch traced here: 90.2 us
  starting transfers between devices  60.6 us (67%)
  waiting for transfers between devices  14.3 us (16%)
  Pallas kernels  13.2 us (15%)
  local copies, waits for them, and re-layouts  1.05 us (1%)
  between operations  0.96 us (1%)
    all_to_all x3, starting transfers between devices, exchange(): return lax.all_to_all(blocks, axes, 0, 0, tiled=False)  25.5 us
    ppermute x3, starting transfers between devices, along_z(): return lax.ppermute(block, ('zh', 'x', 'core', 'zl'), pairs)  14.6 us
    pallas_call x7, Pallas kernels, call(): pl.pallas_call(kernel, out_shape=[jax.ShapeDtypeStruct(s, d) for s, d in...  13.2 us
    ppermute x3, starting transfers between devices, swap(): return lax.ppermute(block, 'core', [(0, 1), (1, 0)])  13.1 us
    all_to_all x3, waiting for transfers between devices, exchange(): return lax.all_to_all(blocks, axes, 0, 0, tiled=False)  7.8 us
    ppermute x3, starting transfers between devices, along_y(): return lax.ppermute(block, 'y', [(y, (y + step) % 4) for y in range(4)])  7.33 us
    ppermute x3, waiting for transfers between devices, along_z(): return lax.ppermute(block, ('zh', 'x', 'core', 'zl'), pairs)  4.6 us
    ppermute x3, waiting for transfers between devices, swap(): return lax.ppermute(block, 'core', [(0, 1), (1, 0)])  1.9 us
  transfers between devices with their start and end apart: 12, of which 6 were waited for; matrix products, arithmetic and copies ran while one was open for 0% of the time, Pallas kernels for 7%

profile of v13, /device:TPU:1, one launch (start us, length us, event | category | flops | bytes accessed | tf_op | source)
XLA Modules:
  0.0 90.2 jit_solution(5069487435072052313)
XLA Ops:
  0.7 2.6 %shard_map.84 = (bf16[192,2048]{1,0:T(8,128)(2,1)S(1)}, f32[192,128]{1,0:T(8,128)S(1)}, bf16[16,16,2048]{2,1,0:T(8,128)(2,1)S(1)}) custom-call(s32[4]{0:T(128)S(1)} %pad_add_fusion.place, bf16[192,2048]{1,0:T(8,128)(2,1)} %tokens.1, f32[1,2048]{1,0:T(1,128)} %bitcast.20, bf16[192,512]{1,0:T(8,128)(2,1)} %key_grad.3), custom_call_target="tpu_custom_call" | custom-call | flops 201326592 | bytes 1982496 | tf_op jit(solution)/shard_map/pallas_call | solution.py:219
  3.4 8.8 %collective-permute-start = (bf16[16,16,2048]{2,1,0:T(8,128)(2,1)S(1)}, bf16[16,16,2048]{2,1,0:T(8,128)(2,1)S(1)}, u32[]{:S(2)}, u32[]{:S(2)}) collective-permute-start(bf16[16,16,2048]{2,1,0:T(8,128)(2,1)S(1)} %get-tuple-element.22), channel_id=1, source_target_pairs={{0,16},{16,0},{1,17},{17,1},{2,18},{18,2},{3,19},{19,3},{4,20},{20... | collective-permute-start | bytes 3145736 | tf_op jit(solution)/shard_map/ppermute | solution.py:32
  12.2 0.9 %copy-done.2 = bf16[192,512]{1,0:T(8,128)(2,1)S(1)} copy-done((bf16[192,512]{1,0:T(8,128)(2,1)S(1)}, bf16[192,512]{1,0:T(8,128)(2,1)}, u32[]{:S(2)}) %copy-start.2) | copy-done | bytes 196632
  13.1 1.0 %shard_map.85.mine = f32[16,16,2048]{2,1,0:T(8,128)S(1)} custom-call(s32[4]{0:T(128)S(1)} %pad_add_fusion.place, bf16[192,2048]{1,0:T(8,128)(2,1)S(1)} %get-tuple-element.21.normed, bf16[192,512]{1,0:T(8,128)(2,1)S(1)} %copy-done.2), custom_call_target="tpu_custom_call" | custom-call | flops 201326592 | bytes 1966112 | tf_op jit(solution)/shard_map/pallas_call | solution.py:219
  14.4 1.1 %shard_map.86 = bf16[16,16,2048]{2,1,0:T(8,128)(2,1)} custom-call(f32[16,16,2048]{2,1,0:T(8,128)S(1)} %shard_map.85.mine, bf16[16,16,2048]{2,1,0:T(8,128)(2,1)S(1)} %collective-permute-done.got), custom_call_target="tpu_custom_call" | custom-call | bytes 6291456 | tf_op jit(solution)/shard_map/pallas_call | solution.py:219
  15.6 3.8 %all-to-all-start = ((bf16[16,16,2048]{2,1,0:T(8,128)(2,1)}), bf16[16,16,2048]{2,1,0:T(8,128)(2,1)S(1)}, u32[]{:S(2)}, u32[]{:S(2)}) async-start(bf16[16,16,2048]{2,1,0:T(8,128)(2,1)} %shard_map.86), calls=%async_computation | async-start | bytes 2097152 | tf_op jit(solution)/shard_map/all_to_all | solution.py:28
  19.4 8.9 %collective-permute-start.1 = (bf16[128,256]{1,0:T(8,128)(2,1)S(1)}, bf16[128,256]{1,0:T(8,128)(2,1)S(1)}, u32[]{:S(2)}, u32[]{:S(2)}) collective-permute-start(bf16[128,256]{1,0:T(8,128)(2,1)S(1)} %get-tuple-element.23.shard), channel_id=1, source_target_pairs={{0,387},{16,403},{32,419},{48,435},{64,451},{80,467},{96,483},{112... | collective-permute-start | bytes 196616 | tf_op jit(solution)/shard_map/ppermute | solution.py:48
  28.3 3.1 %collective-permute-start.2 = (bf16[128,256]{1,0:T(8,128)(2,1)S(1)}, bf16[128,256]{1,0:T(8,128)(2,1)S(1)}, u32[]{:S(2)}, u32[]{:S(2)}) collective-permute-start(bf16[128,256]{1,0:T(8,128)(2,1)S(1)} %get-tuple-element.23.shard), channel_id=1, source_target_pairs={{0,2},{16,402},{32,34},{48,434},{64,66},{80,466},{96,98},{112,498}... | collective-permute-start | bytes 196616 | tf_op jit(solution)/shard_map/ppermute | solution.py:48
  31.4 2.6 %collective-permute-start.3 = (bf16[128,256]{1,0:T(8,128)(2,1)S(1)}, bf16[128,256]{1,0:T(8,128)(2,1)S(1)}, u32[]{:S(2)}, u32[]{:S(2)}) collective-permute-start(bf16[128,256]{1,0:T(8,128)(2,1)S(1)} %get-tuple-element.23.shard), channel_id=1, source_target_pairs={{0,1},{16,17},{32,33},{48,49},{64,65},{80,81},{96,97},{112,113},{1... | collective-permute-start | bytes 196616 | tf_op jit(solution)/shard_map/ppermute | solution.py:48
  34.3 4.3 %collective-permute-done.3.below = bf16[128,256]{1,0:T(8,128)(2,1)S(1)} collective-permute-done((bf16[128,256]{1,0:T(8,128)(2,1)S(1)}, bf16[128,256]{1,0:T(8,128)(2,1)S(1)}, u32[]{:S(2)}, u32[]{:S(2)}) %collective-permute-start.3) | collective-permute-done | bytes 65568 | tf_op jit(solution)/shard_map/ppermute | solution.py:48
  38.7 1.6 %shard_map.87 = bf16[16,8,1152]{2,1,0:T(8,128)(2,1)} custom-call(s32[4]{0:T(128)S(1)} %pad_add_fusion.place, bf16[16,16,2048]{2,1,0:T(8,128)(2,1)S(1)} %all-to-all-done.square, bf16[128,256]{1,0:T(8,128)(2,1)S(1)} %get-tuple-element.23.shard, bf16[128,256]{1,0:T(8,128)(2,1)S(1)} %collective-permute-done.1.above, ...), custom_call_target="tpu_custom_call" | custom-call | bytes 2621472 | tf_op jit(solution)/shard_map/pallas_call | solution.py:219
  40.3 9.7 %all-to-all-start.1 = ((bf16[16,8,1152]{2,1,0:T(8,128)(2,1)}), bf16[16,8,1152]{2,1,0:T(8,128)(2,1)S(1)}, u32[]{:S(2)}, u32[]{:S(2)}) async-start(bf16[16,8,1152]{2,1,0:T(8,128)(2,1)} %shard_map.87), calls=%async_computation.1 | async-start | bytes 589824 | tf_op jit(solution)/shard_map/all_to_all | solution.py:28
  50.1 2.6 %collective-permute-start.4 = (bf16[4,128,256]{2,1,0:T(8,128)(2,1)S(1)}, bf16[4,128,256]{2,1,0:T(8,128)(2,1)S(1)}, u32[]{:S(2)}, u32[]{:S(2)}) collective-permute-start(bf16[4,128,256]{2,1,0:T(8,128)(2,1)S(1)} %pad_maximum_fusion), channel_id=1, source_target_pairs={{0,12},{4,0},{8,4},{12,8},{1,13},{5,1},{9,5},{13,9},{2,14},{6,2},{... | collective-permute-start | bytes 786440 | tf_op jit(solution)/shard_map/ppermute | solution.py:36
  52.7 2.2 %collective-permute-start.5 = (bf16[4,128,256]{2,1,0:T(8,128)(2,1)S(1)}, bf16[4,128,256]{2,1,0:T(8,128)(2,1)S(1)}, u32[]{:S(2)}, u32[]{:S(2)}) collective-permute-start(bf16[4,128,256]{2,1,0:T(8,128)(2,1)S(1)} %pad_maximum_fusion), channel_id=1, source_target_pairs={{0,8},{4,12},{8,0},{12,4},{1,9},{5,13},{9,1},{13,5},{2,10},{6,14},... | collective-permute-start | bytes 786440 | tf_op jit(solution)/shard_map/ppermute | solution.py:36
  55.0 2.5 %collective-permute-start.6 = (bf16[4,128,256]{2,1,0:T(8,128)(2,1)S(1)}, bf16[4,128,256]{2,1,0:T(8,128)(2,1)S(1)}, u32[]{:S(2)}, u32[]{:S(2)}) collective-permute-start(bf16[4,128,256]{2,1,0:T(8,128)(2,1)S(1)} %pad_maximum_fusion), channel_id=1, source_target_pairs={{0,4},{4,8},{8,12},{12,0},{1,5},{5,9},{9,13},{13,1},{2,6},{6,10},{... | collective-permute-start | bytes 786440 | tf_op jit(solution)/shard_map/ppermute | solution.py:36
  57.5 5.6 %all-to-all-done.1.line = bf16[16,8,1152]{2,1,0:T(8,128)(2,1)S(1)} async-done(((bf16[16,8,1152]{2,1,0:T(8,128)(2,1)}), bf16[16,8,1152]{2,1,0:T(8,128)(2,1)S(1)}, u32[]{:S(2)}, u32[]{:S(2)}) %all-to-all-start.1) | async-done | bytes 294944 | tf_op jit(solution)/shard_map/all_to_all | solution.py:28
  63.1 0.9 %shard_map.88 = bf16[32,8,1152]{2,1,0:T(8,128)(2,1)} custom-call(bf16[16,8,1152]{2,1,0:T(8,128)(2,1)S(1)} %all-to-all-done.1.line), custom_call_target="tpu_custom_call" | custom-call | bytes 589824 | tf_op jit(solution)/shard_map/pallas_call | solution.py:219
  64.0 12.0 %all-to-all-start.2 = ((bf16[32,8,1152]{2,1,0:T(8,128)(2,1)}), bf16[32,8,1152]{2,1,0:T(8,128)(2,1)S(1)}, u32[]{:S(2)}, u32[]{:S(2)}) async-start(bf16[32,8,1152]{2,1,0:T(8,128)(2,1)} %shard_map.88), calls=%async_computation.2 | async-start | bytes 1179648 | tf_op jit(solution)/shard_map/all_to_all | solution.py:28
  76.1 2.1 %collective-permute-start.8 = (bf16[8,128,256]{2,1,0:T(8,128)(2,1)S(1)}, bf16[8,128,256]{2,1,0:T(8,128)(2,1)S(1)}, u32[]{:S(2)}, u32[]{:S(2)}) collective-permute-start(bf16[8,128,256]{2,1,0:T(8,128)(2,1)S(1)} %constant_dynamic-update-slice_fusion.5.rest_1_), channel_id=1, source_target_pairs={{0,16},{16,0},{1,17},{17,1},{2,18},{18,2},{3,19},{19,3},{4,20},{20... | collective-permute-start | bytes 1572872 | tf_op jit(solution)/shard_map/ppermute | solution.py:32
  78.3 2.2 %collective-permute-start.7 = (bf16[8,128,256]{2,1,0:T(8,128)(2,1)S(1)}, bf16[8,128,256]{2,1,0:T(8,128)(2,1)S(1)}, u32[]{:S(2)}, u32[]{:S(2)}) collective-permute-start(bf16[8,128,256]{2,1,0:T(8,128)(2,1)S(1)} %constant_dynamic-update-slice_fusion.rest_0_), channel_id=1, source_target_pairs={{0,16},{16,0},{1,17},{17,1},{2,18},{18,2},{3,19},{19,3},{4,20},{20... | collective-permute-start | bytes 1572872 | tf_op jit(solution)/shard_map/ppermute | solution.py:32
  80.5 1.6 %collective-permute-done.7.rest_2_ = bf16[8,128,256]{2,1,0:T(8,128)(2,1)S(1)} collective-permute-done((bf16[8,128,256]{2,1,0:T(8,128)(2,1)S(1)}, bf16[8,128,256]{2,1,0:T(8,128)(2,1)S(1)}, u32[]{:S(2)}, u32[]{:S(2)}) %collective-permute-start.7) | collective-permute-done | bytes 524320 | tf_op jit(solution)/shard_map/ppermute | solution.py:32
  82.1 4.0 %shard_map.89 = (bf16[192,512]{1,0:T(8,128)(2,1)}, bf16[192,2048]{1,0:T(8,128)(2,1)}) custom-call(s32[4]{0:T(128)S(1)} %pad_add_fusion.place, bf16[192,2048]{1,0:T(8,128)(2,1)S(1)} %copy-done.1, f32[192,128]{1,0:T(8,128)S(1)} %get-tuple-element.26.inv_rms, f32[1,2048]{1,0:T(1,128)S(1)} %bitcast.21, bf16[192,512]{1,0:T(8,128)(2,1)S(1)} %copy-done.3, ...), custom_call_target="tpu_custom_call" | custom-call | bytes 6373408 | tf_op jit(solution)/shard_map/pallas_call | solution.py:219
  86.1 2.2 %all-to-all-done.2.blocks = bf16[32,8,1152]{2,1,0:T(8,128)(2,1)S(1)} async-done(((bf16[32,8,1152]{2,1,0:T(8,128)(2,1)}), bf16[32,8,1152]{2,1,0:T(8,128)(2,1)S(1)}, u32[]{:S(2)}, u32[]{:S(2)}) %all-to-all-start.2) | async-done | bytes 589856 | tf_op jit(solution)/shard_map/all_to_all | solution.py:28
  88.3 1.9 %shard_map.90 = (f32[128,512]{1,0:T(8,128)}, f32[16,128]{1,0:T(8,128)}) custom-call(s32[4]{0:T(128)S(1)} %pad_add_fusion.place, bf16[32,8,1152]{2,1,0:T(8,128)(2,1)S(1)} %all-to-all-done.2.blocks, f32[16,128]{1,0:T(8,128)S(1)} %bitcast.22), custom_call_target="tpu_custom_call" | custom-call | bytes 1196064 | tf_op jit(solution)/shard_map/pallas_call | solution.py:219
  (29 shorter events, 0.8 us)
Async XLA Ops:
  0.6 18.7 %copy-start = (f32[1,512]{1,0:T(1,128)S(1)}, f32[1,512]{1,0:T(1,128)}, u32[]{:S(2)}) copy-start(f32[1,512]{1,0:T(1,128)} %param.8) | copy-start | bytes 6148
  3.4 11.1 %collective-permute-start = (bf16[16,16,2048]{2,1,0:T(8,128)(2,1)S(1)}, bf16[16,16,2048]{2,1,0:T(8,128)(2,1)S(1)}, u32[]{:S(2)}, u32[]{:S(2)}) collective-permute-start(bf16[16,16,2048]{2,1,0:T(8,128)(2,1)S(1)} %get-tuple-element.22), channel_id=1, source_target_pairs={{0,16},{16,0},{1,17},{17,1},{2,18},{18,2},{3,19},{19,3},{4,20},{20... | collective-permute-start | bytes 3145736 | tf_op jit(solution)/shard_map/ppermute | solution.py:32
  12.2 0.9 %copy-start.2 = (bf16[192,512]{1,0:T(8,128)(2,1)S(1)}, bf16[192,512]{1,0:T(8,128)(2,1)}, u32[]{:S(2)}) copy-start(bf16[192,512]{1,0:T(8,128)(2,1)} %key_grad.3) | copy-start | bytes 589828
  15.5 3.9 %copy-start.5 = (s32[128,512]{1,0:T(8,128)S(1)}, s32[128,512]{1,0:T(8,128)}, u32[]{:S(2)}) copy-start(s32[128,512]{1,0:T(8,128)} %param.7) | copy-start | bytes 786436
  15.6 23.1 %all-to-all-start = ((bf16[16,16,2048]{2,1,0:T(8,128)(2,1)}), bf16[16,16,2048]{2,1,0:T(8,128)(2,1)S(1)}, u32[]{:S(2)}, u32[]{:S(2)}) async-start(bf16[16,16,2048]{2,1,0:T(8,128)(2,1)} %shard_map.86), calls=%async_computation | async-start | bytes 2097152 | tf_op jit(solution)/shard_map/all_to_all | solution.py:28
  19.4 14.6 %collective-permute-start.1 = (bf16[128,256]{1,0:T(8,128)(2,1)S(1)}, bf16[128,256]{1,0:T(8,128)(2,1)S(1)}, u32[]{:S(2)}, u32[]{:S(2)}) collective-permute-start(bf16[128,256]{1,0:T(8,128)(2,1)S(1)} %get-tuple-element.23.shard), channel_id=1, source_target_pairs={{0,387},{16,403},{32,419},{48,435},{64,451},{80,467},{96,483},{112... | collective-permute-start | bytes 196616 | tf_op jit(solution)/shard_map/ppermute | solution.py:48
  28.3 6.0 %collective-permute-start.2 = (bf16[128,256]{1,0:T(8,128)(2,1)S(1)}, bf16[128,256]{1,0:T(8,128)(2,1)S(1)}, u32[]{:S(2)}, u32[]{:S(2)}) collective-permute-start(bf16[128,256]{1,0:T(8,128)(2,1)S(1)} %get-tuple-element.23.shard), channel_id=1, source_target_pairs={{0,2},{16,402},{32,34},{48,434},{64,66},{80,466},{96,98},{112,498}... | collective-permute-start | bytes 196616 | tf_op jit(solution)/shard_map/ppermute | solution.py:48
  31.4 7.3 %collective-permute-start.3 = (bf16[128,256]{1,0:T(8,128)(2,1)S(1)}, bf16[128,256]{1,0:T(8,128)(2,1)S(1)}, u32[]{:S(2)}, u32[]{:S(2)}) collective-permute-start(bf16[128,256]{1,0:T(8,128)(2,1)S(1)} %get-tuple-element.23.shard), channel_id=1, source_target_pairs={{0,1},{16,17},{32,33},{48,49},{64,65},{80,81},{96,97},{112,113},{1... | collective-permute-start | bytes 196616 | tf_op jit(solution)/shard_map/ppermute | solution.py:48
  40.3 22.8 %all-to-all-start.1 = ((bf16[16,8,1152]{2,1,0:T(8,128)(2,1)}), bf16[16,8,1152]{2,1,0:T(8,128)(2,1)S(1)}, u32[]{:S(2)}, u32[]{:S(2)}) async-start(bf16[16,8,1152]{2,1,0:T(8,128)(2,1)} %shard_map.87), calls=%async_computation.1 | async-start | bytes 589824 | tf_op jit(solution)/shard_map/all_to_all | solution.py:28
  50.0 32.1 %copy-start.1 = (bf16[192,2048]{1,0:T(8,128)(2,1)S(1)}, bf16[192,2048]{1,0:T(8,128)(2,1)}, u32[]{:S(2)}) copy-start(bf16[192,2048]{1,0:T(8,128)(2,1)} %tokens.1) | copy-start | bytes 2359300
  50.0 32.0 %copy-start.3 = (bf16[192,512]{1,0:T(8,128)(2,1)S(1)}, bf16[192,512]{1,0:T(8,128)(2,1)}, u32[]{:S(2)}) copy-start(bf16[192,512]{1,0:T(8,128)(2,1)} %key_grad.3) | copy-start | bytes 589828
  50.1 32.0 %copy-start.4 = (f32[2048]{0:T(1024)S(1)}, f32[2048]{0:T(1024)}, u32[]{:S(2)}) copy-start(f32[2048]{0:T(1024)} %param.6) | copy-start | bytes 24580
  50.1 7.4 %collective-permute-start.4 = (bf16[4,128,256]{2,1,0:T(8,128)(2,1)S(1)}, bf16[4,128,256]{2,1,0:T(8,128)(2,1)S(1)}, u32[]{:S(2)}, u32[]{:S(2)}) collective-permute-start(bf16[4,128,256]{2,1,0:T(8,128)(2,1)S(1)} %pad_maximum_fusion), channel_id=1, source_target_pairs={{0,12},{4,0},{8,4},{12,8},{1,13},{5,1},{9,5},{13,9},{2,14},{6,2},{... | collective-permute-start | bytes 786440 | tf_op jit(solution)/shard_map/ppermute | solution.py:36
  52.7 23.3 %collective-permute-start.5 = (bf16[4,128,256]{2,1,0:T(8,128)(2,1)S(1)}, bf16[4,128,256]{2,1,0:T(8,128)(2,1)S(1)}, u32[]{:S(2)}, u32[]{:S(2)}) collective-permute-start(bf16[4,128,256]{2,1,0:T(8,128)(2,1)S(1)} %pad_maximum_fusion), channel_id=1, source_target_pairs={{0,8},{4,12},{8,0},{12,4},{1,9},{5,13},{9,1},{13,5},{2,10},{6,14},... | collective-permute-start | bytes 786440 | tf_op jit(solution)/shard_map/ppermute | solution.py:36
  55.0 21.1 %collective-permute-start.6 = (bf16[4,128,256]{2,1,0:T(8,128)(2,1)S(1)}, bf16[4,128,256]{2,1,0:T(8,128)(2,1)S(1)}, u32[]{:S(2)}, u32[]{:S(2)}) collective-permute-start(bf16[4,128,256]{2,1,0:T(8,128)(2,1)S(1)} %pad_maximum_fusion), channel_id=1, source_target_pairs={{0,4},{4,8},{8,12},{12,0},{1,5},{5,9},{9,13},{13,1},{2,6},{6,10},{... | collective-permute-start | bytes 786440 | tf_op jit(solution)/shard_map/ppermute | solution.py:36
  64.0 24.3 %all-to-all-start.2 = ((bf16[32,8,1152]{2,1,0:T(8,128)(2,1)}), bf16[32,8,1152]{2,1,0:T(8,128)(2,1)S(1)}, u32[]{:S(2)}, u32[]{:S(2)}) async-start(bf16[32,8,1152]{2,1,0:T(8,128)(2,1)} %shard_map.88), calls=%async_computation.2 | async-start | bytes 1179648 | tf_op jit(solution)/shard_map/all_to_all | solution.py:28
  76.1 4.3 %collective-permute-start.8 = (bf16[8,128,256]{2,1,0:T(8,128)(2,1)S(1)}, bf16[8,128,256]{2,1,0:T(8,128)(2,1)S(1)}, u32[]{:S(2)}, u32[]{:S(2)}) collective-permute-start(bf16[8,128,256]{2,1,0:T(8,128)(2,1)S(1)} %constant_dynamic-update-slice_fusion.5.rest_1_), channel_id=1, source_target_pairs={{0,16},{16,0},{1,17},{17,1},{2,18},{18,2},{3,19},{19,3},{4,20},{20... | collective-permute-start | bytes 1572872 | tf_op jit(solution)/shard_map/ppermute | solution.py:32
  78.3 3.8 %collective-permute-start.7 = (bf16[8,128,256]{2,1,0:T(8,128)(2,1)S(1)}, bf16[8,128,256]{2,1,0:T(8,128)(2,1)S(1)}, u32[]{:S(2)}, u32[]{:S(2)}) collective-permute-start(bf16[8,128,256]{2,1,0:T(8,128)(2,1)S(1)} %constant_dynamic-update-slice_fusion.rest_0_), channel_id=1, source_target_pairs={{0,16},{16,0},{1,17},{17,1},{2,18},{18,2},{3,19},{19,3},{4,20},{20... | collective-permute-start | bytes 1572872 | tf_op jit(solution)/shard_map/ppermute | solution.py:32
